TPU v7x, 32 devices: a whole 2x2x4 slice. The times are simulated.
32 devices in a mesh: wide: 8 (over y, x, core), narrow: 4 (over z).
Axes of the slice: x: 2, y: 2, z: 4, core: 2. Of those that a mesh axis runs over, the one named last changes fastest.
Arguments:
- tokens: bfloat16 [4096, 2048], P(('wide', 'narrow')), may hold values from -6 to 6
- positions: int32 [4096], P(('wide', 'narrow')), may hold values from 0 to 127, as said below
- routes: int32 [4096, 8], P(('wide', 'narrow')), may hold values from 0 to 63, as said below
- cotangent: bfloat16 [4096, 2048], P(('wide', 'narrow')), may hold values from -6 to 6
- w_query: bfloat16 [2048, 2048], P(('wide', 'narrow')), may hold values from -0.125 to 0.125
- w_key: bfloat16 [2048, 2048], P(('wide', 'narrow')), may hold values from -0.125 to 0.125
- w_value: bfloat16 [2048, 2048], P(('wide', 'narrow')), may hold values from -0.125 to 0.125
- w_output: bfloat16 [2048, 2048], P(('wide', 'narrow')), may hold values from -1 to 1
- w_router: bfloat16 [2048, 64], P(('wide', 'narrow')), may hold values from -0.0625 to 0.0625
- gain_attn: bfloat16 [2048], P(('wide', 'narrow')), may hold values from 0.5 to 1.5
- gain_query: bfloat16 [2048], P(('wide', 'narrow')), may hold values from 0.5 to 1.5
- gain_key: bfloat16 [2048], P(('wide', 'narrow')), may hold values from 0.5 to 1.5
- gain_ffn: bfloat16 [2048], P(('wide', 'narrow')), may hold values from 0.5 to 1.5
- w_gate: bfloat16 [64, 2048, 1024], P('wide', 'narrow'), may hold values from -0.125 to 0.125
- w_up: bfloat16 [64, 2048, 1024], P('wide', 'narrow'), may hold values from -0.125 to 0.125
- w_down: bfloat16 [64, 1024, 2048], P('wide', 'narrow'), may hold values from -6 to 6
Outputs:
- block_out: bfloat16 [4096, 2048], P(('wide', 'narrow'))
- input_grad: bfloat16 [4096, 2048], P(('wide', 'narrow'))
- grad_w_query: float32 [2048, 2048], P(('wide', 'narrow'))
- grad_w_key: float32 [2048, 2048], P(('wide', 'narrow'))
- grad_w_value: float32 [2048, 2048], P(('wide', 'narrow'))
- grad_w_output: float32 [2048, 2048], P(('wide', 'narrow'))
- grad_w_router: float32 [2048, 64], P(('wide', 'narrow'))
- grad_gain_attn: float32 [2048], P(('wide', 'narrow'))
- grad_gain_query: float32 [2048], P(('wide', 'narrow'))
- grad_gain_key: float32 [2048], P(('wide', 'narrow'))
- grad_gain_ffn: float32 [2048], P(('wide', 'narrow'))
- grad_w_gate: float32 [64, 2048, 1024], P('wide', 'narrow')
- grad_w_up: float32 [64, 2048, 1024], P('wide', 'narrow')
- grad_w_down: float32 [64, 1024, 2048], P('wide', 'narrow')
- expert_counts: int32 [64], replicated
Inputs may be any that keep to these rules, and one draw needn't show every extreme that they name: `positions`: positions count up by one inside a document and restart at 0 where a new document begins; every block of 128 tokens begins a document. A token's 8 routes are different experts. Among the rows of one device, no expert is named by more than 24 rows, and some expert is named by exactly 24.
All inputs are finite; a program needn't handle non-finite values.
Results may differ from a plain program's by a relative error of at most 0.017.
Values may be sent and summed in bfloat16 or wider, within the bound.
No kernel may reach another device: no remote copies, remote signals or barrier semaphores. Data moves between devices by JAX's collectives and lax.ppermute only.
A program may use at most 512 MiB of HBM per device.

v0:
```python
import jax
import jax.numpy as jnp
from jax import lax
from jax.sharding import PartitionSpec as P

D = 2048
H = 16
HD = 128
E = 64
TOPK = 8
CAP = 24


EPSILON = 1e-05
THETA_BASE = 10000.0


def rms_scale(values, gain_vector):
    return (
        values
        * lax.rsqrt(jnp.mean(values * values, axis=-1, keepdims=True) + EPSILON)
        * gain_vector
    )


def softmax_rows(logits):
    shifted = logits - jnp.max(logits, axis=-1, keepdims=True)
    powers = jnp.exp(shifted)
    return powers / jnp.sum(powers, axis=-1, keepdims=True)


def rotate(values, positions):
    half_width = values.shape[-1] // 2
    frequency = THETA_BASE ** (-2.0 * jnp.arange(half_width, dtype=jnp.float32) / values.shape[-1])
    angles = positions.astype(jnp.float32)[:, None, None] * frequency[None, None, :]
    cosine = jnp.cos(angles)
    sine_part = jnp.sin(angles)
    first_half = values[..., :half_width]
    second_half = values[..., half_width:]
    return jnp.concatenate(
        [
            first_half * cosine - second_half * sine_part,
            second_half * cosine + first_half * sine_part,
        ],
        axis=-1,
    )


def silu_product(gate_value, up_value):
    return jax.nn.silu(gate_value) * up_value


def on_device(
    tokens,
    positions,
    routes,
    cotangent,
    w_query,
    w_key,
    w_value,
    w_output,
    w_router,
    gain_attn,
    gain_query,
    gain_key,
    gain_ffn,
    w_gate,
    w_up,
    w_down,
):
    dense_set = (
        lax.all_gather(w_query, ("wide", "narrow"), axis=0, tiled=True),
        lax.all_gather(w_key, ("wide", "narrow"), axis=0, tiled=True),
        lax.all_gather(w_value, ("wide", "narrow"), axis=0, tiled=True),
        lax.all_gather(w_output, ("wide", "narrow"), axis=0, tiled=True),
        lax.all_gather(w_router, ("wide", "narrow"), axis=0, tiled=True),
        lax.all_gather(gain_attn, ("wide", "narrow"), axis=0, tiled=True),
        lax.all_gather(gain_query, ("wide", "narrow"), axis=0, tiled=True),
        lax.all_gather(gain_key, ("wide", "narrow"), axis=0, tiled=True),
        lax.all_gather(gain_ffn, ("wide", "narrow"), axis=0, tiled=True),
    )
    expert_set = (
        lax.all_gather(w_gate, "narrow", axis=1, tiled=True),
        lax.all_gather(w_up, "narrow", axis=1, tiled=True),
        lax.all_gather(w_down, "narrow", axis=1, tiled=True),
    )
    query_full, key_full, value_full, output_full, router_full = (
        dense_set[0],
        dense_set[1],
        dense_set[2],
        dense_set[3],
        dense_set[4],
    )
    attn_gain = dense_set[5].astype(jnp.float32)
    query_gain = dense_set[6].astype(jnp.float32)
    key_gain = dense_set[7].astype(jnp.float32)
    ffn_gain = dense_set[8].astype(jnp.float32)
    gate_full, up_full, down_full = expert_set
    token_count = tokens.shape[0]
    score_scale = HD ** (-0.5)
    inputs = tokens.astype(jnp.float32)
    normed_attn, attn_norm_back = jax.vjp(rms_scale, inputs, attn_gain)
    normed = normed_attn.astype(jnp.bfloat16)
    query_raw = jnp.dot(normed, query_full, preferred_element_type=jnp.float32)
    key_raw = jnp.dot(normed, key_full, preferred_element_type=jnp.float32)
    values = (
        jnp.dot(normed, value_full, preferred_element_type=jnp.float32)
        .astype(jnp.bfloat16)
        .reshape(token_count, H, HD)
    )

    def norm_rotate(query_in, key_in, query_gain_in, key_gain_in):
        query_heads = rms_scale(query_in, query_gain_in).reshape(token_count, H, HD)
        key_heads = rms_scale(key_in, key_gain_in).reshape(token_count, H, HD)
        return (rotate(query_heads, positions), rotate(key_heads, positions))

    (query_turned, key_turned), rotate_back = jax.vjp(
        norm_rotate, query_raw, key_raw, query_gain, key_gain
    )
    queries = query_turned.astype(jnp.bfloat16)
    key_rows = key_turned.astype(jnp.bfloat16)
    causal = (jnp.arange(token_count)[:, None] >= jnp.arange(token_count)[None, :])[None]
    scores = (
        jnp.einsum("qhd,khd->hqk", queries, key_rows, preferred_element_type=jnp.float32)
        * score_scale
    )
    attn_probs, probs_back = jax.vjp(softmax_rows, jnp.where(causal, scores, -1e30))
    probs_low = attn_probs.astype(jnp.bfloat16)
    attended = (
        jnp.einsum("hqk,khd->qhd", probs_low, values, preferred_element_type=jnp.float32)
        .astype(jnp.bfloat16)
        .reshape(token_count, D)
    )
    residual = inputs + jnp.dot(attended, output_full, preferred_element_type=jnp.float32)
    normed_ffn_f, ffn_norm_back = jax.vjp(rms_scale, residual, ffn_gain)
    normed_ffn = normed_ffn_f.astype(jnp.bfloat16)
    router_logits = jnp.dot(normed_ffn, router_full, preferred_element_type=jnp.float32)
    router_probs, router_back = jax.vjp(softmax_rows, router_logits)
    selector = (routes[:, :, None] == jnp.arange(E, dtype=jnp.int32)[None, None, :]).astype(
        jnp.float32
    )
    gate_weights = jnp.sum(selector * router_probs[:, None, :], axis=-1)
    gate_flat = gate_weights.reshape(-1)
    flat_routes = routes.reshape(-1)
    onehot = (flat_routes[:, None] == jnp.arange(E, dtype=jnp.int32)[None, :]).astype(jnp.int32)
    slot_rank = jnp.sum((jnp.cumsum(onehot, axis=0) - onehot) * onehot, axis=1)
    local_counts = jnp.sum(onehot, axis=0)
    targets = flat_routes * CAP + slot_rank
    slot_table = (
        jnp.full((E * CAP,), -1, jnp.int32)
        .at[targets]
        .set(jnp.arange(flat_routes.shape[0], dtype=jnp.int32))
    )
    slot_live = slot_table >= 0
    pick_index = jnp.where(slot_live, slot_table, 0)
    sources = pick_index // TOPK
    outgoing = jnp.where(
        slot_live[:, None], normed_ffn[sources], jnp.zeros((), jnp.bfloat16)
    ).reshape(E, CAP, D)
    expert_rows = lax.all_to_all(outgoing, "wide", split_axis=0, concat_axis=1, tiled=True)
    gate_value = jnp.einsum(
        "erd,edf->erf", expert_rows, gate_full, preferred_element_type=jnp.float32
    )
    up_value = jnp.einsum("erd,edf->erf", expert_rows, up_full, preferred_element_type=jnp.float32)
    hidden_f, hidden_back = jax.vjp(silu_product, gate_value, up_value)
    hidden = hidden_f.astype(jnp.bfloat16)
    results = jnp.einsum(
        "erf,efd->erd", hidden, down_full, preferred_element_type=jnp.float32
    ).astype(jnp.bfloat16)
    returned = lax.all_to_all(results, "wide", split_axis=1, concat_axis=0, tiled=True).reshape(
        E * CAP, D
    )
    picked = returned[targets].reshape(token_count, TOPK, D)
    mixture = residual
    for column in range(TOPK):
        mixture = mixture + gate_weights[:, column, None] * picked[:, column].astype(jnp.float32)
    block_out = mixture.astype(jnp.bfloat16)
    expert_counts = lax.psum(local_counts, ("wide", "narrow"))
    upstream = cotangent.astype(jnp.float32)
    dense_again = (
        lax.all_gather(w_query, ("wide", "narrow"), axis=0, tiled=True),
        lax.all_gather(w_key, ("wide", "narrow"), axis=0, tiled=True),
        lax.all_gather(w_value, ("wide", "narrow"), axis=0, tiled=True),
        lax.all_gather(w_output, ("wide", "narrow"), axis=0, tiled=True),
        lax.all_gather(w_router, ("wide", "narrow"), axis=0, tiled=True),
    )
    query_back, key_back, value_back, output_back, router_back_full = dense_again
    gate_back, up_back, down_back = (
        lax.all_gather(w_gate, "narrow", axis=1, tiled=True),
        lax.all_gather(w_up, "narrow", axis=1, tiled=True),
        lax.all_gather(w_down, "narrow", axis=1, tiled=True),
    )
    gate_grads = jnp.stack(
        [
            jnp.sum(upstream * picked[:, column].astype(jnp.float32), axis=-1)
            for column in range(TOPK)
        ],
        axis=1,
    )
    prob_grads = jnp.sum(selector * gate_grads[:, :, None], axis=1)
    (logit_grads_f,) = router_back(prob_grads)
    logit_grads = logit_grads_f.astype(jnp.bfloat16)
    grad_router = jnp.einsum(
        "td,te->de", normed_ffn, logit_grads, preferred_element_type=jnp.float32
    )
    ffn_grads = jnp.einsum(
        "te,de->td", logit_grads, router_back_full, preferred_element_type=jnp.float32
    )
    outgoing_grad = (
        jnp.where(slot_live[:, None], gate_flat[pick_index][:, None] * upstream[sources], 0.0)
        .astype(jnp.bfloat16)
        .reshape(E, CAP, D)
    )
    result_grads = lax.all_to_all(outgoing_grad, "wide", split_axis=0, concat_axis=1, tiled=True)
    hidden_grads = jnp.einsum(
        "erd,efd->erf", result_grads, down_back, preferred_element_type=jnp.float32
    )
    gate_grad_f, up_grad_f = hidden_back(hidden_grads)
    gate_value_grads = gate_grad_f.astype(jnp.bfloat16)
    up_value_grads = up_grad_f.astype(jnp.bfloat16)
    row_grads = (
        jnp.einsum("erf,edf->erd", gate_value_grads, gate_back, preferred_element_type=jnp.float32)
        + jnp.einsum("erf,edf->erd", up_value_grads, up_back, preferred_element_type=jnp.float32)
    ).astype(jnp.bfloat16)
    returned_grad = lax.all_to_all(
        row_grads, "wide", split_axis=1, concat_axis=0, tiled=True
    ).reshape(E * CAP, D)
    picked_grad = returned_grad[targets].reshape(token_count, TOPK, D)
    for column in range(TOPK):
        ffn_grads = ffn_grads + picked_grad[:, column].astype(jnp.float32)
    expert_grads = (
        lax.psum_scatter(
            jnp.einsum(
                "erd,erf->edf", expert_rows, gate_value_grads, preferred_element_type=jnp.float32
            ).astype(jnp.bfloat16),
            "narrow",
            scatter_dimension=1,
            tiled=True,
        ).astype(jnp.float32),
        lax.psum_scatter(
            jnp.einsum(
                "erd,erf->edf", expert_rows, up_value_grads, preferred_element_type=jnp.float32
            ).astype(jnp.bfloat16),
            "narrow",
            scatter_dimension=1,
            tiled=True,
        ).astype(jnp.float32),
        lax.psum_scatter(
            jnp.einsum(
                "erf,erd->efd", hidden, result_grads, preferred_element_type=jnp.float32
            ).astype(jnp.bfloat16),
            "narrow",
            scatter_dimension=1,
            tiled=True,
        ).astype(jnp.float32),
    )
    residual_part, ffn_gain_grad = ffn_norm_back(ffn_grads)
    residual_grads = upstream + residual_part
    branch_grads = residual_grads.astype(jnp.bfloat16)
    grad_output = jnp.einsum(
        "td,te->de", attended, branch_grads, preferred_element_type=jnp.float32
    )
    attended_grads = (
        jnp.einsum("te,de->td", branch_grads, output_back, preferred_element_type=jnp.float32)
        .astype(jnp.bfloat16)
        .reshape(token_count, H, HD)
    )
    prob_grads_attn = jnp.einsum(
        "qhd,khd->hqk", attended_grads, values, preferred_element_type=jnp.float32
    )
    value_grads = (
        jnp.einsum("hqk,qhd->khd", probs_low, attended_grads, preferred_element_type=jnp.float32)
        .astype(jnp.bfloat16)
        .reshape(token_count, D)
    )
    (score_grad_f,) = probs_back(prob_grads_attn)
    score_grads = jnp.where(causal, score_grad_f, 0.0).astype(jnp.bfloat16)
    query_grads = (
        jnp.einsum("hqk,khd->qhd", score_grads, key_rows, preferred_element_type=jnp.float32)
        * score_scale
    )
    key_grads = (
        jnp.einsum("hqk,qhd->khd", score_grads, queries, preferred_element_type=jnp.float32)
        * score_scale
    )
    query_raw_f, key_raw_f, query_gain_grad, key_gain_grad = rotate_back((query_grads, key_grads))
    query_raw_grads = query_raw_f.astype(jnp.bfloat16)
    key_raw_grads = key_raw_f.astype(jnp.bfloat16)
    grad_query = jnp.einsum(
        "td,te->de", normed, query_raw_grads, preferred_element_type=jnp.float32
    )
    grad_key = jnp.einsum("td,te->de", normed, key_raw_grads, preferred_element_type=jnp.float32)
    grad_value = jnp.einsum("td,te->de", normed, value_grads, preferred_element_type=jnp.float32)
    normed_grads = jnp.einsum(
        "te,de->td", query_raw_grads, query_back, preferred_element_type=jnp.float32
    )
    normed_grads = normed_grads + jnp.einsum(
        "te,de->td", key_raw_grads, key_back, preferred_element_type=jnp.float32
    )
    normed_grads = normed_grads + jnp.einsum(
        "te,de->td", value_grads, value_back, preferred_element_type=jnp.float32
    )
    input_part, attn_gain_grad = attn_norm_back(normed_grads)
    input_grad = (residual_grads + input_part).astype(jnp.bfloat16)
    dense_grads = (
        lax.psum_scatter(grad_query, ("wide", "narrow"), scatter_dimension=0, tiled=True),
        lax.psum_scatter(grad_key, ("wide", "narrow"), scatter_dimension=0, tiled=True),
        lax.psum_scatter(grad_value, ("wide", "narrow"), scatter_dimension=0, tiled=True),
        lax.psum_scatter(grad_output, ("wide", "narrow"), scatter_dimension=0, tiled=True),
        lax.psum_scatter(grad_router, ("wide", "narrow"), scatter_dimension=0, tiled=True),
        lax.psum_scatter(attn_gain_grad, ("wide", "narrow"), scatter_dimension=0, tiled=True),
        lax.psum_scatter(query_gain_grad, ("wide", "narrow"), scatter_dimension=0, tiled=True),
        lax.psum_scatter(key_gain_grad, ("wide", "narrow"), scatter_dimension=0, tiled=True),
        lax.psum_scatter(ffn_gain_grad, ("wide", "narrow"), scatter_dimension=0, tiled=True),
    )
    return (block_out, input_grad) + tuple(dense_grads) + tuple(expert_grads) + (expert_counts,)


def solution(mesh):
    in_specs = (
        P(("wide", "narrow"), None),
        P(("wide", "narrow")),
        P(("wide", "narrow"), None),
        P(("wide", "narrow"), None),
        P(("wide", "narrow"), None),
        P(("wide", "narrow"), None),
        P(("wide", "narrow"), None),
        P(("wide", "narrow"), None),
        P(("wide", "narrow"), None),
        P(("wide", "narrow")),
        P(("wide", "narrow")),
        P(("wide", "narrow")),
        P(("wide", "narrow")),
        P("wide", "narrow", None),
        P("wide", "narrow", None),
        P("wide", "narrow", None),
    )
    out_specs = (
        P(("wide", "narrow"), None),
        P(("wide", "narrow"), None),
        P(("wide", "narrow"), None),
        P(("wide", "narrow"), None),
        P(("wide", "narrow"), None),
        P(("wide", "narrow"), None),
        P(("wide", "narrow"), None),
        P(("wide", "narrow")),
        P(("wide", "narrow")),
        P(("wide", "narrow")),
        P(("wide", "narrow")),
        P("wide", "narrow", None),
        P("wide", "narrow", None),
        P("wide", "narrow", None),
        P(),
    )
    return jax.shard_map(
        on_device, mesh=mesh, in_specs=in_specs, out_specs=out_specs, check_vma=False
    )
```

profile of v0, /device:TPU:0, one launch (start us, length us, event | category | flops | bytes accessed | tf_op | source)
XLA Modules:
  0.0 5542.1 jit_solution(3920292845983110641)
XLA Ops:
  13.3 42.5 all-reduce.13
  56.1 18.0 reduce-window.6
  97.5 72.8 %all-gather.12.cloned.1.call-done = bf16[2048,2048]{1,0:T(8,128)(2,1)} async-done(((bf16[64,2048]{1,0:T(8,128)(2,1)}), bf16[2048,2048]{1,0:T(8,128)(2,1)}) %all-gather.12.cloned.1.call-update) | async-done | bytes 8388624 | tf_op jit(solution)/shard_map/all_gather | solution.py:73
  180.4 69.0 %all-gather.8.cloned.1.call-done = bf16[2048,2048]{1,0:T(8,128)(2,1)} async-done(((bf16[64,2048]{1,0:T(8,128)(2,1)}), bf16[2048,2048]{1,0:T(8,128)(2,1)}) %all-gather.8.cloned.1.call-update) | async-done | bytes 8388624 | tf_op jit(solution)/shard_map/all_gather | solution.py:74
  255.3 72.8 %all-gather.14.cloned.1.call-done = bf16[2048,2048]{1,0:T(8,128)(2,1)} async-done(((bf16[64,2048]{1,0:T(8,128)(2,1)}), bf16[2048,2048]{1,0:T(8,128)(2,1)}) %all-gather.14.cloned.1.call-update) | async-done | bytes 8388624 | tf_op jit(solution)/shard_map/all_gather | solution.py:75
  345.4 74.5 %all_to_all.66 = bf16[64,24,2048]{2,1,0:T(8,128)(2,1)S(1)} all-to-all(bf16[64,24,2048]{2,1,0:T(8,128)(2,1)S(1)} %broadcast_select_fusion), channel_id=1, replica_groups=mesh['wide'=8,'narrow'=4] {'wide'}, dimensions={0} | all-to-all | bytes 12582912 | tf_op jit(solution)/shard_map/all_to_all | solution.py:160
  423.2 466.4 %all-gather.16.cloned.1.call-done = bf16[8,2048,1024]{2,1,0:T(8,128)(2,1)} async-done(((bf16[8,512,1024]{2,1,0:T(8,128)(2,1)}), bf16[8,2048,1024]{2,1,0:T(8,128)(2,1)}) %all-gather.16.cloned.1.call-update) | async-done | bytes 33554448 | tf_op jit(solution)/shard_map/all_gather | solution.py:83
  889.6 23.4 fusion.89
  913.0 537.6 %all-gather.18.cloned.1.call-done = bf16[8,2048,1024]{2,1,0:T(8,128)(2,1)} async-done(((bf16[8,512,1024]{2,1,0:T(8,128)(2,1)}), bf16[8,2048,1024]{2,1,0:T(8,128)(2,1)}) %all-gather.18.cloned.1.call-update) | async-done | bytes 33554448 | tf_op jit(solution)/shard_map/all_gather | solution.py:84
  1450.6 27.2 multiply_convert_fusion.1
  1477.8 534.0 %all-gather.20.cloned.1.call-done = bf16[8,1024,2048]{2,1,0:T(8,128)(2,1)} async-done(((bf16[8,256,2048]{2,1,0:T(8,128)(2,1)}), bf16[8,1024,2048]{2,1,0:T(8,128)(2,1)}) %all-gather.20.cloned.1.call-update) | async-done | bytes 33554448 | tf_op jit(solution)/shard_map/all_gather | solution.py:85
  2011.8 17.8 convolution_convert_fusion.3
  2051.5 71.6 %all_gather.52 = bf16[2048,64]{1,0:T(8,128)(2,1)S(1)} all-gather(bf16[64,64]{1,0:T(8,128)(2,1)S(1)} %copy-done.68), channel_id=1, replica_groups=mesh['wide'=8,'narrow'=4] {'wide','narrow'}, dimensions={0}, use_global_device_ids=true | all-gather | bytes 270336 | tf_op jit(solution)/shard_map/all_gather | solution.py:76
  2146.7 21.3 fusion.84
  2183.9 74.1 %all_to_all.67 = bf16[64,24,2048]{2,1,0:T(8,128)(2,1)S(1)} all-to-all(bf16[64,24,2048]{2,1,0:T(8,128)(2,1)S(1)} %select_convert_fusion), channel_id=1, replica_groups=mesh['wide'=8,'narrow'=4] {'wide'}, dimensions={0} | all-to-all | bytes 12582912 | tf_op jit(solution)/shard_map/all_to_all | solution.py:214
  2277.3 22.9 multiply_convert_fusion
  2300.2 17.0 convolution_convert_fusion.1
  2317.3 17.5 convolution_convert_fusion.2
  2334.8 21.0 fusion.90
  2355.8 21.2 add_convert_fusion
  2392.7 69.8 %all-to-all-done.3 = bf16[8,192,2048]{2,0,1:T(8,128)(2,1)} async-done(((bf16[8,192,2048]{2,0,1:T(8,128)(2,1)}), bf16[8,192,2048]{2,0,1:T(8,128)(2,1)}, u32[]{:S(2)}, u32[]{:S(2)}) %all-to-all-start.3) | async-done | bytes 6291488 | tf_op jit(solution)/shard_map/all_to_all | solution.py:225
  2484.5 21.1 fusion.83
  2567.2 42.3 psum.7
  2634.7 44.7 all-reduce.12
  2682.9 144.9 %reduce-scatter.23.cloned.1.call-done = bf16[8,256,2048]{2,1,0:T(8,128)(2,1)} async-done(((bf16[8,1024,2048]{2,1,0:T(8,128)(2,1)}), bf16[8,256,2048]{2,1,0:T(8,128)(2,1)}) %reduce-scatter.23.cloned.1.call-update) | async-done | bytes 8388624 | tf_op jit(solution)/shard_map/reduce_scatter | solution.py:248
  2839.6 543.4 %reduce-scatter.21.cloned.1.call-done = bf16[8,512,1024]{2,1,0:T(8,128)(2,1)} async-done(((bf16[8,2048,1024]{2,1,0:T(8,128)(2,1)}), bf16[8,512,1024]{2,1,0:T(8,128)(2,1)}) %reduce-scatter.21.cloned.1.call-update) | async-done | bytes 8388624 | tf_op jit(solution)/shard_map/reduce_scatter | solution.py:240
  3394.9 543.1 %reduce-scatter.19.cloned.1.call-done = bf16[8,512,1024]{2,1,0:T(8,128)(2,1)} async-done(((bf16[8,2048,1024]{2,1,0:T(8,128)(2,1)}), bf16[8,512,1024]{2,1,0:T(8,128)(2,1)}) %reduce-scatter.19.cloned.1.call-update) | async-done | bytes 8388624 | tf_op jit(solution)/shard_map/reduce_scatter | solution.py:232
  3949.7 127.3 %reduce-scatter.17.cloned.1.call-done = f32[64,64]{1,0:T(8,128)} async-done(((f32[2048,64]{1,0:T(8,128)}), f32[64,64]{1,0:T(8,128)}) %reduce-scatter.17.cloned.1.call-update) | async-done | bytes 16400 | tf_op jit(solution)/shard_map/reduce_scatter | solution.py:310
  4077.0 363.5 %reduce-scatter.15.cloned.1.call-done = f32[64,2048]{1,0:T(8,128)} async-done(((f32[2048,2048]{1,0:T(8,128)}), f32[64,2048]{1,0:T(8,128)}) %reduce-scatter.15.cloned.1.call-update) | async-done | bytes 524304 | tf_op jit(solution)/shard_map/reduce_scatter | solution.py:309
  4440.5 365.0 %reduce-scatter.13.cloned.1.call-done = f32[64,2048]{1,0:T(8,128)} async-done(((f32[2048,2048]{1,0:T(8,128)}), f32[64,2048]{1,0:T(8,128)}) %reduce-scatter.13.cloned.1.call-update) | async-done | bytes 524304 | tf_op jit(solution)/shard_map/reduce_scatter | solution.py:308
  4805.6 364.9 %reduce-scatter.11.cloned.1.call-done = f32[64,2048]{1,0:T(8,128)} async-done(((f32[2048,2048]{1,0:T(8,128)}), f32[64,2048]{1,0:T(8,128)}) %reduce-scatter.11.cloned.1.call-update) | async-done | bytes 524304 | tf_op jit(solution)/shard_map/reduce_scatter | solution.py:307
  5170.5 364.9 %reduce-scatter.9.cloned.1.call-done = f32[64,2048]{1,0:T(8,128)} async-done(((f32[2048,2048]{1,0:T(8,128)}), f32[64,2048]{1,0:T(8,128)}) %reduce-scatter.9.cloned.1.call-update) | async-done | bytes 524304 | tf_op jit(solution)/shard_map/reduce_scatter | solution.py:306
  (352 shorter events, 308.8 us)
Async XLA Ops:
  7.2 84.2 %all-gather.10.cloned.1.call-start = ((), (), s32[]{:S(2)}) async-start(), calls=%async_computation.13 | async-start | bytes 8650752 | tf_op jit(solution)/shard_map/all_gather | solution.py:72
  7.9 162.4 %all-gather.12.cloned.1.call-start = ((), (), s32[]{:S(2)}) async-start(), calls=%async_computation.14 | async-start | bytes 8650752 | tf_op jit(solution)/shard_map/all_gather | solution.py:73
  8.7 240.7 %all-gather.8.cloned.1.call-start = ((), (), s32[]{:S(2)}) async-start(), calls=%async_computation.12 | async-start | bytes 8650752 | tf_op jit(solution)/shard_map/all_gather | solution.py:74
  9.4 318.7 %all-gather.14.cloned.1.call-start = ((), (), s32[]{:S(2)}) async-start(), calls=%async_computation.15 | async-start | bytes 8650752 | tf_op jit(solution)/shard_map/all_gather | solution.py:75
  10.0 879.6 %all-gather.16.cloned.1.call-start = ((), (), s32[]{:S(2)}) async-start(), calls=%async_computation.16 | async-start | bytes 41943040 | tf_op jit(solution)/shard_map/all_gather | solution.py:83
  10.6 1440.1 %all-gather.18.cloned.1.call-start = ((), (), s32[]{:S(2)}) async-start(), calls=%async_computation.17 | async-start | bytes 41943040 | tf_op jit(solution)/shard_map/all_gather | solution.py:84
  11.2 69.8 %copy-start.2 = (bf16[128,2048]{1,0:T(8,128)(2,1)S(1)}, bf16[128,2048]{1,0:T(8,128)(2,1)}, u32[]{:S(2)}) copy-start(bf16[128,2048]{1,0:T(8,128)(2,1)} %param.16) | copy-start | bytes 1572868
  11.2 2000.6 %all-gather.20.cloned.1.call-start = ((), (), s32[]{:S(2)}) async-start(), calls=%async_computation.18 | async-start | bytes 41943040 | tf_op jit(solution)/shard_map/all_gather | solution.py:85
  55.8 193.5 %copy-start.33 = (f32[2048]{0:T(1024)}, f32[2048]{0:T(1024)S(1)}, u32[]{:S(2)}) copy-start(f32[2048]{0:T(1024)S(1)} %convert_element_type.228) | copy-start | bytes 24580
  55.8 119.3 %copy-start.50 = (f32[2048]{0:T(1024)}, f32[2048]{0:T(1024)S(1)}, u32[]{:S(2)}) copy-start(f32[2048]{0:T(1024)S(1)} %convert_element_type.233) | copy-start | bytes 24580
  55.9 277.0 %copy-start.56 = (f32[2048]{0:T(1024)}, f32[2048]{0:T(1024)S(1)}, u32[]{:S(2)}) copy-start(f32[2048]{0:T(1024)S(1)} %convert_element_type.237) | copy-start | bytes 24580
  80.4 98.2 %copy-start.46 = (pred[128,128]{0,1:T(8,128)(4,1)}, pred[128,128]{0,1:T(8,128)(4,1)S(1)}, u32[]{:S(2)}) copy-start(pred[128,128]{0,1:T(8,128)(4,1)S(1)} %iota_compare_fusion.3) | copy-start | bytes 49156
  81.2 168.1 %copy-start.52 = (f32[128]{0:T(128)}, f32[128]{0:T(128)S(1)}, u32[]{:S(2)}) copy-start(f32[128]{0:T(128)S(1)} %fusion.62) | copy-start | bytes 1540
  81.5 95.7 %copy-start.41 = (f32[128,64]{1,0:T(8,128)}, f32[128,64]{1,0:T(8,128)S(1)}, u32[]{:S(2)}) copy-start(f32[128,64]{1,0:T(8,128)S(1)} %get-tuple-element.97) | copy-start | bytes 98308
  81.5 95.7 %copy-start.43 = (f32[128,64]{1,0:T(8,128)}, f32[128,64]{1,0:T(8,128)S(1)}, u32[]{:S(2)}) copy-start(f32[128,64]{1,0:T(8,128)S(1)} %get-tuple-element.98) | copy-start | bytes 98308
  96.1 78.9 %copy-start.84 = (f32[128]{0:T(128)}, f32[128]{0:T(128)S(1)}, u32[]{:S(2)}) copy-start(f32[128]{0:T(128)S(1)} %get-tuple-element.99) | copy-start | bytes 1540
  96.2 78.9 %copy-start.71 = (f32[128]{0:T(128)}, f32[128]{0:T(128)S(1)}, u32[]{:S(2)}) copy-start(f32[128]{0:T(128)S(1)} %fusion.63) | copy-start | bytes 1540
  180.2 73.9 %copy-start.10 = (f32[16,128,128]{1,2,0:T(8,128)}, f32[16,128,128]{1,2,0:T(8,128)S(1)}, u32[]{:S(2)}) copy-start(f32[16,128,128]{1,2,0:T(8,128)S(1)} %get-tuple-element.104) | copy-start | bytes 3145732
  180.2 73.9 %copy-start.54 = (f32[16,128]{1,0:T(8,128)}, f32[16,128]{1,0:T(8,128)S(1)}, u32[]{:S(2)}) copy-start(f32[16,128]{1,0:T(8,128)S(1)} %get-tuple-element.103) | copy-start | bytes 24580
  180.4 73.7 %copy-start.58 = (f32[16,128]{1,0:T(8,128)}, f32[16,128]{1,0:T(8,128)S(1)}, u32[]{:S(2)}) copy-start(f32[16,128]{1,0:T(8,128)S(1)} %fusion.44) | copy-start | bytes 24580
  255.3 77.6 %copy-start.31 = (bf16[16,128,128]{2,1,0:T(8,128)(2,1)}, bf16[16,128,128]{2,1,0:T(8,128)(2,1)S(1)}, u32[]{:S(2)}) copy-start(bf16[16,128,128]{2,1,0:T(8,128)(2,1)S(1)} %convolution_convert_fusion.7) | copy-start | bytes 1572868
  334.0 1789.0 %copy-start = (bf16[128,2048]{1,0:T(8,128)(2,1)}, bf16[128,2048]{1,0:T(8,128)(2,1)S(1)}, u32[]{:S(2)}) copy-start(bf16[128,2048]{1,0:T(8,128)(2,1)S(1)} %multiply_convert_fusion.2) | copy-start | bytes 1572868
  2038.5 86.1 %all-to-all-start.1 = ((bf16[8,192,2048]{2,0,1:T(8,128)(2,1)}), bf16[8,192,2048]{2,0,1:T(8,128)(2,1)}, u32[]{:S(2)}, u32[]{:S(2)}) async-start(bf16[8,192,2048]{2,0,1:T(8,128)(2,1)} %copy.206), calls=%async_computation.1 | async-start | bytes 12582912 | tf_op jit(solution)/shard_map/all_to_all | solution.py:170
  2043.3 784.4 %reduce-scatter.23.cloned.1.call-start = ((), (), s32[]{:S(2)}) async-start(), calls=%async_computation.26 | async-start | bytes 41943040 | tf_op jit(solution)/shard_map/reduce_scatter | solution.py:248
  2277.2 1105.8 %reduce-scatter.21.cloned.1.call-start = ((), (), s32[]{:S(2)}) async-start(), calls=%async_computation.25 | async-start | bytes 41943040 | tf_op jit(solution)/shard_map/reduce_scatter | solution.py:240
  2317.2 1620.8 %reduce-scatter.19.cloned.1.call-start = ((), (), s32[]{:S(2)}) async-start(), calls=%async_computation.24 | async-start | bytes 41943040 | tf_op jit(solution)/shard_map/reduce_scatter | solution.py:232
  2386.0 76.5 %all-to-all-start.3 = ((bf16[8,192,2048]{2,0,1:T(8,128)(2,1)}), bf16[8,192,2048]{2,0,1:T(8,128)(2,1)}, u32[]{:S(2)}, u32[]{:S(2)}) async-start(bf16[8,192,2048]{2,0,1:T(8,128)(2,1)} %copy.218), calls=%async_computation.3 | async-start | bytes 12582912 | tf_op jit(solution)/shard_map/all_to_all | solution.py:225
  2390.9 1686.1 %reduce-scatter.17.cloned.1.call-start = ((), (), s32[]{:S(2)}) async-start(), calls=%async_computation.23 | async-start | bytes 1081344 | tf_op jit(solution)/shard_map/reduce_scatter | solution.py:310
  2392.5 2048.0 %reduce-scatter.15.cloned.1.call-start = ((), (), s32[]{:S(2)}) async-start(), calls=%async_computation.22 | async-start | bytes 17301504 | tf_op jit(solution)/shard_map/reduce_scatter | solution.py:309
  2517.4 2288.2 %reduce-scatter.13.cloned.1.call-start = ((), (), s32[]{:S(2)}) async-start(), calls=%async_computation.21 | async-start | bytes 17301504 | tf_op jit(solution)/shard_map/reduce_scatter | solution.py:308
  2535.3 2635.1 %reduce-scatter.11.cloned.1.call-start = ((), (), s32[]{:S(2)}) async-start(), calls=%async_computation.20 | async-start | bytes 17301504 | tf_op jit(solution)/shard_map/reduce_scatter | solution.py:307
  2552.8 2982.6 %reduce-scatter.9.cloned.1.call-start = ((), (), s32[]{:S(2)}) async-start(), calls=%async_computation.19 | async-start | bytes 17301504 | tf_op jit(solution)/shard_map/reduce_scatter | solution.py:306
  (81 other events, 558.6 us)
Sparse Core Ops, SparseCore 0:
  10.9 80.3 all-gather.9
  94.3 75.9 all-gather.11
  173.2 76.0 all-gather.7
  252.1 75.9 all-gather.13
  329.6 559.9 all-gather.15
  891.0 559.5 all-gather.17
  1452.2 559.5 all-gather.19
  2277.3 550.3 reduce-scatter.22
  2830.2 552.7 reduce-scatter.20
  3385.2 552.7 reduce-scatter.18
  3940.9 136.0 reduce-scatter.16
  4079.7 360.7 reduce-scatter.14
  4443.4 362.1 reduce-scatter.12
  4808.3 362.1 reduce-scatter.10
  5173.2 362.1 reduce-scatter.8
where the time goes:
time: 5550 us; the launch traced here: 5540 us
  waiting for transfers between devices  4650 us (84%)
  blocking collectives  350 us (6%)
  matrix products  269 us (5%)
  local copies, waits for them, and re-layouts  151 us (3%)
  other arithmetic  91.4 us (2%)
    reduce_scatter x1, waiting for transfers between devices, on_device(): lax.psum_scatter(jnp.einsum('erd,erf->edf', expert_rows, up_value_grads,...  543 us
    reduce_scatter x1, waiting for transfers between devices, on_device(): lax.psum_scatter(jnp.einsum('erd,erf->edf', expert_rows, gate_value_grads...  543 us
    all_gather x1, waiting for transfers between devices, on_device(): lax.all_gather(w_up, 'narrow', axis=1, tiled=True)  538 us
    all_gather x1, waiting for transfers between devices, on_device(): lax.all_gather(w_down, 'narrow', axis=1, tiled=True)  534 us
    all_gather x1, waiting for transfers between devices, on_device(): lax.all_gather(w_gate, 'narrow', axis=1, tiled=True)  466 us
    reduce_scatter x1, waiting for transfers between devices, on_device(): lax.psum_scatter(grad_value, ('wide', 'narrow'), scatter_dimension=0, til...  365 us
    reduce_scatter x1, waiting for transfers between devices, on_device(): lax.psum_scatter(grad_key, ('wide', 'narrow'), scatter_dimension=0, tiled...  365 us
    reduce_scatter x1, waiting for transfers between devices, on_device(): lax.psum_scatter(grad_query, ('wide', 'narrow'), scatter_dimension=0, til...  365 us
  transfers between devices with their start and end apart: 17, of which 16 were waited for; matrix products, arithmetic and copies ran while one was open for 7% of the time, Pallas kernels for 0%

commit v1 on v0

v1 whole, which is shorter than its diff:
```python
import functools

import jax
import jax.numpy as jnp
from jax import lax
from jax.experimental import pallas as pl
from jax.experimental.pallas import tpu as pltpu
from jax.sharding import PartitionSpec as P

D = 2048
H = 16
HD = 128
E = 64
TOPK = 8
CAP = 24
FF = 1024
LANES = 128
EPSILON = 1e-05
THETA_BASE = 10000.0
CHUNKS = 4

BF = jnp.bfloat16
F32 = jnp.float32
VMEM_BYTES = 56 * 1024 * 1024


def matmul(a, b, dims):
    return lax.dot_general(a, b, (dims, ((), ())), preferred_element_type=F32)


def dispatch_body(pieces, rows_each, *refs):
    picks = refs[0]
    sources = refs[1 : 1 + pieces]
    out = refs[-1]
    experts = out.shape[0]
    for q in range(pieces):
        rows = matmul(picks[q, 0], sources[q][...], ((1,), (0,))).astype(BF)
        out[:, q * rows_each : (q + 1) * rows_each, :] = rows.reshape(
            experts, rows_each, rows.shape[-1]
        )


def dispatch(picks, sources, half, total_rows, buffer=None):
    pieces, pairs, slots, span = picks.shape
    width = sources[0].shape[1]
    rows_each = 2 * CAP
    experts = slots // rows_each
    in_specs = [pl.BlockSpec((pieces, 1, slots, span), lambda j: (0, j, 0, 0))]
    in_specs += [pl.BlockSpec((span, width), lambda j: (j, 0))] * pieces
    args = [picks, *sources]
    aliases = {}
    if buffer is not None:
        in_specs.append(pl.BlockSpec(memory_space=pl.ANY))
        aliases = {len(args): 0}
        args.append(buffer)
    block = pieces * rows_each
    return pl.pallas_call(
        functools.partial(dispatch_body, pieces, rows_each),
        grid=(pairs,),
        in_specs=in_specs,
        out_specs=pl.BlockSpec((experts, block, width), lambda j: (0, half * pairs + j, 0)),
        out_shape=jax.ShapeDtypeStruct((experts, total_rows, width), BF),
        input_output_aliases=aliases,
        compiler_params=pltpu.CompilerParams(vmem_limit_bytes=VMEM_BYTES),
        cost_estimate=pl.CostEstimate(
            flops=2 * pieces * pairs * slots * span * width,
            bytes_accessed=2 * pieces * pairs * (slots + span) * width,
            transcendentals=0,
        ),
        name="dispatch",
    )(*args)


def combine_body(pieces, rows_each, chunks, *refs):
    picks = refs[0]
    rows = refs[1 : 1 + chunks]
    outs = refs[1 + chunks :]
    for q in range(pieces):
        total = None
        at = 0
        for chunk in rows:
            experts = chunk.shape[0]
            part = chunk[:, q * rows_each : (q + 1) * rows_each, :].reshape(
                experts * rows_each, chunk.shape[-1]
            )
            term = matmul(picks[q, 0, at : at + experts * rows_each, :], part, ((0,), (0,)))
            total = term if total is None else total + term
            at += experts * rows_each
        outs[q][...] = total.astype(BF)


def combine(picks, rows, half):
    pieces, pairs, slots, span = picks.shape
    rows_each = 2 * CAP
    width = rows[0].shape[-1]
    block = pieces * rows_each
    in_specs = [pl.BlockSpec((pieces, 1, slots, span), lambda j: (0, j, 0, 0))]
    for chunk in rows:
        in_specs.append(
            pl.BlockSpec((chunk.shape[0], block, width), lambda j: (0, half * pairs + j, 0))
        )
    return pl.pallas_call(
        functools.partial(combine_body, pieces, rows_each, len(rows)),
        grid=(pairs,),
        in_specs=in_specs,
        out_specs=[pl.BlockSpec((span, width), lambda j: (j, 0))] * pieces,
        out_shape=[jax.ShapeDtypeStruct((pairs * span, width), BF)] * pieces,
        compiler_params=pltpu.CompilerParams(vmem_limit_bytes=VMEM_BYTES),
        cost_estimate=pl.CostEstimate(
            flops=2 * pieces * pairs * slots * span * width,
            bytes_accessed=2 * pieces * pairs * (slots + span) * width,
            transcendentals=0,
        ),
        name="combine",
    )(picks, *rows)


def expert_body(parts, tiles, start, first, *refs):
    where = refs[0]
    rows_ref, ups_ref = refs[1], refs[2]
    weights = refs[3 : 3 + parts]
    down_ref = refs[3 + parts]
    rest = refs[4 + parts + (0 if first else 1) :]
    results_ref, row_grads_ref = rest[0], rest[1]
    weight_grads = rest[2 : 2 + parts]
    down_grad_ref = rest[2 + parts]
    sums = rest[3 + parts]
    down_sum = rest[4 + parts]
    mine = where[0]
    tile = pl.program_id(1)
    depth = D // parts
    width = FF // parts
    at = [pl.multiple_of((mine ^ s) * depth, depth) for s in range(parts)]

    both = None
    for s in range(parts):
        term = matmul(rows_ref[0, :, pl.ds(at[s], depth)], weights[s][0], ((1,), (0,)))
        both = term if both is None else both + term
    gate_value = both[:, :width]
    up_value = both[:, width:]
    sigma = 1.0 / (1.0 + jnp.exp(-gate_value))
    silu = gate_value * sigma
    hidden = (silu * up_value).astype(BF)
    down = down_ref[0]
    results = matmul(hidden, down, ((1,), (0,)))

    expert = where[1] + start + pl.program_id(0)
    lane = lax.broadcasted_iota(jnp.int32, (rows_ref.shape[1], LANES), 1)
    high = lane == expert
    low = lane == expert + E
    probs = rows_ref[0, :, D:].astype(F32)
    weight = jnp.sum(jnp.where(high | low, probs, 0.0), axis=1, keepdims=True)
    upstream = ups_ref[0].astype(F32)
    gate_grad = jnp.sum(upstream * results, axis=1, keepdims=True)
    results_ref[0] = (weight * results).astype(BF)
    result_grads = (weight * upstream).astype(BF)

    hidden_grads = matmul(result_grads, down, ((1,), (1,)))
    gate_value_grads = (
        hidden_grads * up_value * (sigma * (1.0 + gate_value * (1.0 - sigma)))
    ).astype(BF)
    up_value_grads = (hidden_grads * silu).astype(BF)
    both_grads = jnp.concatenate([gate_value_grads, up_value_grads], axis=1)
    down_term = matmul(hidden, result_grads, ((0,), (0,)))
    for s in range(parts):
        row_grads_ref[0, :, pl.ds(at[s], depth)] = matmul(
            both_grads, weights[s][0], ((1,), (1,))
        ).astype(BF)
    top = gate_grad.astype(BF)
    bottom = (gate_grad - top.astype(F32)).astype(BF)
    row_grads_ref[0, :, D:] = jnp.where(
        high, top.astype(F32), jnp.where(low, bottom.astype(F32), 0.0)
    ).astype(BF)

    terms = [
        matmul(rows_ref[0, :, pl.ds(at[s], depth)], both_grads, ((0,), (0,)))
        for s in range(parts)
    ]

    @pl.when(tile == 0)
    def _():
        for s in range(parts):
            sums[s] = terms[s]
        down_sum[...] = down_term

    @pl.when(tile > 0)
    def _():
        for s in range(parts):
            sums[s] += terms[s]
        down_sum[...] += down_term

    @pl.when(tile == tiles - 1)
    def _():
        for s in range(parts):
            weight_grads[s][0] = sums[s].astype(BF)
        down_grad_ref[0] = down_sum[...]


def expert_chunk(where, rows, ups, weights, down, start, down_grad):
    parts = len(weights)
    experts, depth, width2 = weights[0].shape
    local, total_rows, wide_row = rows.shape
    tile = 384
    tiles = total_rows // tile
    slice_ff = down.shape[1]
    first = down_grad is None
    in_specs = [
        pl.BlockSpec((1, tile, wide_row), lambda e, i, c: (start + e, i, 0)),
        pl.BlockSpec((1, tile, D), lambda e, i, c: (start + e, i, 0)),
    ]
    in_specs += [pl.BlockSpec((1, depth, width2), lambda e, i, c: (e, 0, 0))] * parts
    in_specs.append(pl.BlockSpec((1, slice_ff, D), lambda e, i, c: (start + e, 0, 0)))
    args = [where, rows, ups, *weights, down]
    aliases = {}
    if not first:
        in_specs.append(pl.BlockSpec(memory_space=pl.ANY))
        aliases = {len(args): 2 + parts}
        args.append(down_grad)
    out_specs = [
        pl.BlockSpec((1, tile, D), lambda e, i, c: (e, i, 0)),
        pl.BlockSpec((1, tile, wide_row), lambda e, i, c: (e, i, 0)),
    ]
    out_specs += [pl.BlockSpec((1, depth, width2), lambda e, i, c: (e, 0, 0))] * parts
    out_specs.append(pl.BlockSpec((1, slice_ff, D), lambda e, i, c: (start + e, 0, 0)))
    out_shape = [
        jax.ShapeDtypeStruct((experts, total_rows, D), BF),
        jax.ShapeDtypeStruct((experts, total_rows, wide_row), BF),
    ]
    out_shape += [jax.ShapeDtypeStruct((experts, depth, width2), BF)] * parts
    out_shape.append(jax.ShapeDtypeStruct((local, slice_ff, D), F32))
    out = pl.pallas_call(
        functools.partial(expert_body, parts, tiles, start, first),
        grid_spec=pltpu.PrefetchScalarGridSpec(
            num_scalar_prefetch=1,
            grid=(experts, tiles),
            in_specs=in_specs,
            out_specs=out_specs,
            scratch_shapes=[
                pltpu.VMEM((parts, depth, width2), F32),
                pltpu.VMEM((slice_ff, D), F32),
            ],
        ),
        out_shape=out_shape,
        input_output_aliases=aliases,
        compiler_params=pltpu.CompilerParams(vmem_limit_bytes=VMEM_BYTES),
        cost_estimate=pl.CostEstimate(
            flops=18 * experts * total_rows * D * slice_ff,
            bytes_accessed=8 * experts * total_rows * D + 18 * experts * D * slice_ff,
            transcendentals=experts * total_rows * slice_ff,
        ),
        name="experts",
    )(*args)
    return out[0], out[1], out[2 : 2 + parts], out[2 + parts]


def assemble_body(parts, width, *refs):
    where = refs[0]
    sources = refs[1 : 1 + parts]
    gate_ref, up_ref = refs[-2], refs[-1]
    for s in range(parts):
        columns = pl.ds(pl.multiple_of((where[0] ^ s) * width, width), width)
        gate_ref[0, :, columns] = sources[s][0, :, :width].astype(F32)
        up_ref[0, :, columns] = sources[s][0, :, width:].astype(F32)


def assemble(where, sources, start, local, buffers):
    parts = len(sources)
    experts, depth, width2 = sources[0].shape
    in_specs = [pl.BlockSpec((1, depth, width2), lambda e, c: (e, 0, 0))] * parts
    args = [where, *sources]
    aliases = {}
    if buffers is not None:
        in_specs = in_specs + [pl.BlockSpec(memory_space=pl.ANY)] * 2
        aliases = {len(args): 0, len(args) + 1: 1}
        args += list(buffers)
    spec = pl.BlockSpec((1, depth, FF), lambda e, c: (start + e, 0, 0))
    return pl.pallas_call(
        functools.partial(assemble_body, parts, width2 // 2),
        grid_spec=pltpu.PrefetchScalarGridSpec(
            num_scalar_prefetch=1,
            grid=(experts,),
            in_specs=in_specs,
            out_specs=[spec, spec],
        ),
        out_shape=[jax.ShapeDtypeStruct((local, depth, FF), F32)] * 2,
        input_output_aliases=aliases,
        compiler_params=pltpu.CompilerParams(vmem_limit_bytes=VMEM_BYTES),
        cost_estimate=pl.CostEstimate(
            flops=0, bytes_accessed=6 * experts * depth * FF * 2, transcendentals=0
        ),
        name="assemble",
    )(*args)


def make_on_device(wide, narrow):
    planes = wide // 2
    local = E // wide
    heads = H // wide
    features = heads * HD
    chunks = min(CHUNKS, local)
    per_chunk = local // chunks

    def swap(x, axis, r):
        size = wide if axis == "wide" else narrow
        return lax.ppermute(x, axis, [(i, i ^ r) for i in range(size)])

    def gather_narrow(x):
        return [x] + [swap(x, "narrow", s) for s in range(1, narrow)]

    def gather_wide(x):
        own = [x] + [swap(x, "wide", 2 * q) for q in range(1, planes)]
        other = [swap(piece, "wide", 1) for piece in own]
        return own, other

    def interleave(own, other):
        return [piece for pair in zip(own, other) for piece in pair]

    def exchange(parts, axis):
        return [parts[0]] + [swap(parts[r], axis, r) for r in range(1, len(parts))]

    def add_up(parts):
        total = parts[0].astype(F32)
        for part in parts[1:]:
            total = total + part.astype(F32)
        return total

    def scatter_wide(own, other):
        sums = []
        for q in range(planes):
            sums.append(own[q].astype(F32) + swap(other[q], "wide", 1).astype(F32))
        total = sums[0]
        for q in range(1, planes):
            total = total + swap(sums[q].astype(BF), "wide", 2 * q).astype(F32)
        return total

    def on_device(
        tokens, positions, routes, cotangent,
        w_query, w_key, w_value, w_output, w_router,
        gain_attn, gain_query, gain_key, gain_ffn,
        w_gate, w_up, w_down,
    ):
        count = tokens.shape[0]
        rows = w_query.shape[0]
        w = lax.axis_index("wide")
        n = lax.axis_index("narrow")
        where = jnp.stack([n, w * local]).astype(jnp.int32)
        wide_order = jnp.arange(wide) ^ w
        narrow_order = jnp.arange(narrow) ^ n
        shard_order = (wide_order[:, None] * narrow + narrow_order[None, :]).reshape(-1)

        routed = jnp.any(
            routes[:, :, None] == jnp.arange(E, dtype=jnp.int32)[None, None, :], axis=1
        )
        earlier = matmul(
            jnp.tril(jnp.ones((count, count), BF), -1), routed.astype(BF), ((1,), (0,))
        )
        slots = jnp.where(routed, earlier, -1.0).astype(BF).T

        small = jnp.concatenate(
            [
                w_router.reshape(-1), gain_attn, gain_query, gain_key, gain_ffn,
                positions.astype(BF),
            ]
        )
        small_rows = -(-small.shape[0] // LANES)
        bundle_rows = -(-(E + small_rows) // 16) * 16
        small = jnp.pad(small, (0, (bundle_rows - E) * LANES - small.shape[0]))
        bundle = jnp.concatenate([slots, small.reshape(-1, LANES)], axis=0)
        bundle_z = jnp.stack(gather_narrow(bundle))
        bundles = jnp.stack([bundle_z] + [swap(bundle_z, "wide", r) for r in range(1, wide)])
        all_slots = bundles[:, :, :E, :]
        all_small = bundles[:, :, E:, :].reshape(wide * narrow, -1)
        plane_positions = all_small.reshape(wide, narrow, -1)[
            :, 0, rows * E + 4 * rows : rows * E + 4 * rows + count
        ].reshape(wide * count)
        all_small = jnp.take(all_small, shard_order, axis=0)
        router_full = all_small[:, : rows * E].reshape(D, E)
        gains = [
            all_small[:, rows * E + i * rows : rows * E + (i + 1) * rows]
            .reshape(D)
            .astype(F32)
            for i in range(4)
        ]
        attn_gain, query_gain, key_gain, ffn_gain = gains
        query_gain = lax.dynamic_slice_in_dim(query_gain, w * features, features)
        key_gain = lax.dynamic_slice_in_dim(key_gain, w * features, features)
        expert_counts = jnp.sum((all_slots >= 0).astype(jnp.int32), axis=(0, 1, 3))

        own, other = gather_wide(tokens)
        plane_tokens = jnp.concatenate(interleave(own, other), axis=0).astype(F32)
        plane_count = plane_tokens.shape[0]

        stacked = jnp.concatenate(
            [x.reshape(rows, wide, features) for x in (w_query, w_key, w_value)], axis=-1
        ).transpose(1, 0, 2)
        stacked = jnp.take(stacked, wide_order, axis=0)
        columns = jnp.stack(exchange([stacked[r] for r in range(wide)], "wide"))
        columns = jnp.stack(gather_narrow(columns), axis=1)
        qkv = jnp.take(
            columns.reshape(wide * narrow, rows, 3 * features), shard_order, axis=0
        ).reshape(D, 3 * features)
        output_rows = jnp.take(
            jnp.stack(gather_narrow(w_output)), narrow_order, axis=0
        ).reshape(features, D)

        cot_z = jnp.concatenate(gather_narrow(cotangent), axis=0)
        cot_own, cot_other = gather_wide(cot_z)

        expert_weights = []
        slice_ff = FF // narrow
        for c in range(chunks):
            lo, hi = c * per_chunk, (c + 1) * per_chunk
            mine = []
            for s in range(narrow):
                at = (n ^ s) * slice_ff
                mine.append(
                    jnp.concatenate(
                        [
                            lax.dynamic_slice_in_dim(w_gate[lo:hi], at, slice_ff, axis=2),
                            lax.dynamic_slice_in_dim(w_up[lo:hi], at, slice_ff, axis=2),
                        ],
                        axis=2,
                    )
                )
            expert_weights.append(exchange(mine, "narrow"))

        inverse = lax.rsqrt(jnp.mean(plane_tokens * plane_tokens, axis=-1, keepdims=True) + EPSILON)
        normed = (plane_tokens * inverse * attn_gain).astype(BF)
        raw = matmul(normed, qkv, ((1,), (0,)))
        query_raw = raw[:, :features]
        key_raw = raw[:, features : 2 * features]
        values = raw[:, 2 * features :].astype(BF).reshape(wide, count, heads, HD)

        def sum_wide(x):
            return add_up([x] + [swap(x, "wide", r) for r in range(1, wide)])

        def row_sums(a, b):
            sums = jnp.stack([jnp.sum(a, axis=-1), jnp.sum(b, axis=-1)])
            blocks = sums.reshape(2, wide, count)
            total = blocks
            for r in range(1, wide):
                came = swap(blocks, "wide", r)
                total = total + jnp.stack([came[:, x ^ r] for x in range(wide)], axis=1)
            total = total.reshape(2, plane_count)
            return total[0][:, None], total[1][:, None]

        query_square, key_square = row_sums(query_raw * query_raw, key_raw * key_raw)
        query_r = lax.rsqrt(query_square / D + EPSILON)
        key_r = lax.rsqrt(key_square / D + EPSILON)
        frequency = THETA_BASE ** (-2.0 * jnp.arange(HD // 2, dtype=F32) / HD)
        angles = plane_positions.astype(F32)[:, None] * frequency[None, :]
        cosine = jnp.cos(angles)[:, None, :]
        sine = jnp.sin(angles)[:, None, :]

        def turn(x, sign):
            x = x.reshape(plane_count, heads, HD)
            a, b = x[..., : HD // 2], x[..., HD // 2 :]
            return jnp.concatenate(
                [a * cosine - sign * b * sine, b * cosine + sign * a * sine], axis=-1
            )

        shape = (wide, count, heads, HD)
        queries = turn(query_raw * query_r * query_gain, 1.0).astype(BF).reshape(shape)
        key_rows = turn(key_raw * key_r * key_gain, 1.0).astype(BF).reshape(shape)
        scale = HD ** (-0.5)
        causal = (jnp.arange(count)[:, None] >= jnp.arange(count)[None, :])[None, None]
        scores = (
            jnp.einsum("bqhd,bkhd->bhqk", queries, key_rows, preferred_element_type=F32) * scale
        )
        scores = jnp.where(causal, scores, -1e30)
        powers = jnp.exp(scores - jnp.max(scores, axis=-1, keepdims=True))
        attn_probs = powers / jnp.sum(powers, axis=-1, keepdims=True)
        probs_low = attn_probs.astype(BF)
        attended = (
            jnp.einsum("bhqk,bkhd->bqhd", probs_low, values, preferred_element_type=F32)
            .astype(BF)
            .reshape(plane_count, features)
        )
        branch = matmul(attended, output_rows, ((1,), (0,))).astype(BF)
        branch = branch.reshape(planes, 2, count, D)
        branch = scatter_wide(
            [branch[q, 0] for q in range(planes)], [branch[q, 1] for q in range(planes)]
        )

        residual = tokens.astype(F32) + branch
        ffn_r = lax.rsqrt(jnp.mean(residual * residual, axis=-1, keepdims=True) + EPSILON)
        normed_ffn = (residual * ffn_r * ffn_gain).astype(BF)
        logits = matmul(normed_ffn, router_full, ((1,), (0,)))
        router_powers = jnp.exp(logits - jnp.max(logits, axis=-1, keepdims=True))
        router_probs = router_powers / jnp.sum(router_powers, axis=-1, keepdims=True)
        probs_top = router_probs.astype(BF)
        probs_rest = (router_probs - probs_top.astype(F32)).astype(BF)

        message = jnp.concatenate([normed_ffn, probs_top, probs_rest], axis=1)
        message_z = jnp.concatenate(gather_narrow(message), axis=0)
        token_own, token_other = gather_wide(message_z)

        local_slots = lax.dynamic_slice_in_dim(all_slots, w * local, local, axis=2)
        pairs = narrow // 2
        local_slots = (
            local_slots.reshape(planes, 2, pairs, 2, local, count)
            .transpose(1, 0, 2, 4, 3, 5)
            .reshape(2, planes, pairs, local, 1, 2 * count)
        )
        row = jnp.arange(2 * CAP)[:, None]
        lane = jnp.arange(2 * count)[None, :]
        picks = (
            ((local_slots == (row % CAP).astype(BF)) & (row // CAP == lane // count))
            .astype(BF)
            .reshape(2, planes, pairs, local * 2 * CAP, 2 * count)
        )
        total_rows = wide * narrow * CAP
        ups = dispatch(picks[0], cot_own, 0, total_rows)
        ups = dispatch(picks[1], cot_other, 1, total_rows, ups)
        expert_rows = dispatch(picks[0], token_own, 0, total_rows)
        expert_rows = dispatch(picks[1], token_other, 1, total_rows, expert_rows)

        results, row_grads, came = [], [], []
        down_grad = None
        for c in range(chunks):
            result, row_grad, weight_grads, down_grad = expert_chunk(
                where, expert_rows, ups, expert_weights[c], w_down, c * per_chunk, down_grad
            )
            results.append(result)
            row_grads.append(row_grad)
            came.append(exchange(weight_grads, "narrow"))
        grads_own = combine(picks[0], row_grads, 0)
        grads_other = combine(picks[1], row_grads, 1)
        mix_own = combine(picks[0], results, 0)
        mix_other = combine(picks[1], results, 1)

        def scatter_tokens(own_terms, other_terms):
            plane_sum = scatter_wide(own_terms, other_terms).astype(BF)
            blocks = plane_sum.reshape(narrow, count, plane_sum.shape[-1])
            return add_up(exchange([blocks[s] for s in range(narrow)], "narrow"))

        ffn_message = scatter_tokens(grads_own, grads_other)
        mixture = scatter_tokens(mix_own, mix_other)
        block_out = (residual + mixture).astype(BF)

        upstream = cotangent.astype(F32)
        prob_grads = ffn_message[:, D : D + E] + ffn_message[:, D + E : D + 2 * E]
        logit_grads = (
            router_probs
            * (prob_grads - jnp.sum(router_probs * prob_grads, axis=-1, keepdims=True))
        ).astype(BF)
        ffn_grads = ffn_message[:, :D] + matmul(logit_grads, router_full, ((1,), (1,)))

        def norm_back(v, r, gain, dy):
            u = dy * gain
            return r * u - v * (r * r * r) * jnp.mean(u * v, axis=-1, keepdims=True)

        residual_grads = upstream + norm_back(residual, ffn_r, ffn_gain, ffn_grads)
        ffn_gain_part = jnp.sum(ffn_grads * residual * ffn_r, axis=0)
        branch_grads = residual_grads.astype(BF)

        logit_z = jnp.concatenate(gather_narrow(logit_grads), axis=0)
        logit_own, logit_other = gather_wide(logit_z)
        shard = (w * narrow + n) * rows
        grad_router = None
        for tokens_in, grads_in in zip(token_own + token_other, logit_own + logit_other):
            part = lax.dynamic_slice_in_dim(tokens_in, shard, rows, axis=1)
            term = matmul(part, grads_in, ((0,), (0,)))
            grad_router = term if grad_router is None else grad_router + term

        own, other = gather_wide(branch_grads)
        plane_grads = jnp.concatenate(interleave(own, other), axis=0)
        attended_grads = (
            matmul(plane_grads, output_rows, ((1,), (1,))).astype(BF).reshape(shape)
        )
        grad_output = matmul(attended, plane_grads, ((0,), (0,)))
        prob_grads_attn = jnp.einsum(
            "bqhd,bkhd->bhqk", attended_grads, values, preferred_element_type=F32
        )
        value_grads = (
            jnp.einsum("bhqk,bqhd->bkhd", probs_low, attended_grads, preferred_element_type=F32)
            .astype(BF)
            .reshape(plane_count, features)
        )
        score_grads = attn_probs * (
            prob_grads_attn - jnp.sum(attn_probs * prob_grads_attn, axis=-1, keepdims=True)
        )
        score_grads = jnp.where(causal, score_grads, 0.0).astype(BF)
        query_grads = (
            jnp.einsum("bhqk,bkhd->bqhd", score_grads, key_rows, preferred_element_type=F32)
            * scale
        )
        key_grads = (
            jnp.einsum("bhqk,bqhd->bkhd", score_grads, queries, preferred_element_type=F32)
            * scale
        )
        query_dy = turn(query_grads, -1.0).reshape(plane_count, features)
        key_dy = turn(key_grads, -1.0).reshape(plane_count, features)
        query_u = query_dy * query_gain
        key_u = key_dy * key_gain
        query_dot, key_dot = row_sums(query_u * query_raw, key_u * key_raw)
        query_raw_grads = query_r * query_u - query_raw * (query_r**3) * (query_dot / D)
        key_raw_grads = key_r * key_u - key_raw * (key_r**3) * (key_dot / D)
        raw_grads = jnp.concatenate(
            [query_raw_grads.astype(BF), key_raw_grads.astype(BF), value_grads], axis=1
        )
        qk_gain_parts = jnp.stack(
            [
                jnp.sum(query_dy * query_raw * query_r, axis=0),
                jnp.sum(key_dy * key_raw * key_r, axis=0),
            ]
        )
        normed_grads = matmul(raw_grads, qkv, ((1,), (1,))).astype(BF)
        normed_grads = normed_grads.reshape(planes, 2, count, D)
        normed_grads = scatter_wide(
            [normed_grads[q, 0] for q in range(planes)],
            [normed_grads[q, 1] for q in range(planes)],
        )
        own_inputs = tokens.astype(F32)
        own_r = inverse[:count]
        input_grad = (
            residual_grads + norm_back(own_inputs, own_r, attn_gain, normed_grads)
        ).astype(BF)
        attn_gain_part = jnp.sum(normed_grads * own_inputs * own_r, axis=0)

        grad_qkv = matmul(normed, raw_grads, ((0,), (0,))).astype(BF)
        grad_qkv = jnp.take(
            grad_qkv.reshape(wide, narrow, rows, 3 * features), narrow_order, axis=1
        )
        grad_qkv = add_up(exchange([grad_qkv[:, s] for s in range(narrow)], "narrow"))
        grad_qkv = jnp.take(grad_qkv, wide_order, axis=0)
        grad_qkv = jnp.stack(exchange([grad_qkv[r] for r in range(wide)], "wide"))
        grad_qkv = jnp.take(grad_qkv, wide_order, axis=0).transpose(1, 0, 2)
        grad_query, grad_key, grad_value = [
            grad_qkv[..., i * features : (i + 1) * features].reshape(rows, D) for i in range(3)
        ]
        grad_output = jnp.take(
            grad_output.astype(BF).reshape(narrow, rows, D), narrow_order, axis=0
        )
        grad_output = add_up(exchange([grad_output[s] for s in range(narrow)], "narrow"))

        gain_parts = jnp.stack([attn_gain_part, ffn_gain_part])
        gain_parts = jnp.take(gain_parts.reshape(2, wide, features), wide_order, axis=1)
        gain_parts = add_up(exchange([gain_parts[:, r] for r in range(wide)], "wide"))
        gain_parts = jnp.concatenate([gain_parts, qk_gain_parts], axis=0)
        gain_parts = jnp.take(gain_parts.reshape(4, narrow, rows), narrow_order, axis=1)
        gain_parts = add_up(exchange([gain_parts[:, s] for s in range(narrow)], "narrow"))

        buffers = None
        for c in range(chunks):
            buffers = assemble(where, came[c], c * per_chunk, local, buffers)
        grad_gate, grad_up = buffers

        return (
            block_out, input_grad, grad_query, grad_key, grad_value, grad_output, grad_router,
            gain_parts[0], gain_parts[2], gain_parts[3], gain_parts[1],
            grad_gate, grad_up, down_grad, expert_counts,
        )

    return on_device


def solution(mesh):
    both = ("wide", "narrow")
    in_specs = (P(both, None), P(both), P(both, None), P(both, None))
    in_specs += (P(both, None),) * 5 + (P(both),) * 4 + (P("wide", "narrow", None),) * 3
    out_specs = (P(both, None),) * 7 + (P(both),) * 4 + (P("wide", "narrow", None),) * 3 + (P(),)
    return jax.shard_map(
        make_on_device(mesh.shape["wide"], mesh.shape["narrow"]),
        mesh=mesh,
        in_specs=in_specs,
        out_specs=out_specs,
        check_vma=False,
    )
```

time: 5550 us -> 1770 us (0.32)
  waiting for transfers between devices: 4650 us -> 886 us
  starting transfers between devices: 11 us -> 368 us
  blocking collectives: 350 us -> 0 us
  Pallas kernels: 0 us -> 230 us
  matrix products: 269 us -> 43 us
    reduce_scatter x8 -> x0, waiting for transfers between devices: 2820 us -> none  [the longest x1 543 us: on_device(): lax.psum_scatter(jnp.einsum('erd,erf->edf', expert_rows, up_value_grads,...]
    all_gather x7 -> x0, waiting for transfers between devices: 1760 us -> none  [the longest x1 538 us: on_device(): lax.all_gather(w_up, 'narrow', axis=1, tiled=True)]
    ppermute x0 -> x162, waiting for transfers between devices: none -> 886 us  [swap(): return lax.ppermute(x, axis, [(i, i ^ r) for i in range(size)])]
    ppermute x0 -> x162, starting transfers between devices: none -> 368 us  [swap(): return lax.ppermute(x, axis, [(i, i ^ r) for i in range(size)])]
    pallas_call x0 -> x16, Pallas kernels: none -> 230 us  [the longest x4 113 us: expert_chunk(): pl.pallas_call(functools.partial(expert_body, parts, tiles, start, first)...]
    dot_general x30 -> x23, matrix products: 269 us -> 43 us  [the longest x17 30.4 us: matmul(): return lax.dot_general(a, b, (dims, ((), ())), preferred_element_type=F32)]
    all_to_all x2 -> x0, blocking collectives: 149 us -> none  [the longest x1 74.5 us: on_device(): lax.all_to_all(outgoing, 'wide', split_axis=0, concat_axis=1, tiled=True)]
    unnamed x2 -> x0, blocking collectives: 87.2 us -> none
  transfers between devices with their start and end apart: 17 -> 162, of which waited for: 16 -> 58; matrix products, arithmetic and copies ran while one was open for 7% -> 11% of each run, Pallas kernels for 0% -> 13%
where the time goes in v1:
time: 1770 us; the launch traced here: 1760 us
  waiting for transfers between devices  886 us (50%)
  starting transfers between devices  368 us (21%)
  Pallas kernels  230 us (13%)
  local copies, waits for them, and re-layouts  124 us (7%)
  other arithmetic  103 us (6%)
  matrix products  43 us (2%)
    ppermute x162, waiting for transfers between devices, swap(): return lax.ppermute(x, axis, [(i, i ^ r) for i in range(size)])  886 us
    ppermute x162, starting transfers between devices, swap(): return lax.ppermute(x, axis, [(i, i ^ r) for i in range(size)])  368 us
    pallas_call x4, Pallas kernels, expert_chunk(): pl.pallas_call(functools.partial(expert_body, parts, tiles, start, first)...  113 us
    pallas_call x4, Pallas kernels, combine(): pl.pallas_call(functools.partial(combine_body, pieces, rows_each, len(row...  56.8 us
    unnamed x299, local copies, waits for them, and re-layouts  37.1 us
    pallas_call x4, Pallas kernels, dispatch(): pl.pallas_call(functools.partial(dispatch_body, pieces, rows_each), grid=...  36.6 us
  transfers between devices with their start and end apart: 162, of which 58 were waited for; matrix products, arithmetic and copies ran while one was open for 11% of the time, Pallas kernels for 13%

profile of v1, /device:TPU:0, one launch (start us, length us, event | category | flops | bytes accessed | tf_op | source)
XLA Modules:
  0.0 1758.0 jit_solution(4823889380041656596)
XLA Ops:
  128.3 46.8 %collective-permute-done.25 = bf16[8,64,768]{2,1,0:T(8,128)(2,1)S(1)} collective-permute-done((bf16[8,64,768]{2,1,0:T(8,128)(2,1)}, bf16[8,64,768]{2,1,0:T(8,128)(2,1)S(1)}, u32[]{:S(2)}, u32[]{:S(2)}) %collective-permute-start.25) | collective-permute-done | bytes 786464 | tf_op jit(solution)/shard_map/ppermute | solution.py:305
  246.2 37.9 %collective-permute-done.55 = bf16[128,2048]{1,0:T(8,128)(2,1)} collective-permute-done((bf16[128,2048]{1,0:T(8,128)(2,1)S(1)}, bf16[128,2048]{1,0:T(8,128)(2,1)}, u32[]{:S(2)}, u32[]{:S(2)}) %collective-permute-start.55) | collective-permute-done | bytes 524320 | tf_op jit(solution)/shard_map/ppermute | solution.py:305
  299.9 54.9 %collective-permute-done.41 = bf16[128,2048]{1,0:T(8,128)(2,1)S(1)} collective-permute-done((bf16[128,2048]{1,0:T(8,128)(2,1)S(1)}, bf16[128,2048]{1,0:T(8,128)(2,1)S(1)}, u32[]{:S(2)}, u32[]{:S(2)}) %collective-permute-start.41) | collective-permute-done | bytes 524320 | tf_op jit(solution)/shard_map/ppermute | solution.py:305
  377.4 29.4 %collective-permute-done.45 = bf16[128,2176]{1,0:T(8,128)(2,1)S(1)} collective-permute-done((bf16[128,2176]{1,0:T(8,128)(2,1)S(1)}, bf16[128,2176]{1,0:T(8,128)(2,1)S(1)}, u32[]{:S(2)}, u32[]{:S(2)}) %collective-permute-start.45) | collective-permute-done | bytes 557088 | tf_op jit(solution)/shard_map/ppermute | solution.py:305
  441.0 32.8 %collective-permute-done.52.refs_4_ = bf16[512,2176]{1,0:T(8,128)(2,1)} collective-permute-done((bf16[512,2176]{1,0:T(8,128)(2,1)S(1)}, bf16[512,2176]{1,0:T(8,128)(2,1)}, u32[]{:S(2)}, u32[]{:S(2)}) %collective-permute-start.52) | collective-permute-done | bytes 2228256 | tf_op jit(solution)/shard_map/ppermute | solution.py:305
  481.1 37.2 %collective-permute-done.50.refs_3_ = bf16[512,2176]{1,0:T(8,128)(2,1)} collective-permute-done((bf16[512,2176]{1,0:T(8,128)(2,1)S(1)}, bf16[512,2176]{1,0:T(8,128)(2,1)}, u32[]{:S(2)}, u32[]{:S(2)}) %collective-permute-start.50) | collective-permute-done | bytes 2228256 | tf_op jit(solution)/shard_map/ppermute | solution.py:305
  525.6 19.4 %collective-permute-start.65 = (bf16[2,512,512]{2,1,0:T(8,128)(2,1)S(1)}, bf16[2,512,512]{2,1,0:T(8,128)(2,1)S(1)}, u32[]{:S(2)}, u32[]{:S(2)}) collective-permute-start(bf16[2,512,512]{2,1,0:T(8,128)(2,1)S(1)} %pad_maximum_fusion.6), channel_id=1, source_target_pairs={{0,2},{1,3},{2,0},{3,1},{4,6},{5,7},{6,4},{7,5},{8,10},{9,11},{10,... | collective-permute-start | bytes 3145736 | tf_op jit(solution)/shard_map/ppermute | solution.py:305
  586.4 33.2 %collective-permute-done.65.refs_5_ = bf16[2,512,512]{2,1,0:T(8,128)(2,1)S(1)} collective-permute-done((bf16[2,512,512]{2,1,0:T(8,128)(2,1)S(1)}, bf16[2,512,512]{2,1,0:T(8,128)(2,1)S(1)}, u32[]{:S(2)}, u32[]{:S(2)}) %collective-permute-start.65) | collective-permute-done | bytes 1048608 | tf_op jit(solution)/shard_map/ppermute | solution.py:305
  621.0 28.3 %experts.4 = (bf16[2,768,2048]{2,1,0:T(8,128)(2,1)}, bf16[2,768,2176]{2,1,0:T(8,128)(2,1)}, bf16[2,512,512]{2,1,0:T(8,128)(2,1)}, bf16[2,512,512]{2,1,0:T(8,128)...) custom-call(s32[2]{0:T(128)} %pad_add_fusion.refs_0_, ...), custom_call_target="tpu_custom_call" | custom-call | flops 14495514624 | bytes 44040192 | tf_op jit(solution)/shard_map/experts/pallas_call | solution.py:231
  651.6 79.6 %collective-permute-done.68.refs_5_ = bf16[2,512,512]{2,1,0:T(8,128)(2,1)S(1)} collective-permute-done((bf16[2,512,512]{2,1,0:T(8,128)(2,1)}, bf16[2,512,512]{2,1,0:T(8,128)(2,1)S(1)}, u32[]{:S(2)}, u32[]{:S(2)}) %collective-permute-start.68) | collective-permute-done | bytes 1048608 | tf_op jit(solution)/shard_map/ppermute | solution.py:305
  731.2 67.8 %collective-permute-start.74 = (bf16[2,512,512]{2,1,0:T(8,128)(2,1)}, bf16[2,512,512]{2,1,0:T(8,128)(2,1)S(1)}, u32[]{:S(2)}, u32[]{:S(2)}) collective-permute-start(bf16[2,512,512]{2,1,0:T(8,128)(2,1)} %pad_maximum_fusion.18), channel_id=1, source_target_pairs={{0,2},{1,3},{2,0},{3,1},{4,6},{5,7},{6,4},{7,5},{8,10},{9,11},{10,... | collective-permute-start | bytes 3145736 | tf_op jit(solution)/shard_map/ppermute | solution.py:305
  799.0 28.1 %experts.5 = (bf16[2,768,2048]{2,1,0:T(8,128)(2,1)}, bf16[2,768,2176]{2,1,0:T(8,128)(2,1)}, bf16[2,512,512]{2,1,0:T(8,128)(2,1)}, bf16[2,512,512]{2,1,0:T(8,128)...) custom-call(s32[2]{0:T(128)} %pad_add_fusion.refs_0_, ...), custom_call_target="tpu_custom_call", output_to_operand_aliasing={{6}: (8, {})} | custom-call | flops 14495514624 | bytes 44040192 | tf_op jit(solution)/shard_map/experts/pallas_call | solution.py:231
  831.6 28.6 %experts.6 = (bf16[2,768,2048]{2,1,0:T(8,128)(2,1)}, bf16[2,768,2176]{2,1,0:T(8,128)(2,1)}, bf16[2,512,512]{2,1,0:T(8,128)(2,1)}, bf16[2,512,512]{2,1,0:T(8,128)...) custom-call(s32[2]{0:T(128)} %pad_add_fusion.refs_0_, ...), custom_call_target="tpu_custom_call", output_to_operand_aliasing={{6}: (8, {})} | custom-call | flops 14495514624 | bytes 44040192 | tf_op jit(solution)/shard_map/experts/pallas_call | solution.py:231
  868.2 69.1 %collective-permute-start.157 = (bf16[2,512,512]{2,1,0:T(8,128)(2,1)}, bf16[2,512,512]{2,1,0:T(8,128)(2,1)}, u32[]{:S(2)}, u32[]{:S(2)}) collective-permute-start(bf16[2,512,512]{2,1,0:T(8,128)(2,1)} %get-tuple-element.106), channel_id=1, source_target_pairs={{0,2},{1,3},{2,0},{3,1},{4,6},{5,7},{6,4},{7,5},{8,10},{9,11},{10,... | collective-permute-start | bytes 3145736 | tf_op jit(solution)/shard_map/ppermute | solution.py:305
  937.3 28.3 %experts.7 = (bf16[2,768,2048]{2,1,0:T(8,128)(2,1)}, bf16[2,768,2176]{2,1,0:T(8,128)(2,1)}, bf16[2,512,512]{2,1,0:T(8,128)(2,1)}, bf16[2,512,512]{2,1,0:T(8,128)...) custom-call(s32[2]{0:T(128)} %pad_add_fusion.refs_0_, ...), custom_call_target="tpu_custom_call", output_to_operand_aliasing={{6}: (8, {})} | custom-call | flops 14495514624 | bytes 44040192 | tf_op jit(solution)/shard_map/experts/pallas_call | solution.py:231
  966.9 14.7 combine.7
  981.7 21.4 %collective-permute-done.160.refs_3_ = bf16[2,512,512]{2,1,0:T(8,128)(2,1)} collective-permute-done((bf16[2,512,512]{2,1,0:T(8,128)(2,1)}, bf16[2,512,512]{2,1,0:T(8,128)(2,1)}, u32[]{:S(2)}, u32[]{:S(2)}) %collective-permute-start.160) | collective-permute-done | bytes 1048608 | tf_op jit(solution)/shard_map/ppermute | solution.py:305
  1003.1 23.0 %collective-permute-start.150 = (bf16[2,512,512]{2,1,0:T(8,128)(2,1)S(1)}, bf16[2,512,512]{2,1,0:T(8,128)(2,1)}, u32[]{:S(2)}, u32[]{:S(2)}) collective-permute-start(bf16[2,512,512]{2,1,0:T(8,128)(2,1)S(1)} %copy-done.127), channel_id=1, source_target_pairs={{0,1},{1,0},{2,3},{3,2},{4,5},{5,4},{6,7},{7,6},{8,9},{9,8},{10,11... | collective-permute-start | bytes 3145736 | tf_op jit(solution)/shard_map/ppermute | solution.py:305
  1027.3 20.7 %collective-permute-done.157.refs_3_ = bf16[2,512,512]{2,1,0:T(8,128)(2,1)} collective-permute-done((bf16[2,512,512]{2,1,0:T(8,128)(2,1)}, bf16[2,512,512]{2,1,0:T(8,128)(2,1)}, u32[]{:S(2)}, u32[]{:S(2)}) %collective-permute-start.157) | collective-permute-done | bytes 1048608 | tf_op jit(solution)/shard_map/ppermute | solution.py:305
  1051.4 18.6 %collective-permute-done.150.refs_2_ = bf16[2,512,512]{2,1,0:T(8,128)(2,1)} collective-permute-done((bf16[2,512,512]{2,1,0:T(8,128)(2,1)S(1)}, bf16[2,512,512]{2,1,0:T(8,128)(2,1)}, u32[]{:S(2)}, u32[]{:S(2)}) %collective-permute-start.150) | collective-permute-done | bytes 1048608 | tf_op jit(solution)/shard_map/ppermute | solution.py:305
  1069.9 46.2 %collective-permute-start.153 = (bf16[2,512,512]{2,1,0:T(8,128)(2,1)}, bf16[2,512,512]{2,1,0:T(8,128)(2,1)}, u32[]{:S(2)}, u32[]{:S(2)}) collective-permute-start(bf16[2,512,512]{2,1,0:T(8,128)(2,1)} %get-tuple-element.101), channel_id=1, source_target_pairs={{0,1},{1,0},{2,3},{3,2},{4,5},{5,4},{6,7},{7,6},{8,9},{9,8},{10,11... | collective-permute-start | bytes 3145736 | tf_op jit(solution)/shard_map/ppermute | solution.py:305
  1119.3 18.7 %collective-permute-done.151.refs_3_ = bf16[2,512,512]{2,1,0:T(8,128)(2,1)} collective-permute-done((bf16[2,512,512]{2,1,0:T(8,128)(2,1)}, bf16[2,512,512]{2,1,0:T(8,128)(2,1)}, u32[]{:S(2)}, u32[]{:S(2)}) %collective-permute-start.151) | collective-permute-done | bytes 1048608 | tf_op jit(solution)/shard_map/ppermute | solution.py:305
  1184.2 38.4 %collective-permute-done.154.refs_3_ = bf16[2,512,512]{2,1,0:T(8,128)(2,1)S(1)} collective-permute-done((bf16[2,512,512]{2,1,0:T(8,128)(2,1)S(1)}, bf16[2,512,512]{2,1,0:T(8,128)(2,1)S(1)}, u32[]{:S(2)}, u32[]{:S(2)}) %collective-permute-start.154) | collective-permute-done | bytes 1048608 | tf_op jit(solution)/shard_map/ppermute | solution.py:305
  1257.9 18.1 %collective-permute-done.155.refs_4_ = bf16[2,512,512]{2,1,0:T(8,128)(2,1)S(1)} collective-permute-done((bf16[2,512,512]{2,1,0:T(8,128)(2,1)S(1)}, bf16[2,512,512]{2,1,0:T(8,128)(2,1)S(1)}, u32[]{:S(2)}, u32[]{:S(2)}) %collective-permute-start.155) | collective-permute-done | bytes 1048608 | tf_op jit(solution)/shard_map/ppermute | solution.py:305
  1278.1 46.0 %collective-permute-done.90 = bf16[512,2176]{1,0:T(8,128)(2,1)S(1)} collective-permute-done((bf16[512,2176]{1,0:T(8,128)(2,1)}, bf16[512,2176]{1,0:T(8,128)(2,1)S(1)}, u32[]{:S(2)}, u32[]{:S(2)}) %collective-permute-start.90) | collective-permute-done | bytes 2228256 | tf_op jit(solution)/shard_map/ppermute | solution.py:305
  1368.0 45.7 %collective-permute-done.80 = bf16[512,2048]{1,0:T(8,128)(2,1)} collective-permute-done((bf16[512,2048]{1,0:T(8,128)(2,1)}, bf16[512,2048]{1,0:T(8,128)(2,1)}, u32[]{:S(2)}, u32[]{:S(2)}) %collective-permute-start.80) | collective-permute-done | bytes 2097184 | tf_op jit(solution)/shard_map/ppermute | solution.py:305
  1426.8 17.8 %collective-permute-done.83 = bf16[128,2048]{1,0:T(8,128)(2,1)S(1)} collective-permute-done((bf16[128,2048]{1,0:T(8,128)(2,1)S(1)}, bf16[128,2048]{1,0:T(8,128)(2,1)S(1)}, u32[]{:S(2)}, u32[]{:S(2)}) %collective-permute-start.83) | collective-permute-done | bytes 524320 | tf_op jit(solution)/shard_map/ppermute | solution.py:305
  1445.1 25.2 %collective-permute-done.84 = bf16[128,2048]{1,0:T(8,128)(2,1)S(1)} collective-permute-done((bf16[128,2048]{1,0:T(8,128)(2,1)S(1)}, bf16[128,2048]{1,0:T(8,128)(2,1)S(1)}, u32[]{:S(2)}, u32[]{:S(2)}) %collective-permute-start.84) | collective-permute-done | bytes 524320 | tf_op jit(solution)/shard_map/ppermute | solution.py:305
  1481.2 21.3 %collective-permute-done.134 = bf16[512,64]{1,0:T(8,128)(2,1)S(1)} collective-permute-done((bf16[512,64]{1,0:T(8,128)(2,1)S(1)}, bf16[512,64]{1,0:T(8,128)(2,1)S(1)}, u32[]{:S(2)}, u32[]{:S(2)}) %collective-permute-start.134) | collective-permute-done | bytes 65568 | tf_op jit(solution)/shard_map/ppermute | solution.py:305
  1597.6 27.5 %collective-permute-done.117 = bf16[8,64,768]{2,1,0:T(8,128)(2,1)S(1)} collective-permute-done((bf16[8,64,768]{2,1,0:T(8,128)(2,1)S(1)}, bf16[8,64,768]{2,1,0:T(8,128)(2,1)S(1)}, u32[]{:S(2)}, u32[]{:S(2)}) %collective-permute-start.117) | collective-permute-done | bytes 786464 | tf_op jit(solution)/shard_map/ppermute | solution.py:305
  1627.7 32.8 %collective-permute-done.118 = bf16[8,64,768]{2,1,0:T(8,128)(2,1)S(1)} collective-permute-done((bf16[8,64,768]{2,1,0:T(8,128)(2,1)S(1)}, bf16[8,64,768]{2,1,0:T(8,128)(2,1)S(1)}, u32[]{:S(2)}, u32[]{:S(2)}) %collective-permute-start.118) | collective-permute-done | bytes 786464 | tf_op jit(solution)/shard_map/ppermute | solution.py:305
  1669.8 25.7 %collective-permute-done.121 = f32[64,768]{1,0:T(8,128)S(1)} collective-permute-done((f32[64,768]{1,0:T(8,128)S(1)}, f32[64,768]{1,0:T(8,128)S(1)}, u32[]{:S(2)}, u32[]{:S(2)}) %collective-permute-start.121) | collective-permute-done | bytes 196640 | tf_op jit(solution)/shard_map/ppermute | solution.py:305
  (842 shorter events, 671.5 us)
Async XLA Ops:
  11.5 90.5 %collective-permute-start.34 = (bf16[64,2048]{1,0:T(8,128)(2,1)}, bf16[64,2048]{1,0:T(8,128)(2,1)S(1)}, u32[]{:S(2)}, u32[]{:S(2)}) collective-permute-start(bf16[64,2048]{1,0:T(8,128)(2,1)} %param.27), channel_id=1, source_target_pairs={{0,1},{1,0},{2,3},{3,2},{4,5},{5,4},{6,7},{7,6},{8,9},{9,8},{10,11... | collective-permute-start | bytes 786440 | tf_op jit(solution)/shard_map/ppermute | solution.py:305
  12.4 90.8 %collective-permute-start.36 = (bf16[64,2048]{1,0:T(8,128)(2,1)}, bf16[64,2048]{1,0:T(8,128)(2,1)}, u32[]{:S(2)}, u32[]{:S(2)}) collective-permute-start(bf16[64,2048]{1,0:T(8,128)(2,1)} %param.27), channel_id=1, source_target_pairs={{0,3},{1,2},{2,1},{3,0},{4,7},{5,6},{6,5},{7,4},{8,11},{9,10},{10,... | collective-permute-start | bytes 786440 | tf_op jit(solution)/shard_map/ppermute | solution.py:305
  21.6 87.2 %collective-permute-start.1 = (bf16[128,2048]{1,0:T(8,128)(2,1)S(1)}, bf16[128,2048]{1,0:T(8,128)(2,1)}, u32[]{:S(2)}, u32[]{:S(2)}) collective-permute-start(bf16[128,2048]{1,0:T(8,128)(2,1)S(1)} %copy-done.6), channel_id=1, source_target_pairs={{0,8},{4,12},{8,0},{12,4},{16,24},{20,28},{24,16},{28,20},{1,9},{5... | collective-permute-start | bytes 1572872 | tf_op jit(solution)/shard_map/ppermute | solution.py:305
  291.4 129.4 %collective-permute-start.62 = (bf16[512,2048]{1,0:T(8,128)(2,1)}, bf16[512,2048]{1,0:T(8,128)(2,1)}, u32[]{:S(2)}, u32[]{:S(2)}) collective-permute-start(bf16[512,2048]{1,0:T(8,128)(2,1)} %constant_dynamic-update-slice_fusion.8.refs_1_), channel_id=1, source_target_pairs={{0,24},{4,28},{8,16},{12,20},{16,8},{20,12},{24,0},{28,4},{1,25},{... | collective-permute-start | bytes 6291464 | tf_op jit(solution)/shard_map/ppermute | solution.py:305
  293.2 127.8 %collective-permute-start.60 = (bf16[512,2048]{1,0:T(8,128)(2,1)}, bf16[512,2048]{1,0:T(8,128)(2,1)}, u32[]{:S(2)}, u32[]{:S(2)}) collective-permute-start(bf16[512,2048]{1,0:T(8,128)(2,1)} %constant_dynamic-update-slice_fusion.8.refs_1_), channel_id=1, source_target_pairs={{0,16},{4,20},{8,24},{12,28},{16,0},{20,4},{24,8},{28,12},{1,17},{... | collective-permute-start | bytes 6291464 | tf_op jit(solution)/shard_map/ppermute | solution.py:305
  430.0 88.3 %collective-permute-start.50 = (bf16[512,2176]{1,0:T(8,128)(2,1)S(1)}, bf16[512,2176]{1,0:T(8,128)(2,1)}, u32[]{:S(2)}, u32[]{:S(2)}) collective-permute-start(bf16[512,2176]{1,0:T(8,128)(2,1)S(1)} %pad_maximum_fusion.1.refs_1_), channel_id=1, source_target_pairs={{0,16},{4,20},{8,24},{12,28},{16,0},{20,4},{24,8},{28,12},{1,17},{... | collective-permute-start | bytes 6684680 | tf_op jit(solution)/shard_map/ppermute | solution.py:305
  431.0 87.3 %collective-permute-start.48 = (bf16[512,2176]{1,0:T(8,128)(2,1)S(1)}, bf16[512,2176]{1,0:T(8,128)(2,1)}, u32[]{:S(2)}, u32[]{:S(2)}) collective-permute-start(bf16[512,2176]{1,0:T(8,128)(2,1)S(1)} %pad_maximum_fusion.1.refs_1_), channel_id=1, source_target_pairs={{0,8},{4,12},{8,0},{12,4},{16,24},{20,28},{24,16},{28,20},{1,9},{5... | collective-permute-start | bytes 6684680 | tf_op jit(solution)/shard_map/ppermute | solution.py:305
  525.6 94.1 %collective-permute-start.65 = (bf16[2,512,512]{2,1,0:T(8,128)(2,1)S(1)}, bf16[2,512,512]{2,1,0:T(8,128)(2,1)S(1)}, u32[]{:S(2)}, u32[]{:S(2)}) collective-permute-start(bf16[2,512,512]{2,1,0:T(8,128)(2,1)S(1)} %pad_maximum_fusion.6), channel_id=1, source_target_pairs={{0,2},{1,3},{2,0},{3,1},{4,6},{5,7},{6,4},{7,5},{8,10},{9,11},{10,... | collective-permute-start | bytes 3145736 | tf_op jit(solution)/shard_map/ppermute | solution.py:305
  574.3 156.9 %collective-permute-start.68 = (bf16[2,512,512]{2,1,0:T(8,128)(2,1)}, bf16[2,512,512]{2,1,0:T(8,128)(2,1)S(1)}, u32[]{:S(2)}, u32[]{:S(2)}) collective-permute-start(bf16[2,512,512]{2,1,0:T(8,128)(2,1)} %pad_maximum_fusion.10), channel_id=1, source_target_pairs={{0,2},{1,3},{2,0},{3,1},{4,6},{5,7},{6,4},{7,5},{8,10},{9,11},{10,... | collective-permute-start | bytes 3145736 | tf_op jit(solution)/shard_map/ppermute | solution.py:305
  584.9 242.2 %collective-permute-start.72 = (bf16[2,512,512]{2,1,0:T(8,128)(2,1)}, bf16[2,512,512]{2,1,0:T(8,128)(2,1)S(1)}, u32[]{:S(2)}, u32[]{:S(2)}) collective-permute-start(bf16[2,512,512]{2,1,0:T(8,128)(2,1)} %pad_maximum_fusion.15), channel_id=1, source_target_pairs={{0,3},{1,2},{2,1},{3,0},{4,7},{5,6},{6,5},{7,4},{8,11},{9,10},{10,... | collective-permute-start | bytes 3145736 | tf_op jit(solution)/shard_map/ppermute | solution.py:305
  619.7 210.2 %collective-permute-start.71 = (bf16[2,512,512]{2,1,0:T(8,128)(2,1)}, bf16[2,512,512]{2,1,0:T(8,128)(2,1)S(1)}, u32[]{:S(2)}, u32[]{:S(2)}) collective-permute-start(bf16[2,512,512]{2,1,0:T(8,128)(2,1)} %pad_maximum_fusion.14), channel_id=1, source_target_pairs={{0,2},{1,3},{2,0},{3,1},{4,6},{5,7},{6,4},{7,5},{8,10},{9,11},{10,... | collective-permute-start | bytes 3145736 | tf_op jit(solution)/shard_map/ppermute | solution.py:305
  619.7 111.5 %collective-permute-start.69 = (bf16[2,512,512]{2,1,0:T(8,128)(2,1)}, bf16[2,512,512]{2,1,0:T(8,128)(2,1)}, u32[]{:S(2)}, u32[]{:S(2)}) collective-permute-start(bf16[2,512,512]{2,1,0:T(8,128)(2,1)} %pad_maximum_fusion.11), channel_id=1, source_target_pairs={{0,3},{1,2},{2,1},{3,0},{4,7},{5,6},{6,5},{7,4},{8,11},{9,10},{10,... | collective-permute-start | bytes 3145736 | tf_op jit(solution)/shard_map/ppermute | solution.py:305
  649.3 180.6 %collective-permute-start.70 = (bf16[2,512,512]{2,1,0:T(8,128)(2,1)}, bf16[2,512,512]{2,1,0:T(8,128)(2,1)S(1)}, u32[]{:S(2)}, u32[]{:S(2)}) collective-permute-start(bf16[2,512,512]{2,1,0:T(8,128)(2,1)} %pad_maximum_fusion.13), channel_id=1, source_target_pairs={{0,1},{1,0},{2,3},{3,2},{4,5},{5,4},{6,7},{7,6},{8,9},{9,8},{10,11... | collective-permute-start | bytes 3145736 | tf_op jit(solution)/shard_map/ppermute | solution.py:305
  731.2 129.0 %collective-permute-start.73 = (bf16[2,512,512]{2,1,0:T(8,128)(2,1)}, bf16[2,512,512]{2,1,0:T(8,128)(2,1)S(1)}, u32[]{:S(2)}, u32[]{:S(2)}) collective-permute-start(bf16[2,512,512]{2,1,0:T(8,128)(2,1)} %pad_maximum_fusion.17), channel_id=1, source_target_pairs={{0,1},{1,0},{2,3},{3,2},{4,5},{5,4},{6,7},{7,6},{8,9},{9,8},{10,11... | collective-permute-start | bytes 3145736 | tf_op jit(solution)/shard_map/ppermute | solution.py:305
  731.2 137.0 %collective-permute-start.74 = (bf16[2,512,512]{2,1,0:T(8,128)(2,1)}, bf16[2,512,512]{2,1,0:T(8,128)(2,1)S(1)}, u32[]{:S(2)}, u32[]{:S(2)}) collective-permute-start(bf16[2,512,512]{2,1,0:T(8,128)(2,1)} %pad_maximum_fusion.18), channel_id=1, source_target_pairs={{0,2},{1,3},{2,0},{3,1},{4,6},{5,7},{6,4},{7,5},{8,10},{9,11},{10,... | collective-permute-start | bytes 3145736 | tf_op jit(solution)/shard_map/ppermute | solution.py:305
  829.9 135.7 %collective-permute-start.159 = (bf16[2,512,512]{2,1,0:T(8,128)(2,1)}, bf16[2,512,512]{2,1,0:T(8,128)(2,1)S(1)}, u32[]{:S(2)}, u32[]{:S(2)}) collective-permute-start(bf16[2,512,512]{2,1,0:T(8,128)(2,1)} %get-tuple-element.109), channel_id=1, source_target_pairs={{0,1},{1,0},{2,3},{3,2},{4,5},{5,4},{6,7},{7,6},{8,9},{9,8},{10,11... | collective-permute-start | bytes 3145736 | tf_op jit(solution)/shard_map/ppermute | solution.py:305
  829.9 173.2 %collective-permute-start.160 = (bf16[2,512,512]{2,1,0:T(8,128)(2,1)}, bf16[2,512,512]{2,1,0:T(8,128)(2,1)}, u32[]{:S(2)}, u32[]{:S(2)}) collective-permute-start(bf16[2,512,512]{2,1,0:T(8,128)(2,1)} %get-tuple-element.110), channel_id=1, source_target_pairs={{0,2},{1,3},{2,0},{3,1},{4,6},{5,7},{6,4},{7,5},{8,10},{9,11},{10,... | collective-permute-start | bytes 3145736 | tf_op jit(solution)/shard_map/ppermute | solution.py:305
  860.2 142.9 %collective-permute-start.161 = (bf16[2,512,512]{2,1,0:T(8,128)(2,1)}, bf16[2,512,512]{2,1,0:T(8,128)(2,1)}, u32[]{:S(2)}, u32[]{:S(2)}) collective-permute-start(bf16[2,512,512]{2,1,0:T(8,128)(2,1)} %get-tuple-element.111), channel_id=1, source_target_pairs={{0,3},{1,2},{2,1},{3,0},{4,7},{5,6},{6,5},{7,4},{8,11},{9,10},{10,... | collective-permute-start | bytes 3145736 | tf_op jit(solution)/shard_map/ppermute | solution.py:305
  868.1 158.0 %collective-permute-start.156 = (bf16[2,512,512]{2,1,0:T(8,128)(2,1)}, bf16[2,512,512]{2,1,0:T(8,128)(2,1)}, u32[]{:S(2)}, u32[]{:S(2)}) collective-permute-start(bf16[2,512,512]{2,1,0:T(8,128)(2,1)} %get-tuple-element.105), channel_id=1, source_target_pairs={{0,1},{1,0},{2,3},{3,2},{4,5},{5,4},{6,7},{7,6},{8,9},{9,8},{10,11... | collective-permute-start | bytes 3145736 | tf_op jit(solution)/shard_map/ppermute | solution.py:305
  868.2 179.9 %collective-permute-start.157 = (bf16[2,512,512]{2,1,0:T(8,128)(2,1)}, bf16[2,512,512]{2,1,0:T(8,128)(2,1)}, u32[]{:S(2)}, u32[]{:S(2)}) collective-permute-start(bf16[2,512,512]{2,1,0:T(8,128)(2,1)} %get-tuple-element.106), channel_id=1, source_target_pairs={{0,2},{1,3},{2,0},{3,1},{4,6},{5,7},{6,4},{7,5},{8,10},{9,11},{10,... | collective-permute-start | bytes 3145736 | tf_op jit(solution)/shard_map/ppermute | solution.py:305
  1003.1 173.3 %collective-permute-start.87 = (bf16[512,2176]{1,0:T(8,128)(2,1)}, bf16[512,2176]{1,0:T(8,128)(2,1)S(1)}, u32[]{:S(2)}, u32[]{:S(2)}) collective-permute-start(bf16[512,2176]{1,0:T(8,128)(2,1)} %get-tuple-element.91), channel_id=1, source_target_pairs={{0,4},{4,0},{8,12},{12,8},{16,20},{20,16},{24,28},{28,24},{1,5},{5... | collective-permute-start | bytes 6684680 | tf_op jit(solution)/shard_map/ppermute | solution.py:305
  1026.1 111.9 %collective-permute-start.151 = (bf16[2,512,512]{2,1,0:T(8,128)(2,1)}, bf16[2,512,512]{2,1,0:T(8,128)(2,1)}, u32[]{:S(2)}, u32[]{:S(2)}) collective-permute-start(bf16[2,512,512]{2,1,0:T(8,128)(2,1)} %get-tuple-element.98), channel_id=1, source_target_pairs={{0,2},{1,3},{2,0},{3,1},{4,6},{5,7},{6,4},{7,5},{8,10},{9,11},{10,... | collective-permute-start | bytes 3145736 | tf_op jit(solution)/shard_map/ppermute | solution.py:305
  1048.0 103.6 %collective-permute-start.152 = (bf16[2,512,512]{2,1,0:T(8,128)(2,1)}, bf16[2,512,512]{2,1,0:T(8,128)(2,1)}, u32[]{:S(2)}, u32[]{:S(2)}) collective-permute-start(bf16[2,512,512]{2,1,0:T(8,128)(2,1)} %get-tuple-element.99), channel_id=1, source_target_pairs={{0,3},{1,2},{2,1},{3,0},{4,7},{5,6},{6,5},{7,4},{8,11},{9,10},{10,... | collective-permute-start | bytes 3145736 | tf_op jit(solution)/shard_map/ppermute | solution.py:305
  1051.3 128.9 %collective-permute-start.89 = (bf16[512,2176]{1,0:T(8,128)(2,1)}, bf16[512,2176]{1,0:T(8,128)(2,1)}, u32[]{:S(2)}, u32[]{:S(2)}) collective-permute-start(bf16[512,2176]{1,0:T(8,128)(2,1)} %get-tuple-element.93), channel_id=1, source_target_pairs={{0,4},{4,0},{8,12},{12,8},{16,20},{20,16},{24,28},{28,24},{1,5},{5... | collective-permute-start | bytes 6684680 | tf_op jit(solution)/shard_map/ppermute | solution.py:305
  1069.9 96.9 %collective-permute-start.153 = (bf16[2,512,512]{2,1,0:T(8,128)(2,1)}, bf16[2,512,512]{2,1,0:T(8,128)(2,1)}, u32[]{:S(2)}, u32[]{:S(2)}) collective-permute-start(bf16[2,512,512]{2,1,0:T(8,128)(2,1)} %get-tuple-element.101), channel_id=1, source_target_pairs={{0,1},{1,0},{2,3},{3,2},{4,5},{5,4},{6,7},{7,6},{8,9},{9,8},{10,11... | collective-permute-start | bytes 3145736 | tf_op jit(solution)/shard_map/ppermute | solution.py:305
  1138.0 87.0 %collective-permute-start.91 = (bf16[512,2176]{1,0:T(8,128)(2,1)}, bf16[512,2176]{1,0:T(8,128)(2,1)}, u32[]{:S(2)}, u32[]{:S(2)}) collective-permute-start(bf16[512,2176]{1,0:T(8,128)(2,1)} %get-tuple-element.95), channel_id=1, source_target_pairs={{0,4},{4,0},{8,12},{12,8},{16,20},{20,16},{24,28},{28,24},{1,5},{5... | collective-permute-start | bytes 6684680 | tf_op jit(solution)/shard_map/ppermute | solution.py:305
  1225.0 99.2 %collective-permute-start.90 = (bf16[512,2176]{1,0:T(8,128)(2,1)}, bf16[512,2176]{1,0:T(8,128)(2,1)S(1)}, u32[]{:S(2)}, u32[]{:S(2)}) collective-permute-start(bf16[512,2176]{1,0:T(8,128)(2,1)} %add_convert_fusion.2), channel_id=1, source_target_pairs={{0,16},{4,20},{8,24},{12,28},{16,0},{20,4},{24,8},{28,12},{1,17},{... | collective-permute-start | bytes 6684680 | tf_op jit(solution)/shard_map/ppermute | solution.py:305
  1229.2 120.1 %collective-permute-start.92 = (bf16[512,2176]{1,0:T(8,128)(2,1)}, bf16[512,2176]{1,0:T(8,128)(2,1)}, u32[]{:S(2)}, u32[]{:S(2)}) collective-permute-start(bf16[512,2176]{1,0:T(8,128)(2,1)} %add_convert_fusion.1), channel_id=1, source_target_pairs={{0,24},{4,28},{8,16},{12,20},{16,8},{20,12},{24,0},{28,4},{1,25},{... | collective-permute-start | bytes 6684680 | tf_op jit(solution)/shard_map/ppermute | solution.py:305
  1276.1 92.0 %collective-permute-start.78 = (bf16[512,2048]{1,0:T(8,128)(2,1)}, bf16[512,2048]{1,0:T(8,128)(2,1)}, u32[]{:S(2)}, u32[]{:S(2)}) collective-permute-start(bf16[512,2048]{1,0:T(8,128)(2,1)} %add_convert_fusion.7), channel_id=1, source_target_pairs={{0,8},{4,12},{8,0},{12,4},{16,24},{20,28},{24,16},{28,20},{1,9},{5... | collective-permute-start | bytes 6291464 | tf_op jit(solution)/shard_map/ppermute | solution.py:305
  1277.4 136.4 %collective-permute-start.80 = (bf16[512,2048]{1,0:T(8,128)(2,1)}, bf16[512,2048]{1,0:T(8,128)(2,1)}, u32[]{:S(2)}, u32[]{:S(2)}) collective-permute-start(bf16[512,2048]{1,0:T(8,128)(2,1)} %add_convert_fusion.6), channel_id=1, source_target_pairs={{0,16},{4,20},{8,24},{12,28},{16,0},{20,4},{24,8},{28,12},{1,17},{... | collective-permute-start | bytes 6291464 | tf_op jit(solution)/shard_map/ppermute | solution.py:305
  1324.1 89.6 %collective-permute-start.82 = (bf16[512,2048]{1,0:T(8,128)(2,1)}, bf16[512,2048]{1,0:T(8,128)(2,1)}, u32[]{:S(2)}, u32[]{:S(2)}) collective-permute-start(bf16[512,2048]{1,0:T(8,128)(2,1)} %add_convert_fusion.5), channel_id=1, source_target_pairs={{0,24},{4,28},{8,16},{12,20},{16,8},{20,12},{24,0},{28,4},{1,25},{... | collective-permute-start | bytes 6291464 | tf_op jit(solution)/shard_map/ppermute | solution.py:305
  1595.0 138.9 %collective-permute-start.110 = (bf16[128,2048]{1,0:T(8,128)(2,1)}, bf16[128,2048]{1,0:T(8,128)(2,1)}, u32[]{:S(2)}, u32[]{:S(2)}) collective-permute-start(bf16[128,2048]{1,0:T(8,128)(2,1)} %get-tuple-element.147), channel_id=1, source_target_pairs={{0,4},{4,0},{8,12},{12,8},{16,20},{20,16},{24,28},{28,24},{1,5},{5... | collective-permute-start | bytes 1572872 | tf_op jit(solution)/shard_map/ppermute | solution.py:305
  (258 other events, 6345.6 us)

commit v2 on v1

v2 whole, which is shorter than its diff:
```python
import functools

import jax
import jax.numpy as jnp
from jax import lax
from jax.experimental import pallas as pl
from jax.experimental.pallas import tpu as pltpu
from jax.sharding import PartitionSpec as P

D = 2048
H = 16
HD = 128
E = 64
TOPK = 8
CAP = 24
FF = 1024
LANES = 128
EPSILON = 1e-05
THETA_BASE = 10000.0

BF = jnp.bfloat16
F32 = jnp.float32
VMEM_BYTES = 56 * 1024 * 1024


def matmul(a, b, dims):
    return lax.dot_general(a, b, (dims, ((), ())), preferred_element_type=F32)


def dispatch_body(pieces, each, *refs):
    picks = refs[0]
    sources = refs[1 : 1 + pieces]
    out = refs[-1]
    for q in range(pieces):
        rows = matmul(picks[q, 0], sources[q][...], ((1,), (0,))).astype(BF)
        out[:, q * each : (q + 1) * each, :] = rows.reshape(-1, each, rows.shape[-1])


def dispatch(picks, sources, half, buffer=None):
    pieces, pairs, slots, span = picks.shape
    width = sources[0].shape[1]
    each = 2 * CAP
    block = pieces * each
    in_specs = [pl.BlockSpec((pieces, 1, slots, span), lambda j: (0, j, 0, 0))]
    in_specs += [pl.BlockSpec((span, width), lambda j: (j, 0))] * pieces
    args = [picks, *sources]
    aliases = {}
    if buffer is not None:
        in_specs.append(pl.BlockSpec(memory_space=pl.ANY))
        aliases = {len(args): 0}
        args.append(buffer)
    return pl.pallas_call(
        functools.partial(dispatch_body, pieces, each),
        grid=(pairs,),
        in_specs=in_specs,
        out_specs=pl.BlockSpec(
            (slots // each, block, width), lambda j: (0, half * pairs + j, 0)
        ),
        out_shape=jax.ShapeDtypeStruct((slots // each, 2 * pairs * block, width), BF),
        input_output_aliases=aliases,
        compiler_params=pltpu.CompilerParams(vmem_limit_bytes=VMEM_BYTES),
        cost_estimate=pl.CostEstimate(
            flops=2 * pieces * pairs * slots * span * width,
            bytes_accessed=2 * pieces * pairs * (slots + span) * width,
            transcendentals=0,
        ),
        name="dispatch",
    )(*args)


def combine_body(pieces, each, chunks, *refs):
    picks = refs[0]
    rows = refs[1 : 1 + chunks]
    outs = refs[1 + chunks :]
    for q in range(pieces):
        total = None
        at = 0
        for chunk in rows:
            part = chunk[:, q * each : (q + 1) * each, :].reshape(-1, chunk.shape[-1])
            size = part.shape[0]
            term = matmul(picks[q, 0, at : at + size, :], part, ((0,), (0,)))
            total = term if total is None else total + term
            at += size
        outs[q][...] = total.astype(BF)


def combine(picks, rows, half):
    pieces, pairs, slots, span = picks.shape
    each = 2 * CAP
    width = rows[0].shape[-1]
    in_specs = [pl.BlockSpec((pieces, 1, slots, span), lambda j: (0, j, 0, 0))]
    for chunk in rows:
        in_specs.append(
            pl.BlockSpec(
                (chunk.shape[0], pieces * each, width), lambda j: (0, half * pairs + j, 0)
            )
        )
    return pl.pallas_call(
        functools.partial(combine_body, pieces, each, len(rows)),
        grid=(pairs,),
        in_specs=in_specs,
        out_specs=[pl.BlockSpec((span, width), lambda j: (j, 0))] * pieces,
        out_shape=[jax.ShapeDtypeStruct((pairs * span, width), BF)] * pieces,
        compiler_params=pltpu.CompilerParams(vmem_limit_bytes=VMEM_BYTES),
        cost_estimate=pl.CostEstimate(
            flops=2 * pieces * pairs * slots * span * width,
            bytes_accessed=2 * pieces * pairs * (slots + span) * width,
            transcendentals=0,
        ),
        name="combine",
    )(picks, *rows)


def expert_body(parts, tiles, start, aliased, *refs):
    where, rows_ref, ups_ref, weights_ref, down_ref = refs[:5]
    rest = refs[5 + aliased :]
    results_ref, row_grads_ref, weight_grads_ref, down_grad_ref, sums, down_sum = rest
    tile = pl.program_id(1)
    width = FF // parts

    weights = weights_ref[...].reshape(D, 2 * width)
    tokens = rows_ref[0, :, :D]
    both = matmul(tokens, weights, ((1,), (0,)))
    gate_value = both[:, :width]
    up_value = both[:, width:]
    sigma = 1.0 / (1.0 + jnp.exp(-gate_value))
    silu = gate_value * sigma
    hidden = (silu * up_value).astype(BF)
    down = down_ref[0]
    results = matmul(hidden, down, ((1,), (0,)))

    expert = where[1] + start + pl.program_id(0)
    lane = lax.broadcasted_iota(jnp.int32, (rows_ref.shape[1], LANES), 1)
    high = lane == expert
    low = lane == expert + E
    probs = rows_ref[0, :, D:].astype(F32)
    weight = jnp.sum(jnp.where(high | low, probs, 0.0), axis=1, keepdims=True)
    upstream = ups_ref[0].astype(F32)
    gate_grad = jnp.sum(upstream * results, axis=1, keepdims=True)
    results_ref[0] = (weight * results).astype(BF)
    result_grads = (weight * upstream).astype(BF)

    hidden_grads = matmul(result_grads, down, ((1,), (1,)))
    gate_value_grads = (
        hidden_grads * up_value * (sigma * (1.0 + gate_value * (1.0 - sigma)))
    ).astype(BF)
    up_value_grads = (hidden_grads * silu).astype(BF)
    both_grads = jnp.concatenate([gate_value_grads, up_value_grads], axis=1)
    row_grads_ref[0, :, :D] = matmul(both_grads, weights, ((1,), (1,))).astype(BF)
    top = gate_grad.astype(BF)
    bottom = (gate_grad - top.astype(F32)).astype(BF)
    row_grads_ref[0, :, D:] = jnp.where(
        high, top.astype(F32), jnp.where(low, bottom.astype(F32), 0.0)
    ).astype(BF)

    term = matmul(tokens, both_grads, ((0,), (0,)))
    down_term = matmul(hidden, result_grads, ((0,), (0,)))

    @pl.when(tile == 0)
    def _():
        sums[...] = term
        down_sum[...] = down_term

    @pl.when(tile > 0)
    def _():
        sums[...] += term
        down_sum[...] += down_term

    @pl.when(tile == tiles - 1)
    def _():
        weight_grads_ref[...] = sums[...].astype(BF).reshape(weight_grads_ref.shape)
        down_grad_ref[0] = down_sum[...]


def expert_chunk(where, rows, ups, weights, down, start, down_grad, group, at, grads):
    parts, experts, depth, width2 = weights.shape
    local, total_rows, wide_row = rows.shape
    tile = 384
    tiles = total_rows // tile
    slice_ff = down.shape[1]
    weight_spec = pl.BlockSpec((parts, 1, depth, width2), lambda e, i, c: (0, e, 0, 0))
    down_spec = pl.BlockSpec((1, slice_ff, D), lambda e, i, c: (start + e, 0, 0))
    in_specs = [
        pl.BlockSpec((1, tile, wide_row), lambda e, i, c: (start + e, i, 0)),
        pl.BlockSpec((1, tile, D), lambda e, i, c: (start + e, i, 0)),
        weight_spec,
        down_spec,
    ]
    args = [where, rows, ups, weights, down]
    aliases = {}
    for buffer, index in ((down_grad, 3), (grads, 2)):
        if buffer is not None:
            in_specs.append(pl.BlockSpec(memory_space=pl.ANY))
            aliases[len(args)] = index
            args.append(buffer)
    return pl.pallas_call(
        functools.partial(expert_body, parts, tiles, start, len(aliases)),
        grid_spec=pltpu.PrefetchScalarGridSpec(
            num_scalar_prefetch=1,
            grid=(experts, tiles),
            in_specs=in_specs,
            out_specs=[
                pl.BlockSpec((1, tile, D), lambda e, i, c: (e, i, 0)),
                pl.BlockSpec((1, tile, wide_row), lambda e, i, c: (e, i, 0)),
                pl.BlockSpec((parts, 1, depth, width2), lambda e, i, c: (0, at + e, 0, 0)),
                down_spec,
            ],
            scratch_shapes=[
                pltpu.VMEM((parts * depth, width2), F32),
                pltpu.VMEM((slice_ff, D), F32),
            ],
        ),
        out_shape=[
            jax.ShapeDtypeStruct((experts, total_rows, D), BF),
            jax.ShapeDtypeStruct((experts, total_rows, wide_row), BF),
            jax.ShapeDtypeStruct((parts, group, depth, width2), BF),
            jax.ShapeDtypeStruct((local, slice_ff, D), F32),
        ],
        input_output_aliases=aliases,
        compiler_params=pltpu.CompilerParams(vmem_limit_bytes=VMEM_BYTES),
        cost_estimate=pl.CostEstimate(
            flops=18 * experts * total_rows * D * slice_ff,
            bytes_accessed=8 * experts * total_rows * D + 18 * experts * D * slice_ff,
            transcendentals=experts * total_rows * slice_ff,
        ),
        name="experts",
    )(*args)


def slice_body(parts, width, gate_ref, up_ref, out):
    for s in range(parts):
        columns = slice(s * width, (s + 1) * width)
        out[s, 0, :, :width] = gate_ref[0, :, columns]
        out[s, 0, :, width:] = up_ref[0, :, columns]


def slice_weights(gate, up, start, experts, parts):
    depth = gate.shape[1]
    width = FF // parts
    spec = pl.BlockSpec((1, depth, FF), lambda e: (start + e, 0, 0))
    return pl.pallas_call(
        functools.partial(slice_body, parts, width),
        grid=(experts,),
        in_specs=[spec, spec],
        out_specs=pl.BlockSpec((parts, 1, depth, 2 * width), lambda e: (0, e, 0, 0)),
        out_shape=jax.ShapeDtypeStruct((parts, experts, depth, 2 * width), BF),
        compiler_params=pltpu.CompilerParams(vmem_limit_bytes=VMEM_BYTES),
        cost_estimate=pl.CostEstimate(
            flops=0, bytes_accessed=8 * experts * depth * FF, transcendentals=0
        ),
        name="slice_weights",
    )(gate, up)


def assemble_body(parts, width, *refs):
    source = refs[0]
    gate_ref, up_ref = refs[-2], refs[-1]
    for s in range(parts):
        columns = slice(s * width, (s + 1) * width)
        gate_ref[0, :, columns] = source[s, 0, :, :width].astype(F32)
        up_ref[0, :, columns] = source[s, 0, :, width:].astype(F32)


def assemble(source, start, local, buffers):
    parts, experts, depth, width2 = source.shape
    in_specs = [pl.BlockSpec((parts, 1, depth, width2), lambda e: (0, e, 0, 0))]
    args = [source]
    aliases = {}
    if buffers is not None:
        in_specs += [pl.BlockSpec(memory_space=pl.ANY)] * 2
        aliases = {1: 0, 2: 1}
        args += list(buffers)
    spec = pl.BlockSpec((1, depth, FF), lambda e: (start + e, 0, 0))
    return pl.pallas_call(
        functools.partial(assemble_body, parts, width2 // 2),
        grid=(experts,),
        in_specs=in_specs,
        out_specs=[spec, spec],
        out_shape=[jax.ShapeDtypeStruct((local, depth, FF), F32)] * 2,
        input_output_aliases=aliases,
        compiler_params=pltpu.CompilerParams(vmem_limit_bytes=VMEM_BYTES),
        cost_estimate=pl.CostEstimate(
            flops=0, bytes_accessed=6 * experts * depth * FF * 2, transcendentals=0
        ),
        name="assemble",
    )(*args)


def pick_body(where, *refs):
    out = refs[-1]
    for i, source in enumerate(refs[:-1]):
        at = 0 if i == 0 else out.shape[1] - 1
        out[0, at : at + source.shape[0]] = source[:, 0]


def pick_blocks(order, *sources):
    _, _, rows, width = sources[0].shape
    count = order.shape[0]
    outer = sum(x.shape[0] for x in sources)
    return pl.pallas_call(
        pick_body,
        grid_spec=pltpu.PrefetchScalarGridSpec(
            num_scalar_prefetch=1,
            grid=(count,),
            in_specs=[
                pl.BlockSpec((x.shape[0], 1, rows, width), lambda k, c: (0, c[k], 0, 0))
                for x in sources
            ],
            out_specs=pl.BlockSpec((1, outer, rows, width), lambda k, c: (k, 0, 0, 0)),
        ),
        out_shape=jax.ShapeDtypeStruct((count, outer, rows, width), BF),
        compiler_params=pltpu.CompilerParams(vmem_limit_bytes=VMEM_BYTES),
        cost_estimate=pl.CostEstimate(
            flops=0, bytes_accessed=4 * count * outer * rows * width, transcendentals=0
        ),
        name="pick_blocks",
    )(order, *sources)


def tie(value, *after):
    return lax.optimization_barrier((value, *after))[0]


def split_low(x):
    top = x.astype(BF)
    return top, (x - top.astype(F32)).astype(BF)


def add_up(parts):
    total = parts[0].astype(F32)
    for part in parts[1:]:
        total = total + part.astype(F32)
    return total


def make_on_device(wide, narrow):
    planes = wide // 2
    local = E // wide
    heads = H // wide
    features = heads * HD
    if local == 8:
        sizes, early, groups = [2, 1, 1, 2, 2], 3, [[0], [1, 2, 3], [4]]
    else:
        sizes = [1] * local
        early, groups = min(2, local), [[c] for c in range(local)]
    calls = len(sizes)
    starts = [sum(sizes[:c]) for c in range(calls)]
    slice_ff = FF // narrow
    both_axes = ("wide", "narrow")

    def swap(x, axis, r):
        size = wide if axis == "wide" else narrow
        return lax.ppermute(x, axis, [(i, i ^ r) for i in range(size)])

    bits = [1 << i for i in reversed(range(narrow.bit_length() - 1))]
    near = [0]
    for bit in bits:
        near = near + [r ^ bit for r in near]

    def gather_narrow(x, *after):
        for i, bit in enumerate(bits):
            if i and after:
                x = tie(x, *after)
            x = jnp.concatenate([x, swap(x, "narrow", bit)], axis=0)
        return x

    def scatter_narrow(keep, send, *after):
        first = None
        for bit in reversed(bits):
            total = keep.astype(F32) + swap(send, "narrow", bit).astype(F32)
            first = total if first is None else first
            half = total.shape[0] // 2
            keep, send = total[:half], total[half:].astype(BF)
            if after:
                send = tie(send, *after)
        return total[0], first

    def gather_planes(x):
        return [x] + [swap(x, "wide", 2 * q) for q in range(1, planes)]

    def cross(pieces):
        return [swap(piece, "wide", 1) for piece in pieces]

    def gather_wide(x):
        own = gather_planes(x)
        return own, cross(own)

    def join(own, other):
        return jnp.concatenate([piece for pair in zip(own, other) for piece in pair], axis=0)

    def scatter_wide(own, other):
        return scatter_plane(own, swap(other, "wide", 1))[0]

    def scatter_plane(own, came, *after):
        sums = [own[q].astype(F32) + came[q].astype(F32) for q in range(planes)]
        sent = [x.astype(BF) for x in sums[1:]]
        if after:
            sent = list(lax.optimization_barrier((*sent, *after))[: planes - 1])
        total = sums[0]
        for q in range(1, planes):
            total = total + swap(sent[q - 1], "wide", 2 * q).astype(F32)
        return total, sent

    def on_device(
        tokens, positions, routes, cotangent,
        w_query, w_key, w_value, w_output, w_router,
        gain_attn, gain_query, gain_key, gain_ffn,
        w_gate, w_up, w_down,
    ):
        count = tokens.shape[0]
        rows = w_query.shape[0]
        w = lax.axis_index("wide")
        n = lax.axis_index("narrow")
        where = jnp.stack([n, w * local, w]).astype(jnp.int32)
        wide_order = jnp.arange(wide) ^ w
        near_order = jnp.array(near) ^ n
        narrow_order = jnp.array([near.index(r) for r in range(narrow)])[jnp.arange(narrow) ^ n]

        def by_narrow(*x):
            half = narrow // 2
            send = pick_blocks(near_order[half:], *x)
            return pick_blocks(near_order[:half], *x), send

        routed = jnp.any(
            routes[:, :, None] == jnp.arange(E, dtype=jnp.int32)[None, None, :], axis=1
        )
        earlier = matmul(
            jnp.tril(jnp.ones((count, count), BF), -1), routed.astype(BF), ((1,), (0,))
        )
        slots = jnp.where(routed, earlier, -1.0).astype(BF).T

        small = jnp.concatenate(
            [
                w_router.reshape(-1), gain_attn, gain_query, gain_key, gain_ffn,
                positions.astype(BF),
            ]
        )
        small_rows = -(-small.shape[0] // LANES)
        bundle_rows = -(-(E + small_rows) // 16) * 16
        small = jnp.pad(small, (0, (bundle_rows - E) * LANES - small.shape[0]))
        bundle = jnp.concatenate([slots, small.reshape(-1, LANES)], axis=0)
        bundle_z = lax.all_gather(bundle, "narrow")
        stacked = jnp.concatenate(
            [x.reshape(rows, wide, features) for x in (w_query, w_key, w_value)], axis=-1
        ).transpose(1, 0, 2)
        columns = lax.all_to_all(stacked, "wide", 0, 0, tiled=True)
        bundles = lax.all_gather(bundle_z, "wide")
        all_slots = bundles[:, :, :E, :]
        all_small = bundles[:, :, E:, :].reshape(wide, narrow, -1)
        base = rows * E
        plane_positions = lax.dynamic_index_in_dim(
            all_small[:, :, base + 4 * rows : base + 4 * rows + count], n, 1, keepdims=False
        )
        plane_positions = jnp.take(plane_positions, wide_order, axis=0).reshape(wide * count)
        router_full = all_small[:, :, :base].reshape(D, E)
        gains = [
            all_small[:, :, base + i * rows : base + (i + 1) * rows].reshape(D).astype(F32)
            for i in range(4)
        ]
        attn_gain, query_gain, key_gain, ffn_gain = gains
        query_gain = lax.dynamic_slice_in_dim(query_gain, w * features, features)
        key_gain = lax.dynamic_slice_in_dim(key_gain, w * features, features)
        expert_counts = jnp.sum((all_slots >= 0).astype(jnp.int32), axis=(0, 1, 3))

        tokens_near = gather_wide(tokens)
        plane_tokens = join(*tokens_near).astype(F32)
        plane_count = plane_tokens.shape[0]

        sliced = [
            slice_weights(w_gate, w_up, starts[c], sizes[c], narrow) for c in range(calls)
        ]
        expert_weights = []

        def send_weights(*after):
            part = tie(sliced[len(expert_weights)], *after)
            expert_weights.append(lax.all_to_all(part, "narrow", 0, 0, tiled=True))

        ups_z = gather_narrow(cotangent, bundle_z)
        send_weights(columns, bundles, ups_z)
        ups_own = gather_planes(tie(ups_z, *tokens_near[0], *tokens_near[1]))
        columns, w_output = lax.optimization_barrier(
            (columns, w_output, expert_weights[0], *tokens_near[0], *tokens_near[1], *ups_own[:3])
        )[:2]
        columns = gather_narrow(columns[None])
        columns = jnp.take(columns, narrow_order, axis=0)
        qkv = columns.transpose(1, 0, 2, 3).reshape(D, 3 * features)
        output_rows = gather_narrow(w_output[None])
        output_rows = jnp.take(output_rows, narrow_order, axis=0).reshape(features, D)
        while len(expert_weights) < early:
            send_weights(qkv, output_rows, *expert_weights[1:])

        local_slots = lax.dynamic_slice_in_dim(all_slots, w * local, local, axis=2)
        local_slots = jnp.take(jnp.take(local_slots, wide_order, axis=0), near_order, axis=1)
        pairs = narrow // 2
        local_slots = (
            local_slots.reshape(planes, 2, pairs, 2, local, count)
            .transpose(1, 0, 2, 4, 3, 5)
            .reshape(2, planes, pairs, local, 1, 2 * count)
        )
        row = jnp.arange(2 * CAP)[:, None]
        lane = jnp.arange(2 * count)[None, :]
        picks = (
            ((local_slots == (row % CAP).astype(BF)) & (row // CAP == lane // count))
            .astype(BF)
            .reshape(2, planes, pairs, local * 2 * CAP, 2 * count)
        )
        picks_own, picks_other = picks[0], picks[1]
        inverse = lax.rsqrt(jnp.mean(plane_tokens * plane_tokens, axis=-1, keepdims=True) + EPSILON)
        normed = (plane_tokens * inverse * attn_gain).astype(BF)
        raw = matmul(normed, tie(qkv, *ups_own), ((1,), (0,)))
        query_raw = raw[:, :features]
        key_raw = raw[:, features : 2 * features]
        values = raw[:, 2 * features :].astype(BF).reshape(wide, count, heads, HD)

        def row_sums(a, b):
            sums = jnp.stack([jnp.sum(a, axis=-1), jnp.sum(b, axis=-1)])
            sums = jnp.take(sums.reshape(2, wide, count), wide_order, axis=1)
            sums = jnp.sum(lax.all_gather(sums, "wide"), axis=0)
            sums = jnp.take(sums, wide_order, axis=1).reshape(2, plane_count)
            return sums[0][:, None], sums[1][:, None]

        query_square, key_square = row_sums(query_raw * query_raw, key_raw * key_raw)
        query_r = lax.rsqrt(query_square / D + EPSILON)
        key_r = lax.rsqrt(key_square / D + EPSILON)
        frequency = THETA_BASE ** (-2.0 * jnp.arange(HD // 2, dtype=F32) / HD)
        angles = plane_positions.astype(F32)[:, None] * frequency[None, :]
        cosine = jnp.cos(angles)[:, None, :]
        sine = jnp.sin(angles)[:, None, :]

        def turn(x, sign):
            x = x.reshape(plane_count, heads, HD)
            a, b = x[..., : HD // 2], x[..., HD // 2 :]
            return jnp.concatenate(
                [a * cosine - sign * b * sine, b * cosine + sign * a * sine], axis=-1
            )

        shape = (wide, count, heads, HD)
        queries = turn(query_raw * query_r * query_gain, 1.0).astype(BF).reshape(shape)
        key_rows = turn(key_raw * key_r * key_gain, 1.0).astype(BF).reshape(shape)
        if early > 2:
            queries = tie(queries, expert_weights[1])
        scale = HD ** (-0.5)
        causal = (jnp.arange(count)[:, None] >= jnp.arange(count)[None, :])[None, None]
        scores = (
            jnp.einsum("bqhd,bkhd->bhqk", queries, key_rows, preferred_element_type=F32) * scale
        )
        scores = jnp.where(causal, scores, -1e30)
        powers = jnp.exp(scores - jnp.max(scores, axis=-1, keepdims=True))
        attn_probs = powers / jnp.sum(powers, axis=-1, keepdims=True)
        probs_low = attn_probs.astype(BF)
        attended = (
            jnp.einsum("bhqk,bkhd->bqhd", probs_low, values, preferred_element_type=F32)
            .astype(BF)
            .reshape(plane_count, features)
        )
        branch = matmul(attended, output_rows, ((1,), (0,))).astype(BF)
        branch = branch.reshape(planes, 2, count, D)
        branch = scatter_wide(branch[:, 0], branch[:, 1])

        residual = tokens.astype(F32) + branch
        ffn_r = lax.rsqrt(jnp.mean(residual * residual, axis=-1, keepdims=True) + EPSILON)
        normed_ffn = (residual * ffn_r * ffn_gain).astype(BF)
        logits = matmul(normed_ffn, router_full, ((1,), (0,)))
        router_powers = jnp.exp(logits - jnp.max(logits, axis=-1, keepdims=True))
        router_probs = router_powers / jnp.sum(router_powers, axis=-1, keepdims=True)

        message = jnp.concatenate([normed_ffn, *split_low(router_probs)], axis=1)
        ups = dispatch(picks_own, ups_own, 0)
        ups = dispatch(picks_other, cross(ups_own), 1, ups)
        message = gather_narrow(tie(message, ups, expert_weights[-1]))
        if calls > early:
            send_weights(message)
        tokens_own = gather_planes(message)
        while len(expert_weights) < calls:
            send_weights(*tokens_own)
        tokens_own[0] = tie(tokens_own[0], expert_weights[min(early, calls - 1)])
        tokens_other = cross(tokens_own)
        expert_rows = dispatch(picks_own, tokens_own, 0)
        expert_rows = dispatch(picks_other, tokens_other, 1, expert_rows)

        results, row_grads, came = [], [], []
        down_grad = None
        for c in range(calls):
            if c == 1:
                expert_rows = tie(expert_rows, expert_weights[-1])
            group = next(g for g in groups if c in g)
            grads = came[-1] if c != group[0] else None
            result, row_grad, grads, down_grad = expert_chunk(
                where, expert_rows, ups, expert_weights[c], w_down, starts[c], down_grad,
                sum(sizes[g] for g in group), starts[c] - starts[group[0]], grads,
            )
            results.append(result)
            row_grads.append(row_grad)
            if c == group[0]:
                came.append(grads)
            else:
                came[-1] = grads
        buffers, arrived = [None], []

        def send_grads(*after):
            g = len(buffers) - 1
            part = tie(came[g], *after) if after else came[g]
            part = lax.all_to_all(part, "narrow", 0, 0, tiled=True)
            arrived.append(part)
            buffers.append(assemble(part, starts[groups[g][0]], local, buffers[-1]))

        for g in range(len(groups) - 1):
            send_grads(*([row_grads[-1]] if g else []))

        def combine_tokens(terms, *after):
            terms = [tie(terms[0], *after), *terms[1:]] if after else terms
            other = combine(picks_other, terms, 1)
            other = [swap(x, "wide", 1) for x in other]
            return list(combine(picks_own, terms, 0)), other

        def scatter_rest(plane_sum):
            blocks = plane_sum.reshape(narrow, count, plane_sum.shape[-1])
            return scatter_narrow(blocks[: narrow // 2], blocks[narrow // 2 :])[0]

        own, other = combine_tokens(row_grads)
        plane_sum, sent = scatter_plane(own, other)
        mix_own, mix_other = combine_tokens(results, *sent)
        mix_sums = [mix_own[q].astype(F32) + mix_other[q].astype(F32) for q in range(planes)]
        mix_sent = [x.astype(BF) for x in mix_sums[1:]]
        plane_sum = tie(plane_sum.astype(BF), *arrived, *mix_sent)
        ffn_message = scatter_rest(plane_sum)
        send_grads(ffn_message)

        upstream = cotangent.astype(F32)
        prob_grads = ffn_message[:, D : D + E] + ffn_message[:, D + E : D + 2 * E]
        logit_grads = (
            router_probs
            * (prob_grads - jnp.sum(router_probs * prob_grads, axis=-1, keepdims=True))
        ).astype(BF)
        ffn_grads = ffn_message[:, :D] + matmul(logit_grads, router_full, ((1,), (1,)))

        def norm_back(v, r, gain, dy):
            u = dy * gain
            return r * u - v * (r * r * r) * jnp.mean(u * v, axis=-1, keepdims=True)

        residual_grads = upstream + norm_back(residual, ffn_r, ffn_gain, ffn_grads)
        ffn_gain_part = jnp.sum(ffn_grads * residual * ffn_r, axis=0)
        message = jnp.concatenate(
            [residual_grads.astype(BF), logit_grads, jnp.zeros_like(logit_grads)], axis=1
        )

        plane_message = join(*gather_wide(message))
        mix_came = [swap(tie(mix_sent[0], plane_message), "wide", 2)]
        plane_grads = plane_message[:, :D]
        attended_grads = (
            matmul(plane_grads, output_rows, ((1,), (1,))).astype(BF).reshape(shape)
        )
        plane_rows = lax.dynamic_slice_in_dim(
            join([x[:count] for x in tokens_own], [x[:count] for x in tokens_other]),
            w * features,
            features,
            axis=1,
        )
        prob_grads_attn = jnp.einsum(
            "bqhd,bkhd->bhqk", attended_grads, values, preferred_element_type=F32
        )
        value_grads = (
            jnp.einsum("bhqk,bqhd->bkhd", probs_low, attended_grads, preferred_element_type=F32)
            .astype(BF)
            .reshape(plane_count, features)
        )
        score_grads = attn_probs * (
            prob_grads_attn - jnp.sum(attn_probs * prob_grads_attn, axis=-1, keepdims=True)
        )
        score_grads = jnp.where(causal, score_grads, 0.0).astype(BF)
        query_grads = (
            jnp.einsum("bhqk,bkhd->bqhd", score_grads, key_rows, preferred_element_type=F32)
            * scale
        )
        key_grads = (
            jnp.einsum("bhqk,bqhd->bkhd", score_grads, queries, preferred_element_type=F32)
            * scale
        )
        query_dy = turn(query_grads, -1.0).reshape(plane_count, features)
        key_dy = turn(key_grads, -1.0).reshape(plane_count, features)
        query_u = tie(query_dy, *mix_came) * query_gain
        key_u = key_dy * key_gain
        query_dot, key_dot = row_sums(query_u * query_raw, key_u * key_raw)
        query_raw_grads = query_r * query_u - query_raw * (query_r**3) * (query_dot / D)
        key_raw_grads = key_r * key_u - key_raw * (key_r**3) * (key_dot / D)
        mix_came += [
            swap(tie(mix_sent[q - 1], query_dot), "wide", 2 * q) for q in range(2, planes)
        ]
        raw_grads = jnp.concatenate(
            [query_raw_grads.astype(BF), key_raw_grads.astype(BF), value_grads], axis=1
        )
        normed_grads = matmul(raw_grads, qkv, ((1,), (1,))).astype(BF)
        raw_grads = tie(raw_grads, arrived[-1])

        grad_output = jnp.concatenate(
            [
                matmul(attended, plane_grads, ((0,), (0,))).astype(BF),
                matmul(plane_rows, plane_message[:, D:], ((0,), (0,))).astype(BF),
            ],
            axis=1,
        )
        grad_output, _ = scatter_narrow(
            *by_narrow(tie(grad_output, query_dot).reshape(1, narrow, rows, D + LANES))
        )
        grad_output = grad_output[0]

        attn_gain_part = jnp.sum(normed_grads.astype(F32) * plane_tokens * inverse, axis=0)
        grad_qkv = matmul(normed, raw_grads, ((0,), (0,))).astype(BF)
        grad_qkv = grad_qkv.reshape(wide, narrow, rows, 3 * features)
        gain_parts = jnp.concatenate(
            [
                jnp.stack([attn_gain_part, ffn_gain_part]).reshape(2 * wide, narrow, rows),
                jnp.stack(
                    [
                        jnp.sum(query_dy * query_raw * query_r, axis=0),
                        jnp.sum(key_dy * key_raw * key_r, axis=0),
                    ]
                ).reshape(2, narrow, rows),
            ]
        ).transpose(1, 2, 0)
        columns_each = 2 * wide + 2
        gain_parts = jnp.concatenate(split_low(gain_parts), axis=-1)
        gain_parts = jnp.pad(
            gain_parts, ((0, 0), (0, 0), (0, 3 * features - 2 * columns_each))
        )
        grad_qkv, first_sums = scatter_narrow(*by_narrow(grad_qkv, gain_parts[None]))
        gain_parts = grad_qkv[wide, :, :columns_each] + grad_qkv[wide, :, columns_each : 2 * columns_each]
        gain_parts = gain_parts.T
        grad_qkv = grad_qkv[:wide]
        grad_gain_query, grad_gain_key = gain_parts[2 * wide], gain_parts[2 * wide + 1]
        mix_came = list(lax.optimization_barrier((*mix_came, first_sums))[:-1])
        mixture = scatter_rest(add_up([mix_sums[0], *mix_came]).astype(BF))
        block_out = (residual + mixture).astype(BF)
        gain_rows = jnp.concatenate(
            [*split_low(gain_parts[:wide]), *split_low(gain_parts[wide : 2 * wide])], axis=1
        )
        gain_rows = jnp.pad(
            gain_rows[:, None, :], ((0, 0), (0, 15), (0, 3 * features - 4 * rows))
        )
        grad_qkv = jnp.concatenate([grad_qkv.astype(BF), gain_rows], axis=1)
        grad_qkv = lax.all_to_all(grad_qkv, "wide", 0, 0, tiled=True)
        gain_rows = jnp.sum(grad_qkv[:, rows, : 4 * rows].astype(F32), axis=0).reshape(4, rows)
        gain_sums = [gain_rows[0] + gain_rows[1], gain_rows[2] + gain_rows[3]]
        grad_qkv = grad_qkv[:, :rows].transpose(1, 0, 2).astype(F32)
        grad_query, grad_key, grad_value = [
            grad_qkv[..., i * features : (i + 1) * features].reshape(rows, D) for i in range(3)
        ]

        normed_grads = normed_grads.reshape(planes, 2, count, D)
        normed_grads, _ = scatter_plane(
            normed_grads[:, 0], swap(normed_grads[:, 1], "wide", 1), first_sums
        )
        input_grad = (
            residual_grads
            + norm_back(tokens.astype(F32), inverse[:count], attn_gain, normed_grads)
        ).astype(BF)

        grad_gate, grad_up = buffers[-1]

        return (
            block_out, input_grad, grad_query, grad_key, grad_value,
            grad_output[:, :D], grad_output[:, D : D + E],
            gain_sums[0], grad_gain_query, grad_gain_key, gain_sums[1],
            grad_gate, grad_up, down_grad, expert_counts,
        )

    return on_device


def solution(mesh):
    both = ("wide", "narrow")
    in_specs = (P(both, None), P(both), P(both, None), P(both, None))
    in_specs += (P(both, None),) * 5 + (P(both),) * 4 + (P("wide", "narrow", None),) * 3
    out_specs = (P(both, None),) * 7 + (P(both),) * 4 + (P("wide", "narrow", None),) * 3 + (P(),)
    return jax.shard_map(
        make_on_device(mesh.shape["wide"], mesh.shape["narrow"]),
        mesh=mesh,
        in_specs=in_specs,
        out_specs=out_specs,
        check_vma=False,
    )
```

time: 1770 us -> 1300 us (0.73)
  waiting for transfers between devices: 886 us -> 599 us
  starting transfers between devices: 368 us -> 98 us
  blocking collectives: 0 us -> 59.4 us
  Pallas kernels: 230 us -> 283 us
  local copies, waits for them, and re-layouts: 124 us -> 99 us
    ppermute x162 -> x66, waiting for transfers between devices: 886 us -> 512 us  [swap(): return lax.ppermute(x, axis, [(i, i ^ r) for i in range(size)])]
    ppermute x162 -> x66, starting transfers between devices: 368 us -> 49.5 us  [swap(): return lax.ppermute(x, axis, [(i, i ^ r) for i in range(size)])]
    all_to_all x0 -> x10, waiting for transfers between devices: none -> 86.9 us  [the longest x5 72.8 us: send_weights(): expert_weights.append(lax.all_to_all(part, 'narrow', 0, 0, tiled=True))]
    all_gather x0 -> x4, blocking collectives: none -> 59.4 us  [the longest x1 26.5 us: on_device(): bundle_z = lax.all_gather(bundle, 'narrow')]
    pallas_call x12 -> x22, Pallas kernels: 207 us -> 262 us  [the longest x5 132 us: expert_chunk(): pl.pallas_call(functools.partial(expert_body, parts, tiles, start, len(al...]
    all_to_all x0 -> x10, starting transfers between devices: none -> 48.5 us  [the longest x5 24.3 us: send_weights(): expert_weights.append(lax.all_to_all(part, 'narrow', 0, 0, tiled=True))]
    slice x22 -> x17, local copies, waits for them, and re-layouts: 25 us -> 6.99 us  [the longest x1 2.05 us: on_device(): picks_own, picks_other = (picks[0], picks[1])]
    unnamed x299 -> x239, local copies, waits for them, and re-layouts: 37.1 us -> 45.5 us
  transfers between devices with their start and end apart: 162 -> 76, of which waited for: 58 -> 37; matrix products, arithmetic and copies ran while one was open for 11% -> 17% of each run, Pallas kernels for 13% -> 22%
where the time goes in v2:
time: 1300 us; the launch traced here: 1290 us
  waiting for transfers between devices  599 us (46%)
  Pallas kernels  283 us (22%)
  other arithmetic  100 us (8%)
  local copies, waits for them, and re-layouts  99 us (8%)
  starting transfers between devices  98 us (8%)
  blocking collectives  59.4 us (5%)
  matrix products  46 us (4%)
    ppermute x66, waiting for transfers between devices, swap(): return lax.ppermute(x, axis, [(i, i ^ r) for i in range(size)])  512 us
    pallas_call x5, Pallas kernels, expert_chunk(): pl.pallas_call(functools.partial(expert_body, parts, tiles, start, len(al...  132 us
    all_to_all x5, waiting for transfers between devices, send_weights(): expert_weights.append(lax.all_to_all(part, 'narrow', 0, 0, tiled=True))  72.8 us
    pallas_call x4, Pallas kernels, combine(): pl.pallas_call(functools.partial(combine_body, pieces, each, len(rows)),...  64.4 us
    ppermute x66, starting transfers between devices, swap(): return lax.ppermute(x, axis, [(i, i ^ r) for i in range(size)])  49.5 us
    unnamed x239, local copies, waits for them, and re-layouts  45.5 us
    pallas_call x4, Pallas kernels, dispatch(): pl.pallas_call(functools.partial(dispatch_body, pieces, each), grid=(pair...  36.4 us
    dot_general x10, matrix products, matmul(): return lax.dot_general(a, b, (dims, ((), ())), preferred_element_type=F32)  31.8 us
  transfers between devices with their start and end apart: 76, of which 37 were waited for; matrix products, arithmetic and copies ran while one was open for 17% of the time, Pallas kernels for 22%

profile of v2, /device:TPU:0, one launch (start us, length us, event | category | flops | bytes accessed | tf_op | source)
XLA Modules:
  0.0 1287.1 jit_solution(9447207884150884857)
XLA Ops:
  9.9 26.5 %all-gather = bf16[448,128]{1,0:T(8,128)(2,1)S(1)} all-gather(bf16[112,128]{1,0:T(8,128)(2,1)S(1)} %pad_maximum_fusion.13), channel_id=2, replica_groups=mesh['wide'=8,'narrow'=4] {'narrow'}, dimensions={0}, use_global_device_ids=true | all-gather | bytes 143360 | tf_op jit(solution)/shard_map/all_gather | solution.py:442
  47.1 15.0 %all-gather.1 = bf16[32,112,128]{2,1,0:T(8,128)(2,1)S(1)} all-gather(bf16[4,112,128]{2,1,0:T(8,128)(2,1)S(1)} %bitcast.353), channel_id=3, replica_groups=mesh['wide'=8,'narrow'=4] {'wide'}, dimensions={0}, use_global_device_ids=true | all-gather | bytes 1032192 | tf_op jit(solution)/shard_map/all_gather | solution.py:447
  86.3 10.6 collective-permute-done.3
  114.2 33.7 %collective-permute-done.10.refs_3_ = bf16[512,2048]{1,0:T(8,128)(2,1)} collective-permute-done((bf16[512,2048]{1,0:T(8,128)(2,1)}, bf16[512,2048]{1,0:T(8,128)(2,1)}, u32[]{:S(2)}, u32[]{:S(2)}) %collective-permute-start.10) | collective-permute-done | bytes 2097184 | tf_op jit(solution)/shard_map/ppermute | solution.py:353
  147.9 16.6 %all-to-all-done.1.refs_3_ = bf16[4,2,512,512]{3,2,1,0:T(8,128)(2,1)} async-done(((bf16[4,2,512,512]{3,2,1,0:T(8,128)(2,1)}), bf16[4,2,512,512]{3,2,1,0:T(8,128)(2,1)}, u32[]{:S(2)}, u32[]{:S(2)}) %all-to-all-start.1) | async-done | bytes 4194336 | tf_op jit(solution)/shard_map/all_to_all | solution.py:476
  172.5 39.4 %collective-permute-done.14 = bf16[1,64,2048]{2,1,0:T(8,128)(2,1)S(1)} collective-permute-done((bf16[1,64,2048]{2,1,0:T(8,128)(2,1)S(1)}, bf16[1,64,2048]{2,1,0:T(8,128)(2,1)S(1)}, u32[]{:S(2)}, u32[]{:S(2)}) %collective-permute-start.14) | collective-permute-done | bytes 262176 | tf_op jit(solution)/shard_map/ppermute | solution.py:353
  229.8 29.9 %collective-permute-done.12 = bf16[2,8,64,768]{3,2,1,0:T(8,128)(2,1)} collective-permute-done((bf16[2,8,64,768]{3,2,1,0:T(8,128)(2,1)}, bf16[2,8,64,768]{3,2,1,0:T(8,128)(2,1)}, u32[]{:S(2)}, u32[]{:S(2)}) %collective-permute-start.12) | collective-permute-done | bytes 1572896 | tf_op jit(solution)/shard_map/ppermute | solution.py:353
  310.5 10.0 all-to-all-done.2.refs_3_
  390.9 25.8 %collective-permute-done.24 = bf16[128,2176]{1,0:T(8,128)(2,1)S(1)} collective-permute-done((bf16[128,2176]{1,0:T(8,128)(2,1)S(1)}, bf16[128,2176]{1,0:T(8,128)(2,1)S(1)}, u32[]{:S(2)}, u32[]{:S(2)}) %collective-permute-start.24) | collective-permute-done | bytes 557088 | tf_op jit(solution)/shard_map/ppermute | solution.py:353
  420.7 22.6 %collective-permute-done.25 = bf16[256,2176]{1,0:T(8,128)(2,1)S(1)} collective-permute-done((bf16[256,2176]{1,0:T(8,128)(2,1)S(1)}, bf16[256,2176]{1,0:T(8,128)(2,1)S(1)}, u32[]{:S(2)}, u32[]{:S(2)}) %collective-permute-start.25) | collective-permute-done | bytes 1114144 | tf_op jit(solution)/shard_map/ppermute | solution.py:353
  455.7 45.0 %collective-permute-done.31.refs_4_ = bf16[512,2176]{1,0:T(8,128)(2,1)S(1)} collective-permute-done((bf16[512,2176]{1,0:T(8,128)(2,1)S(1)}, bf16[512,2176]{1,0:T(8,128)(2,1)S(1)}, u32[]{:S(2)}, u32[]{:S(2)}) %collective-permute-start.31) | collective-permute-done | bytes 2228256 | tf_op jit(solution)/shard_map/ppermute | solution.py:353
  500.7 45.8 %collective-permute-done.29.refs_3_ = bf16[512,2176]{1,0:T(8,128)(2,1)S(1)} collective-permute-done((bf16[512,2176]{1,0:T(8,128)(2,1)S(1)}, bf16[512,2176]{1,0:T(8,128)(2,1)S(1)}, u32[]{:S(2)}, u32[]{:S(2)}) %collective-permute-start.29) | collective-permute-done | bytes 2228256 | tf_op jit(solution)/shard_map/ppermute | solution.py:353
  578.1 31.3 %experts.5 = (bf16[2,768,2048]{2,1,0:T(8,128)(2,1)}, bf16[2,768,2176]{2,1,0:T(8,128)(2,1)}, bf16[4,2,512,512]{3,2,1,0:T(8,128)(2,1)}, f32[8,256,2048]{2,1,0:T(8,128)}) custom-call(s32[3]{0:T(128)} %pad_add_fusion.refs_0_, bf16[8,768,2176]{2,1,0:T(8,128)(2,1)} %dispatch.7.refs_1_, bf16[8,768,2048]{2,1,0:T(8,128)(2,1)} %dispatch.5.refs_2_, ...), custom_call_target="tpu_custom_call" | custom-call | flops 14495514624 | bytes 44040192 | tf_op jit(solution)/shard_map/experts/pallas_call | solution.py:196
  609.3 37.3 %all-to-all-done.5.refs_3_ = bf16[4,2,512,512]{3,2,1,0:T(8,128)(2,1)} async-done(((bf16[4,2,512,512]{3,2,1,0:T(8,128)(2,1)}), bf16[4,2,512,512]{3,2,1,0:T(8,128)(2,1)}, u32[]{:S(2)}, u32[]{:S(2)}) %all-to-all-start.5) | async-done | bytes 4194336 | tf_op jit(solution)/shard_map/all_to_all | solution.py:476
  651.7 18.9 %experts.6 = (bf16[1,768,2048]{2,1,0:T(8,128)(2,1)}, bf16[1,768,2176]{2,1,0:T(8,128)(2,1)}, bf16[4,4,512,512]{3,2,1,0:T(8,128)(2,1)}, f32[8,256,2048]{2,1,0:T(8,128)}) custom-call(s32[3]{0:T(128)} %pad_add_fusion.refs_0_, bf16[8,768,2176]{2,1,0:T(8,128)(2,1)} %dispatch.7.refs_1_, ...), custom_call_target="tpu_custom_call", output_to_operand_aliasing={{3}: (5, {})} | custom-call | flops 7247757312 | bytes 22020096 | tf_op jit(solution)/shard_map/experts/pallas_call | solution.py:196
  670.7 18.9 %experts.7 = (bf16[1,768,2048]{2,1,0:T(8,128)(2,1)}, bf16[1,768,2176]{2,1,0:T(8,128)(2,1)}, bf16[4,4,512,512]{3,2,1,0:T(8,128)(2,1)}, f32[8,256,2048]{2,1,0:T(8,128)}) custom-call(s32[3]{0:T(128)} %pad_add_fusion.refs_0_, bf16[8,768,2176]{2,1,0:T(8,128)(2,1)} %dispatch.7.refs_1_, ...), custom_call_target="tpu_custom_call", output_to_operand_aliasing={{3}: (5, {}), {2}: (6, {})} | custom-call | flops 7247757312 | bytes 22020096 | tf_op jit(solution)/shard_map/experts/pallas_call | solution.py:196
  689.6 31.8 %experts.8 = (bf16[2,768,2048]{2,1,0:T(8,128)(2,1)}, bf16[2,768,2176]{2,1,0:T(8,128)(2,1)}, bf16[4,4,512,512]{3,2,1,0:T(8,128)(2,1)}, f32[8,256,2048]{2,1,0:T(8,128)}) custom-call(s32[3]{0:T(128)} %pad_add_fusion.refs_0_, bf16[8,768,2176]{2,1,0:T(8,128)(2,1)} %dispatch.7.refs_1_, ...), custom_call_target="tpu_custom_call", output_to_operand_aliasing={{3}: (5, {}), {2}: (6, {})} | custom-call | flops 14495514624 | bytes 44040192 | tf_op jit(solution)/shard_map/experts/pallas_call | solution.py:196
  721.4 31.4 %experts.9 = (bf16[2,768,2048]{2,1,0:T(8,128)(2,1)}, bf16[2,768,2176]{2,1,0:T(8,128)(2,1)}, bf16[4,2,512,512]{3,2,1,0:T(8,128)(2,1)}, f32[8,256,2048]{2,1,0:T(8,128)}) custom-call(s32[3]{0:T(128)} %pad_add_fusion.refs_0_, bf16[8,768,2176]{2,1,0:T(8,128)(2,1)} %dispatch.7.refs_1_, ...), custom_call_target="tpu_custom_call", output_to_operand_aliasing={{3}: (5, {})} | custom-call | flops 14495514624 | bytes 44040192 | tf_op jit(solution)/shard_map/experts/pallas_call | solution.py:196
  758.6 16.6 %combine.5 = (bf16[512,2176]{1,0:T(8,128)(2,1)}, bf16[512,2176]{1,0:T(8,128)(2,1)}, bf16[512,2176]{1,0:T(8,128)(2,1)}, bf16[512,2176]{1,0:T(8,128)(2,1)}) custom-call(bf16[4,2,384,256]{3,2,1,0:T(8,128)(2,1)} %bitcast.299, bf16[2,768,2176]{2,1,0:T(8,128)(2,1)} %get-tuple-element.101.refs_1_, bf16[1,768,2176]{2,1,0:T(8,128)(2,1)} %get-tuple-element.105.refs_2_, ...), custom_call_target="tpu_custom_call" | custom-call | flops 3422552064 | bytes 22282240 | tf_op jit(solution)/shard_map/combine/pallas_call | solution.py:98
  776.5 16.6 %combine.4 = (bf16[512,2176]{1,0:T(8,128)(2,1)}, bf16[512,2176]{1,0:T(8,128)(2,1)}, bf16[512,2176]{1,0:T(8,128)(2,1)}, bf16[512,2176]{1,0:T(8,128)(2,1)}) custom-call(bf16[4,2,384,256]{3,2,1,0:T(8,128)(2,1)} %bitcast.295, bf16[2,768,2176]{2,1,0:T(8,128)(2,1)} %get-tuple-element.101.refs_1_, bf16[1,768,2176]{2,1,0:T(8,128)(2,1)} %get-tuple-element.105.refs_2_, ...), custom_call_target="tpu_custom_call" | custom-call | flops 3422552064 | bytes 22282240 | tf_op jit(solution)/shard_map/combine/pallas_call | solution.py:98
  801.3 15.7 %combine.7 = (bf16[512,2048]{1,0:T(8,128)(2,1)}, bf16[512,2048]{1,0:T(8,128)(2,1)}, bf16[512,2048]{1,0:T(8,128)(2,1)}, bf16[512,2048]{1,0:T(8,128)(2,1)}) custom-call(bf16[4,2,384,256]{3,2,1,0:T(8,128)(2,1)} %bitcast.300, bf16[2,768,2048]{2,1,0:T(8,128)(2,1)} %get-tuple-element.120.refs_1_, bf16[1,768,2048]{2,1,0:T(8,128)(2,1)} %get-tuple-element.121.refs_2_, ...), custom_call_target="tpu_custom_call" | custom-call | flops 3221225472 | bytes 20971520 | tf_op jit(solution)/shard_map/combine/pallas_call | solution.py:98
  829.8 15.5 %combine.6 = (bf16[512,2048]{1,0:T(8,128)(2,1)}, bf16[512,2048]{1,0:T(8,128)(2,1)}, bf16[512,2048]{1,0:T(8,128)(2,1)}, bf16[512,2048]{1,0:T(8,128)(2,1)}) custom-call(bf16[4,2,384,256]{3,2,1,0:T(8,128)(2,1)} %bitcast.296, bf16[2,768,2048]{2,1,0:T(8,128)(2,1)} %get-tuple-element.120.refs_1_, bf16[1,768,2048]{2,1,0:T(8,128)(2,1)} %get-tuple-element.121.refs_2_, ...), custom_call_target="tpu_custom_call" | custom-call | flops 3221225472 | bytes 20971520 | tf_op jit(solution)/shard_map/combine/pallas_call | solution.py:98
  857.6 17.5 %collective-permute-done.39 = bf16[512,2176]{1,0:T(8,128)(2,1)S(1)} collective-permute-done((bf16[512,2176]{1,0:T(8,128)(2,1)}, bf16[512,2176]{1,0:T(8,128)(2,1)S(1)}, u32[]{:S(2)}, u32[]{:S(2)}) %collective-permute-start.39) | collective-permute-done | bytes 2228256 | tf_op jit(solution)/shard_map/ppermute | solution.py:353
  875.1 47.1 %collective-permute-done.40 = bf16[512,2176]{1,0:T(8,128)(2,1)S(1)} collective-permute-done((bf16[512,2176]{1,0:T(8,128)(2,1)}, bf16[512,2176]{1,0:T(8,128)(2,1)S(1)}, u32[]{:S(2)}, u32[]{:S(2)}) %collective-permute-start.40) | collective-permute-done | bytes 2228256 | tf_op jit(solution)/shard_map/ppermute | solution.py:353
  927.3 14.1 %all-to-all-done.7.refs_0_ = bf16[4,4,512,512]{3,2,1,0:T(8,128)(2,1)} async-done(((bf16[4,4,512,512]{3,2,1,0:T(8,128)(2,1)}), bf16[4,4,512,512]{3,2,1,0:T(8,128)(2,1)}, u32[]{:S(2)}, u32[]{:S(2)}) %all-to-all-start.7) | async-done | bytes 8388640 | tf_op jit(solution)/shard_map/all_to_all | solution.py:603
  945.4 21.7 %collective-permute-done.44 = bf16[2,128,2176]{2,1,0:T(8,128)(2,1)S(1)} collective-permute-done((bf16[2,128,2176]{2,1,0:T(8,128)(2,1)S(1)}, bf16[2,128,2176]{2,1,0:T(8,128)(2,1)S(1)}, u32[]{:S(2)}, u32[]{:S(2)}) %collective-permute-start.44) | collective-permute-done | bytes 1114144 | tf_op jit(solution)/shard_map/ppermute | solution.py:353
  969.6 23.5 %collective-permute-done.45 = bf16[1,128,2176]{2,1,0:T(8,128)(2,1)S(1)} collective-permute-done((bf16[1,128,2176]{2,1,0:T(8,128)(2,1)S(1)}, bf16[1,128,2176]{2,1,0:T(8,128)(2,1)S(1)}, u32[]{:S(2)}, u32[]{:S(2)}) %collective-permute-start.45) | collective-permute-done | bytes 557088 | tf_op jit(solution)/shard_map/ppermute | solution.py:353
  1012.4 10.9 collective-permute-done.49
  1064.6 15.2 %collective-permute-done.53 = bf16[512,2048]{1,0:T(8,128)(2,1)} collective-permute-done((bf16[512,2048]{1,0:T(8,128)(2,1)}, bf16[512,2048]{1,0:T(8,128)(2,1)}, u32[]{:S(2)}, u32[]{:S(2)}) %collective-permute-start.53) | collective-permute-done | bytes 2097184 | tf_op jit(solution)/shard_map/ppermute | solution.py:353
  1172.5 47.3 %collective-permute-done.54 = bf16[512,2048]{1,0:T(8,128)(2,1)} collective-permute-done((bf16[512,2048]{1,0:T(8,128)(2,1)}, bf16[512,2048]{1,0:T(8,128)(2,1)}, u32[]{:S(2)}, u32[]{:S(2)}) %collective-permute-start.54) | collective-permute-done | bytes 2097184 | tf_op jit(solution)/shard_map/ppermute | solution.py:353
  1230.5 13.4 %collective-permute-done.61 = bf16[128,2048]{1,0:T(8,128)(2,1)S(1)} collective-permute-done((bf16[128,2048]{1,0:T(8,128)(2,1)S(1)}, bf16[128,2048]{1,0:T(8,128)(2,1)S(1)}, u32[]{:S(2)}, u32[]{:S(2)}) %collective-permute-start.61) | collective-permute-done | bytes 524320 | tf_op jit(solution)/shard_map/ppermute | solution.py:353
  1262.2 18.4 %collective-permute-done.58 = bf16[1,128,2048]{2,1,0:T(8,128)(2,1)S(1)} collective-permute-done((bf16[1,128,2048]{2,1,0:T(8,128)(2,1)S(1)}, bf16[1,128,2048]{2,1,0:T(8,128)(2,1)S(1)}, u32[]{:S(2)}, u32[]{:S(2)}) %collective-permute-start.58) | collective-permute-done | bytes 524320 | tf_op jit(solution)/shard_map/ppermute | solution.py:353
  (603 shorter events, 500.3 us)
Async XLA Ops:
  0.7 35.7 %collective-permute-start.7 = (bf16[128,2048]{1,0:T(8,128)(2,1)}, bf16[128,2048]{1,0:T(8,128)(2,1)S(1)}, u32[]{:S(2)}, u32[]{:S(2)}) collective-permute-start(bf16[128,2048]{1,0:T(8,128)(2,1)} %param.23), channel_id=1, source_target_pairs={{0,2},{1,3},{2,0},{3,1},{4,6},{5,7},{6,4},{7,5},{8,10},{9,11},{10,... | collective-permute-start | bytes 1572872 | tf_op jit(solution)/shard_map/ppermute | solution.py:353
  65.5 99.0 %all-to-all-start.1 = ((bf16[4,2,512,512]{3,2,1,0:T(8,128)(2,1)}), bf16[4,2,512,512]{3,2,1,0:T(8,128)(2,1)}, u32[]{:S(2)}, u32[]{:S(2)}) async-start(bf16[4,2,512,512]{3,2,1,0:T(8,128)(2,1)} %slice_weights.5), calls=%async_computation.1 | async-start | bytes 8388608 | tf_op jit(solution)/shard_map/all_to_all | solution.py:476
  99.8 48.0 %collective-permute-start.10 = (bf16[512,2048]{1,0:T(8,128)(2,1)}, bf16[512,2048]{1,0:T(8,128)(2,1)}, u32[]{:S(2)}, u32[]{:S(2)}) collective-permute-start(bf16[512,2048]{1,0:T(8,128)(2,1)} %constant_dynamic-update-slice_fusion.8.refs_1_), channel_id=1, source_target_pairs={{0,16},{4,20},{8,24},{12,28},{16,0},{20,4},{24,8},{28,12},{1,17},{... | collective-permute-start | bytes 6291464 | tf_op jit(solution)/shard_map/ppermute | solution.py:353
  100.2 47.7 %collective-permute-start.9 = (bf16[512,2048]{1,0:T(8,128)(2,1)}, bf16[512,2048]{1,0:T(8,128)(2,1)}, u32[]{:S(2)}, u32[]{:S(2)}) collective-permute-start(bf16[512,2048]{1,0:T(8,128)(2,1)} %constant_dynamic-update-slice_fusion.8.refs_1_), channel_id=1, source_target_pairs={{0,8},{4,12},{8,0},{12,4},{16,24},{20,28},{24,16},{28,20},{1,9},{5... | collective-permute-start | bytes 6291464 | tf_op jit(solution)/shard_map/ppermute | solution.py:353
  164.5 47.5 %collective-permute-start.11 = (bf16[1,8,64,768]{3,2,1,0:T(8,128)(2,1)S(1)}, bf16[1,8,64,768]{3,2,1,0:T(8,128)(2,1)S(1)}, u32[]{:S(2)}, u32[]{:S(2)}) collective-permute-start(bf16[1,8,64,768]{3,2,1,0:T(8,128)(2,1)S(1)} %bitcast.312), channel_id=1, source_target_pairs={{0,2},{1,3},{2,0},{3,1},{4,6},{5,7},{6,4},{7,5},{8,10},{9,11},{10,... | collective-permute-start | bytes 2359304 | tf_op jit(solution)/shard_map/ppermute | solution.py:353
  165.4 46.5 %collective-permute-start.14 = (bf16[1,64,2048]{2,1,0:T(8,128)(2,1)S(1)}, bf16[1,64,2048]{2,1,0:T(8,128)(2,1)S(1)}, u32[]{:S(2)}, u32[]{:S(2)}) collective-permute-start(bf16[1,64,2048]{2,1,0:T(8,128)(2,1)S(1)} %bitcast.347), channel_id=1, source_target_pairs={{0,2},{1,3},{2,0},{3,1},{4,6},{5,7},{6,4},{7,5},{8,10},{9,11},{10,... | collective-permute-start | bytes 786440 | tf_op jit(solution)/shard_map/ppermute | solution.py:353
  171.0 97.1 %collective-permute-start.13 = (bf16[512,2048]{1,0:T(8,128)(2,1)}, bf16[512,2048]{1,0:T(8,128)(2,1)}, u32[]{:S(2)}, u32[]{:S(2)}) collective-permute-start(bf16[512,2048]{1,0:T(8,128)(2,1)} %constant_dynamic-update-slice_fusion.8.refs_1_), channel_id=1, source_target_pairs={{0,24},{4,28},{8,16},{12,20},{16,8},{20,12},{24,0},{28,4},{1,25},{... | collective-permute-start | bytes 6291464 | tf_op jit(solution)/shard_map/ppermute | solution.py:353
  213.4 46.3 %collective-permute-start.12 = (bf16[2,8,64,768]{3,2,1,0:T(8,128)(2,1)}, bf16[2,8,64,768]{3,2,1,0:T(8,128)(2,1)}, u32[]{:S(2)}, u32[]{:S(2)}) collective-permute-start(bf16[2,8,64,768]{3,2,1,0:T(8,128)(2,1)} %pad_maximum_fusion.1), channel_id=1, source_target_pairs={{0,1},{1,0},{2,3},{3,2},{4,5},{5,4},{6,7},{7,6},{8,9},{9,8},{10,11... | collective-permute-start | bytes 4718600 | tf_op jit(solution)/shard_map/ppermute | solution.py:353
  268.1 52.4 %all-to-all-start.2 = ((bf16[4,1,512,512]{3,2,1,0:T(8,128)(2,1)}), bf16[4,1,512,512]{3,2,1,0:T(8,128)(2,1)}, u32[]{:S(2)}, u32[]{:S(2)}) async-start(bf16[4,1,512,512]{3,2,1,0:T(8,128)(2,1)} %slice_weights.6), calls=%async_computation.2 | async-start | bytes 4194304 | tf_op jit(solution)/shard_map/all_to_all | solution.py:476
  335.4 27.7 %collective-permute-start.22 = (bf16[512,2048]{1,0:T(8,128)(2,1)}, bf16[512,2048]{1,0:T(8,128)(2,1)}, u32[]{:S(2)}, u32[]{:S(2)}) collective-permute-start(bf16[512,2048]{1,0:T(8,128)(2,1)} %collective-permute-done.10.refs_3_), channel_id=1, source_target_pairs={{0,4},{4,0},{8,12},{12,8},{16,20},{20,16},{24,28},{28,24},{1,5},{5... | collective-permute-start | bytes 6291464 | tf_op jit(solution)/shard_map/ppermute | solution.py:353
  336.7 54.1 %all-to-all-start.3 = ((bf16[4,1,512,512]{3,2,1,0:T(8,128)(2,1)}), bf16[4,1,512,512]{3,2,1,0:T(8,128)(2,1)}, u32[]{:S(2)}, u32[]{:S(2)}) async-start(bf16[4,1,512,512]{3,2,1,0:T(8,128)(2,1)} %slice_weights.7), calls=%async_computation.3 | async-start | bytes 4194304 | tf_op jit(solution)/shard_map/all_to_all | solution.py:476
  443.5 104.5 %all-to-all-start.4 = ((bf16[4,2,512,512]{3,2,1,0:T(8,128)(2,1)}), bf16[4,2,512,512]{3,2,1,0:T(8,128)(2,1)}, u32[]{:S(2)}, u32[]{:S(2)}) async-start(bf16[4,2,512,512]{3,2,1,0:T(8,128)(2,1)} %slice_weights.8), calls=%async_computation.4 | async-start | bytes 8388608 | tf_op jit(solution)/shard_map/all_to_all | solution.py:476
  448.4 52.4 %collective-permute-start.31 = (bf16[512,2176]{1,0:T(8,128)(2,1)S(1)}, bf16[512,2176]{1,0:T(8,128)(2,1)S(1)}, u32[]{:S(2)}, u32[]{:S(2)}) collective-permute-start(bf16[512,2176]{1,0:T(8,128)(2,1)S(1)} %constant_dynamic-update-slice_fusion.10.refs_1_), channel_id=1, source_target_pairs={{0,24},{4,28},{8,16},{12,20},{16,8},{20,12},{24,0},{28,4},{1,25},{... | collective-permute-start | bytes 6684680 | tf_op jit(solution)/shard_map/ppermute | solution.py:353
  449.9 96.7 %collective-permute-start.29 = (bf16[512,2176]{1,0:T(8,128)(2,1)S(1)}, bf16[512,2176]{1,0:T(8,128)(2,1)S(1)}, u32[]{:S(2)}, u32[]{:S(2)}) collective-permute-start(bf16[512,2176]{1,0:T(8,128)(2,1)S(1)} %constant_dynamic-update-slice_fusion.10.refs_1_), channel_id=1, source_target_pairs={{0,16},{4,20},{8,24},{12,28},{16,0},{20,4},{24,8},{28,12},{1,17},{... | collective-permute-start | bytes 6684680 | tf_op jit(solution)/shard_map/ppermute | solution.py:353
  450.2 97.7 %collective-permute-start.27 = (bf16[512,2176]{1,0:T(8,128)(2,1)S(1)}, bf16[512,2176]{1,0:T(8,128)(2,1)}, u32[]{:S(2)}, u32[]{:S(2)}) collective-permute-start(bf16[512,2176]{1,0:T(8,128)(2,1)S(1)} %constant_dynamic-update-slice_fusion.10.refs_1_), channel_id=1, source_target_pairs={{0,8},{4,12},{8,0},{12,4},{16,24},{20,28},{24,16},{28,20},{1,9},{5... | collective-permute-start | bytes 6684680 | tf_op jit(solution)/shard_map/ppermute | solution.py:353
  548.0 98.7 %all-to-all-start.5 = ((bf16[4,2,512,512]{3,2,1,0:T(8,128)(2,1)}), bf16[4,2,512,512]{3,2,1,0:T(8,128)(2,1)}, u32[]{:S(2)}, u32[]{:S(2)}) async-start(bf16[4,2,512,512]{3,2,1,0:T(8,128)(2,1)} %slice_weights.9), calls=%async_computation.5 | async-start | bytes 8388608 | tf_op jit(solution)/shard_map/all_to_all | solution.py:476
  646.6 106.2 %all-to-all-start.6 = ((bf16[4,2,512,512]{3,2,1,0:T(8,128)(2,1)}), bf16[4,2,512,512]{3,2,1,0:T(8,128)(2,1)}, u32[]{:S(2)}, u32[]{:S(2)}) async-start(bf16[4,2,512,512]{3,2,1,0:T(8,128)(2,1)} %get-tuple-element.131), calls=%async_computation.6 | async-start | bytes 8388608 | tf_op jit(solution)/shard_map/all_to_all | solution.py:603
  752.8 188.6 %all-to-all-start.7 = ((bf16[4,4,512,512]{3,2,1,0:T(8,128)(2,1)}), bf16[4,4,512,512]{3,2,1,0:T(8,128)(2,1)}, u32[]{:S(2)}, u32[]{:S(2)}) async-start(bf16[4,4,512,512]{3,2,1,0:T(8,128)(2,1)} %get-tuple-element.133), calls=%async_computation.7 | async-start | bytes 16777216 | tf_op jit(solution)/shard_map/all_to_all | solution.py:603
  819.3 38.2 %collective-permute-start.38 = (bf16[512,2176]{1,0:T(8,128)(2,1)}, bf16[512,2176]{1,0:T(8,128)(2,1)S(1)}, u32[]{:S(2)}, u32[]{:S(2)}) collective-permute-start(bf16[512,2176]{1,0:T(8,128)(2,1)} %get-tuple-element.130), channel_id=1, source_target_pairs={{0,4},{4,0},{8,12},{12,8},{16,20},{20,16},{24,28},{28,24},{1,5},{5... | collective-permute-start | bytes 6684680 | tf_op jit(solution)/shard_map/ppermute | solution.py:353
  823.6 51.5 %collective-permute-start.39 = (bf16[512,2176]{1,0:T(8,128)(2,1)}, bf16[512,2176]{1,0:T(8,128)(2,1)S(1)}, u32[]{:S(2)}, u32[]{:S(2)}) collective-permute-start(bf16[512,2176]{1,0:T(8,128)(2,1)} %add_convert_fusion.3), channel_id=1, source_target_pairs={{0,8},{4,12},{8,0},{12,4},{16,24},{20,28},{24,16},{28,20},{1,9},{5... | collective-permute-start | bytes 6684680 | tf_op jit(solution)/shard_map/ppermute | solution.py:353
  824.0 98.1 %collective-permute-start.40 = (bf16[512,2176]{1,0:T(8,128)(2,1)}, bf16[512,2176]{1,0:T(8,128)(2,1)S(1)}, u32[]{:S(2)}, u32[]{:S(2)}) collective-permute-start(bf16[512,2176]{1,0:T(8,128)(2,1)} %add_convert_fusion.2), channel_id=1, source_target_pairs={{0,16},{4,20},{8,24},{12,28},{16,0},{20,4},{24,8},{28,12},{1,17},{... | collective-permute-start | bytes 6684680 | tf_op jit(solution)/shard_map/ppermute | solution.py:353
  825.6 96.5 %collective-permute-start.41 = (bf16[512,2176]{1,0:T(8,128)(2,1)}, bf16[512,2176]{1,0:T(8,128)(2,1)}, u32[]{:S(2)}, u32[]{:S(2)}) collective-permute-start(bf16[512,2176]{1,0:T(8,128)(2,1)} %add_convert_fusion.1), channel_id=1, source_target_pairs={{0,24},{4,28},{8,16},{12,20},{16,8},{20,12},{24,0},{28,4},{1,25},{... | collective-permute-start | bytes 6684680 | tf_op jit(solution)/shard_map/ppermute | solution.py:353
  1001.4 112.6 %all-to-all-start.8 = ((bf16[4,2,512,512]{3,2,1,0:T(8,128)(2,1)}), bf16[4,2,512,512]{3,2,1,0:T(8,128)(2,1)}, u32[]{:S(2)}, u32[]{:S(2)}) async-start(bf16[4,2,512,512]{3,2,1,0:T(8,128)(2,1)} %get-tuple-element.144), calls=%async_computation.8 | async-start | bytes 8388608 | tf_op jit(solution)/shard_map/all_to_all | solution.py:603
  1031.8 48.0 %collective-permute-start.53 = (bf16[512,2048]{1,0:T(8,128)(2,1)}, bf16[512,2048]{1,0:T(8,128)(2,1)}, u32[]{:S(2)}, u32[]{:S(2)}) collective-permute-start(bf16[512,2048]{1,0:T(8,128)(2,1)} %add_convert_fusion.7), channel_id=1, source_target_pairs={{0,8},{4,12},{8,0},{12,4},{16,24},{20,28},{24,16},{28,20},{1,9},{5... | collective-permute-start | bytes 6291464 | tf_op jit(solution)/shard_map/ppermute | solution.py:353
  1109.7 37.0 %collective-permute-start.59 = (bf16[4,128,2048]{2,1,0:T(8,128)(2,1)}, bf16[4,128,2048]{2,1,0:T(8,128)(2,1)}, u32[]{:S(2)}, u32[]{:S(2)}) collective-permute-start(bf16[4,128,2048]{2,1,0:T(8,128)(2,1)} %slice_bitcast_fusion), channel_id=1, source_target_pairs={{0,4},{4,0},{8,12},{12,8},{16,20},{20,16},{24,28},{28,24},{1,5},{5... | collective-permute-start | bytes 6291464 | tf_op jit(solution)/shard_map/ppermute | solution.py:353
  1125.5 42.0 %collective-permute-start.56 = (bf16[2,9,64,768]{3,2,1,0:T(8,128)(2,1)}, bf16[2,9,64,768]{3,2,1,0:T(8,128)(2,1)}, u32[]{:S(2)}, u32[]{:S(2)}) collective-permute-start(bf16[2,9,64,768]{3,2,1,0:T(8,128)(2,1)} %pick_blocks.5), channel_id=1, source_target_pairs={{0,1},{1,0},{2,3},{3,2},{4,5},{5,4},{6,7},{7,6},{8,9},{9,8},{10,11... | collective-permute-start | bytes 5308424 | tf_op jit(solution)/shard_map/ppermute | solution.py:353
  1127.5 92.3 %collective-permute-start.54 = (bf16[512,2048]{1,0:T(8,128)(2,1)}, bf16[512,2048]{1,0:T(8,128)(2,1)}, u32[]{:S(2)}, u32[]{:S(2)}) collective-permute-start(bf16[512,2048]{1,0:T(8,128)(2,1)} %add_convert_fusion.6), channel_id=1, source_target_pairs={{0,16},{4,20},{8,24},{12,28},{16,0},{20,4},{24,8},{28,12},{1,17},{... | collective-permute-start | bytes 6291464 | tf_op jit(solution)/shard_map/ppermute | solution.py:353
  1128.2 93.0 %collective-permute-start.55 = (bf16[512,2048]{1,0:T(8,128)(2,1)S(1)}, bf16[512,2048]{1,0:T(8,128)(2,1)}, u32[]{:S(2)}, u32[]{:S(2)}) collective-permute-start(bf16[512,2048]{1,0:T(8,128)(2,1)S(1)} %copy-done.43), channel_id=1, source_target_pairs={{0,24},{4,28},{8,16},{12,20},{16,8},{20,12},{24,0},{28,4},{1,25},{... | collective-permute-start | bytes 6291464 | tf_op jit(solution)/shard_map/ppermute | solution.py:353
  1129.7 93.0 %collective-permute-start.36 = (bf16[512,2048]{1,0:T(8,128)(2,1)}, bf16[512,2048]{1,0:T(8,128)(2,1)}, u32[]{:S(2)}, u32[]{:S(2)}) collective-permute-start(bf16[512,2048]{1,0:T(8,128)(2,1)} %get-tuple-element.126), channel_id=1, source_target_pairs={{0,4},{4,0},{8,12},{12,8},{16,20},{20,16},{24,28},{28,24},{1,5},{5... | collective-permute-start | bytes 6291464 | tf_op jit(solution)/shard_map/ppermute | solution.py:353
  1169.5 76.5 %collective-permute-start.63 = (bf16[1,9,64,768]{3,2,1,0:T(8,128)(2,1)S(1)}, bf16[1,9,64,768]{3,2,1,0:T(8,128)(2,1)S(1)}, u32[]{:S(2)}, u32[]{:S(2)}) collective-permute-start(bf16[1,9,64,768]{3,2,1,0:T(8,128)(2,1)S(1)} %slice.681), channel_id=1, source_target_pairs={{0,2},{1,3},{2,0},{3,1},{4,6},{5,7},{6,4},{7,5},{8,10},{9,11},{10,... | collective-permute-start | bytes 2654216 | tf_op jit(solution)/shard_map/ppermute | solution.py:353
  1171.1 59.4 %collective-permute-start.60 = (bf16[128,2048]{1,0:T(8,128)(2,1)S(1)}, bf16[128,2048]{1,0:T(8,128)(2,1)S(1)}, u32[]{:S(2)}, u32[]{:S(2)}) collective-permute-start(bf16[128,2048]{1,0:T(8,128)(2,1)S(1)} %get-tuple-element.149), channel_id=1, source_target_pairs={{0,8},{4,12},{8,0},{12,4},{16,24},{20,28},{24,16},{28,20},{1,9},{5... | collective-permute-start | bytes 1572872 | tf_op jit(solution)/shard_map/ppermute | solution.py:353
  1248.0 33.6 %all-to-all-start.9 = ((bf16[8,80,768]{2,1,0:T(8,128)(2,1)}), bf16[8,80,768]{2,1,0:T(8,128)(2,1)}, u32[]{:S(2)}, u32[]{:S(2)}) async-start(bf16[8,80,768]{2,1,0:T(8,128)(2,1)} %fusion.61), calls=%async_computation.9 | async-start | bytes 1966080 | tf_op jit(solution)/shard_map/all_to_all | solution.py:741
  (148 other events, 2788.9 us)

commit v3 on v2

--- a/solution.py
+++ b/solution.py
@@ -286,24 +286,155 @@
     )(*args)
 
 
+def turn(x, cosine, sine):
+    return x * cosine + pltpu.roll(x, HD // 2, 1) * sine
+
+
+def probabilities(query, key):
+    scores = matmul(query, key, ((1,), (1,))) * HD ** (-0.5)
+    row = lax.broadcasted_iota(jnp.int32, scores.shape, 0)
+    column = lax.broadcasted_iota(jnp.int32, scores.shape, 1)
+    causal = row >= column
+    scores = jnp.where(causal, scores, -1e30)
+    powers = jnp.exp(scores - jnp.max(scores, axis=-1, keepdims=True))
+    return powers / jnp.sum(powers, axis=-1, keepdims=True), causal
+
+
+def attend_body(raw, scales, cosine, sine, gains, turned, attended):
+    features = attended.shape[1]
+    for part in range(2):
+        scale = scales[:, part : part + 1]
+        for at in range(0, features, HD):
+            columns = slice(part * features + at, part * features + at + HD)
+            x = raw[:, columns] * scale * gains[part : part + 1, at : at + HD]
+            turned[:, columns] = turn(x, cosine[...], sine[...]).astype(BF)
+    turned[:, 2 * features :] = raw[:, 2 * features :].astype(BF)
+    for at in range(0, features, HD):
+        query = turned[:, at : at + HD]
+        key = turned[:, features + at : features + at + HD]
+        value = turned[:, 2 * features + at : 2 * features + at + HD]
+        probs, _ = probabilities(query, key)
+        attended[:, at : at + HD] = matmul(probs.astype(BF), value, ((1,), (0,))).astype(BF)
+
+
+def attend(raw, scales, cosine, sine, gains, count):
+    total, features = raw.shape[0], raw.shape[1] // 3
+
+    def block(x):
+        return pl.BlockSpec((count, x.shape[1]), lambda i: (i, 0))
+
+    return pl.pallas_call(
+        attend_body,
+        grid=(total // count,),
+        in_specs=[block(x) for x in (raw, scales, cosine, sine)]
+        + [pl.BlockSpec(gains.shape, lambda i: (0, 0))],
+        out_specs=[
+            pl.BlockSpec((count, 3 * features), lambda i: (i, 0)),
+            pl.BlockSpec((count, features), lambda i: (i, 0)),
+        ],
+        out_shape=[
+            jax.ShapeDtypeStruct((total, 3 * features), BF),
+            jax.ShapeDtypeStruct((total, features), BF),
+        ],
+        compiler_params=pltpu.CompilerParams(vmem_limit_bytes=VMEM_BYTES),
+        cost_estimate=pl.CostEstimate(
+            flops=4 * total * count * features,
+            bytes_accessed=20 * total * features,
+            transcendentals=total * count,
+        ),
+        name="attend",
+    )(raw, scales, cosine, sine, gains)
+
+
+def attend_back_body(turned, grads, raw, scales, cosine, sine, gains, scaled, value_grads, sums, gain_grads):
+    features = grads.shape[1]
+    scale = HD ** (-0.5)
+    dots = [0.0, 0.0]
+    first = pl.program_id(0) == 0
+    for at in range(0, features, HD):
+        query = turned[:, at : at + HD]
+        key = turned[:, features + at : features + at + HD]
+        value = turned[:, 2 * features + at : 2 * features + at + HD]
+        grad = grads[:, at : at + HD]
+        probs, causal = probabilities(query, key)
+        value_grads[:, at : at + HD] = matmul(probs.astype(BF), grad, ((0,), (0,))).astype(BF)
+        prob_grads = matmul(grad, value, ((1,), (1,)))
+        score_grads = probs * (prob_grads - jnp.sum(probs * prob_grads, axis=-1, keepdims=True))
+        score_grads = jnp.where(causal, score_grads, 0.0).astype(BF)
+        turned_grads = (
+            matmul(score_grads, key, ((1,), (0,))) * scale,
+            matmul(score_grads, query, ((0,), (0,))) * scale,
+        )
+        for part in range(2):
+            columns = slice(part * features + at, part * features + at + HD)
+            x = raw[:, columns]
+            dy = turn(turned_grads[part], cosine[...], -sine[...])
+            u = dy * gains[part : part + 1, at : at + HD]
+            scaled[:, columns] = u
+            dots[part] = dots[part] + jnp.sum(u * x, axis=-1, keepdims=True)
+            gain_grad = jnp.sum(dy * x * scales[:, part : part + 1], axis=0, keepdims=True)
+            old = gain_grads[part : part + 1, at : at + HD]
+            gain_grads[part : part + 1, at : at + HD] = gain_grad + jnp.where(first, 0.0, old)
+    sums[...] = jnp.concatenate(dots, axis=1)
+
+
+def attend_back(turned, grads, raw, scales, cosine, sine, gains, count):
+    total, features = grads.shape
+
+    def block(x):
+        return pl.BlockSpec((count, x.shape[1]), lambda i: (i, 0))
+
+    out_shape = [
+        jax.ShapeDtypeStruct((total, 2 * features), F32),
+        jax.ShapeDtypeStruct((total, features), BF),
+        jax.ShapeDtypeStruct((total, 2), F32),
+    ]
+    return pl.pallas_call(
+        attend_back_body,
+        grid=(total // count,),
+        in_specs=[block(x) for x in (turned, grads, raw, scales, cosine, sine)]
+        + [pl.BlockSpec(gains.shape, lambda i: (0, 0))],
+        out_specs=[block(x) for x in out_shape] + [pl.BlockSpec(gains.shape, lambda i: (0, 0))],
+        out_shape=[*out_shape, jax.ShapeDtypeStruct(gains.shape, F32)],
+        compiler_params=pltpu.CompilerParams(vmem_limit_bytes=VMEM_BYTES),
+        cost_estimate=pl.CostEstimate(
+            flops=12 * total * count * features,
+            bytes_accessed=30 * total * features,
+            transcendentals=total * count,
+        ),
+        name="attend_back",
+    )(turned, grads, raw, scales, cosine, sine, gains)
+
+
 def pick_body(where, *refs):
     out = refs[-1]
-    for i, source in enumerate(refs[:-1]):
-        at = 0 if i == 0 else out.shape[1] - 1
-        out[0, at : at + source.shape[0]] = source[:, 0]
-
-
-def pick_blocks(order, *sources):
-    _, _, rows, width = sources[0].shape
+    width = out.shape[-1]
+    at = 0
+    for source in refs[:-1]:
+        outer, _, _, own = source.shape
+        if own >= width:
+            for i in range(outer):
+                for column in range(0, own, width):
+                    out[0, at] = source[i, 0, :, column : column + width]
+                    at += 1
+        else:
+            for i in range(0, outer, width // own):
+                for k in range(width // own):
+                    out[0, at, :, k * own : (k + 1) * own] = source[i + k, 0]
+                at += 1
+
+
+def pick_blocks(order, width, *sources):
+    rows = sources[0].shape[2]
     count = order.shape[0]
-    outer = sum(x.shape[0] for x in sources)
+    outer = sum(x.shape[0] * x.shape[3] for x in sources) // width
     return pl.pallas_call(
         pick_body,
         grid_spec=pltpu.PrefetchScalarGridSpec(
             num_scalar_prefetch=1,
             grid=(count,),
             in_specs=[
-                pl.BlockSpec((x.shape[0], 1, rows, width), lambda k, c: (0, c[k], 0, 0))
+                pl.BlockSpec((x.shape[0], 1, *x.shape[2:]), lambda k, c: (0, c[k], 0, 0))
                 for x in sources
             ],
             out_specs=pl.BlockSpec((1, outer, rows, width), lambda k, c: (k, 0, 0, 0)),
@@ -364,16 +495,19 @@
             x = jnp.concatenate([x, swap(x, "narrow", bit)], axis=0)
         return x
 
-    def scatter_narrow(keep, send, *after):
-        first = None
+    def scatter_narrow(keep, send, step=(), last=()):
+        arrivals = []
         for bit in reversed(bits):
-            total = keep.astype(F32) + swap(send, "narrow", bit).astype(F32)
-            first = total if first is None else first
+            came = swap(send, "narrow", bit)
+            if last and bit == bits[0]:
+                came = tie(came, *last)
+            arrivals.append(came)
+            total = keep.astype(F32) + came.astype(F32)
             half = total.shape[0] // 2
             keep, send = total[:half], total[half:].astype(BF)
-            if after:
-                send = tie(send, *after)
-        return total[0], first
+            if step:
+                send = tie(send, *step)
+        return total[0], arrivals
 
     def gather_planes(x):
         return [x] + [swap(x, "wide", 2 * q) for q in range(1, planes)]
@@ -418,8 +552,8 @@
 
         def by_narrow(*x):
             half = narrow // 2
-            send = pick_blocks(near_order[half:], *x)
-            return pick_blocks(near_order[:half], *x), send
+            send = pick_blocks(near_order[half:], 2 * features, *x)
+            return pick_blocks(near_order[:half], 2 * features, *x), send
 
         routed = jnp.any(
             routes[:, :, None] == jnp.arange(E, dtype=jnp.int32)[None, None, :], axis=1
@@ -508,51 +642,29 @@
         inverse = lax.rsqrt(jnp.mean(plane_tokens * plane_tokens, axis=-1, keepdims=True) + EPSILON)
         normed = (plane_tokens * inverse * attn_gain).astype(BF)
         raw = matmul(normed, tie(qkv, *ups_own), ((1,), (0,)))
-        query_raw = raw[:, :features]
-        key_raw = raw[:, features : 2 * features]
-        values = raw[:, 2 * features :].astype(BF).reshape(wide, count, heads, HD)
-
-        def row_sums(a, b):
-            sums = jnp.stack([jnp.sum(a, axis=-1), jnp.sum(b, axis=-1)])
+
+        def row_sums(sums):
             sums = jnp.take(sums.reshape(2, wide, count), wide_order, axis=1)
-            sums = jnp.sum(lax.all_gather(sums, "wide"), axis=0)
-            sums = jnp.take(sums, wide_order, axis=1).reshape(2, plane_count)
-            return sums[0][:, None], sums[1][:, None]
-
-        query_square, key_square = row_sums(query_raw * query_raw, key_raw * key_raw)
-        query_r = lax.rsqrt(query_square / D + EPSILON)
-        key_r = lax.rsqrt(key_square / D + EPSILON)
+            gathered = lax.all_gather(sums, "wide")
+            sums = jnp.sum(gathered, axis=0)
+            return jnp.take(sums, wide_order, axis=1).reshape(2, plane_count), gathered
+
+        squares = jnp.stack(
+            [
+                jnp.sum(x * x, axis=-1)
+                for x in (raw[:, :features], raw[:, features : 2 * features])
+            ]
+        )
+        scales = lax.rsqrt(row_sums(squares)[0] / D + EPSILON).T
         frequency = THETA_BASE ** (-2.0 * jnp.arange(HD // 2, dtype=F32) / HD)
         angles = plane_positions.astype(F32)[:, None] * frequency[None, :]
-        cosine = jnp.cos(angles)[:, None, :]
-        sine = jnp.sin(angles)[:, None, :]
-
-        def turn(x, sign):
-            x = x.reshape(plane_count, heads, HD)
-            a, b = x[..., : HD // 2], x[..., HD // 2 :]
-            return jnp.concatenate(
-                [a * cosine - sign * b * sine, b * cosine + sign * a * sine], axis=-1
-            )
-
-        shape = (wide, count, heads, HD)
-        queries = turn(query_raw * query_r * query_gain, 1.0).astype(BF).reshape(shape)
-        key_rows = turn(key_raw * key_r * key_gain, 1.0).astype(BF).reshape(shape)
+        cosine, sine = jnp.cos(angles), jnp.sin(angles)
+        cosine = jnp.concatenate([cosine, cosine], axis=1)
+        sine = jnp.concatenate([-sine, sine], axis=1)
+        head_gains = jnp.stack([query_gain, key_gain])
+        turned, attended = attend(raw, scales, cosine, sine, head_gains, count)
         if early > 2:
-            queries = tie(queries, expert_weights[1])
-        scale = HD ** (-0.5)
-        causal = (jnp.arange(count)[:, None] >= jnp.arange(count)[None, :])[None, None]
-        scores = (
-            jnp.einsum("bqhd,bkhd->bhqk", queries, key_rows, preferred_element_type=F32) * scale
-        )
-        scores = jnp.where(causal, scores, -1e30)
-        powers = jnp.exp(scores - jnp.max(scores, axis=-1, keepdims=True))
-        attn_probs = powers / jnp.sum(powers, axis=-1, keepdims=True)
-        probs_low = attn_probs.astype(BF)
-        attended = (
-            jnp.einsum("bhqk,bkhd->bqhd", probs_low, values, preferred_element_type=F32)
-            .astype(BF)
-            .reshape(plane_count, features)
-        )
+            attended = tie(attended, expert_weights[1])
         branch = matmul(attended, output_rows, ((1,), (0,))).astype(BF)
         branch = branch.reshape(planes, 2, count, D)
         branch = scatter_wide(branch[:, 0], branch[:, 1])
@@ -595,16 +707,16 @@
                 came.append(grads)
             else:
                 came[-1] = grads
-        buffers, arrived = [None], []
+        arrived = []
 
         def send_grads(*after):
-            g = len(buffers) - 1
-            part = tie(came[g], *after) if after else came[g]
-            part = lax.all_to_all(part, "narrow", 0, 0, tiled=True)
-            arrived.append(part)
-            buffers.append(assemble(part, starts[groups[g][0]], local, buffers[-1]))
-
-        for g in range(len(groups) - 1):
+            part = came[len(arrived)]
+            part = tie(part, *after) if after else part
+            arrived.append(lax.all_to_all(part, "narrow", 0, 0, tiled=True))
+
+        grad_starts = [starts[group[0]] for group in groups]
+        sent_early = len(groups) - 1
+        for g in range(sent_early):
             send_grads(*([row_grads[-1]] if g else []))
 
         def combine_tokens(terms, *after):
@@ -613,18 +725,26 @@
             other = [swap(x, "wide", 1) for x in other]
             return list(combine(picks_own, terms, 0)), other
 
-        def scatter_rest(plane_sum):
+        def scatter_rest(plane_sum, *after):
             blocks = plane_sum.reshape(narrow, count, plane_sum.shape[-1])
-            return scatter_narrow(blocks[: narrow // 2], blocks[narrow // 2 :])[0]
+            return scatter_narrow(blocks[: narrow // 2], blocks[narrow // 2 :], (), after)[0]
 
         own, other = combine_tokens(row_grads)
         plane_sum, sent = scatter_plane(own, other)
         mix_own, mix_other = combine_tokens(results, *sent)
         mix_sums = [mix_own[q].astype(F32) + mix_other[q].astype(F32) for q in range(planes)]
         mix_sent = [x.astype(BF) for x in mix_sums[1:]]
-        plane_sum = tie(plane_sum.astype(BF), *arrived, *mix_sent)
-        ffn_message = scatter_rest(plane_sum)
+        plane_done = plane_sum.astype(BF)
+        plane_sum = tie(plane_done, *arrived, *mix_other)
+        mix_came = [
+            swap(tie(mix_sent[q - 1], plane_done), "wide", 2 * q) for q in range(1, planes)[:2]
+        ]
+        ffn_message = scatter_rest(plane_sum, *mix_came)
         send_grads(ffn_message)
+        buffers = None
+        for start, part in zip(grad_starts, arrived[:sent_early]):
+            buffers = assemble(part, start, local, buffers)
+        ffn_message = tie(ffn_message, *buffers)
 
         upstream = cotangent.astype(F32)
         prob_grads = ffn_message[:, D : D + E] + ffn_message[:, D + E : D + 2 * E]
@@ -645,92 +765,86 @@
         )
 
         plane_message = join(*gather_wide(message))
-        mix_came = [swap(tie(mix_sent[0], plane_message), "wide", 2)]
         plane_grads = plane_message[:, :D]
-        attended_grads = (
-            matmul(plane_grads, output_rows, ((1,), (1,))).astype(BF).reshape(shape)
-        )
+        attended_grads = matmul(plane_grads, output_rows, ((1,), (1,))).astype(BF)
         plane_rows = lax.dynamic_slice_in_dim(
             join([x[:count] for x in tokens_own], [x[:count] for x in tokens_other]),
             w * features,
             features,
             axis=1,
         )
-        prob_grads_attn = jnp.einsum(
-            "bqhd,bkhd->bhqk", attended_grads, values, preferred_element_type=F32
-        )
-        value_grads = (
-            jnp.einsum("bhqk,bqhd->bkhd", probs_low, attended_grads, preferred_element_type=F32)
-            .astype(BF)
-            .reshape(plane_count, features)
-        )
-        score_grads = attn_probs * (
-            prob_grads_attn - jnp.sum(attn_probs * prob_grads_attn, axis=-1, keepdims=True)
-        )
-        score_grads = jnp.where(causal, score_grads, 0.0).astype(BF)
-        query_grads = (
-            jnp.einsum("bhqk,bkhd->bqhd", score_grads, key_rows, preferred_element_type=F32)
-            * scale
-        )
-        key_grads = (
-            jnp.einsum("bhqk,bqhd->bkhd", score_grads, queries, preferred_element_type=F32)
-            * scale
-        )
-        query_dy = turn(query_grads, -1.0).reshape(plane_count, features)
-        key_dy = turn(key_grads, -1.0).reshape(plane_count, features)
-        query_u = tie(query_dy, *mix_came) * query_gain
-        key_u = key_dy * key_gain
-        query_dot, key_dot = row_sums(query_u * query_raw, key_u * key_raw)
-        query_raw_grads = query_r * query_u - query_raw * (query_r**3) * (query_dot / D)
-        key_raw_grads = key_r * key_u - key_raw * (key_r**3) * (key_dot / D)
+        scaled, value_grads, dots, head_gain_parts = attend_back(
+            turned, attended_grads, raw, scales, cosine, sine, head_gains, count
+        )
+
+        grad_output = matmul(attended, plane_grads, ((0,), (0,))).astype(BF)
+        grad_value = matmul(normed, value_grads, ((0,), (0,))).astype(BF)
+        early_parts = by_narrow(
+            grad_output.reshape(1, narrow, rows, D),
+            grad_value.reshape(wide, narrow, rows, features),
+        )
+
+        dots, dots_gathered = row_sums(dots.T)
+        dots = dots.T / D
+        shrink = scales * scales * scales * dots
+        raw_grads = (
+            scaled.reshape(plane_count, 2, features) * scales[:, :, None]
+            - raw[:, : 2 * features].reshape(plane_count, 2, features) * shrink[:, :, None]
+        ).astype(BF)
+        raw_grads = jnp.concatenate([raw_grads.reshape(plane_count, 2 * features), value_grads], axis=1)
         mix_came += [
-            swap(tie(mix_sent[q - 1], query_dot), "wide", 2 * q) for q in range(2, planes)
+            swap(tie(mix_sent[q - 1], dots_gathered), "wide", 2 * q) for q in range(3, planes)
         ]
-        raw_grads = jnp.concatenate(
-            [query_raw_grads.astype(BF), key_raw_grads.astype(BF), value_grads], axis=1
-        )
+        grad_early, early_came = scatter_narrow(*early_parts)
+        raw_grads = tie(raw_grads, arrived[-1], early_came[0])
         normed_grads = matmul(raw_grads, qkv, ((1,), (1,))).astype(BF)
-        raw_grads = tie(raw_grads, arrived[-1])
-
-        grad_output = jnp.concatenate(
-            [
-                matmul(attended, plane_grads, ((0,), (0,))).astype(BF),
-                matmul(plane_rows, plane_message[:, D:], ((0,), (0,))).astype(BF),
-            ],
-            axis=1,
-        )
-        grad_output, _ = scatter_narrow(
-            *by_narrow(tie(grad_output, query_dot).reshape(1, narrow, rows, D + LANES))
-        )
-        grad_output = grad_output[0]
 
         attn_gain_part = jnp.sum(normed_grads.astype(F32) * plane_tokens * inverse, axis=0)
-        grad_qkv = matmul(normed, raw_grads, ((0,), (0,))).astype(BF)
-        grad_qkv = grad_qkv.reshape(wide, narrow, rows, 3 * features)
         gain_parts = jnp.concatenate(
             [
-                jnp.stack([attn_gain_part, ffn_gain_part]).reshape(2 * wide, narrow, rows),
-                jnp.stack(
-                    [
-                        jnp.sum(query_dy * query_raw * query_r, axis=0),
-                        jnp.sum(key_dy * key_raw * key_r, axis=0),
-                    ]
-                ).reshape(2, narrow, rows),
+                jnp.stack([attn_gain_part, ffn_gain_part]).reshape(2 * wide, features),
+                head_gain_parts,
             ]
-        ).transpose(1, 2, 0)
-        columns_each = 2 * wide + 2
-        gain_parts = jnp.concatenate(split_low(gain_parts), axis=-1)
-        gain_parts = jnp.pad(
-            gain_parts, ((0, 0), (0, 0), (0, 3 * features - 2 * columns_each))
-        )
-        grad_qkv, first_sums = scatter_narrow(*by_narrow(grad_qkv, gain_parts[None]))
-        gain_parts = grad_qkv[wide, :, :columns_each] + grad_qkv[wide, :, columns_each : 2 * columns_each]
-        gain_parts = gain_parts.T
-        grad_qkv = grad_qkv[:wide]
+        ).T
+        gain_columns = 2 * wide + 2
+        router_part = matmul(plane_rows, plane_message[:, D : D + E], ((0,), (0,)))
+        small_parts = jnp.concatenate([router_part.astype(BF), *split_low(gain_parts)], axis=1)
+        small_parts = jnp.pad(
+            small_parts, ((0, 0), (0, 2 * features - E - 2 * gain_columns))
+        )
+        plane_normed = normed_grads.reshape(planes, 2, count, D)
+        normed_other = swap(plane_normed[:, 1], "wide", 1)
+        normed_sums = [add_up([plane_normed[q, 0], normed_other[q]]) for q in range(planes)]
+        normed_came = [
+            swap(normed_sums[q].astype(BF), "wide", 2 * q)
+            for q in range(1, planes)
+        ]
+        grad_raw = matmul(normed, raw_grads[:, : 2 * features], ((0,), (0,))).astype(BF)
+        grad_raw, raw_came = scatter_narrow(
+            *by_narrow(
+                grad_raw.reshape(wide, narrow, rows, 2 * features),
+                small_parts.reshape(1, narrow, rows, 2 * features),
+            ),
+            (),
+            normed_came,
+        )
+        small_parts = grad_raw[wide]
+        grad_router = small_parts[:, :E]
+        gain_parts = small_parts[:, E : E + 2 * gain_columns]
+        gain_parts = (gain_parts[:, :gain_columns] + gain_parts[:, gain_columns:]).T
         grad_gain_query, grad_gain_key = gain_parts[2 * wide], gain_parts[2 * wide + 1]
-        mix_came = list(lax.optimization_barrier((*mix_came, first_sums))[:-1])
-        mixture = scatter_rest(add_up([mix_sums[0], *mix_came]).astype(BF))
-        block_out = (residual + mixture).astype(BF)
+        blocks = D // (2 * features)
+        grad_output = jnp.concatenate([grad_early[i] for i in range(blocks)], axis=1)
+        grad_value = (
+            grad_early[blocks:]
+            .reshape(wide // 2, rows, 2, features)
+            .transpose(0, 2, 1, 3)
+            .reshape(wide, rows, features)
+        )
+        grad_qkv = jnp.concatenate([grad_raw[:wide], grad_value], axis=-1)
+        mix_came[-1] = tie(mix_came[-1], raw_came[0])
+        mixture = add_up([mix_sums[0], *mix_came]).astype(BF)
+        block_out = (residual + scatter_rest(mixture)).astype(BF)
         gain_rows = jnp.concatenate(
             [*split_low(gain_parts[:wide]), *split_low(gain_parts[wide : 2 * wide])], axis=1
         )
@@ -746,20 +860,19 @@
             grad_qkv[..., i * features : (i + 1) * features].reshape(rows, D) for i in range(3)
         ]
 
-        normed_grads = normed_grads.reshape(planes, 2, count, D)
-        normed_grads, _ = scatter_plane(
-            normed_grads[:, 0], swap(normed_grads[:, 1], "wide", 1), first_sums
-        )
+        normed_grads = add_up([normed_sums[0], *normed_came])
         input_grad = (
             residual_grads
             + norm_back(tokens.astype(F32), inverse[:count], attn_gain, normed_grads)
         ).astype(BF)
 
-        grad_gate, grad_up = buffers[-1]
+        for start, part in zip(grad_starts[sent_early:], arrived[sent_early:]):
+            buffers = assemble(tie(part, raw_came[0]), start, local, buffers)
+        grad_gate, grad_up = buffers
 
         return (
             block_out, input_grad, grad_query, grad_key, grad_value,
-            grad_output[:, :D], grad_output[:, D : D + E],
+            grad_output, grad_router,
             gain_sums[0], grad_gain_query, grad_gain_key, gain_sums[1],
             grad_gate, grad_up, down_grad, expert_counts,
         )

time: 1300 us -> 1240 us (0.954)
  waiting for transfers between devices: 599 us -> 555 us
  Pallas kernels: 283 us -> 306 us
    ppermute x66, waiting for transfers between devices: 512 us -> 451 us  [swap(): return lax.ppermute(x, axis, [(i, i ^ r) for i in range(size)])]
    pallas_call x0 -> x2, Pallas kernels: none -> 23.2 us  [the longest x1 13.4 us: attend_back(): pl.pallas_call(attend_back_body, grid=(total // count,), in_specs=[block(...]
    all_to_all x3, waiting for transfers between devices: 14.1 us -> 31.4 us  [send_grads(): arrived.append(lax.all_to_all(part, 'narrow', 0, 0, tiled=True))]
    dot_general x6 -> x0, matrix products: 14.2 us -> none  [the longest x1 4 us: on_device(): jnp.einsum('bhqk,bkhd->bqhd', score_grads, key_rows, preferred_element_ty...]
    dot_general x10 -> x11, matrix products: 31.8 us -> 37.6 us  [matmul(): return lax.dot_general(a, b, (dims, ((), ())), preferred_element_type=F32)]
    unnamed x239 -> x201, local copies, waits for them, and re-layouts: 45.5 us -> 44.1 us
  transfers between devices with their start and end apart: 76 -> 76, of which waited for: 37 -> 35; matrix products, arithmetic and copies ran while one was open for 17% -> 16% of each run, Pallas kernels for 22% -> 25%
where the time goes in v3:
time: 1240 us
  waiting for transfers between devices  555 us (45%)
  Pallas kernels  306 us (25%)
  starting transfers between devices  94 us (8%)
  local copies, waits for them, and re-layouts  92 us (7%)
  other arithmetic  89.6 us (7%)
  blocking collectives  59 us (5%)
  matrix products  37.6 us (3%)
    ppermute x66, waiting for transfers between devices, swap(): return lax.ppermute(x, axis, [(i, i ^ r) for i in range(size)])  451 us
    pallas_call x5, Pallas kernels, expert_chunk(): pl.pallas_call(functools.partial(expert_body, parts, tiles, start, len(al...  132 us
    all_to_all x5, waiting for transfers between devices, send_weights(): expert_weights.append(lax.all_to_all(part, 'narrow', 0, 0, tiled=True))  67.3 us
    pallas_call x4, Pallas kernels, combine(): pl.pallas_call(functools.partial(combine_body, pieces, each, len(rows)),...  64.7 us
    ppermute x66, starting transfers between devices, swap(): return lax.ppermute(x, axis, [(i, i ^ r) for i in range(size)])  45.1 us
    unnamed x201, local copies, waits for them, and re-layouts  44.1 us
    dot_general x11, matrix products, matmul(): return lax.dot_general(a, b, (dims, ((), ())), preferred_element_type=F32)  37.6 us
    pallas_call x4, Pallas kernels, dispatch(): pl.pallas_call(functools.partial(dispatch_body, pieces, each), grid=(pair...  36.5 us
  transfers between devices with their start and end apart: 76, of which 35 were waited for; matrix products, arithmetic and copies ran while one was open for 16% of the time, Pallas kernels for 25%

profile of v3, /device:TPU:0, one launch (start us, length us, event | category | flops | bytes accessed | tf_op | source)
XLA Modules:
  0.0 1235.2 jit_solution(5959136319825754978)
XLA Ops:
  9.9 26.5 %all-gather = bf16[448,128]{1,0:T(8,128)(2,1)S(1)} all-gather(bf16[112,128]{1,0:T(8,128)(2,1)S(1)} %pad_maximum_fusion.11), channel_id=2, replica_groups=mesh['wide'=8,'narrow'=4] {'narrow'}, dimensions={0}, use_global_device_ids=true | all-gather | bytes 143360 | tf_op jit(solution)/shard_map/all_gather | solution.py:576
  47.1 15.0 %all-gather.1 = bf16[32,112,128]{2,1,0:T(8,128)(2,1)S(1)} all-gather(bf16[4,112,128]{2,1,0:T(8,128)(2,1)S(1)} %bitcast.314), channel_id=3, replica_groups=mesh['wide'=8,'narrow'=4] {'wide'}, dimensions={0}, use_global_device_ids=true | all-gather | bytes 1032192 | tf_op jit(solution)/shard_map/all_gather | solution.py:581
  74.0 11.4 collective-permute-done.1
  85.4 10.8 collective-permute-done.3
  104.4 42.7 %collective-permute-done.10.refs_3_ = bf16[512,2048]{1,0:T(8,128)(2,1)} collective-permute-done((bf16[512,2048]{1,0:T(8,128)(2,1)}, bf16[512,2048]{1,0:T(8,128)(2,1)}, u32[]{:S(2)}, u32[]{:S(2)}) %collective-permute-start.10) | collective-permute-done | bytes 2097184 | tf_op jit(solution)/shard_map/ppermute | solution.py:484
  148.5 15.9 %all-to-all-done.1.refs_3_ = bf16[4,2,512,512]{3,2,1,0:T(8,128)(2,1)} async-done(((bf16[4,2,512,512]{3,2,1,0:T(8,128)(2,1)}), bf16[4,2,512,512]{3,2,1,0:T(8,128)(2,1)}, u32[]{:S(2)}, u32[]{:S(2)}) %all-to-all-start.1) | async-done | bytes 4194336 | tf_op jit(solution)/shard_map/all_to_all | solution.py:610
  175.6 30.7 %collective-permute-done.11 = bf16[1,8,64,768]{3,2,1,0:T(8,128)(2,1)S(1)} collective-permute-done((bf16[1,8,64,768]{3,2,1,0:T(8,128)(2,1)S(1)}, bf16[1,8,64,768]{3,2,1,0:T(8,128)(2,1)S(1)}, u32[]{:S(2)}, u32[]{:S(2)}) %collective-permute-start.11) | collective-permute-done | bytes 786464 | tf_op jit(solution)/shard_map/ppermute | solution.py:484
  219.2 37.6 %collective-permute-done.15 = bf16[2,64,2048]{2,1,0:T(8,128)(2,1)S(1)} collective-permute-done((bf16[2,64,2048]{2,1,0:T(8,128)(2,1)S(1)}, bf16[2,64,2048]{2,1,0:T(8,128)(2,1)S(1)}, u32[]{:S(2)}, u32[]{:S(2)}) %collective-permute-start.15) | collective-permute-done | bytes 524320 | tf_op jit(solution)/shard_map/ppermute | solution.py:484
  389.0 25.8 %collective-permute-done.24 = bf16[128,2176]{1,0:T(8,128)(2,1)S(1)} collective-permute-done((bf16[128,2176]{1,0:T(8,128)(2,1)S(1)}, bf16[128,2176]{1,0:T(8,128)(2,1)S(1)}, u32[]{:S(2)}, u32[]{:S(2)}) %collective-permute-start.24) | collective-permute-done | bytes 557088 | tf_op jit(solution)/shard_map/ppermute | solution.py:484
  418.9 22.6 %collective-permute-done.25 = bf16[256,2176]{1,0:T(8,128)(2,1)S(1)} collective-permute-done((bf16[256,2176]{1,0:T(8,128)(2,1)S(1)}, bf16[256,2176]{1,0:T(8,128)(2,1)S(1)}, u32[]{:S(2)}, u32[]{:S(2)}) %collective-permute-start.25) | collective-permute-done | bytes 1114144 | tf_op jit(solution)/shard_map/ppermute | solution.py:484
  453.8 44.2 %collective-permute-done.27.refs_2_ = bf16[512,2176]{1,0:T(8,128)(2,1)S(1)} collective-permute-done((bf16[512,2176]{1,0:T(8,128)(2,1)S(1)}, bf16[512,2176]{1,0:T(8,128)(2,1)S(1)}, u32[]{:S(2)}, u32[]{:S(2)}) %collective-permute-start.27) | collective-permute-done | bytes 2228256 | tf_op jit(solution)/shard_map/ppermute | solution.py:484
  498.0 46.0 %collective-permute-done.29.refs_3_ = bf16[512,2176]{1,0:T(8,128)(2,1)S(1)} collective-permute-done((bf16[512,2176]{1,0:T(8,128)(2,1)S(1)}, bf16[512,2176]{1,0:T(8,128)(2,1)S(1)}, u32[]{:S(2)}, u32[]{:S(2)}) %collective-permute-start.29) | collective-permute-done | bytes 2228256 | tf_op jit(solution)/shard_map/ppermute | solution.py:484
  575.5 31.3 %experts.5 = (bf16[2,768,2048]{2,1,0:T(8,128)(2,1)}, bf16[2,768,2176]{2,1,0:T(8,128)(2,1)}, bf16[4,2,512,512]{3,2,1,0:T(8,128)(2,1)}, f32[8,256,2048]{2,1,0:T(8,128)}) custom-call(s32[3]{0:T(128)} %pad_add_fusion.refs_0_, bf16[8,768,2176]{2,1,0:T(8,128)(2,1)} %dispatch.7.refs_1_, bf16[8,768,2048]{2,1,0:T(8,128)(2,1)} %dispatch.5.refs_2_, ...), custom_call_target="tpu_custom_call" | custom-call | flops 14495514624 | bytes 44040192 | tf_op jit(solution)/shard_map/experts/pallas_call | solution.py:196
  606.8 34.0 %all-to-all-done.5.refs_3_ = bf16[4,2,512,512]{3,2,1,0:T(8,128)(2,1)} async-done(((bf16[4,2,512,512]{3,2,1,0:T(8,128)(2,1)}), bf16[4,2,512,512]{3,2,1,0:T(8,128)(2,1)}, u32[]{:S(2)}, u32[]{:S(2)}) %all-to-all-start.5) | async-done | bytes 4194336 | tf_op jit(solution)/shard_map/all_to_all | solution.py:610
  646.0 18.9 %experts.6 = (bf16[1,768,2048]{2,1,0:T(8,128)(2,1)}, bf16[1,768,2176]{2,1,0:T(8,128)(2,1)}, bf16[4,4,512,512]{3,2,1,0:T(8,128)(2,1)}, f32[8,256,2048]{2,1,0:T(8,128)}) custom-call(s32[3]{0:T(128)} %pad_add_fusion.refs_0_, bf16[8,768,2176]{2,1,0:T(8,128)(2,1)} %dispatch.7.refs_1_, ...), custom_call_target="tpu_custom_call", output_to_operand_aliasing={{3}: (5, {})} | custom-call | flops 7247757312 | bytes 22020096 | tf_op jit(solution)/shard_map/experts/pallas_call | solution.py:196
  665.0 18.9 %experts.7 = (bf16[1,768,2048]{2,1,0:T(8,128)(2,1)}, bf16[1,768,2176]{2,1,0:T(8,128)(2,1)}, bf16[4,4,512,512]{3,2,1,0:T(8,128)(2,1)}, f32[8,256,2048]{2,1,0:T(8,128)}) custom-call(s32[3]{0:T(128)} %pad_add_fusion.refs_0_, bf16[8,768,2176]{2,1,0:T(8,128)(2,1)} %dispatch.7.refs_1_, ...), custom_call_target="tpu_custom_call", output_to_operand_aliasing={{3}: (5, {}), {2}: (6, {})} | custom-call | flops 7247757312 | bytes 22020096 | tf_op jit(solution)/shard_map/experts/pallas_call | solution.py:196
  683.9 31.6 %experts.8 = (bf16[2,768,2048]{2,1,0:T(8,128)(2,1)}, bf16[2,768,2176]{2,1,0:T(8,128)(2,1)}, bf16[4,4,512,512]{3,2,1,0:T(8,128)(2,1)}, f32[8,256,2048]{2,1,0:T(8,128)}) custom-call(s32[3]{0:T(128)} %pad_add_fusion.refs_0_, bf16[8,768,2176]{2,1,0:T(8,128)(2,1)} %dispatch.7.refs_1_, ...), custom_call_target="tpu_custom_call", output_to_operand_aliasing={{3}: (5, {}), {2}: (6, {})} | custom-call | flops 14495514624 | bytes 44040192 | tf_op jit(solution)/shard_map/experts/pallas_call | solution.py:196
  715.5 31.4 %experts.9 = (bf16[2,768,2048]{2,1,0:T(8,128)(2,1)}, bf16[2,768,2176]{2,1,0:T(8,128)(2,1)}, bf16[4,2,512,512]{3,2,1,0:T(8,128)(2,1)}, f32[8,256,2048]{2,1,0:T(8,128)}) custom-call(s32[3]{0:T(128)} %pad_add_fusion.refs_0_, bf16[8,768,2176]{2,1,0:T(8,128)(2,1)} %dispatch.7.refs_1_, ...), custom_call_target="tpu_custom_call", output_to_operand_aliasing={{3}: (5, {})} | custom-call | flops 14495514624 | bytes 44040192 | tf_op jit(solution)/shard_map/experts/pallas_call | solution.py:196
  752.8 16.7 %combine.5 = (bf16[512,2176]{1,0:T(8,128)(2,1)}, bf16[512,2176]{1,0:T(8,128)(2,1)}, bf16[512,2176]{1,0:T(8,128)(2,1)}, bf16[512,2176]{1,0:T(8,128)(2,1)}) custom-call(bf16[4,2,384,256]{3,2,1,0:T(8,128)(2,1)} %bitcast.265, bf16[2,768,2176]{2,1,0:T(8,128)(2,1)} %get-tuple-element.105.refs_1_, bf16[1,768,2176]{2,1,0:T(8,128)(2,1)} %get-tuple-element.109.refs_2_, ...), custom_call_target="tpu_custom_call" | custom-call | flops 3422552064 | bytes 22282240 | tf_op jit(solution)/shard_map/combine/pallas_call | solution.py:98
  778.3 17.0 %combine.4 = (bf16[512,2176]{1,0:T(8,128)(2,1)}, bf16[512,2176]{1,0:T(8,128)(2,1)}, bf16[512,2176]{1,0:T(8,128)(2,1)}, bf16[512,2176]{1,0:T(8,128)(2,1)}) custom-call(bf16[4,2,384,256]{3,2,1,0:T(8,128)(2,1)} %bitcast.261, bf16[2,768,2176]{2,1,0:T(8,128)(2,1)} %get-tuple-element.105.refs_1_, bf16[1,768,2176]{2,1,0:T(8,128)(2,1)} %get-tuple-element.109.refs_2_, ...), custom_call_target="tpu_custom_call" | custom-call | flops 3422552064 | bytes 22282240 | tf_op jit(solution)/shard_map/combine/pallas_call | solution.py:98
  806.7 15.4 %combine.7 = (bf16[512,2048]{1,0:T(8,128)(2,1)}, bf16[512,2048]{1,0:T(8,128)(2,1)}, bf16[512,2048]{1,0:T(8,128)(2,1)}, bf16[512,2048]{1,0:T(8,128)(2,1)}) custom-call(bf16[4,2,384,256]{3,2,1,0:T(8,128)(2,1)} %bitcast.266, bf16[2,768,2048]{2,1,0:T(8,128)(2,1)} %get-tuple-element.124.refs_1_, bf16[1,768,2048]{2,1,0:T(8,128)(2,1)} %get-tuple-element.125.refs_2_, ...), custom_call_target="tpu_custom_call" | custom-call | flops 3221225472 | bytes 20971520 | tf_op jit(solution)/shard_map/combine/pallas_call | solution.py:98
  830.4 21.7 %collective-permute-done.41 = bf16[512,2176]{1,0:T(8,128)(2,1)S(1)} collective-permute-done((bf16[512,2176]{1,0:T(8,128)(2,1)}, bf16[512,2176]{1,0:T(8,128)(2,1)S(1)}, u32[]{:S(2)}, u32[]{:S(2)}) %collective-permute-start.41) | collective-permute-done | bytes 2228256 | tf_op jit(solution)/shard_map/ppermute | solution.py:484
  854.4 15.6 %combine.6 = (bf16[512,2048]{1,0:T(8,128)(2,1)}, bf16[512,2048]{1,0:T(8,128)(2,1)}, bf16[512,2048]{1,0:T(8,128)(2,1)}, bf16[512,2048]{1,0:T(8,128)(2,1)}) custom-call(bf16[4,2,384,256]{3,2,1,0:T(8,128)(2,1)} %bitcast.262, bf16[2,768,2048]{2,1,0:T(8,128)(2,1)} %get-tuple-element.124.refs_1_, bf16[1,768,2048]{2,1,0:T(8,128)(2,1)} %get-tuple-element.125.refs_2_, ...), custom_call_target="tpu_custom_call" | custom-call | flops 3221225472 | bytes 20971520 | tf_op jit(solution)/shard_map/combine/pallas_call | solution.py:98
  874.7 24.2 %collective-permute-done.40 = bf16[512,2176]{1,0:T(8,128)(2,1)S(1)} collective-permute-done((bf16[512,2176]{1,0:T(8,128)(2,1)}, bf16[512,2176]{1,0:T(8,128)(2,1)S(1)}, u32[]{:S(2)}, u32[]{:S(2)}) %collective-permute-start.40) | collective-permute-done | bytes 2228256 | tf_op jit(solution)/shard_map/ppermute | solution.py:484
  904.0 31.4 %all-to-all-done.7.refs_0_ = bf16[4,4,512,512]{3,2,1,0:T(8,128)(2,1)} async-done(((bf16[4,4,512,512]{3,2,1,0:T(8,128)(2,1)}), bf16[4,4,512,512]{3,2,1,0:T(8,128)(2,1)}, u32[]{:S(2)}, u32[]{:S(2)}) %all-to-all-start.7) | async-done | bytes 8388640 | tf_op jit(solution)/shard_map/all_to_all | solution.py:715
  944.7 16.4 %collective-permute-done.46 = bf16[2,128,2176]{2,1,0:T(8,128)(2,1)S(1)} collective-permute-done((bf16[2,128,2176]{2,1,0:T(8,128)(2,1)S(1)}, bf16[2,128,2176]{2,1,0:T(8,128)(2,1)S(1)}, u32[]{:S(2)}, u32[]{:S(2)}) %collective-permute-start.46) | collective-permute-done | bytes 1114144 | tf_op jit(solution)/shard_map/ppermute | solution.py:484
  1008.5 11.5 collective-permute-done.51
  1025.1 13.4 %attend_back.1 = (f32[1024,512]{1,0:T(8,128)}, bf16[1024,256]{1,0:T(8,128)(2,1)}, f32[1024,2]{1,0:T(8,128)}, f32[2,256]{1,0:T(2,128)}) custom-call(bf16[1024,768]{1,0:T(8,128)(2,1)} %get-tuple-element.141.turned, bf16[1024,256]{1,0:T(8,128)(2,1)} %fusion.15.grads, f32[1024,768]{1,0:T(8,128)} %copy.258.raw, f32[1024,2]{1,0:T(8,128)} %bitcast.271, ...), custom_call_target="tpu_custom_call" | custom-call | flops 402653184 | bytes 7864320 | tf_op jit(solution)/shard_map/attend_back/pallas_call | solution.py:392
  1075.7 21.9 %collective-permute-done.56 = bf16[2,8,64,512]{3,2,1,0:T(8,128)(2,1)} collective-permute-done((bf16[2,8,64,512]{3,2,1,0:T(8,128)(2,1)}, bf16[2,8,64,512]{3,2,1,0:T(8,128)(2,1)}, u32[]{:S(2)}, u32[]{:S(2)}) %collective-permute-start.56) | collective-permute-done | bytes 1048608 | tf_op jit(solution)/shard_map/ppermute | solution.py:484
  1130.4 19.4 %collective-permute-done.57 = bf16[2,9,64,512]{3,2,1,0:T(8,128)(2,1)} collective-permute-done((bf16[2,9,64,512]{3,2,1,0:T(8,128)(2,1)}, bf16[2,9,64,512]{3,2,1,0:T(8,128)(2,1)}, u32[]{:S(2)}, u32[]{:S(2)}) %collective-permute-start.57) | collective-permute-done | bytes 1179680 | tf_op jit(solution)/shard_map/ppermute | solution.py:484
  1175.9 16.1 %collective-permute-done.58 = bf16[2,128,2048]{2,1,0:T(8,128)(2,1)S(1)} collective-permute-done((bf16[2,128,2048]{2,1,0:T(8,128)(2,1)S(1)}, bf16[2,128,2048]{2,1,0:T(8,128)(2,1)S(1)}, u32[]{:S(2)}, u32[]{:S(2)}) %collective-permute-start.58) | collective-permute-done | bytes 1048608 | tf_op jit(solution)/shard_map/ppermute | solution.py:484
  1193.3 14.3 %collective-permute-done.64 = bf16[1,9,64,512]{3,2,1,0:T(8,128)(2,1)S(1)} collective-permute-done((bf16[1,9,64,512]{3,2,1,0:T(8,128)(2,1)S(1)}, bf16[1,9,64,512]{3,2,1,0:T(8,128)(2,1)S(1)}, u32[]{:S(2)}, u32[]{:S(2)}) %collective-permute-start.64) | collective-permute-done | bytes 589856 | tf_op jit(solution)/shard_map/ppermute | solution.py:484
  (544 shorter events, 482.2 us)
Async XLA Ops:
  65.5 99.0 %all-to-all-start.1 = ((bf16[4,2,512,512]{3,2,1,0:T(8,128)(2,1)}), bf16[4,2,512,512]{3,2,1,0:T(8,128)(2,1)}, u32[]{:S(2)}, u32[]{:S(2)}) async-start(bf16[4,2,512,512]{3,2,1,0:T(8,128)(2,1)} %slice_weights.5), calls=%async_computation.1 | async-start | bytes 8388608 | tf_op jit(solution)/shard_map/all_to_all | solution.py:610
  99.2 48.0 %collective-permute-start.10 = (bf16[512,2048]{1,0:T(8,128)(2,1)}, bf16[512,2048]{1,0:T(8,128)(2,1)}, u32[]{:S(2)}, u32[]{:S(2)}) collective-permute-start(bf16[512,2048]{1,0:T(8,128)(2,1)} %constant_dynamic-update-slice_fusion.8.refs_1_), channel_id=1, source_target_pairs={{0,16},{4,20},{8,24},{12,28},{16,0},{20,4},{24,8},{28,12},{1,17},{... | collective-permute-start | bytes 6291464 | tf_op jit(solution)/shard_map/ppermute | solution.py:484
  100.8 47.7 %collective-permute-start.9 = (bf16[512,2048]{1,0:T(8,128)(2,1)}, bf16[512,2048]{1,0:T(8,128)(2,1)}, u32[]{:S(2)}, u32[]{:S(2)}) collective-permute-start(bf16[512,2048]{1,0:T(8,128)(2,1)} %constant_dynamic-update-slice_fusion.8.refs_1_), channel_id=1, source_target_pairs={{0,8},{4,12},{8,0},{12,4},{16,24},{20,28},{24,16},{28,20},{1,9},{5... | collective-permute-start | bytes 6291464 | tf_op jit(solution)/shard_map/ppermute | solution.py:484
  164.5 41.8 %collective-permute-start.11 = (bf16[1,8,64,768]{3,2,1,0:T(8,128)(2,1)S(1)}, bf16[1,8,64,768]{3,2,1,0:T(8,128)(2,1)S(1)}, u32[]{:S(2)}, u32[]{:S(2)}) collective-permute-start(bf16[1,8,64,768]{3,2,1,0:T(8,128)(2,1)S(1)} %bitcast.279), channel_id=1, source_target_pairs={{0,2},{1,3},{2,0},{3,1},{4,6},{5,7},{6,4},{7,5},{8,10},{9,11},{10,... | collective-permute-start | bytes 2359304 | tf_op jit(solution)/shard_map/ppermute | solution.py:484
  172.1 39.8 %collective-permute-start.14 = (bf16[1,64,2048]{2,1,0:T(8,128)(2,1)S(1)}, bf16[1,64,2048]{2,1,0:T(8,128)(2,1)S(1)}, u32[]{:S(2)}, u32[]{:S(2)}) collective-permute-start(bf16[1,64,2048]{2,1,0:T(8,128)(2,1)S(1)} %bitcast.307), channel_id=1, source_target_pairs={{0,2},{1,3},{2,0},{3,1},{4,6},{5,7},{6,4},{7,5},{8,10},{9,11},{10,... | collective-permute-start | bytes 786440 | tf_op jit(solution)/shard_map/ppermute | solution.py:484
  207.7 51.0 %collective-permute-start.12 = (bf16[2,8,64,768]{3,2,1,0:T(8,128)(2,1)}, bf16[2,8,64,768]{3,2,1,0:T(8,128)(2,1)}, u32[]{:S(2)}, u32[]{:S(2)}) collective-permute-start(bf16[2,8,64,768]{3,2,1,0:T(8,128)(2,1)} %pad_maximum_fusion.1), channel_id=1, source_target_pairs={{0,1},{1,0},{2,3},{3,2},{4,5},{5,4},{6,7},{7,6},{8,9},{9,8},{10,11... | collective-permute-start | bytes 4718600 | tf_op jit(solution)/shard_map/ppermute | solution.py:484
  212.0 44.8 %collective-permute-start.15 = (bf16[2,64,2048]{2,1,0:T(8,128)(2,1)S(1)}, bf16[2,64,2048]{2,1,0:T(8,128)(2,1)S(1)}, u32[]{:S(2)}, u32[]{:S(2)}) collective-permute-start(bf16[2,64,2048]{2,1,0:T(8,128)(2,1)S(1)} %pad_maximum_fusion.8), channel_id=1, source_target_pairs={{0,1},{1,0},{2,3},{3,2},{4,5},{5,4},{6,7},{7,6},{8,9},{9,8},{10,11... | collective-permute-start | bytes 1572872 | tf_op jit(solution)/shard_map/ppermute | solution.py:484
  217.7 65.7 %collective-permute-start.13 = (bf16[512,2048]{1,0:T(8,128)(2,1)}, bf16[512,2048]{1,0:T(8,128)(2,1)}, u32[]{:S(2)}, u32[]{:S(2)}) collective-permute-start(bf16[512,2048]{1,0:T(8,128)(2,1)} %constant_dynamic-update-slice_fusion.8.refs_1_), channel_id=1, source_target_pairs={{0,24},{4,28},{8,16},{12,20},{16,8},{20,12},{24,0},{28,4},{1,25},{... | collective-permute-start | bytes 6291464 | tf_op jit(solution)/shard_map/ppermute | solution.py:484
  267.6 53.8 %all-to-all-start.2 = ((bf16[4,1,512,512]{3,2,1,0:T(8,128)(2,1)}), bf16[4,1,512,512]{3,2,1,0:T(8,128)(2,1)}, u32[]{:S(2)}, u32[]{:S(2)}) async-start(bf16[4,1,512,512]{3,2,1,0:T(8,128)(2,1)} %slice_weights.6), calls=%async_computation.2 | async-start | bytes 4194304 | tf_op jit(solution)/shard_map/all_to_all | solution.py:610
  335.1 53.9 %all-to-all-start.3 = ((bf16[4,1,512,512]{3,2,1,0:T(8,128)(2,1)}), bf16[4,1,512,512]{3,2,1,0:T(8,128)(2,1)}, u32[]{:S(2)}, u32[]{:S(2)}) async-start(bf16[4,1,512,512]{3,2,1,0:T(8,128)(2,1)} %slice_weights.7), calls=%async_computation.3 | async-start | bytes 4194304 | tf_op jit(solution)/shard_map/all_to_all | solution.py:610
  441.7 103.6 %all-to-all-start.4 = ((bf16[4,2,512,512]{3,2,1,0:T(8,128)(2,1)}), bf16[4,2,512,512]{3,2,1,0:T(8,128)(2,1)}, u32[]{:S(2)}, u32[]{:S(2)}) async-start(bf16[4,2,512,512]{3,2,1,0:T(8,128)(2,1)} %slice_weights.8), calls=%async_computation.4 | async-start | bytes 8388608 | tf_op jit(solution)/shard_map/all_to_all | solution.py:610
  446.5 51.4 %collective-permute-start.27 = (bf16[512,2176]{1,0:T(8,128)(2,1)S(1)}, bf16[512,2176]{1,0:T(8,128)(2,1)S(1)}, u32[]{:S(2)}, u32[]{:S(2)}) collective-permute-start(bf16[512,2176]{1,0:T(8,128)(2,1)S(1)} %constant_dynamic-update-slice_fusion.10.refs_1_), channel_id=1, source_target_pairs={{0,8},{4,12},{8,0},{12,4},{16,24},{20,28},{24,16},{28,20},{1,9},{5... | collective-permute-start | bytes 6684680 | tf_op jit(solution)/shard_map/ppermute | solution.py:484
  446.9 97.0 %collective-permute-start.29 = (bf16[512,2176]{1,0:T(8,128)(2,1)S(1)}, bf16[512,2176]{1,0:T(8,128)(2,1)S(1)}, u32[]{:S(2)}, u32[]{:S(2)}) collective-permute-start(bf16[512,2176]{1,0:T(8,128)(2,1)S(1)} %constant_dynamic-update-slice_fusion.10.refs_1_), channel_id=1, source_target_pairs={{0,16},{4,20},{8,24},{12,28},{16,0},{20,4},{24,8},{28,12},{1,17},{... | collective-permute-start | bytes 6684680 | tf_op jit(solution)/shard_map/ppermute | solution.py:484
  448.6 96.7 %collective-permute-start.31 = (bf16[512,2176]{1,0:T(8,128)(2,1)S(1)}, bf16[512,2176]{1,0:T(8,128)(2,1)}, u32[]{:S(2)}, u32[]{:S(2)}) collective-permute-start(bf16[512,2176]{1,0:T(8,128)(2,1)S(1)} %constant_dynamic-update-slice_fusion.10.refs_1_), channel_id=1, source_target_pairs={{0,24},{4,28},{8,16},{12,20},{16,8},{20,12},{24,0},{28,4},{1,25},{... | collective-permute-start | bytes 6684680 | tf_op jit(solution)/shard_map/ppermute | solution.py:484
  545.3 95.5 %all-to-all-start.5 = ((bf16[4,2,512,512]{3,2,1,0:T(8,128)(2,1)}), bf16[4,2,512,512]{3,2,1,0:T(8,128)(2,1)}, u32[]{:S(2)}, u32[]{:S(2)}) async-start(bf16[4,2,512,512]{3,2,1,0:T(8,128)(2,1)} %slice_weights.9), calls=%async_computation.5 | async-start | bytes 8388608 | tf_op jit(solution)/shard_map/all_to_all | solution.py:610
  640.8 106.1 %all-to-all-start.6 = ((bf16[4,2,512,512]{3,2,1,0:T(8,128)(2,1)}), bf16[4,2,512,512]{3,2,1,0:T(8,128)(2,1)}, u32[]{:S(2)}, u32[]{:S(2)}) async-start(bf16[4,2,512,512]{3,2,1,0:T(8,128)(2,1)} %get-tuple-element.142), calls=%async_computation.6 | async-start | bytes 8388608 | tf_op jit(solution)/shard_map/all_to_all | solution.py:715
  746.9 188.5 %all-to-all-start.7 = ((bf16[4,4,512,512]{3,2,1,0:T(8,128)(2,1)}), bf16[4,4,512,512]{3,2,1,0:T(8,128)(2,1)}, u32[]{:S(2)}, u32[]{:S(2)}) async-start(bf16[4,4,512,512]{3,2,1,0:T(8,128)(2,1)} %get-tuple-element.144), calls=%async_computation.7 | async-start | bytes 16777216 | tf_op jit(solution)/shard_map/all_to_all | solution.py:715
  776.0 53.9 %collective-permute-start.38 = (bf16[512,2176]{1,0:T(8,128)(2,1)}, bf16[512,2176]{1,0:T(8,128)(2,1)S(1)}, u32[]{:S(2)}, u32[]{:S(2)}) collective-permute-start(bf16[512,2176]{1,0:T(8,128)(2,1)} %get-tuple-element.134), channel_id=1, source_target_pairs={{0,4},{4,0},{8,12},{12,8},{16,20},{20,16},{24,28},{28,24},{1,5},{5... | collective-permute-start | bytes 6684680 | tf_op jit(solution)/shard_map/ppermute | solution.py:484
  799.6 52.5 %collective-permute-start.41 = (bf16[512,2176]{1,0:T(8,128)(2,1)}, bf16[512,2176]{1,0:T(8,128)(2,1)S(1)}, u32[]{:S(2)}, u32[]{:S(2)}) collective-permute-start(bf16[512,2176]{1,0:T(8,128)(2,1)} %add_convert_fusion.1), channel_id=1, source_target_pairs={{0,24},{4,28},{8,16},{12,20},{16,8},{20,12},{24,0},{28,4},{1,25},{... | collective-permute-start | bytes 6684680 | tf_op jit(solution)/shard_map/ppermute | solution.py:484
  826.0 72.9 %collective-permute-start.40 = (bf16[512,2176]{1,0:T(8,128)(2,1)}, bf16[512,2176]{1,0:T(8,128)(2,1)S(1)}, u32[]{:S(2)}, u32[]{:S(2)}) collective-permute-start(bf16[512,2176]{1,0:T(8,128)(2,1)} %add_convert_fusion.2), channel_id=1, source_target_pairs={{0,16},{4,20},{8,24},{12,28},{16,0},{20,4},{24,8},{28,12},{1,17},{... | collective-permute-start | bytes 6684680 | tf_op jit(solution)/shard_map/ppermute | solution.py:484
  827.6 71.6 %collective-permute-start.39 = (bf16[512,2176]{1,0:T(8,128)(2,1)}, bf16[512,2176]{1,0:T(8,128)(2,1)}, u32[]{:S(2)}, u32[]{:S(2)}) collective-permute-start(bf16[512,2176]{1,0:T(8,128)(2,1)} %add_convert_fusion.3), channel_id=1, source_target_pairs={{0,8},{4,12},{8,0},{12,4},{16,24},{20,28},{24,16},{28,20},{1,9},{5... | collective-permute-start | bytes 6684680 | tf_op jit(solution)/shard_map/ppermute | solution.py:484
  829.9 74.0 %collective-permute-start.37 = (bf16[512,2048]{1,0:T(8,128)(2,1)}, bf16[512,2048]{1,0:T(8,128)(2,1)}, u32[]{:S(2)}, u32[]{:S(2)}) collective-permute-start(bf16[512,2048]{1,0:T(8,128)(2,1)} %get-tuple-element.132), channel_id=1, source_target_pairs={{0,4},{4,0},{8,12},{12,8},{16,20},{20,16},{24,28},{28,24},{1,5},{5... | collective-permute-start | bytes 6291464 | tf_op jit(solution)/shard_map/ppermute | solution.py:484
  829.9 74.0 %collective-permute-start.36 = (bf16[512,2048]{1,0:T(8,128)(2,1)}, bf16[512,2048]{1,0:T(8,128)(2,1)}, u32[]{:S(2)}, u32[]{:S(2)}) collective-permute-start(bf16[512,2048]{1,0:T(8,128)(2,1)} %get-tuple-element.130), channel_id=1, source_target_pairs={{0,4},{4,0},{8,12},{12,8},{16,20},{20,16},{24,28},{28,24},{1,5},{5... | collective-permute-start | bytes 6291464 | tf_op jit(solution)/shard_map/ppermute | solution.py:484
  852.1 51.8 %collective-permute-start.45 = (bf16[512,2048]{1,0:T(8,128)(2,1)}, bf16[512,2048]{1,0:T(8,128)(2,1)}, u32[]{:S(2)}, u32[]{:S(2)}) collective-permute-start(bf16[512,2048]{1,0:T(8,128)(2,1)} %get-tuple-element.140), channel_id=1, source_target_pairs={{0,4},{4,0},{8,12},{12,8},{16,20},{20,16},{24,28},{28,24},{1,5},{5... | collective-permute-start | bytes 6291464 | tf_op jit(solution)/shard_map/ppermute | solution.py:484
  940.8 46.7 %collective-permute-start.44 = (bf16[512,2048]{1,0:T(8,128)(2,1)S(1)}, bf16[512,2048]{1,0:T(8,128)(2,1)}, u32[]{:S(2)}, u32[]{:S(2)}) collective-permute-start(bf16[512,2048]{1,0:T(8,128)(2,1)S(1)} %copy-done.42), channel_id=1, source_target_pairs={{0,16},{4,20},{8,24},{12,28},{16,0},{20,4},{24,8},{28,12},{1,17},{... | collective-permute-start | bytes 6291464 | tf_op jit(solution)/shard_map/ppermute | solution.py:484
  942.5 46.6 %collective-permute-start.42 = (bf16[512,2048]{1,0:T(8,128)(2,1)}, bf16[512,2048]{1,0:T(8,128)(2,1)}, u32[]{:S(2)}, u32[]{:S(2)}) collective-permute-start(bf16[512,2048]{1,0:T(8,128)(2,1)} %add_convert_fusion.7), channel_id=1, source_target_pairs={{0,8},{4,12},{8,0},{12,4},{16,24},{20,28},{24,16},{28,20},{1,9},{5... | collective-permute-start | bytes 6291464 | tf_op jit(solution)/shard_map/ppermute | solution.py:484
  996.5 103.6 %all-to-all-start.8 = ((bf16[4,2,512,512]{3,2,1,0:T(8,128)(2,1)}), bf16[4,2,512,512]{3,2,1,0:T(8,128)(2,1)}, u32[]{:S(2)}, u32[]{:S(2)}) async-start(bf16[4,2,512,512]{3,2,1,0:T(8,128)(2,1)} %get-tuple-element.157), calls=%async_computation.8 | async-start | bytes 8388608 | tf_op jit(solution)/shard_map/all_to_all | solution.py:715
  1050.7 46.9 %collective-permute-start.56 = (bf16[2,8,64,512]{3,2,1,0:T(8,128)(2,1)}, bf16[2,8,64,512]{3,2,1,0:T(8,128)(2,1)}, u32[]{:S(2)}, u32[]{:S(2)}) collective-permute-start(bf16[2,8,64,512]{3,2,1,0:T(8,128)(2,1)} %pick_blocks.4), channel_id=1, source_target_pairs={{0,1},{1,0},{2,3},{3,2},{4,5},{5,4},{6,7},{7,6},{8,9},{9,8},{10,11... | collective-permute-start | bytes 3145736 | tf_op jit(solution)/shard_map/ppermute | solution.py:484
  1068.6 61.9 %collective-permute-start.55 = (bf16[512,2048]{1,0:T(8,128)(2,1)}, bf16[512,2048]{1,0:T(8,128)(2,1)}, u32[]{:S(2)}, u32[]{:S(2)}) collective-permute-start(bf16[512,2048]{1,0:T(8,128)(2,1)} %add_convert_fusion.5), channel_id=1, source_target_pairs={{0,24},{4,28},{8,16},{12,20},{16,8},{20,12},{24,0},{28,4},{1,25},{... | collective-permute-start | bytes 6291464 | tf_op jit(solution)/shard_map/ppermute | solution.py:484
  1130.4 39.3 %collective-permute-start.60 = (bf16[4,128,2048]{2,1,0:T(8,128)(2,1)}, bf16[4,128,2048]{2,1,0:T(8,128)(2,1)S(1)}, u32[]{:S(2)}, u32[]{:S(2)}) collective-permute-start(bf16[4,128,2048]{2,1,0:T(8,128)(2,1)} %slice_bitcast_fusion), channel_id=1, source_target_pairs={{0,4},{4,0},{8,12},{12,8},{16,20},{20,16},{24,28},{28,24},{1,5},{5... | collective-permute-start | bytes 6291464 | tf_op jit(solution)/shard_map/ppermute | solution.py:484
  1156.0 36.0 %collective-permute-start.58 = (bf16[2,128,2048]{2,1,0:T(8,128)(2,1)S(1)}, bf16[2,128,2048]{2,1,0:T(8,128)(2,1)S(1)}, u32[]{:S(2)}, u32[]{:S(2)}) collective-permute-start(bf16[2,128,2048]{2,1,0:T(8,128)(2,1)S(1)} %bitcast.306), channel_id=1, source_target_pairs={{0,1},{1,0},{2,3},{3,2},{4,5},{5,4},{6,7},{7,6},{8,9},{9,8},{10,11... | collective-permute-start | bytes 3145736 | tf_op jit(solution)/shard_map/ppermute | solution.py:484
  1167.1 40.5 %collective-permute-start.64 = (bf16[1,9,64,512]{3,2,1,0:T(8,128)(2,1)S(1)}, bf16[1,9,64,512]{3,2,1,0:T(8,128)(2,1)S(1)}, u32[]{:S(2)}, u32[]{:S(2)}) collective-permute-start(bf16[1,9,64,512]{3,2,1,0:T(8,128)(2,1)S(1)} %slice.623), channel_id=1, source_target_pairs={{0,2},{1,3},{2,0},{3,1},{4,6},{5,7},{6,4},{7,5},{8,10},{9,11},{10,... | collective-permute-start | bytes 1769480 | tf_op jit(solution)/shard_map/ppermute | solution.py:484
  (131 other events, 2952.8 us)

commit v4 on v3

--- a/solution.py
+++ b/solution.py
@@ -15,6 +15,7 @@
 CAP = 24
 FF = 1024
 LANES = 128
+EXPERT_TILE = 768
 EPSILON = 1e-05
 THETA_BASE = 10000.0
 
@@ -68,37 +69,23 @@
     )(*args)
 
 
-def combine_body(pieces, each, chunks, *refs):
-    picks = refs[0]
-    rows = refs[1 : 1 + chunks]
-    outs = refs[1 + chunks :]
+def combine_body(pieces, each, picks, rows, *outs):
     for q in range(pieces):
-        total = None
-        at = 0
-        for chunk in rows:
-            part = chunk[:, q * each : (q + 1) * each, :].reshape(-1, chunk.shape[-1])
-            size = part.shape[0]
-            term = matmul(picks[q, 0, at : at + size, :], part, ((0,), (0,)))
-            total = term if total is None else total + term
-            at += size
-        outs[q][...] = total.astype(BF)
+        part = rows[:, q * each : (q + 1) * each, :].reshape(-1, rows.shape[-1])
+        outs[q][...] = matmul(picks[q, 0], part, ((0,), (0,))).astype(BF)
 
 
 def combine(picks, rows, half):
     pieces, pairs, slots, span = picks.shape
     each = 2 * CAP
-    width = rows[0].shape[-1]
-    in_specs = [pl.BlockSpec((pieces, 1, slots, span), lambda j: (0, j, 0, 0))]
-    for chunk in rows:
-        in_specs.append(
-            pl.BlockSpec(
-                (chunk.shape[0], pieces * each, width), lambda j: (0, half * pairs + j, 0)
-            )
-        )
+    local, _, width = rows.shape
     return pl.pallas_call(
-        functools.partial(combine_body, pieces, each, len(rows)),
+        functools.partial(combine_body, pieces, each),
         grid=(pairs,),
-        in_specs=in_specs,
+        in_specs=[
+            pl.BlockSpec((pieces, 1, slots, span), lambda j: (0, j, 0, 0)),
+            pl.BlockSpec((local, pieces * each, width), lambda j: (0, half * pairs + j, 0)),
+        ],
         out_specs=[pl.BlockSpec((span, width), lambda j: (j, 0))] * pieces,
         out_shape=[jax.ShapeDtypeStruct((pairs * span, width), BF)] * pieces,
         compiler_params=pltpu.CompilerParams(vmem_limit_bytes=VMEM_BYTES),
@@ -108,26 +95,27 @@
             transcendentals=0,
         ),
         name="combine",
-    )(picks, *rows)
+    )(picks, rows)
 
 
 def expert_body(parts, tiles, start, aliased, *refs):
     where, rows_ref, ups_ref, weights_ref, down_ref = refs[:5]
     rest = refs[5 + aliased :]
-    results_ref, row_grads_ref, weight_grads_ref, down_grad_ref, sums, down_sum = rest
+    results_ref, row_grads_ref, weight_grads_ref, down_grad_ref, result_grads, *sums = rest
     tile = pl.program_id(1)
     width = FF // parts
-
-    weights = weights_ref[...].reshape(D, 2 * width)
-    tokens = rows_ref[0, :, :D]
-    both = matmul(tokens, weights, ((1,), (0,)))
+    depth = D // parts
+    slices = [slice(s * depth, (s + 1) * depth) for s in range(parts)]
+
+    both = None
+    for s in range(parts):
+        term = matmul(rows_ref[0, :, slices[s]], weights_ref[s, 0], ((1,), (0,)))
+        both = term if both is None else both + term
     gate_value = both[:, :width]
     up_value = both[:, width:]
     sigma = 1.0 / (1.0 + jnp.exp(-gate_value))
     silu = gate_value * sigma
     hidden = (silu * up_value).astype(BF)
-    down = down_ref[0]
-    results = matmul(hidden, down, ((1,), (0,)))
 
     expert = where[1] + start + pl.program_id(0)
     lane = lax.broadcasted_iota(jnp.int32, (rows_ref.shape[1], LANES), 1)
@@ -135,47 +123,72 @@
     low = lane == expert + E
     probs = rows_ref[0, :, D:].astype(F32)
     weight = jnp.sum(jnp.where(high | low, probs, 0.0), axis=1, keepdims=True)
-    upstream = ups_ref[0].astype(F32)
-    gate_grad = jnp.sum(upstream * results, axis=1, keepdims=True)
-    results_ref[0] = (weight * results).astype(BF)
-    result_grads = (weight * upstream).astype(BF)
-
-    hidden_grads = matmul(result_grads, down, ((1,), (1,)))
+
+    gate_grad = None
+    hidden_grads = None
+    for columns in slices:
+        down = down_ref[0, :, columns]
+        results = matmul(hidden, down, ((1,), (0,)))
+        upstream = ups_ref[0, :, columns].astype(F32)
+        dot = jnp.sum(upstream * results, axis=1, keepdims=True)
+        gate_grad = dot if gate_grad is None else gate_grad + dot
+        results_ref[0, :, columns] = (weight * results).astype(BF)
+        part = (weight * upstream).astype(BF)
+        result_grads[:, columns] = part
+        term = matmul(part, down, ((1,), (1,)))
+        hidden_grads = term if hidden_grads is None else hidden_grads + term
+
     gate_value_grads = (
         hidden_grads * up_value * (sigma * (1.0 + gate_value * (1.0 - sigma)))
     ).astype(BF)
     up_value_grads = (hidden_grads * silu).astype(BF)
     both_grads = jnp.concatenate([gate_value_grads, up_value_grads], axis=1)
-    row_grads_ref[0, :, :D] = matmul(both_grads, weights, ((1,), (1,))).astype(BF)
     top = gate_grad.astype(BF)
     bottom = (gate_grad - top.astype(F32)).astype(BF)
     row_grads_ref[0, :, D:] = jnp.where(
         high, top.astype(F32), jnp.where(low, bottom.astype(F32), 0.0)
     ).astype(BF)
-
-    term = matmul(tokens, both_grads, ((0,), (0,)))
-    down_term = matmul(hidden, result_grads, ((0,), (0,)))
-
-    @pl.when(tile == 0)
+    for s in range(parts):
+        row_grads_ref[0, :, slices[s]] = matmul(
+            both_grads, weights_ref[s, 0], ((1,), (1,))
+        ).astype(BF)
+
+    def weight_term(s):
+        return matmul(rows_ref[0, :, slices[s]], both_grads, ((0,), (0,)))
+
+    def down_term(columns):
+        return matmul(hidden, result_grads[:, columns], ((0,), (0,)))
+
+    if tiles == 1:
+        for s in range(parts):
+            weight_grads_ref[s, 0] = weight_term(s).astype(BF)
+            down_grad_ref[0, :, slices[s]] = down_term(slices[s])
+        return
+    weight_sums = sums[0]
+    first = tile == 0
+
+    @pl.when(first)
     def _():
-        sums[...] = term
-        down_sum[...] = down_term
-
-    @pl.when(tile > 0)
+        for s in range(parts):
+            weight_sums[s] = weight_term(s)
+            down_grad_ref[0, :, slices[s]] = down_term(slices[s])
+
+    @pl.when(jnp.logical_not(first))
     def _():
-        sums[...] += term
-        down_sum[...] += down_term
+        for s in range(parts):
+            weight_sums[s] += weight_term(s)
+            down_grad_ref[0, :, slices[s]] += down_term(slices[s])
 
     @pl.when(tile == tiles - 1)
     def _():
-        weight_grads_ref[...] = sums[...].astype(BF).reshape(weight_grads_ref.shape)
-        down_grad_ref[0] = down_sum[...]
-
-
-def expert_chunk(where, rows, ups, weights, down, start, down_grad, group, at, grads):
+        for s in range(parts):
+            weight_grads_ref[s, 0] = weight_sums[s].astype(BF)
+
+
+def expert_chunk(where, rows, ups, weights, down, start, group, at, buffers):
     parts, experts, depth, width2 = weights.shape
     local, total_rows, wide_row = rows.shape
-    tile = 384
+    tile = EXPERT_TILE
     tiles = total_rows // tile
     slice_ff = down.shape[1]
     weight_spec = pl.BlockSpec((parts, 1, depth, width2), lambda e, i, c: (0, e, 0, 0))
@@ -188,7 +201,7 @@
     ]
     args = [where, rows, ups, weights, down]
     aliases = {}
-    for buffer, index in ((down_grad, 3), (grads, 2)):
+    for index, buffer in enumerate(buffers):
         if buffer is not None:
             in_specs.append(pl.BlockSpec(memory_space=pl.ANY))
             aliases[len(args)] = index
@@ -200,19 +213,17 @@
             grid=(experts, tiles),
             in_specs=in_specs,
             out_specs=[
-                pl.BlockSpec((1, tile, D), lambda e, i, c: (e, i, 0)),
-                pl.BlockSpec((1, tile, wide_row), lambda e, i, c: (e, i, 0)),
+                pl.BlockSpec((1, tile, D), lambda e, i, c: (start + e, i, 0)),
+                pl.BlockSpec((1, tile, wide_row), lambda e, i, c: (start + e, i, 0)),
                 pl.BlockSpec((parts, 1, depth, width2), lambda e, i, c: (0, at + e, 0, 0)),
                 down_spec,
             ],
-            scratch_shapes=[
-                pltpu.VMEM((parts * depth, width2), F32),
-                pltpu.VMEM((slice_ff, D), F32),
-            ],
+            scratch_shapes=[pltpu.VMEM((tile, D), BF)]
+            + ([pltpu.VMEM((parts, depth, width2), F32)] if tiles > 1 else []),
         ),
         out_shape=[
-            jax.ShapeDtypeStruct((experts, total_rows, D), BF),
-            jax.ShapeDtypeStruct((experts, total_rows, wide_row), BF),
+            jax.ShapeDtypeStruct((local, total_rows, D), BF),
+            jax.ShapeDtypeStruct((local, total_rows, wide_row), BF),
             jax.ShapeDtypeStruct((parts, group, depth, width2), BF),
             jax.ShapeDtypeStruct((local, slice_ff, D), F32),
         ],
@@ -407,42 +418,56 @@
 
 
 def pick_body(where, *refs):
-    out = refs[-1]
-    width = out.shape[-1]
-    at = 0
-    for source in refs[:-1]:
-        outer, _, _, own = source.shape
-        if own >= width:
-            for i in range(outer):
-                for column in range(0, own, width):
-                    out[0, at] = source[i, 0, :, column : column + width]
+    half = pl.num_programs(0) // 2
+
+    def fill(out):
+        width = out.shape[-1]
+        at = 0
+        for source in refs[:-2]:
+            outer, _, _, own = source.shape
+            if own >= width:
+                for i in range(outer):
+                    for column in range(0, own, width):
+                        out[0, at] = source[i, 0, :, column : column + width]
+                        at += 1
+            else:
+                for i in range(0, outer, width // own):
+                    for k in range(width // own):
+                        out[0, at, :, k * own : (k + 1) * own] = source[i + k, 0]
                     at += 1
-        else:
-            for i in range(0, outer, width // own):
-                for k in range(width // own):
-                    out[0, at, :, k * own : (k + 1) * own] = source[i + k, 0]
-                at += 1
+
+    @pl.when(pl.program_id(0) < half)
+    def _():
+        fill(refs[-2])
+
+    @pl.when(pl.program_id(0) >= half)
+    def _():
+        fill(refs[-1])
 
 
 def pick_blocks(order, width, *sources):
     rows = sources[0].shape[2]
-    count = order.shape[0]
+    half = order.shape[0] // 2
     outer = sum(x.shape[0] * x.shape[3] for x in sources) // width
+    shape = (1, outer, rows, width)
     return pl.pallas_call(
         pick_body,
         grid_spec=pltpu.PrefetchScalarGridSpec(
             num_scalar_prefetch=1,
-            grid=(count,),
+            grid=(2 * half,),
             in_specs=[
                 pl.BlockSpec((x.shape[0], 1, *x.shape[2:]), lambda k, c: (0, c[k], 0, 0))
                 for x in sources
             ],
-            out_specs=pl.BlockSpec((1, outer, rows, width), lambda k, c: (k, 0, 0, 0)),
-        ),
-        out_shape=jax.ShapeDtypeStruct((count, outer, rows, width), BF),
+            out_specs=[
+                pl.BlockSpec(shape, lambda k, c: (jnp.minimum(k, half - 1), 0, 0, 0)),
+                pl.BlockSpec(shape, lambda k, c: (jnp.maximum(k - half, 0), 0, 0, 0)),
+            ],
+        ),
+        out_shape=[jax.ShapeDtypeStruct((half, *shape[1:]), BF)] * 2,
         compiler_params=pltpu.CompilerParams(vmem_limit_bytes=VMEM_BYTES),
         cost_estimate=pl.CostEstimate(
-            flops=0, bytes_accessed=4 * count * outer * rows * width, transcendentals=0
+            flops=0, bytes_accessed=8 * half * outer * rows * width, transcendentals=0
         ),
         name="pick_blocks",
     )(order, *sources)
@@ -488,6 +513,11 @@
     for bit in bits:
         near = near + [r ^ bit for r in near]
 
+    def swap_marked(x, bit, small):
+        rest = swap(x[:-small], "narrow", bit)
+        marker = swap(x[-small:], "narrow", bit)
+        return jnp.concatenate([rest, marker], axis=0), marker
+
     def gather_narrow(x, *after):
         for i, bit in enumerate(bits):
             if i and after:
@@ -495,13 +525,20 @@
             x = jnp.concatenate([x, swap(x, "narrow", bit)], axis=0)
         return x
 
-    def scatter_narrow(keep, send, step=(), last=()):
+    def scatter_narrow(keep, send, step=(), last=(), small=0):
         arrivals = []
         for bit in reversed(bits):
-            came = swap(send, "narrow", bit)
+            marker = None
+            if small and bit == bits[0]:
+                came, marker = swap_marked(send[0], bit, small)
+                came = came[None]
+            else:
+                came = swap(send, "narrow", bit)
             if last and bit == bits[0]:
                 came = tie(came, *last)
             arrivals.append(came)
+            if marker is not None:
+                arrivals.append(marker)
             total = keep.astype(F32) + came.astype(F32)
             half = total.shape[0] // 2
             keep, send = total[:half], total[half:].astype(BF)
@@ -551,9 +588,7 @@
         narrow_order = jnp.array([near.index(r) for r in range(narrow)])[jnp.arange(narrow) ^ n]
 
         def by_narrow(*x):
-            half = narrow // 2
-            send = pick_blocks(near_order[half:], 2 * features, *x)
-            return pick_blocks(near_order[:half], 2 * features, *x), send
+            return pick_blocks(near_order, 2 * features, *x)
 
         routed = jnp.any(
             routes[:, :, None] == jnp.arange(E, dtype=jnp.int32)[None, None, :], axis=1
@@ -690,23 +725,21 @@
         expert_rows = dispatch(picks_own, tokens_own, 0)
         expert_rows = dispatch(picks_other, tokens_other, 1, expert_rows)
 
-        results, row_grads, came = [], [], []
-        down_grad = None
+        came = []
+        held = [None] * 4
         for c in range(calls):
             if c == 1:
                 expert_rows = tie(expert_rows, expert_weights[-1])
             group = next(g for g in groups if c in g)
-            grads = came[-1] if c != group[0] else None
-            result, row_grad, grads, down_grad = expert_chunk(
-                where, expert_rows, ups, expert_weights[c], w_down, starts[c], down_grad,
-                sum(sizes[g] for g in group), starts[c] - starts[group[0]], grads,
-            )
-            results.append(result)
-            row_grads.append(row_grad)
             if c == group[0]:
-                came.append(grads)
-            else:
-                came[-1] = grads
+                held[2] = None
+            held = [*expert_chunk(
+                where, expert_rows, ups, expert_weights[c], w_down, starts[c],
+                sum(sizes[g] for g in group), starts[c] - starts[group[0]], held,
+            )]
+            if c == group[-1]:
+                came.append(held[2])
+        results, row_grads, _, down_grad = held
         arrived = []
 
         def send_grads(*after):
@@ -717,17 +750,18 @@
         grad_starts = [starts[group[0]] for group in groups]
         sent_early = len(groups) - 1
         for g in range(sent_early):
-            send_grads(*([row_grads[-1]] if g else []))
+            send_grads(*([row_grads] if g else []))
 
         def combine_tokens(terms, *after):
-            terms = [tie(terms[0], *after), *terms[1:]] if after else terms
-            other = combine(picks_other, terms, 1)
-            other = [swap(x, "wide", 1) for x in other]
+            terms = tie(terms, *after) if after else terms
+            other = cross(combine(picks_other, terms, 1))
             return list(combine(picks_own, terms, 0)), other
 
-        def scatter_rest(plane_sum, *after):
+        def scatter_rest(plane_sum, last=(), small=0):
             blocks = plane_sum.reshape(narrow, count, plane_sum.shape[-1])
-            return scatter_narrow(blocks[: narrow // 2], blocks[narrow // 2 :], (), after)[0]
+            return scatter_narrow(
+                blocks[: narrow // 2], blocks[narrow // 2 :], (), last, small
+            )
 
         own, other = combine_tokens(row_grads)
         plane_sum, sent = scatter_plane(own, other)
@@ -739,11 +773,11 @@
         mix_came = [
             swap(tie(mix_sent[q - 1], plane_done), "wide", 2 * q) for q in range(1, planes)[:2]
         ]
-        ffn_message = scatter_rest(plane_sum, *mix_came)
-        send_grads(ffn_message)
+        ffn_message, ffn_came = scatter_rest(plane_sum, mix_came, 16)
+        send_grads(ffn_came[-1])
         buffers = None
         for start, part in zip(grad_starts, arrived[:sent_early]):
-            buffers = assemble(part, start, local, buffers)
+            buffers = assemble(tie(part, ffn_came[-1]), start, local, buffers)
         ffn_message = tie(ffn_message, *buffers)
 
         upstream = cotangent.astype(F32)
@@ -844,7 +878,7 @@
         grad_qkv = jnp.concatenate([grad_raw[:wide], grad_value], axis=-1)
         mix_came[-1] = tie(mix_came[-1], raw_came[0])
         mixture = add_up([mix_sums[0], *mix_came]).astype(BF)
-        block_out = (residual + scatter_rest(mixture)).astype(BF)
+        block_out = (residual + scatter_rest(mixture)[0]).astype(BF)
         gain_rows = jnp.concatenate(
             [*split_low(gain_parts[:wide]), *split_low(gain_parts[wide : 2 * wide])], axis=1
         )
@@ -867,7 +901,7 @@
         ).astype(BF)
 
         for start, part in zip(grad_starts[sent_early:], arrived[sent_early:]):
-            buffers = assemble(tie(part, raw_came[0]), start, local, buffers)
+            buffers = assemble(tie(part, raw_came[1]), start, local, buffers)
         grad_gate, grad_up = buffers
 
         return (

time: 1240 us -> 1240 us (level)
  Pallas kernels: 306 us -> 250 us
  waiting for transfers between devices: 555 us -> 603 us
    ppermute x66 -> x67, waiting for transfers between devices: 451 us -> 486 us  [swap(): return lax.ppermute(x, axis, [(i, i ^ r) for i in range(size)])]
    pallas_call x5, Pallas kernels: 132 us -> 104 us  [expert_chunk(): pl.pallas_call(functools.partial(expert_body, parts, tiles, start, len(al...]
    pallas_call x4, Pallas kernels: 64.7 us -> 38.6 us  [combine(): pl.pallas_call(functools.partial(combine_body, pieces, each), grid=(pairs...]
    ppermute x66 -> x67, starting transfers between devices: 45.1 us -> 50.8 us  [swap(): return lax.ppermute(x, axis, [(i, i ^ r) for i in range(size)])]
  transfers between devices with their start and end apart: 76 -> 77, of which waited for: 35 -> 34; matrix products, arithmetic and copies ran while one was open for 16% -> 16% of each run, Pallas kernels for 25% -> 20%
where the time goes in v4:
time: 1240 us; the launch traced here: 1230 us
  waiting for transfers between devices  603 us (49%)
  Pallas kernels  250 us (20%)
  starting transfers between devices  99.2 us (8%)
  local copies, waits for them, and re-layouts  88.3 us (7%)
  other arithmetic  87.1 us (7%)
  blocking collectives  57.6 us (5%)
  matrix products  37.7 us (3%)
    ppermute x67, waiting for transfers between devices, swap(): return lax.ppermute(x, axis, [(i, i ^ r) for i in range(size)])  486 us
    pallas_call x5, Pallas kernels, expert_chunk(): pl.pallas_call(functools.partial(expert_body, parts, tiles, start, len(al...  104 us
    all_to_all x5, waiting for transfers between devices, send_weights(): expert_weights.append(lax.all_to_all(part, 'narrow', 0, 0, tiled=True))  74.5 us
    ppermute x67, starting transfers between devices, swap(): return lax.ppermute(x, axis, [(i, i ^ r) for i in range(size)])  50.8 us
    all_to_all x3, waiting for transfers between devices, send_grads(): arrived.append(lax.all_to_all(part, 'narrow', 0, 0, tiled=True))  42.7 us
    unnamed x201, local copies, waits for them, and re-layouts  41.7 us
    pallas_call x4, Pallas kernels, combine(): pl.pallas_call(functools.partial(combine_body, pieces, each), grid=(pairs...  38.6 us
    dot_general x11, matrix products, matmul(): return lax.dot_general(a, b, (dims, ((), ())), preferred_element_type=F32)  37.7 us
  transfers between devices with their start and end apart: 77, of which 34 were waited for; matrix products, arithmetic and copies ran while one was open for 16% of the time, Pallas kernels for 20%

profile of v4, /device:TPU:0, one launch (start us, length us, event | category | flops | bytes accessed | tf_op | source)
XLA Modules:
  0.0 1225.5 jit_solution(13580367932524775598)
XLA Ops:
  9.9 26.5 %all-gather = bf16[448,128]{1,0:T(8,128)(2,1)S(1)} all-gather(bf16[112,128]{1,0:T(8,128)(2,1)S(1)} %pad_maximum_fusion.11), channel_id=2, replica_groups=mesh['wide'=8,'narrow'=4] {'narrow'}, dimensions={0}, use_global_device_ids=true | all-gather | bytes 143360 | tf_op jit(solution)/shard_map/all_gather | solution.py:611
  47.1 15.0 %all-gather.1 = bf16[32,112,128]{2,1,0:T(8,128)(2,1)S(1)} all-gather(bf16[4,112,128]{2,1,0:T(8,128)(2,1)S(1)} %bitcast.316), channel_id=3, replica_groups=mesh['wide'=8,'narrow'=4] {'wide'}, dimensions={0}, use_global_device_ids=true | all-gather | bytes 1032192 | tf_op jit(solution)/shard_map/all_gather | solution.py:616
  74.0 11.4 collective-permute-done.1
  85.4 10.8 collective-permute-done.3
  104.4 42.7 %collective-permute-done.10.refs_3_ = bf16[512,2048]{1,0:T(8,128)(2,1)} collective-permute-done((bf16[512,2048]{1,0:T(8,128)(2,1)}, bf16[512,2048]{1,0:T(8,128)(2,1)}, u32[]{:S(2)}, u32[]{:S(2)}) %collective-permute-start.10) | collective-permute-done | bytes 2097184 | tf_op jit(solution)/shard_map/ppermute | solution.py:509
  148.5 15.9 %all-to-all-done.1.refs_3_ = bf16[4,2,512,512]{3,2,1,0:T(8,128)(2,1)} async-done(((bf16[4,2,512,512]{3,2,1,0:T(8,128)(2,1)}), bf16[4,2,512,512]{3,2,1,0:T(8,128)(2,1)}, u32[]{:S(2)}, u32[]{:S(2)}) %all-to-all-start.1) | async-done | bytes 4194336 | tf_op jit(solution)/shard_map/all_to_all | solution.py:645
  175.7 30.6 %collective-permute-done.11 = bf16[1,8,64,768]{3,2,1,0:T(8,128)(2,1)S(1)} collective-permute-done((bf16[1,8,64,768]{3,2,1,0:T(8,128)(2,1)S(1)}, bf16[1,8,64,768]{3,2,1,0:T(8,128)(2,1)S(1)}, u32[]{:S(2)}, u32[]{:S(2)}) %collective-permute-start.11) | collective-permute-done | bytes 786464 | tf_op jit(solution)/shard_map/ppermute | solution.py:509
  219.2 37.6 %collective-permute-done.15 = bf16[2,64,2048]{2,1,0:T(8,128)(2,1)S(1)} collective-permute-done((bf16[2,64,2048]{2,1,0:T(8,128)(2,1)S(1)}, bf16[2,64,2048]{2,1,0:T(8,128)(2,1)S(1)}, u32[]{:S(2)}, u32[]{:S(2)}) %collective-permute-start.15) | collective-permute-done | bytes 524320 | tf_op jit(solution)/shard_map/ppermute | solution.py:509
  302.4 9.8 attend.1
  388.9 25.8 %collective-permute-done.24 = bf16[128,2176]{1,0:T(8,128)(2,1)S(1)} collective-permute-done((bf16[128,2176]{1,0:T(8,128)(2,1)S(1)}, bf16[128,2176]{1,0:T(8,128)(2,1)S(1)}, u32[]{:S(2)}, u32[]{:S(2)}) %collective-permute-start.24) | collective-permute-done | bytes 557088 | tf_op jit(solution)/shard_map/ppermute | solution.py:509
  418.8 22.6 %collective-permute-done.25 = bf16[256,2176]{1,0:T(8,128)(2,1)S(1)} collective-permute-done((bf16[256,2176]{1,0:T(8,128)(2,1)S(1)}, bf16[256,2176]{1,0:T(8,128)(2,1)S(1)}, u32[]{:S(2)}, u32[]{:S(2)}) %collective-permute-start.25) | collective-permute-done | bytes 1114144 | tf_op jit(solution)/shard_map/ppermute | solution.py:509
  453.7 44.1 %collective-permute-done.27.refs_2_ = bf16[512,2176]{1,0:T(8,128)(2,1)S(1)} collective-permute-done((bf16[512,2176]{1,0:T(8,128)(2,1)S(1)}, bf16[512,2176]{1,0:T(8,128)(2,1)S(1)}, u32[]{:S(2)}, u32[]{:S(2)}) %collective-permute-start.27) | collective-permute-done | bytes 2228256 | tf_op jit(solution)/shard_map/ppermute | solution.py:509
  497.9 46.0 %collective-permute-done.29.refs_3_ = bf16[512,2176]{1,0:T(8,128)(2,1)S(1)} collective-permute-done((bf16[512,2176]{1,0:T(8,128)(2,1)S(1)}, bf16[512,2176]{1,0:T(8,128)(2,1)S(1)}, u32[]{:S(2)}, u32[]{:S(2)}) %collective-permute-start.29) | collective-permute-done | bytes 2228256 | tf_op jit(solution)/shard_map/ppermute | solution.py:509
  575.2 24.4 %experts.5 = (bf16[8,768,2048]{2,1,0:T(8,128)(2,1)}, bf16[8,768,2176]{2,1,0:T(8,128)(2,1)}, bf16[4,2,512,512]{3,2,1,0:T(8,128)(2,1)}, f32[8,256,2048]{2,1,0:T(8,128)}) custom-call(s32[3]{0:T(128)} %pad_add_fusion.refs_0_, bf16[8,768,2176]{2,1,0:T(8,128)(2,1)} %dispatch.7.refs_1_, bf16[8,768,2048]{2,1,0:T(8,128)(2,1)} %dispatch.5.refs_2_, ...), custom_call_target="tpu_custom_call" | custom-call | flops 14495514624 | bytes 44040192 | tf_op jit(solution)/shard_map/experts/pallas_call | solution.py:209
  599.5 41.1 %all-to-all-done.5.refs_3_ = bf16[4,2,512,512]{3,2,1,0:T(8,128)(2,1)} async-done(((bf16[4,2,512,512]{3,2,1,0:T(8,128)(2,1)}), bf16[4,2,512,512]{3,2,1,0:T(8,128)(2,1)}, u32[]{:S(2)}, u32[]{:S(2)}) %all-to-all-start.5) | async-done | bytes 4194336 | tf_op jit(solution)/shard_map/all_to_all | solution.py:645
  645.7 15.3 %experts.6 = (bf16[8,768,2048]{2,1,0:T(8,128)(2,1)}, bf16[8,768,2176]{2,1,0:T(8,128)(2,1)}, bf16[4,4,512,512]{3,2,1,0:T(8,128)(2,1)}, f32[8,256,2048]{2,1,0:T(8,128)}) custom-call(s32[3]{0:T(128)} %pad_add_fusion.refs_0_, bf16[8,768,2176]{2,1,0:T(8,128)(2,1)} %dispatch.7.refs_1_, ...), custom_call_target="tpu_custom_call", output_to_operand_aliasing={{0}: (5, {}), {1}: (6, {}), {3}: (7, {})} | custom-call | flops 7247757312 | bytes 22020096 | tf_op jit(solution)/shard_map/experts/pallas_call | solution.py:209
  661.1 15.8 %experts.7 = (bf16[8,768,2048]{2,1,0:T(8,128)(2,1)}, bf16[8,768,2176]{2,1,0:T(8,128)(2,1)}, bf16[4,4,512,512]{3,2,1,0:T(8,128)(2,1)}, f32[8,256,2048]{2,1,0:T(8,128)}) custom-call(s32[3]{0:T(128)} %pad_add_fusion.refs_0_, bf16[8,768,2176]{2,1,0:T(8,128)(2,1)} %dispatch.7.refs_1_, ...), custom_call_target="tpu_custom_call", output_to_operand_aliasing={{0}: (5, {}), {1}: (6, {}), {2}: (7, {}), {3}: (8, {})} | custom-call | flops 7247757312 | bytes 22020096 | tf_op jit(solution)/shard_map/experts/pallas_call | solution.py:209
  676.8 24.4 %experts.8 = (bf16[8,768,2048]{2,1,0:T(8,128)(2,1)}, bf16[8,768,2176]{2,1,0:T(8,128)(2,1)}, bf16[4,4,512,512]{3,2,1,0:T(8,128)(2,1)}, f32[8,256,2048]{2,1,0:T(8,128)}) custom-call(s32[3]{0:T(128)} %pad_add_fusion.refs_0_, bf16[8,768,2176]{2,1,0:T(8,128)(2,1)} %dispatch.7.refs_1_, ...), custom_call_target="tpu_custom_call", output_to_operand_aliasing={{0}: (5, {}), {1}: (6, {}), {2}: (7, {}), {3}: (8, {})} | custom-call | flops 14495514624 | bytes 44040192 | tf_op jit(solution)/shard_map/experts/pallas_call | solution.py:209
  701.2 24.6 %experts.9 = (bf16[8,768,2048]{2,1,0:T(8,128)(2,1)}, bf16[8,768,2176]{2,1,0:T(8,128)(2,1)}, bf16[4,2,512,512]{3,2,1,0:T(8,128)(2,1)}, f32[8,256,2048]{2,1,0:T(8,128)}) custom-call(s32[3]{0:T(128)} %pad_add_fusion.refs_0_, bf16[8,768,2176]{2,1,0:T(8,128)(2,1)} %dispatch.7.refs_1_, ...), custom_call_target="tpu_custom_call", output_to_operand_aliasing={{0}: (5, {}), {1}: (6, {}), {3}: (7, {})} | custom-call | flops 14495514624 | bytes 44040192 | tf_op jit(solution)/shard_map/experts/pallas_call | solution.py:209
  725.8 12.4 %all-to-all-done.6.refs_0_ = bf16[4,2,512,512]{3,2,1,0:T(8,128)(2,1)} async-done(((bf16[4,2,512,512]{3,2,1,0:T(8,128)(2,1)}), bf16[4,2,512,512]{3,2,1,0:T(8,128)(2,1)}, u32[]{:S(2)}, u32[]{:S(2)}) %all-to-all-start.6) | async-done | bytes 4194336 | tf_op jit(solution)/shard_map/all_to_all | solution.py:748
  766.2 10.2 combine.4
  802.1 30.4 %collective-permute-done.41 = bf16[512,2176]{1,0:T(8,128)(2,1)S(1)} collective-permute-done((bf16[512,2176]{1,0:T(8,128)(2,1)}, bf16[512,2176]{1,0:T(8,128)(2,1)S(1)}, u32[]{:S(2)}, u32[]{:S(2)}) %collective-permute-start.41) | collective-permute-done | bytes 2228256 | tf_op jit(solution)/shard_map/ppermute | solution.py:509
  832.5 46.8 %collective-permute-done.40 = bf16[512,2176]{1,0:T(8,128)(2,1)S(1)} collective-permute-done((bf16[512,2176]{1,0:T(8,128)(2,1)}, bf16[512,2176]{1,0:T(8,128)(2,1)S(1)}, u32[]{:S(2)}, u32[]{:S(2)}) %collective-permute-start.40) | collective-permute-done | bytes 2228256 | tf_op jit(solution)/shard_map/ppermute | solution.py:509
  881.8 10.1 combine.6
  896.4 30.2 %all-to-all-done.7.refs_0_ = bf16[4,4,512,512]{3,2,1,0:T(8,128)(2,1)} async-done(((bf16[4,4,512,512]{3,2,1,0:T(8,128)(2,1)}), bf16[4,4,512,512]{3,2,1,0:T(8,128)(2,1)}, u32[]{:S(2)}, u32[]{:S(2)}) %all-to-all-start.7) | async-done | bytes 8388640 | tf_op jit(solution)/shard_map/all_to_all | solution.py:748
  937.7 14.6 %collective-permute-done.46 = bf16[2,128,2176]{2,1,0:T(8,128)(2,1)S(1)} collective-permute-done((bf16[2,128,2176]{2,1,0:T(8,128)(2,1)S(1)}, bf16[2,128,2176]{2,1,0:T(8,128)(2,1)S(1)}, u32[]{:S(2)}, u32[]{:S(2)}) %collective-permute-start.46) | collective-permute-done | bytes 1114144 | tf_op jit(solution)/shard_map/ppermute | solution.py:509
  958.4 9.8 collective-permute-done.48
  1007.5 12.9 %collective-permute-done.52 = bf16[128,2176]{1,0:T(8,128)(2,1)S(1)} collective-permute-done((bf16[128,2176]{1,0:T(8,128)(2,1)S(1)}, bf16[128,2176]{1,0:T(8,128)(2,1)S(1)}, u32[]{:S(2)}, u32[]{:S(2)}) %collective-permute-start.52) | collective-permute-done | bytes 557088 | tf_op jit(solution)/shard_map/ppermute | solution.py:509
  1025.5 13.4 %attend_back.1 = (f32[1024,512]{1,0:T(8,128)}, bf16[1024,256]{1,0:T(8,128)(2,1)}, f32[1024,2]{1,0:T(8,128)}, f32[2,256]{1,0:T(2,128)}) custom-call(bf16[1024,768]{1,0:T(8,128)(2,1)} %get-tuple-element.147.turned, bf16[1024,256]{1,0:T(8,128)(2,1)} %fusion.15.grads, f32[1024,768]{1,0:T(8,128)} %copy.266.raw, f32[1024,2]{1,0:T(8,128)} %bitcast.278, ...), custom_call_target="tpu_custom_call" | custom-call | flops 402653184 | bytes 7864320 | tf_op jit(solution)/shard_map/attend_back/pallas_call | solution.py:403
  1072.1 21.7 %collective-permute-done.57 = bf16[2,8,64,512]{3,2,1,0:T(8,128)(2,1)S(1)} collective-permute-done((bf16[2,8,64,512]{3,2,1,0:T(8,128)(2,1)}, bf16[2,8,64,512]{3,2,1,0:T(8,128)(2,1)S(1)}, u32[]{:S(2)}, u32[]{:S(2)}) %collective-permute-start.57) | collective-permute-done | bytes 1048608 | tf_op jit(solution)/shard_map/ppermute | solution.py:509
  1127.2 20.7 %collective-permute-done.58 = bf16[2,9,64,512]{3,2,1,0:T(8,128)(2,1)} collective-permute-done((bf16[2,9,64,512]{3,2,1,0:T(8,128)(2,1)}, bf16[2,9,64,512]{3,2,1,0:T(8,128)(2,1)}, u32[]{:S(2)}, u32[]{:S(2)}) %collective-permute-start.58) | collective-permute-done | bytes 1179680 | tf_op jit(solution)/shard_map/ppermute | solution.py:509
  1165.8 26.1 %collective-permute-done.59 = bf16[2,128,2048]{2,1,0:T(8,128)(2,1)S(1)} collective-permute-done((bf16[2,128,2048]{2,1,0:T(8,128)(2,1)S(1)}, bf16[2,128,2048]{2,1,0:T(8,128)(2,1)S(1)}, u32[]{:S(2)}, u32[]{:S(2)}) %collective-permute-start.59) | collective-permute-done | bytes 1048608 | tf_op jit(solution)/shard_map/ppermute | solution.py:509
  (545 shorter events, 479.3 us)
Async XLA Ops:
  0.7 35.7 %collective-permute-start.7 = (bf16[128,2048]{1,0:T(8,128)(2,1)}, bf16[128,2048]{1,0:T(8,128)(2,1)S(1)}, u32[]{:S(2)}, u32[]{:S(2)}) collective-permute-start(bf16[128,2048]{1,0:T(8,128)(2,1)} %param.23), channel_id=1, source_target_pairs={{0,2},{1,3},{2,0},{3,1},{4,6},{5,7},{6,4},{7,5},{8,10},{9,11},{10,... | collective-permute-start | bytes 1572872 | tf_op jit(solution)/shard_map/ppermute | solution.py:509
  65.5 99.0 %all-to-all-start.1 = ((bf16[4,2,512,512]{3,2,1,0:T(8,128)(2,1)}), bf16[4,2,512,512]{3,2,1,0:T(8,128)(2,1)}, u32[]{:S(2)}, u32[]{:S(2)}) async-start(bf16[4,2,512,512]{3,2,1,0:T(8,128)(2,1)} %slice_weights.5), calls=%async_computation.1 | async-start | bytes 8388608 | tf_op jit(solution)/shard_map/all_to_all | solution.py:645
  99.2 48.0 %collective-permute-start.10 = (bf16[512,2048]{1,0:T(8,128)(2,1)}, bf16[512,2048]{1,0:T(8,128)(2,1)}, u32[]{:S(2)}, u32[]{:S(2)}) collective-permute-start(bf16[512,2048]{1,0:T(8,128)(2,1)} %constant_dynamic-update-slice_fusion.8.refs_1_), channel_id=1, source_target_pairs={{0,16},{4,20},{8,24},{12,28},{16,0},{20,4},{24,8},{28,12},{1,17},{... | collective-permute-start | bytes 6291464 | tf_op jit(solution)/shard_map/ppermute | solution.py:509
  100.8 47.7 %collective-permute-start.9 = (bf16[512,2048]{1,0:T(8,128)(2,1)}, bf16[512,2048]{1,0:T(8,128)(2,1)}, u32[]{:S(2)}, u32[]{:S(2)}) collective-permute-start(bf16[512,2048]{1,0:T(8,128)(2,1)} %constant_dynamic-update-slice_fusion.8.refs_1_), channel_id=1, source_target_pairs={{0,8},{4,12},{8,0},{12,4},{16,24},{20,28},{24,16},{28,20},{1,9},{5... | collective-permute-start | bytes 6291464 | tf_op jit(solution)/shard_map/ppermute | solution.py:509
  164.5 41.8 %collective-permute-start.11 = (bf16[1,8,64,768]{3,2,1,0:T(8,128)(2,1)S(1)}, bf16[1,8,64,768]{3,2,1,0:T(8,128)(2,1)S(1)}, u32[]{:S(2)}, u32[]{:S(2)}) collective-permute-start(bf16[1,8,64,768]{3,2,1,0:T(8,128)(2,1)S(1)} %bitcast.284), channel_id=1, source_target_pairs={{0,2},{1,3},{2,0},{3,1},{4,6},{5,7},{6,4},{7,5},{8,10},{9,11},{10,... | collective-permute-start | bytes 2359304 | tf_op jit(solution)/shard_map/ppermute | solution.py:509
  172.2 39.8 %collective-permute-start.14 = (bf16[1,64,2048]{2,1,0:T(8,128)(2,1)S(1)}, bf16[1,64,2048]{2,1,0:T(8,128)(2,1)S(1)}, u32[]{:S(2)}, u32[]{:S(2)}) collective-permute-start(bf16[1,64,2048]{2,1,0:T(8,128)(2,1)S(1)} %bitcast.309), channel_id=1, source_target_pairs={{0,2},{1,3},{2,0},{3,1},{4,6},{5,7},{6,4},{7,5},{8,10},{9,11},{10,... | collective-permute-start | bytes 786440 | tf_op jit(solution)/shard_map/ppermute | solution.py:509
  207.7 51.0 %collective-permute-start.12 = (bf16[2,8,64,768]{3,2,1,0:T(8,128)(2,1)}, bf16[2,8,64,768]{3,2,1,0:T(8,128)(2,1)}, u32[]{:S(2)}, u32[]{:S(2)}) collective-permute-start(bf16[2,8,64,768]{3,2,1,0:T(8,128)(2,1)} %pad_maximum_fusion.1), channel_id=1, source_target_pairs={{0,1},{1,0},{2,3},{3,2},{4,5},{5,4},{6,7},{7,6},{8,9},{9,8},{10,11... | collective-permute-start | bytes 4718600 | tf_op jit(solution)/shard_map/ppermute | solution.py:509
  212.0 44.8 %collective-permute-start.15 = (bf16[2,64,2048]{2,1,0:T(8,128)(2,1)S(1)}, bf16[2,64,2048]{2,1,0:T(8,128)(2,1)S(1)}, u32[]{:S(2)}, u32[]{:S(2)}) collective-permute-start(bf16[2,64,2048]{2,1,0:T(8,128)(2,1)S(1)} %pad_maximum_fusion.8), channel_id=1, source_target_pairs={{0,1},{1,0},{2,3},{3,2},{4,5},{5,4},{6,7},{7,6},{8,9},{9,8},{10,11... | collective-permute-start | bytes 1572872 | tf_op jit(solution)/shard_map/ppermute | solution.py:509
  217.7 65.3 %collective-permute-start.13 = (bf16[512,2048]{1,0:T(8,128)(2,1)}, bf16[512,2048]{1,0:T(8,128)(2,1)}, u32[]{:S(2)}, u32[]{:S(2)}) collective-permute-start(bf16[512,2048]{1,0:T(8,128)(2,1)} %constant_dynamic-update-slice_fusion.8.refs_1_), channel_id=1, source_target_pairs={{0,24},{4,28},{8,16},{12,20},{16,8},{20,12},{24,0},{28,4},{1,25},{... | collective-permute-start | bytes 6291464 | tf_op jit(solution)/shard_map/ppermute | solution.py:509
  267.6 53.5 %all-to-all-start.2 = ((bf16[4,1,512,512]{3,2,1,0:T(8,128)(2,1)}), bf16[4,1,512,512]{3,2,1,0:T(8,128)(2,1)}, u32[]{:S(2)}, u32[]{:S(2)}) async-start(bf16[4,1,512,512]{3,2,1,0:T(8,128)(2,1)} %slice_weights.6), calls=%async_computation.2 | async-start | bytes 4194304 | tf_op jit(solution)/shard_map/all_to_all | solution.py:645
  334.8 54.2 %all-to-all-start.3 = ((bf16[4,1,512,512]{3,2,1,0:T(8,128)(2,1)}), bf16[4,1,512,512]{3,2,1,0:T(8,128)(2,1)}, u32[]{:S(2)}, u32[]{:S(2)}) async-start(bf16[4,1,512,512]{3,2,1,0:T(8,128)(2,1)} %slice_weights.7), calls=%async_computation.3 | async-start | bytes 4194304 | tf_op jit(solution)/shard_map/all_to_all | solution.py:645
  441.6 103.7 %all-to-all-start.4 = ((bf16[4,2,512,512]{3,2,1,0:T(8,128)(2,1)}), bf16[4,2,512,512]{3,2,1,0:T(8,128)(2,1)}, u32[]{:S(2)}, u32[]{:S(2)}) async-start(bf16[4,2,512,512]{3,2,1,0:T(8,128)(2,1)} %slice_weights.8), calls=%async_computation.4 | async-start | bytes 8388608 | tf_op jit(solution)/shard_map/all_to_all | solution.py:645
  446.4 51.4 %collective-permute-start.27 = (bf16[512,2176]{1,0:T(8,128)(2,1)S(1)}, bf16[512,2176]{1,0:T(8,128)(2,1)S(1)}, u32[]{:S(2)}, u32[]{:S(2)}) collective-permute-start(bf16[512,2176]{1,0:T(8,128)(2,1)S(1)} %constant_dynamic-update-slice_fusion.10.refs_1_), channel_id=1, source_target_pairs={{0,8},{4,12},{8,0},{12,4},{16,24},{20,28},{24,16},{28,20},{1,9},{5... | collective-permute-start | bytes 6684680 | tf_op jit(solution)/shard_map/ppermute | solution.py:509
  446.9 97.0 %collective-permute-start.29 = (bf16[512,2176]{1,0:T(8,128)(2,1)S(1)}, bf16[512,2176]{1,0:T(8,128)(2,1)S(1)}, u32[]{:S(2)}, u32[]{:S(2)}) collective-permute-start(bf16[512,2176]{1,0:T(8,128)(2,1)S(1)} %constant_dynamic-update-slice_fusion.10.refs_1_), channel_id=1, source_target_pairs={{0,16},{4,20},{8,24},{12,28},{16,0},{20,4},{24,8},{28,12},{1,17},{... | collective-permute-start | bytes 6684680 | tf_op jit(solution)/shard_map/ppermute | solution.py:509
  448.5 96.7 %collective-permute-start.31 = (bf16[512,2176]{1,0:T(8,128)(2,1)S(1)}, bf16[512,2176]{1,0:T(8,128)(2,1)}, u32[]{:S(2)}, u32[]{:S(2)}) collective-permute-start(bf16[512,2176]{1,0:T(8,128)(2,1)S(1)} %constant_dynamic-update-slice_fusion.10.refs_1_), channel_id=1, source_target_pairs={{0,24},{4,28},{8,16},{12,20},{16,8},{20,12},{24,0},{28,4},{1,25},{... | collective-permute-start | bytes 6684680 | tf_op jit(solution)/shard_map/ppermute | solution.py:509
  545.2 95.4 %all-to-all-start.5 = ((bf16[4,2,512,512]{3,2,1,0:T(8,128)(2,1)}), bf16[4,2,512,512]{3,2,1,0:T(8,128)(2,1)}, u32[]{:S(2)}, u32[]{:S(2)}) async-start(bf16[4,2,512,512]{3,2,1,0:T(8,128)(2,1)} %slice_weights.9), calls=%async_computation.5 | async-start | bytes 8388608 | tf_op jit(solution)/shard_map/all_to_all | solution.py:645
  640.6 97.6 %all-to-all-start.6 = ((bf16[4,2,512,512]{3,2,1,0:T(8,128)(2,1)}), bf16[4,2,512,512]{3,2,1,0:T(8,128)(2,1)}, u32[]{:S(2)}, u32[]{:S(2)}) async-start(bf16[4,2,512,512]{3,2,1,0:T(8,128)(2,1)} %get-tuple-element.148), calls=%async_computation.6 | async-start | bytes 8388608 | tf_op jit(solution)/shard_map/all_to_all | solution.py:748
  738.2 188.4 %all-to-all-start.7 = ((bf16[4,4,512,512]{3,2,1,0:T(8,128)(2,1)}), bf16[4,4,512,512]{3,2,1,0:T(8,128)(2,1)}, u32[]{:S(2)}, u32[]{:S(2)}) async-start(bf16[4,4,512,512]{3,2,1,0:T(8,128)(2,1)} %get-tuple-element.150), calls=%async_computation.7 | async-start | bytes 16777216 | tf_op jit(solution)/shard_map/all_to_all | solution.py:748
  760.0 41.6 %collective-permute-start.38 = (bf16[512,2176]{1,0:T(8,128)(2,1)}, bf16[512,2176]{1,0:T(8,128)(2,1)S(1)}, u32[]{:S(2)}, u32[]{:S(2)}) collective-permute-start(bf16[512,2176]{1,0:T(8,128)(2,1)} %get-tuple-element.140), channel_id=1, source_target_pairs={{0,4},{4,0},{8,12},{12,8},{16,20},{20,16},{24,28},{28,24},{1,5},{5... | collective-permute-start | bytes 6684680 | tf_op jit(solution)/shard_map/ppermute | solution.py:509
  780.1 52.4 %collective-permute-start.41 = (bf16[512,2176]{1,0:T(8,128)(2,1)}, bf16[512,2176]{1,0:T(8,128)(2,1)S(1)}, u32[]{:S(2)}, u32[]{:S(2)}) collective-permute-start(bf16[512,2176]{1,0:T(8,128)(2,1)} %add_convert_fusion.1), channel_id=1, source_target_pairs={{0,24},{4,28},{8,16},{12,20},{16,8},{20,12},{24,0},{28,4},{1,25},{... | collective-permute-start | bytes 6684680 | tf_op jit(solution)/shard_map/ppermute | solution.py:509
  783.5 95.9 %collective-permute-start.40 = (bf16[512,2176]{1,0:T(8,128)(2,1)}, bf16[512,2176]{1,0:T(8,128)(2,1)S(1)}, u32[]{:S(2)}, u32[]{:S(2)}) collective-permute-start(bf16[512,2176]{1,0:T(8,128)(2,1)} %add_convert_fusion.2), channel_id=1, source_target_pairs={{0,16},{4,20},{8,24},{12,28},{16,0},{20,4},{24,8},{28,12},{1,17},{... | collective-permute-start | bytes 6684680 | tf_op jit(solution)/shard_map/ppermute | solution.py:509
  788.6 103.3 %collective-permute-start.39 = (bf16[512,2176]{1,0:T(8,128)(2,1)}, bf16[512,2176]{1,0:T(8,128)(2,1)}, u32[]{:S(2)}, u32[]{:S(2)}) collective-permute-start(bf16[512,2176]{1,0:T(8,128)(2,1)} %add_convert_fusion.3), channel_id=1, source_target_pairs={{0,8},{4,12},{8,0},{12,4},{16,24},{20,28},{24,16},{28,20},{1,9},{5... | collective-permute-start | bytes 6684680 | tf_op jit(solution)/shard_map/ppermute | solution.py:509
  801.6 94.7 %collective-permute-start.36 = (bf16[512,2048]{1,0:T(8,128)(2,1)}, bf16[512,2048]{1,0:T(8,128)(2,1)}, u32[]{:S(2)}, u32[]{:S(2)}) collective-permute-start(bf16[512,2048]{1,0:T(8,128)(2,1)} %get-tuple-element.136), channel_id=1, source_target_pairs={{0,4},{4,0},{8,12},{12,8},{16,20},{20,16},{24,28},{28,24},{1,5},{5... | collective-permute-start | bytes 6291464 | tf_op jit(solution)/shard_map/ppermute | solution.py:509
  801.6 94.7 %collective-permute-start.37 = (bf16[512,2048]{1,0:T(8,128)(2,1)}, bf16[512,2048]{1,0:T(8,128)(2,1)}, u32[]{:S(2)}, u32[]{:S(2)}) collective-permute-start(bf16[512,2048]{1,0:T(8,128)(2,1)} %get-tuple-element.138), channel_id=1, source_target_pairs={{0,4},{4,0},{8,12},{12,8},{16,20},{20,16},{24,28},{28,24},{1,5},{5... | collective-permute-start | bytes 6291464 | tf_op jit(solution)/shard_map/ppermute | solution.py:509
  832.5 63.8 %collective-permute-start.43 = (bf16[512,2048]{1,0:T(8,128)(2,1)}, bf16[512,2048]{1,0:T(8,128)(2,1)}, u32[]{:S(2)}, u32[]{:S(2)}) collective-permute-start(bf16[512,2048]{1,0:T(8,128)(2,1)} %get-tuple-element.143), channel_id=1, source_target_pairs={{0,4},{4,0},{8,12},{12,8},{16,20},{20,16},{24,28},{28,24},{1,5},{5... | collective-permute-start | bytes 6291464 | tf_op jit(solution)/shard_map/ppermute | solution.py:509
  935.7 53.4 %collective-permute-start.44 = (bf16[512,2048]{1,0:T(8,128)(2,1)}, bf16[512,2048]{1,0:T(8,128)(2,1)}, u32[]{:S(2)}, u32[]{:S(2)}) collective-permute-start(bf16[512,2048]{1,0:T(8,128)(2,1)} %add_convert_fusion.6), channel_id=1, source_target_pairs={{0,16},{4,20},{8,24},{12,28},{16,0},{20,4},{24,8},{28,12},{1,17},{... | collective-permute-start | bytes 6291464 | tf_op jit(solution)/shard_map/ppermute | solution.py:509
  937.4 51.8 %collective-permute-start.42 = (bf16[512,2048]{1,0:T(8,128)(2,1)}, bf16[512,2048]{1,0:T(8,128)(2,1)}, u32[]{:S(2)}, u32[]{:S(2)}) collective-permute-start(bf16[512,2048]{1,0:T(8,128)(2,1)} %add_convert_fusion.7), channel_id=1, source_target_pairs={{0,8},{4,12},{8,0},{12,4},{16,24},{20,28},{24,16},{28,20},{1,9},{5... | collective-permute-start | bytes 6291464 | tf_op jit(solution)/shard_map/ppermute | solution.py:509
  973.4 123.8 %all-to-all-start.8 = ((bf16[4,2,512,512]{3,2,1,0:T(8,128)(2,1)}), bf16[4,2,512,512]{3,2,1,0:T(8,128)(2,1)}, u32[]{:S(2)}, u32[]{:S(2)}) async-start(bf16[4,2,512,512]{3,2,1,0:T(8,128)(2,1)} %get-tuple-element.165), calls=%async_computation.8 | async-start | bytes 8388608 | tf_op jit(solution)/shard_map/all_to_all | solution.py:748
  1053.1 40.7 %collective-permute-start.57 = (bf16[2,8,64,512]{3,2,1,0:T(8,128)(2,1)}, bf16[2,8,64,512]{3,2,1,0:T(8,128)(2,1)S(1)}, u32[]{:S(2)}, u32[]{:S(2)}) collective-permute-start(bf16[2,8,64,512]{3,2,1,0:T(8,128)(2,1)} %get-tuple-element.166), channel_id=1, source_target_pairs={{0,1},{1,0},{2,3},{3,2},{4,5},{5,4},{6,7},{7,6},{8,9},{9,8},{10,11... | collective-permute-start | bytes 3145736 | tf_op jit(solution)/shard_map/ppermute | solution.py:509
  1066.8 60.4 %collective-permute-start.56 = (bf16[512,2048]{1,0:T(8,128)(2,1)}, bf16[512,2048]{1,0:T(8,128)(2,1)}, u32[]{:S(2)}, u32[]{:S(2)}) collective-permute-start(bf16[512,2048]{1,0:T(8,128)(2,1)} %add_convert_fusion.5), channel_id=1, source_target_pairs={{0,24},{4,28},{8,16},{12,20},{16,8},{20,12},{24,0},{28,4},{1,25},{... | collective-permute-start | bytes 6291464 | tf_op jit(solution)/shard_map/ppermute | solution.py:509
  1154.0 37.8 %collective-permute-start.59 = (bf16[2,128,2048]{2,1,0:T(8,128)(2,1)S(1)}, bf16[2,128,2048]{2,1,0:T(8,128)(2,1)S(1)}, u32[]{:S(2)}, u32[]{:S(2)}) collective-permute-start(bf16[2,128,2048]{2,1,0:T(8,128)(2,1)S(1)} %bitcast.308), channel_id=1, source_target_pairs={{0,1},{1,0},{2,3},{3,2},{4,5},{5,4},{6,7},{7,6},{8,9},{9,8},{10,11... | collective-permute-start | bytes 3145736 | tf_op jit(solution)/shard_map/ppermute | solution.py:509
  1157.6 35.7 %collective-permute-start.65 = (bf16[1,9,64,512]{3,2,1,0:T(8,128)(2,1)S(1)}, bf16[1,9,64,512]{3,2,1,0:T(8,128)(2,1)S(1)}, u32[]{:S(2)}, u32[]{:S(2)}) collective-permute-start(bf16[1,9,64,512]{3,2,1,0:T(8,128)(2,1)S(1)} %slice.630), channel_id=1, source_target_pairs={{0,2},{1,3},{2,0},{3,1},{4,6},{5,7},{6,4},{7,5},{8,10},{9,11},{10,... | collective-permute-start | bytes 1769480 | tf_op jit(solution)/shard_map/ppermute | solution.py:509
  (132 other events, 2812.1 us)

commit v5 on v4

--- a/solution.py
+++ b/solution.py
@@ -185,13 +185,13 @@
             weight_grads_ref[s, 0] = weight_sums[s].astype(BF)
 
 
-def expert_chunk(where, rows, ups, weights, down, start, group, at, buffers):
-    parts, experts, depth, width2 = weights.shape
+def expert_chunk(where, rows, ups, weights, down, start, experts, offset, group, at, buffers):
+    parts, _, depth, width2 = weights.shape
     local, total_rows, wide_row = rows.shape
     tile = EXPERT_TILE
     tiles = total_rows // tile
     slice_ff = down.shape[1]
-    weight_spec = pl.BlockSpec((parts, 1, depth, width2), lambda e, i, c: (0, e, 0, 0))
+    weight_spec = pl.BlockSpec((parts, 1, depth, width2), lambda e, i, c: (0, offset + e, 0, 0))
     down_spec = pl.BlockSpec((1, slice_ff, D), lambda e, i, c: (start + e, 0, 0))
     in_specs = [
         pl.BlockSpec((1, tile, wide_row), lambda e, i, c: (start + e, i, 0)),
@@ -495,10 +495,12 @@
     heads = H // wide
     features = heads * HD
     if local == 8:
-        sizes, early, groups = [2, 1, 1, 2, 2], 3, [[0], [1, 2, 3], [4]]
+        sizes, early, groups = [2, 1, 1, 1, 1, 2], 3, [[0], [1, 2, 3], [4, 5]]
+        parts = [[0], [1], [2], [3, 4], [5]]
     else:
         sizes = [1] * local
         early, groups = min(2, local), [[c] for c in range(local)]
+        parts = groups
     calls = len(sizes)
     starts = [sum(sizes[:c]) for c in range(calls)]
     slice_ff = FF // narrow
@@ -636,7 +638,8 @@
         plane_count = plane_tokens.shape[0]
 
         sliced = [
-            slice_weights(w_gate, w_up, starts[c], sizes[c], narrow) for c in range(calls)
+            slice_weights(w_gate, w_up, starts[p[0]], sum(sizes[c] for c in p), narrow)
+            for p in parts
         ]
         expert_weights = []
 
@@ -715,12 +718,12 @@
         ups = dispatch(picks_own, ups_own, 0)
         ups = dispatch(picks_other, cross(ups_own), 1, ups)
         message = gather_narrow(tie(message, ups, expert_weights[-1]))
-        if calls > early:
+        if len(parts) > early:
             send_weights(message)
         tokens_own = gather_planes(message)
-        while len(expert_weights) < calls:
+        while len(expert_weights) < len(parts):
             send_weights(*tokens_own)
-        tokens_own[0] = tie(tokens_own[0], expert_weights[min(early, calls - 1)])
+        tokens_own[0] = tie(tokens_own[0], expert_weights[min(early, len(parts) - 1)])
         tokens_other = cross(tokens_own)
         expert_rows = dispatch(picks_own, tokens_own, 0)
         expert_rows = dispatch(picks_other, tokens_other, 1, expert_rows)
@@ -731,11 +734,12 @@
             if c == 1:
                 expert_rows = tie(expert_rows, expert_weights[-1])
             group = next(g for g in groups if c in g)
+            part = next(i for i, p in enumerate(parts) if c in p)
             if c == group[0]:
                 held[2] = None
             held = [*expert_chunk(
-                where, expert_rows, ups, expert_weights[c], w_down, starts[c],
-                sum(sizes[g] for g in group), starts[c] - starts[group[0]], held,
+                where, expert_rows, ups, expert_weights[part], w_down, starts[c], sizes[c],
+                starts[c] - starts[parts[part][0]], sum(sizes[g] for g in group), starts[c] - starts[group[0]], held,
             )]
             if c == group[-1]:
                 came.append(held[2])

time: 1240 us -> 1220 us (0.984)
  waiting for transfers between devices: 603 us -> 572 us
  starting transfers between devices: 99.2 us -> 113 us
    all_to_all x3, waiting for transfers between devices: 42.7 us -> 20.6 us  [send_grads(): arrived.append(lax.all_to_all(part, 'narrow', 0, 0, tiled=True))]
    pallas_call x5 -> x6, Pallas kernels: 104 us -> 111 us  [expert_chunk(): pl.pallas_call(functools.partial(expert_body, parts, tiles, start, len(al...]
    unnamed x201 -> x199, local copies, waits for them, and re-layouts: 41.7 us -> 39.3 us
  transfers between devices with their start and end apart: 77 -> 77, of which waited for: 34 -> 32; matrix products, arithmetic and copies ran while one was open for 16% -> 16% of each run, Pallas kernels for 20% -> 21%
where the time goes in v5:
time: 1220 us; the launch traced here: 1210 us
  waiting for transfers between devices  572 us (47%)
  Pallas kernels  256 us (21%)
  starting transfers between devices  113 us (9%)
  local copies, waits for them, and re-layouts  87.2 us (7%)
  other arithmetic  87.1 us (7%)
  blocking collectives  57.9 us (5%)
  matrix products  37.6 us (3%)
    ppermute x67, waiting for transfers between devices, swap(): return lax.ppermute(x, axis, [(i, i ^ r) for i in range(size)])  476 us
    pallas_call x6, Pallas kernels, expert_chunk(): pl.pallas_call(functools.partial(expert_body, parts, tiles, start, len(al...  111 us
    all_to_all x5, waiting for transfers between devices, send_weights(): expert_weights.append(lax.all_to_all(part, 'narrow', 0, 0, tiled=True))  75.1 us
    ppermute x67, starting transfers between devices, swap(): return lax.ppermute(x, axis, [(i, i ^ r) for i in range(size)])  54.7 us
    unnamed x199, local copies, waits for them, and re-layouts  39.3 us
    pallas_call x4, Pallas kernels, combine(): pl.pallas_call(functools.partial(combine_body, pieces, each), grid=(pairs...  38.3 us
    dot_general x11, matrix products, matmul(): return lax.dot_general(a, b, (dims, ((), ())), preferred_element_type=F32)  37.6 us
    pallas_call x4, Pallas kernels, dispatch(): pl.pallas_call(functools.partial(dispatch_body, pieces, each), grid=(pair...  36.4 us
  transfers between devices with their start and end apart: 77, of which 32 were waited for; matrix products, arithmetic and copies ran while one was open for 16% of the time, Pallas kernels for 21%

profile of v5, /device:TPU:0, one launch (start us, length us, event | category | flops | bytes accessed | tf_op | source)
XLA Modules:
  0.0 1213.1 jit_solution(2534624350183496226)
XLA Ops:
  9.9 26.5 %all-gather = bf16[448,128]{1,0:T(8,128)(2,1)S(1)} all-gather(bf16[112,128]{1,0:T(8,128)(2,1)S(1)} %pad_maximum_fusion.11), channel_id=2, replica_groups=mesh['wide'=8,'narrow'=4] {'narrow'}, dimensions={0}, use_global_device_ids=true | all-gather | bytes 143360 | tf_op jit(solution)/shard_map/all_gather | solution.py:613
  47.1 15.0 %all-gather.1 = bf16[32,112,128]{2,1,0:T(8,128)(2,1)S(1)} all-gather(bf16[4,112,128]{2,1,0:T(8,128)(2,1)S(1)} %bitcast.316), channel_id=3, replica_groups=mesh['wide'=8,'narrow'=4] {'wide'}, dimensions={0}, use_global_device_ids=true | all-gather | bytes 1032192 | tf_op jit(solution)/shard_map/all_gather | solution.py:618
  74.1 11.4 collective-permute-done.1
  85.4 10.8 collective-permute-done.3
  104.8 42.2 %collective-permute-done.10.refs_3_ = bf16[512,2048]{1,0:T(8,128)(2,1)} collective-permute-done((bf16[512,2048]{1,0:T(8,128)(2,1)}, bf16[512,2048]{1,0:T(8,128)(2,1)}, u32[]{:S(2)}, u32[]{:S(2)}) %collective-permute-start.10) | collective-permute-done | bytes 2097184 | tf_op jit(solution)/shard_map/ppermute | solution.py:511
  148.4 16.1 %all-to-all-done.1.refs_3_ = bf16[4,2,512,512]{3,2,1,0:T(8,128)(2,1)} async-done(((bf16[4,2,512,512]{3,2,1,0:T(8,128)(2,1)}), bf16[4,2,512,512]{3,2,1,0:T(8,128)(2,1)}, u32[]{:S(2)}, u32[]{:S(2)}) %all-to-all-start.1) | async-done | bytes 4194336 | tf_op jit(solution)/shard_map/all_to_all | solution.py:648
  175.7 30.6 %collective-permute-done.11 = bf16[1,8,64,768]{3,2,1,0:T(8,128)(2,1)S(1)} collective-permute-done((bf16[1,8,64,768]{3,2,1,0:T(8,128)(2,1)S(1)}, bf16[1,8,64,768]{3,2,1,0:T(8,128)(2,1)S(1)}, u32[]{:S(2)}, u32[]{:S(2)}) %collective-permute-start.11) | collective-permute-done | bytes 786464 | tf_op jit(solution)/shard_map/ppermute | solution.py:511
  219.3 37.6 %collective-permute-done.15 = bf16[2,64,2048]{2,1,0:T(8,128)(2,1)S(1)} collective-permute-done((bf16[2,64,2048]{2,1,0:T(8,128)(2,1)S(1)}, bf16[2,64,2048]{2,1,0:T(8,128)(2,1)S(1)}, u32[]{:S(2)}, u32[]{:S(2)}) %collective-permute-start.15) | collective-permute-done | bytes 524320 | tf_op jit(solution)/shard_map/ppermute | solution.py:511
  302.4 9.8 attend.1
  388.8 25.8 %collective-permute-done.24 = bf16[128,2176]{1,0:T(8,128)(2,1)S(1)} collective-permute-done((bf16[128,2176]{1,0:T(8,128)(2,1)S(1)}, bf16[128,2176]{1,0:T(8,128)(2,1)S(1)}, u32[]{:S(2)}, u32[]{:S(2)}) %collective-permute-start.24) | collective-permute-done | bytes 557088 | tf_op jit(solution)/shard_map/ppermute | solution.py:511
  418.6 22.6 %collective-permute-done.25 = bf16[256,2176]{1,0:T(8,128)(2,1)S(1)} collective-permute-done((bf16[256,2176]{1,0:T(8,128)(2,1)S(1)}, bf16[256,2176]{1,0:T(8,128)(2,1)S(1)}, u32[]{:S(2)}, u32[]{:S(2)}) %collective-permute-start.25) | collective-permute-done | bytes 1114144 | tf_op jit(solution)/shard_map/ppermute | solution.py:511
  453.6 44.1 %collective-permute-done.27.refs_2_ = bf16[512,2176]{1,0:T(8,128)(2,1)S(1)} collective-permute-done((bf16[512,2176]{1,0:T(8,128)(2,1)S(1)}, bf16[512,2176]{1,0:T(8,128)(2,1)S(1)}, u32[]{:S(2)}, u32[]{:S(2)}) %collective-permute-start.27) | collective-permute-done | bytes 2228256 | tf_op jit(solution)/shard_map/ppermute | solution.py:511
  497.7 46.0 %collective-permute-done.29.refs_3_ = bf16[512,2176]{1,0:T(8,128)(2,1)S(1)} collective-permute-done((bf16[512,2176]{1,0:T(8,128)(2,1)S(1)}, bf16[512,2176]{1,0:T(8,128)(2,1)S(1)}, u32[]{:S(2)}, u32[]{:S(2)}) %collective-permute-start.29) | collective-permute-done | bytes 2228256 | tf_op jit(solution)/shard_map/ppermute | solution.py:511
  575.0 24.4 %experts.6 = (bf16[8,768,2048]{2,1,0:T(8,128)(2,1)}, bf16[8,768,2176]{2,1,0:T(8,128)(2,1)}, bf16[4,2,512,512]{3,2,1,0:T(8,128)(2,1)}, f32[8,256,2048]{2,1,0:T(8,128)}) custom-call(s32[3]{0:T(128)} %pad_add_fusion.refs_0_, bf16[8,768,2176]{2,1,0:T(8,128)(2,1)} %dispatch.7.refs_1_, bf16[8,768,2048]{2,1,0:T(8,128)(2,1)} %dispatch.5.refs_2_, ...), custom_call_target="tpu_custom_call" | custom-call | flops 14495514624 | bytes 44040192 | tf_op jit(solution)/shard_map/experts/pallas_call | solution.py:209
  599.4 41.1 %all-to-all-done.5.refs_3_ = bf16[4,2,512,512]{3,2,1,0:T(8,128)(2,1)} async-done(((bf16[4,2,512,512]{3,2,1,0:T(8,128)(2,1)}), bf16[4,2,512,512]{3,2,1,0:T(8,128)(2,1)}, u32[]{:S(2)}, u32[]{:S(2)}) %all-to-all-start.5) | async-done | bytes 4194336 | tf_op jit(solution)/shard_map/all_to_all | solution.py:648
  649.9 15.3 %experts.7 = (bf16[8,768,2048]{2,1,0:T(8,128)(2,1)}, bf16[8,768,2176]{2,1,0:T(8,128)(2,1)}, bf16[4,3,512,512]{3,2,1,0:T(8,128)(2,1)}, f32[8,256,2048]{2,1,0:T(8,128)}) custom-call(s32[3]{0:T(128)} %pad_add_fusion.refs_0_, bf16[8,768,2176]{2,1,0:T(8,128)(2,1)} %dispatch.7.refs_1_, ...), custom_call_target="tpu_custom_call", output_to_operand_aliasing={{0}: (5, {}), {1}: (6, {}), {3}: (7, {})} | custom-call | flops 7247757312 | bytes 22020096 | tf_op jit(solution)/shard_map/experts/pallas_call | solution.py:209
  665.2 15.5 %experts.8 = (bf16[8,768,2048]{2,1,0:T(8,128)(2,1)}, bf16[8,768,2176]{2,1,0:T(8,128)(2,1)}, bf16[4,3,512,512]{3,2,1,0:T(8,128)(2,1)}, f32[8,256,2048]{2,1,0:T(8,128)}) custom-call(s32[3]{0:T(128)} %pad_add_fusion.refs_0_, bf16[8,768,2176]{2,1,0:T(8,128)(2,1)} %dispatch.7.refs_1_, ...), custom_call_target="tpu_custom_call", output_to_operand_aliasing={{0}: (5, {}), {1}: (6, {}), {2}: (7, {}), {3}: (8, {})} | custom-call | flops 7247757312 | bytes 22020096 | tf_op jit(solution)/shard_map/experts/pallas_call | solution.py:209
  680.7 15.3 %experts.9 = (bf16[8,768,2048]{2,1,0:T(8,128)(2,1)}, bf16[8,768,2176]{2,1,0:T(8,128)(2,1)}, bf16[4,3,512,512]{3,2,1,0:T(8,128)(2,1)}, f32[8,256,2048]{2,1,0:T(8,128)}) custom-call(s32[3]{0:T(128)} %pad_add_fusion.refs_0_, bf16[8,768,2176]{2,1,0:T(8,128)(2,1)} %dispatch.7.refs_1_, ...), custom_call_target="tpu_custom_call", output_to_operand_aliasing={{0}: (5, {}), {1}: (6, {}), {2}: (7, {}), {3}: (8, {})} | custom-call | flops 7247757312 | bytes 22020096 | tf_op jit(solution)/shard_map/experts/pallas_call | solution.py:209
  696.1 15.7 %experts.10 = (bf16[8,768,2048]{2,1,0:T(8,128)(2,1)}, bf16[8,768,2176]{2,1,0:T(8,128)(2,1)}, bf16[4,3,512,512]{3,2,1,0:T(8,128)(2,1)}, f32[8,256,2048]{2,1,0:T(8,128)}) custom-call(s32[3]{0:T(128)} %pad_add_fusion.refs_0_, bf16[8,768,2176]{2,1,0:T(8,128)(2,1)} %dispatch.7.refs_1_, ...), custom_call_target="tpu_custom_call", output_to_operand_aliasing={{0}: (5, {}), {1}: (6, {}), {3}: (7, {})} | custom-call | flops 7247757312 | bytes 22020096 | tf_op jit(solution)/shard_map/experts/pallas_call | solution.py:209
  711.8 24.4 %experts.11 = (bf16[8,768,2048]{2,1,0:T(8,128)(2,1)}, bf16[8,768,2176]{2,1,0:T(8,128)(2,1)}, bf16[4,3,512,512]{3,2,1,0:T(8,128)(2,1)}, f32[8,256,2048]{2,1,0:T(8,128)}) custom-call(s32[3]{0:T(128)} %pad_add_fusion.refs_0_, bf16[8,768,2176]{2,1,0:T(8,128)(2,1)} %dispatch.7.refs_1_, ...), custom_call_target="tpu_custom_call", output_to_operand_aliasing={{0}: (5, {}), {1}: (6, {}), {2}: (7, {}), {3}: (8, {})} | custom-call | flops 14495514624 | bytes 44040192 | tf_op jit(solution)/shard_map/experts/pallas_call | solution.py:209
  761.7 10.3 combine.4
  797.6 30.4 %collective-permute-done.41 = bf16[512,2176]{1,0:T(8,128)(2,1)S(1)} collective-permute-done((bf16[512,2176]{1,0:T(8,128)(2,1)}, bf16[512,2176]{1,0:T(8,128)(2,1)S(1)}, u32[]{:S(2)}, u32[]{:S(2)}) %collective-permute-start.41) | collective-permute-done | bytes 2228256 | tf_op jit(solution)/shard_map/ppermute | solution.py:511
  828.0 46.8 %collective-permute-done.40 = bf16[512,2176]{1,0:T(8,128)(2,1)S(1)} collective-permute-done((bf16[512,2176]{1,0:T(8,128)(2,1)}, bf16[512,2176]{1,0:T(8,128)(2,1)S(1)}, u32[]{:S(2)}, u32[]{:S(2)}) %collective-permute-start.40) | collective-permute-done | bytes 2228256 | tf_op jit(solution)/shard_map/ppermute | solution.py:511
  877.3 9.9 combine.6
  903.5 15.5 %collective-permute-done.46 = bf16[2,128,2176]{2,1,0:T(8,128)(2,1)S(1)} collective-permute-done((bf16[2,128,2176]{2,1,0:T(8,128)(2,1)S(1)}, bf16[2,128,2176]{2,1,0:T(8,128)(2,1)S(1)}, u32[]{:S(2)}, u32[]{:S(2)}) %collective-permute-start.46) | collective-permute-done | bytes 1114144 | tf_op jit(solution)/shard_map/ppermute | solution.py:511
  931.1 15.4 %all-to-all-start.8 = ((bf16[4,3,512,512]{3,2,1,0:T(8,128)(2,1)}), bf16[4,3,512,512]{3,2,1,0:T(8,128)(2,1)}, u32[]{:S(2)}, u32[]{:S(2)}) async-start(bf16[4,3,512,512]{3,2,1,0:T(8,128)(2,1)} %get-tuple-element.173), calls=%async_computation.8 | async-start | bytes 12582912 | tf_op jit(solution)/shard_map/all_to_all | solution.py:752
  973.5 12.6 %collective-permute-done.52 = bf16[128,2176]{1,0:T(8,128)(2,1)S(1)} collective-permute-done((bf16[128,2176]{1,0:T(8,128)(2,1)S(1)}, bf16[128,2176]{1,0:T(8,128)(2,1)S(1)}, u32[]{:S(2)}, u32[]{:S(2)}) %collective-permute-start.52) | collective-permute-done | bytes 557088 | tf_op jit(solution)/shard_map/ppermute | solution.py:511
  991.3 13.4 %attend_back.1 = (f32[1024,512]{1,0:T(8,128)}, bf16[1024,256]{1,0:T(8,128)(2,1)}, f32[1024,2]{1,0:T(8,128)}, f32[2,256]{1,0:T(2,128)}) custom-call(bf16[1024,768]{1,0:T(8,128)(2,1)} %get-tuple-element.155.turned, bf16[1024,256]{1,0:T(8,128)(2,1)} %fusion.15.grads, f32[1024,768]{1,0:T(8,128)} %copy.270.raw, f32[1024,2]{1,0:T(8,128)} %bitcast.278, ...), custom_call_target="tpu_custom_call" | custom-call | flops 402653184 | bytes 7864320 | tf_op jit(solution)/shard_map/attend_back/pallas_call | solution.py:403
  1038.3 31.2 %collective-permute-done.57 = bf16[2,8,64,512]{3,2,1,0:T(8,128)(2,1)S(1)} collective-permute-done((bf16[2,8,64,512]{3,2,1,0:T(8,128)(2,1)}, bf16[2,8,64,512]{3,2,1,0:T(8,128)(2,1)S(1)}, u32[]{:S(2)}, u32[]{:S(2)}) %collective-permute-start.57) | collective-permute-done | bytes 1048608 | tf_op jit(solution)/shard_map/ppermute | solution.py:511
  1078.2 18.7 %all-to-all-done.8.refs_0_ = bf16[4,3,512,512]{3,2,1,0:T(8,128)(2,1)} async-done(((bf16[4,3,512,512]{3,2,1,0:T(8,128)(2,1)}), bf16[4,3,512,512]{3,2,1,0:T(8,128)(2,1)}, u32[]{:S(2)}, u32[]{:S(2)}) %all-to-all-start.8) | async-done | bytes 6291488 | tf_op jit(solution)/shard_map/all_to_all | solution.py:752
  1122.9 20.1 %collective-permute-done.58 = bf16[2,9,64,512]{3,2,1,0:T(8,128)(2,1)} collective-permute-done((bf16[2,9,64,512]{3,2,1,0:T(8,128)(2,1)}, bf16[2,9,64,512]{3,2,1,0:T(8,128)(2,1)}, u32[]{:S(2)}, u32[]{:S(2)}) %collective-permute-start.58) | collective-permute-done | bytes 1179680 | tf_op jit(solution)/shard_map/ppermute | solution.py:511
  1159.5 22.9 %collective-permute-done.59 = bf16[2,128,2048]{2,1,0:T(8,128)(2,1)S(1)} collective-permute-done((bf16[2,128,2048]{2,1,0:T(8,128)(2,1)S(1)}, bf16[2,128,2048]{2,1,0:T(8,128)(2,1)S(1)}, u32[]{:S(2)}, u32[]{:S(2)}) %collective-permute-start.59) | collective-permute-done | bytes 1048608 | tf_op jit(solution)/shard_map/ppermute | solution.py:511
  (544 shorter events, 473.2 us)
Async XLA Ops:
  0.7 35.7 %collective-permute-start.7 = (bf16[128,2048]{1,0:T(8,128)(2,1)}, bf16[128,2048]{1,0:T(8,128)(2,1)S(1)}, u32[]{:S(2)}, u32[]{:S(2)}) collective-permute-start(bf16[128,2048]{1,0:T(8,128)(2,1)} %param.23), channel_id=1, source_target_pairs={{0,2},{1,3},{2,0},{3,1},{4,6},{5,7},{6,4},{7,5},{8,10},{9,11},{10,... | collective-permute-start | bytes 1572872 | tf_op jit(solution)/shard_map/ppermute | solution.py:511
  65.5 99.0 %all-to-all-start.1 = ((bf16[4,2,512,512]{3,2,1,0:T(8,128)(2,1)}), bf16[4,2,512,512]{3,2,1,0:T(8,128)(2,1)}, u32[]{:S(2)}, u32[]{:S(2)}) async-start(bf16[4,2,512,512]{3,2,1,0:T(8,128)(2,1)} %slice_weights.5), calls=%async_computation.1 | async-start | bytes 8388608 | tf_op jit(solution)/shard_map/all_to_all | solution.py:648
  99.0 48.0 %collective-permute-start.10 = (bf16[512,2048]{1,0:T(8,128)(2,1)}, bf16[512,2048]{1,0:T(8,128)(2,1)}, u32[]{:S(2)}, u32[]{:S(2)}) collective-permute-start(bf16[512,2048]{1,0:T(8,128)(2,1)} %constant_dynamic-update-slice_fusion.8.refs_1_), channel_id=1, source_target_pairs={{0,16},{4,20},{8,24},{12,28},{16,0},{20,4},{24,8},{28,12},{1,17},{... | collective-permute-start | bytes 6291464 | tf_op jit(solution)/shard_map/ppermute | solution.py:511
  100.7 47.7 %collective-permute-start.9 = (bf16[512,2048]{1,0:T(8,128)(2,1)}, bf16[512,2048]{1,0:T(8,128)(2,1)}, u32[]{:S(2)}, u32[]{:S(2)}) collective-permute-start(bf16[512,2048]{1,0:T(8,128)(2,1)} %constant_dynamic-update-slice_fusion.8.refs_1_), channel_id=1, source_target_pairs={{0,8},{4,12},{8,0},{12,4},{16,24},{20,28},{24,16},{28,20},{1,9},{5... | collective-permute-start | bytes 6291464 | tf_op jit(solution)/shard_map/ppermute | solution.py:511
  164.5 41.8 %collective-permute-start.11 = (bf16[1,8,64,768]{3,2,1,0:T(8,128)(2,1)S(1)}, bf16[1,8,64,768]{3,2,1,0:T(8,128)(2,1)S(1)}, u32[]{:S(2)}, u32[]{:S(2)}) collective-permute-start(bf16[1,8,64,768]{3,2,1,0:T(8,128)(2,1)S(1)} %bitcast.284), channel_id=1, source_target_pairs={{0,2},{1,3},{2,0},{3,1},{4,6},{5,7},{6,4},{7,5},{8,10},{9,11},{10,... | collective-permute-start | bytes 2359304 | tf_op jit(solution)/shard_map/ppermute | solution.py:511
  172.2 39.8 %collective-permute-start.14 = (bf16[1,64,2048]{2,1,0:T(8,128)(2,1)S(1)}, bf16[1,64,2048]{2,1,0:T(8,128)(2,1)S(1)}, u32[]{:S(2)}, u32[]{:S(2)}) collective-permute-start(bf16[1,64,2048]{2,1,0:T(8,128)(2,1)S(1)} %bitcast.309), channel_id=1, source_target_pairs={{0,2},{1,3},{2,0},{3,1},{4,6},{5,7},{6,4},{7,5},{8,10},{9,11},{10,... | collective-permute-start | bytes 786440 | tf_op jit(solution)/shard_map/ppermute | solution.py:511
  207.8 51.1 %collective-permute-start.12 = (bf16[2,8,64,768]{3,2,1,0:T(8,128)(2,1)}, bf16[2,8,64,768]{3,2,1,0:T(8,128)(2,1)}, u32[]{:S(2)}, u32[]{:S(2)}) collective-permute-start(bf16[2,8,64,768]{3,2,1,0:T(8,128)(2,1)} %pad_maximum_fusion.1), channel_id=1, source_target_pairs={{0,1},{1,0},{2,3},{3,2},{4,5},{5,4},{6,7},{7,6},{8,9},{9,8},{10,11... | collective-permute-start | bytes 4718600 | tf_op jit(solution)/shard_map/ppermute | solution.py:511
  212.0 44.8 %collective-permute-start.15 = (bf16[2,64,2048]{2,1,0:T(8,128)(2,1)S(1)}, bf16[2,64,2048]{2,1,0:T(8,128)(2,1)S(1)}, u32[]{:S(2)}, u32[]{:S(2)}) collective-permute-start(bf16[2,64,2048]{2,1,0:T(8,128)(2,1)S(1)} %pad_maximum_fusion.8), channel_id=1, source_target_pairs={{0,1},{1,0},{2,3},{3,2},{4,5},{5,4},{6,7},{7,6},{8,9},{9,8},{10,11... | collective-permute-start | bytes 1572872 | tf_op jit(solution)/shard_map/ppermute | solution.py:511
  217.8 64.8 %collective-permute-start.13 = (bf16[512,2048]{1,0:T(8,128)(2,1)}, bf16[512,2048]{1,0:T(8,128)(2,1)}, u32[]{:S(2)}, u32[]{:S(2)}) collective-permute-start(bf16[512,2048]{1,0:T(8,128)(2,1)} %constant_dynamic-update-slice_fusion.8.refs_1_), channel_id=1, source_target_pairs={{0,24},{4,28},{8,16},{12,20},{16,8},{20,12},{24,0},{28,4},{1,25},{... | collective-permute-start | bytes 6291464 | tf_op jit(solution)/shard_map/ppermute | solution.py:511
  267.8 53.7 %all-to-all-start.2 = ((bf16[4,1,512,512]{3,2,1,0:T(8,128)(2,1)}), bf16[4,1,512,512]{3,2,1,0:T(8,128)(2,1)}, u32[]{:S(2)}, u32[]{:S(2)}) async-start(bf16[4,1,512,512]{3,2,1,0:T(8,128)(2,1)} %slice_weights.6), calls=%async_computation.2 | async-start | bytes 4194304 | tf_op jit(solution)/shard_map/all_to_all | solution.py:648
  334.6 54.1 %all-to-all-start.3 = ((bf16[4,1,512,512]{3,2,1,0:T(8,128)(2,1)}), bf16[4,1,512,512]{3,2,1,0:T(8,128)(2,1)}, u32[]{:S(2)}, u32[]{:S(2)}) async-start(bf16[4,1,512,512]{3,2,1,0:T(8,128)(2,1)} %slice_weights.7), calls=%async_computation.3 | async-start | bytes 4194304 | tf_op jit(solution)/shard_map/all_to_all | solution.py:648
  441.4 103.7 %all-to-all-start.4 = ((bf16[4,2,512,512]{3,2,1,0:T(8,128)(2,1)}), bf16[4,2,512,512]{3,2,1,0:T(8,128)(2,1)}, u32[]{:S(2)}, u32[]{:S(2)}) async-start(bf16[4,2,512,512]{3,2,1,0:T(8,128)(2,1)} %slice_weights.8), calls=%async_computation.4 | async-start | bytes 8388608 | tf_op jit(solution)/shard_map/all_to_all | solution.py:648
  446.3 51.4 %collective-permute-start.27 = (bf16[512,2176]{1,0:T(8,128)(2,1)S(1)}, bf16[512,2176]{1,0:T(8,128)(2,1)S(1)}, u32[]{:S(2)}, u32[]{:S(2)}) collective-permute-start(bf16[512,2176]{1,0:T(8,128)(2,1)S(1)} %constant_dynamic-update-slice_fusion.10.refs_1_), channel_id=1, source_target_pairs={{0,8},{4,12},{8,0},{12,4},{16,24},{20,28},{24,16},{28,20},{1,9},{5... | collective-permute-start | bytes 6684680 | tf_op jit(solution)/shard_map/ppermute | solution.py:511
  446.7 97.0 %collective-permute-start.29 = (bf16[512,2176]{1,0:T(8,128)(2,1)S(1)}, bf16[512,2176]{1,0:T(8,128)(2,1)S(1)}, u32[]{:S(2)}, u32[]{:S(2)}) collective-permute-start(bf16[512,2176]{1,0:T(8,128)(2,1)S(1)} %constant_dynamic-update-slice_fusion.10.refs_1_), channel_id=1, source_target_pairs={{0,16},{4,20},{8,24},{12,28},{16,0},{20,4},{24,8},{28,12},{1,17},{... | collective-permute-start | bytes 6684680 | tf_op jit(solution)/shard_map/ppermute | solution.py:511
  448.4 96.7 %collective-permute-start.31 = (bf16[512,2176]{1,0:T(8,128)(2,1)S(1)}, bf16[512,2176]{1,0:T(8,128)(2,1)}, u32[]{:S(2)}, u32[]{:S(2)}) collective-permute-start(bf16[512,2176]{1,0:T(8,128)(2,1)S(1)} %constant_dynamic-update-slice_fusion.10.refs_1_), channel_id=1, source_target_pairs={{0,24},{4,28},{8,16},{12,20},{16,8},{20,12},{24,0},{28,4},{1,25},{... | collective-permute-start | bytes 6684680 | tf_op jit(solution)/shard_map/ppermute | solution.py:511
  545.1 95.4 %all-to-all-start.5 = ((bf16[4,2,512,512]{3,2,1,0:T(8,128)(2,1)}), bf16[4,2,512,512]{3,2,1,0:T(8,128)(2,1)}, u32[]{:S(2)}, u32[]{:S(2)}) async-start(bf16[4,2,512,512]{3,2,1,0:T(8,128)(2,1)} %slice_weights.9), calls=%async_computation.5 | async-start | bytes 8388608 | tf_op jit(solution)/shard_map/all_to_all | solution.py:648
  640.5 97.7 %all-to-all-start.6 = ((bf16[4,2,512,512]{3,2,1,0:T(8,128)(2,1)}), bf16[4,2,512,512]{3,2,1,0:T(8,128)(2,1)}, u32[]{:S(2)}, u32[]{:S(2)}) async-start(bf16[4,2,512,512]{3,2,1,0:T(8,128)(2,1)} %get-tuple-element.156), calls=%async_computation.6 | async-start | bytes 8388608 | tf_op jit(solution)/shard_map/all_to_all | solution.py:752
  738.1 153.4 %all-to-all-start.7 = ((bf16[4,3,512,512]{3,2,1,0:T(8,128)(2,1)}), bf16[4,3,512,512]{3,2,1,0:T(8,128)(2,1)}, u32[]{:S(2)}, u32[]{:S(2)}) async-start(bf16[4,3,512,512]{3,2,1,0:T(8,128)(2,1)} %get-tuple-element.158), calls=%async_computation.7 | async-start | bytes 12582912 | tf_op jit(solution)/shard_map/all_to_all | solution.py:752
  755.5 41.6 %collective-permute-start.38 = (bf16[512,2176]{1,0:T(8,128)(2,1)}, bf16[512,2176]{1,0:T(8,128)(2,1)S(1)}, u32[]{:S(2)}, u32[]{:S(2)}) collective-permute-start(bf16[512,2176]{1,0:T(8,128)(2,1)} %get-tuple-element.148), channel_id=1, source_target_pairs={{0,4},{4,0},{8,12},{12,8},{16,20},{20,16},{24,28},{28,24},{1,5},{5... | collective-permute-start | bytes 6684680 | tf_op jit(solution)/shard_map/ppermute | solution.py:511
  775.6 52.4 %collective-permute-start.41 = (bf16[512,2176]{1,0:T(8,128)(2,1)}, bf16[512,2176]{1,0:T(8,128)(2,1)S(1)}, u32[]{:S(2)}, u32[]{:S(2)}) collective-permute-start(bf16[512,2176]{1,0:T(8,128)(2,1)} %add_convert_fusion.1), channel_id=1, source_target_pairs={{0,24},{4,28},{8,16},{12,20},{16,8},{20,12},{24,0},{28,4},{1,25},{... | collective-permute-start | bytes 6684680 | tf_op jit(solution)/shard_map/ppermute | solution.py:511
  779.0 95.9 %collective-permute-start.40 = (bf16[512,2176]{1,0:T(8,128)(2,1)}, bf16[512,2176]{1,0:T(8,128)(2,1)S(1)}, u32[]{:S(2)}, u32[]{:S(2)}) collective-permute-start(bf16[512,2176]{1,0:T(8,128)(2,1)} %add_convert_fusion.2), channel_id=1, source_target_pairs={{0,16},{4,20},{8,24},{12,28},{16,0},{20,4},{24,8},{28,12},{1,17},{... | collective-permute-start | bytes 6684680 | tf_op jit(solution)/shard_map/ppermute | solution.py:511
  784.1 103.1 %collective-permute-start.39 = (bf16[512,2176]{1,0:T(8,128)(2,1)}, bf16[512,2176]{1,0:T(8,128)(2,1)}, u32[]{:S(2)}, u32[]{:S(2)}) collective-permute-start(bf16[512,2176]{1,0:T(8,128)(2,1)} %add_convert_fusion.3), channel_id=1, source_target_pairs={{0,8},{4,12},{8,0},{12,4},{16,24},{20,28},{24,16},{28,20},{1,9},{5... | collective-permute-start | bytes 6684680 | tf_op jit(solution)/shard_map/ppermute | solution.py:511
  797.1 94.4 %collective-permute-start.36 = (bf16[512,2048]{1,0:T(8,128)(2,1)}, bf16[512,2048]{1,0:T(8,128)(2,1)}, u32[]{:S(2)}, u32[]{:S(2)}) collective-permute-start(bf16[512,2048]{1,0:T(8,128)(2,1)} %get-tuple-element.144), channel_id=1, source_target_pairs={{0,4},{4,0},{8,12},{12,8},{16,20},{20,16},{24,28},{28,24},{1,5},{5... | collective-permute-start | bytes 6291464 | tf_op jit(solution)/shard_map/ppermute | solution.py:511
  797.1 94.4 %collective-permute-start.37 = (bf16[512,2048]{1,0:T(8,128)(2,1)}, bf16[512,2048]{1,0:T(8,128)(2,1)}, u32[]{:S(2)}, u32[]{:S(2)}) collective-permute-start(bf16[512,2048]{1,0:T(8,128)(2,1)} %get-tuple-element.146), channel_id=1, source_target_pairs={{0,4},{4,0},{8,12},{12,8},{16,20},{20,16},{24,28},{28,24},{1,5},{5... | collective-permute-start | bytes 6291464 | tf_op jit(solution)/shard_map/ppermute | solution.py:511
  828.0 63.5 %collective-permute-start.43 = (bf16[512,2048]{1,0:T(8,128)(2,1)}, bf16[512,2048]{1,0:T(8,128)(2,1)}, u32[]{:S(2)}, u32[]{:S(2)}) collective-permute-start(bf16[512,2048]{1,0:T(8,128)(2,1)} %get-tuple-element.151), channel_id=1, source_target_pairs={{0,4},{4,0},{8,12},{12,8},{16,20},{20,16},{24,28},{28,24},{1,5},{5... | collective-permute-start | bytes 6291464 | tf_op jit(solution)/shard_map/ppermute | solution.py:511
  901.5 53.7 %collective-permute-start.44 = (bf16[512,2048]{1,0:T(8,128)(2,1)}, bf16[512,2048]{1,0:T(8,128)(2,1)}, u32[]{:S(2)}, u32[]{:S(2)}) collective-permute-start(bf16[512,2048]{1,0:T(8,128)(2,1)} %add_convert_fusion.6), channel_id=1, source_target_pairs={{0,16},{4,20},{8,24},{12,28},{16,0},{20,4},{24,8},{28,12},{1,17},{... | collective-permute-start | bytes 6291464 | tf_op jit(solution)/shard_map/ppermute | solution.py:511
  903.0 52.2 %collective-permute-start.42 = (bf16[512,2048]{1,0:T(8,128)(2,1)}, bf16[512,2048]{1,0:T(8,128)(2,1)}, u32[]{:S(2)}, u32[]{:S(2)}) collective-permute-start(bf16[512,2048]{1,0:T(8,128)(2,1)} %add_convert_fusion.7), channel_id=1, source_target_pairs={{0,8},{4,12},{8,0},{12,4},{16,24},{20,28},{24,16},{28,20},{1,9},{5... | collective-permute-start | bytes 6291464 | tf_op jit(solution)/shard_map/ppermute | solution.py:511
  931.1 165.7 %all-to-all-start.8 = ((bf16[4,3,512,512]{3,2,1,0:T(8,128)(2,1)}), bf16[4,3,512,512]{3,2,1,0:T(8,128)(2,1)}, u32[]{:S(2)}, u32[]{:S(2)}) async-start(bf16[4,3,512,512]{3,2,1,0:T(8,128)(2,1)} %get-tuple-element.173), calls=%async_computation.8 | async-start | bytes 12582912 | tf_op jit(solution)/shard_map/all_to_all | solution.py:752
  1018.8 50.7 %collective-permute-start.57 = (bf16[2,8,64,512]{3,2,1,0:T(8,128)(2,1)}, bf16[2,8,64,512]{3,2,1,0:T(8,128)(2,1)S(1)}, u32[]{:S(2)}, u32[]{:S(2)}) collective-permute-start(bf16[2,8,64,512]{3,2,1,0:T(8,128)(2,1)} %get-tuple-element.174), channel_id=1, source_target_pairs={{0,1},{1,0},{2,3},{3,2},{4,5},{5,4},{6,7},{7,6},{8,9},{9,8},{10,11... | collective-permute-start | bytes 3145736 | tf_op jit(solution)/shard_map/ppermute | solution.py:511
  1033.1 89.8 %collective-permute-start.56 = (bf16[512,2048]{1,0:T(8,128)(2,1)}, bf16[512,2048]{1,0:T(8,128)(2,1)}, u32[]{:S(2)}, u32[]{:S(2)}) collective-permute-start(bf16[512,2048]{1,0:T(8,128)(2,1)} %add_convert_fusion.5), channel_id=1, source_target_pairs={{0,24},{4,28},{8,16},{12,20},{16,8},{20,12},{24,0},{28,4},{1,25},{... | collective-permute-start | bytes 6291464 | tf_op jit(solution)/shard_map/ppermute | solution.py:511
  1072.9 45.4 %collective-permute-start.66 = (bf16[1,8,64,512]{3,2,1,0:T(8,128)(2,1)}, bf16[1,8,64,512]{3,2,1,0:T(8,128)(2,1)}, u32[]{:S(2)}, u32[]{:S(2)}) collective-permute-start(bf16[1,8,64,512]{3,2,1,0:T(8,128)(2,1)} %slice.631), channel_id=1, source_target_pairs={{0,2},{1,3},{2,0},{3,1},{4,6},{5,7},{6,4},{7,5},{8,10},{9,11},{10,... | collective-permute-start | bytes 1572872 | tf_op jit(solution)/shard_map/ppermute | solution.py:511
  1149.1 33.3 %collective-permute-start.59 = (bf16[2,128,2048]{2,1,0:T(8,128)(2,1)S(1)}, bf16[2,128,2048]{2,1,0:T(8,128)(2,1)S(1)}, u32[]{:S(2)}, u32[]{:S(2)}) collective-permute-start(bf16[2,128,2048]{2,1,0:T(8,128)(2,1)S(1)} %bitcast.308), channel_id=1, source_target_pairs={{0,1},{1,0},{2,3},{3,2},{4,5},{5,4},{6,7},{7,6},{8,9},{9,8},{10,11... | collective-permute-start | bytes 3145736 | tf_op jit(solution)/shard_map/ppermute | solution.py:511
  (131 other events, 2461.9 us)

commit v6 on v5

--- a/solution.py
+++ b/solution.py
@@ -648,18 +648,19 @@
             expert_weights.append(lax.all_to_all(part, "narrow", 0, 0, tiled=True))
 
         ups_z = gather_narrow(cotangent, bundle_z)
+        output_rows = gather_narrow(w_output[None])
         send_weights(columns, bundles, ups_z)
+        output_rows = jnp.take(output_rows, narrow_order, axis=0).reshape(features, D)
         ups_own = gather_planes(tie(ups_z, *tokens_near[0], *tokens_near[1]))
-        columns, w_output = lax.optimization_barrier(
-            (columns, w_output, expert_weights[0], *tokens_near[0], *tokens_near[1], *ups_own[:3])
-        )[:2]
+        columns = lax.optimization_barrier(
+            (columns, expert_weights[0], *tokens_near[0], *tokens_near[1], *ups_own[:3])
+        )[0]
         columns = gather_narrow(columns[None])
+        gathered = columns
         columns = jnp.take(columns, narrow_order, axis=0)
         qkv = columns.transpose(1, 0, 2, 3).reshape(D, 3 * features)
-        output_rows = gather_narrow(w_output[None])
-        output_rows = jnp.take(output_rows, narrow_order, axis=0).reshape(features, D)
         while len(expert_weights) < early:
-            send_weights(qkv, output_rows, *expert_weights[1:])
+            send_weights(gathered, *expert_weights[1:])
 
         local_slots = lax.dynamic_slice_in_dim(all_slots, w * local, local, axis=2)
         local_slots = jnp.take(jnp.take(local_slots, wide_order, axis=0), near_order, axis=1)
@@ -702,7 +703,7 @@
         head_gains = jnp.stack([query_gain, key_gain])
         turned, attended = attend(raw, scales, cosine, sine, head_gains, count)
         if early > 2:
-            attended = tie(attended, expert_weights[1])
+            attended = tie(attended, expert_weights[1], sliced[2])
         branch = matmul(attended, output_rows, ((1,), (0,))).astype(BF)
         branch = branch.reshape(planes, 2, count, D)
         branch = scatter_wide(branch[:, 0], branch[:, 1])

time: 1220 us -> 1210 us (level)
  waiting for transfers between devices: 572 us -> 556 us
    ppermute x67, waiting for transfers between devices: 476 us -> 460 us  [swap(): return lax.ppermute(x, axis, [(i, i ^ r) for i in range(size)])]
  transfers between devices with their start and end apart: 77 -> 77, of which waited for: 32 -> 31; matrix products, arithmetic and copies ran while one was open for 16% -> 16% of each run, Pallas kernels for 21% -> 21%
where the time goes in v6:
time: 1210 us; the launch traced here: 1200 us
  waiting for transfers between devices  556 us (46%)
  Pallas kernels  256 us (21%)
  starting transfers between devices  113 us (9%)
  other arithmetic  87.9 us (7%)
  local copies, waits for them, and re-layouts  87.8 us (7%)
  blocking collectives  57.9 us (5%)
  matrix products  37.6 us (3%)
    ppermute x67, waiting for transfers between devices, swap(): return lax.ppermute(x, axis, [(i, i ^ r) for i in range(size)])  460 us
    pallas_call x6, Pallas kernels, expert_chunk(): pl.pallas_call(functools.partial(expert_body, parts, tiles, start, len(al...  111 us
    all_to_all x5, waiting for transfers between devices, send_weights(): expert_weights.append(lax.all_to_all(part, 'narrow', 0, 0, tiled=True))  74.6 us
    ppermute x67, starting transfers between devices, swap(): return lax.ppermute(x, axis, [(i, i ^ r) for i in range(size)])  54.3 us
    unnamed x199, local copies, waits for them, and re-layouts  41.4 us
    pallas_call x4, Pallas kernels, combine(): pl.pallas_call(functools.partial(combine_body, pieces, each), grid=(pairs...  38.3 us
    dot_general x11, matrix products, matmul(): return lax.dot_general(a, b, (dims, ((), ())), preferred_element_type=F32)  37.6 us
    pallas_call x4, Pallas kernels, dispatch(): pl.pallas_call(functools.partial(dispatch_body, pieces, each), grid=(pair...  36.4 us
  transfers between devices with their start and end apart: 77, of which 31 were waited for; matrix products, arithmetic and copies ran while one was open for 16% of the time, Pallas kernels for 21%

profile of v6, /device:TPU:0, one launch (start us, length us, event | category | flops | bytes accessed | tf_op | source)
XLA Modules:
  0.0 1198.1 jit_solution(1667238960159837363)
XLA Ops:
  9.9 26.5 %all-gather = bf16[448,128]{1,0:T(8,128)(2,1)S(1)} all-gather(bf16[112,128]{1,0:T(8,128)(2,1)S(1)} %pad_maximum_fusion.11), channel_id=2, replica_groups=mesh['wide'=8,'narrow'=4] {'narrow'}, dimensions={0}, use_global_device_ids=true | all-gather | bytes 143360 | tf_op jit(solution)/shard_map/all_gather | solution.py:613
  47.1 15.0 %all-gather.1 = bf16[32,112,128]{2,1,0:T(8,128)(2,1)S(1)} all-gather(bf16[4,112,128]{2,1,0:T(8,128)(2,1)S(1)} %bitcast.316), channel_id=3, replica_groups=mesh['wide'=8,'narrow'=4] {'wide'}, dimensions={0}, use_global_device_ids=true | all-gather | bytes 1032192 | tf_op jit(solution)/shard_map/all_gather | solution.py:618
  74.1 11.4 collective-permute-done.1
  85.5 10.8 collective-permute-done.3
  109.0 38.9 %collective-permute-done.10.refs_3_ = bf16[512,2048]{1,0:T(8,128)(2,1)} collective-permute-done((bf16[512,2048]{1,0:T(8,128)(2,1)}, bf16[512,2048]{1,0:T(8,128)(2,1)}, u32[]{:S(2)}, u32[]{:S(2)}) %collective-permute-start.10) | collective-permute-done | bytes 2097184 | tf_op jit(solution)/shard_map/ppermute | solution.py:511
  149.4 21.3 %all-to-all-done.1.refs_3_ = bf16[4,2,512,512]{3,2,1,0:T(8,128)(2,1)} async-done(((bf16[4,2,512,512]{3,2,1,0:T(8,128)(2,1)}), bf16[4,2,512,512]{3,2,1,0:T(8,128)(2,1)}, u32[]{:S(2)}, u32[]{:S(2)}) %all-to-all-start.1) | async-done | bytes 4194336 | tf_op jit(solution)/shard_map/all_to_all | solution.py:648
  179.0 14.0 %collective-permute-done.14 = bf16[1,64,2048]{2,1,0:T(8,128)(2,1)S(1)} collective-permute-done((bf16[1,64,2048]{2,1,0:T(8,128)(2,1)S(1)}, bf16[1,64,2048]{2,1,0:T(8,128)(2,1)S(1)}, u32[]{:S(2)}, u32[]{:S(2)}) %collective-permute-start.14) | collective-permute-done | bytes 262176 | tf_op jit(solution)/shard_map/ppermute | solution.py:511
  193.2 16.3 %collective-permute-done.11 = bf16[1,8,64,768]{3,2,1,0:T(8,128)(2,1)S(1)} collective-permute-done((bf16[1,8,64,768]{3,2,1,0:T(8,128)(2,1)S(1)}, bf16[1,8,64,768]{3,2,1,0:T(8,128)(2,1)S(1)}, u32[]{:S(2)}, u32[]{:S(2)}) %collective-permute-start.11) | collective-permute-done | bytes 786464 | tf_op jit(solution)/shard_map/ppermute | solution.py:511
  228.7 25.7 %collective-permute-done.12 = bf16[2,8,64,768]{3,2,1,0:T(8,128)(2,1)} collective-permute-done((bf16[2,8,64,768]{3,2,1,0:T(8,128)(2,1)}, bf16[2,8,64,768]{3,2,1,0:T(8,128)(2,1)}, u32[]{:S(2)}, u32[]{:S(2)}) %collective-permute-start.12) | collective-permute-done | bytes 1572896 | tf_op jit(solution)/shard_map/ppermute | solution.py:511
  373.9 25.8 %collective-permute-done.24 = bf16[128,2176]{1,0:T(8,128)(2,1)S(1)} collective-permute-done((bf16[128,2176]{1,0:T(8,128)(2,1)S(1)}, bf16[128,2176]{1,0:T(8,128)(2,1)S(1)}, u32[]{:S(2)}, u32[]{:S(2)}) %collective-permute-start.24) | collective-permute-done | bytes 557088 | tf_op jit(solution)/shard_map/ppermute | solution.py:511
  403.7 22.6 %collective-permute-done.25 = bf16[256,2176]{1,0:T(8,128)(2,1)S(1)} collective-permute-done((bf16[256,2176]{1,0:T(8,128)(2,1)S(1)}, bf16[256,2176]{1,0:T(8,128)(2,1)S(1)}, u32[]{:S(2)}, u32[]{:S(2)}) %collective-permute-start.25) | collective-permute-done | bytes 1114144 | tf_op jit(solution)/shard_map/ppermute | solution.py:511
  438.6 44.1 %collective-permute-done.27.refs_2_ = bf16[512,2176]{1,0:T(8,128)(2,1)S(1)} collective-permute-done((bf16[512,2176]{1,0:T(8,128)(2,1)S(1)}, bf16[512,2176]{1,0:T(8,128)(2,1)S(1)}, u32[]{:S(2)}, u32[]{:S(2)}) %collective-permute-start.27) | collective-permute-done | bytes 2228256 | tf_op jit(solution)/shard_map/ppermute | solution.py:511
  482.8 46.0 %collective-permute-done.29.refs_3_ = bf16[512,2176]{1,0:T(8,128)(2,1)S(1)} collective-permute-done((bf16[512,2176]{1,0:T(8,128)(2,1)S(1)}, bf16[512,2176]{1,0:T(8,128)(2,1)S(1)}, u32[]{:S(2)}, u32[]{:S(2)}) %collective-permute-start.29) | collective-permute-done | bytes 2228256 | tf_op jit(solution)/shard_map/ppermute | solution.py:511
  560.1 24.4 %experts.6 = (bf16[8,768,2048]{2,1,0:T(8,128)(2,1)}, bf16[8,768,2176]{2,1,0:T(8,128)(2,1)}, bf16[4,2,512,512]{3,2,1,0:T(8,128)(2,1)}, f32[8,256,2048]{2,1,0:T(8,128)}) custom-call(s32[3]{0:T(128)} %pad_add_fusion.refs_0_, bf16[8,768,2176]{2,1,0:T(8,128)(2,1)} %dispatch.7.refs_1_, bf16[8,768,2048]{2,1,0:T(8,128)(2,1)} %dispatch.5.refs_2_, ...), custom_call_target="tpu_custom_call" | custom-call | flops 14495514624 | bytes 44040192 | tf_op jit(solution)/shard_map/experts/pallas_call | solution.py:209
  584.4 41.1 %all-to-all-done.5.refs_3_ = bf16[4,2,512,512]{3,2,1,0:T(8,128)(2,1)} async-done(((bf16[4,2,512,512]{3,2,1,0:T(8,128)(2,1)}), bf16[4,2,512,512]{3,2,1,0:T(8,128)(2,1)}, u32[]{:S(2)}, u32[]{:S(2)}) %all-to-all-start.5) | async-done | bytes 4194336 | tf_op jit(solution)/shard_map/all_to_all | solution.py:648
  634.9 15.3 %experts.7 = (bf16[8,768,2048]{2,1,0:T(8,128)(2,1)}, bf16[8,768,2176]{2,1,0:T(8,128)(2,1)}, bf16[4,3,512,512]{3,2,1,0:T(8,128)(2,1)}, f32[8,256,2048]{2,1,0:T(8,128)}) custom-call(s32[3]{0:T(128)} %pad_add_fusion.refs_0_, bf16[8,768,2176]{2,1,0:T(8,128)(2,1)} %dispatch.7.refs_1_, ...), custom_call_target="tpu_custom_call", output_to_operand_aliasing={{0}: (5, {}), {1}: (6, {}), {3}: (7, {})} | custom-call | flops 7247757312 | bytes 22020096 | tf_op jit(solution)/shard_map/experts/pallas_call | solution.py:209
  650.3 15.5 %experts.8 = (bf16[8,768,2048]{2,1,0:T(8,128)(2,1)}, bf16[8,768,2176]{2,1,0:T(8,128)(2,1)}, bf16[4,3,512,512]{3,2,1,0:T(8,128)(2,1)}, f32[8,256,2048]{2,1,0:T(8,128)}) custom-call(s32[3]{0:T(128)} %pad_add_fusion.refs_0_, bf16[8,768,2176]{2,1,0:T(8,128)(2,1)} %dispatch.7.refs_1_, ...), custom_call_target="tpu_custom_call", output_to_operand_aliasing={{0}: (5, {}), {1}: (6, {}), {2}: (7, {}), {3}: (8, {})} | custom-call | flops 7247757312 | bytes 22020096 | tf_op jit(solution)/shard_map/experts/pallas_call | solution.py:209
  665.8 15.3 %experts.9 = (bf16[8,768,2048]{2,1,0:T(8,128)(2,1)}, bf16[8,768,2176]{2,1,0:T(8,128)(2,1)}, bf16[4,3,512,512]{3,2,1,0:T(8,128)(2,1)}, f32[8,256,2048]{2,1,0:T(8,128)}) custom-call(s32[3]{0:T(128)} %pad_add_fusion.refs_0_, bf16[8,768,2176]{2,1,0:T(8,128)(2,1)} %dispatch.7.refs_1_, ...), custom_call_target="tpu_custom_call", output_to_operand_aliasing={{0}: (5, {}), {1}: (6, {}), {2}: (7, {}), {3}: (8, {})} | custom-call | flops 7247757312 | bytes 22020096 | tf_op jit(solution)/shard_map/experts/pallas_call | solution.py:209
  681.1 15.7 %experts.10 = (bf16[8,768,2048]{2,1,0:T(8,128)(2,1)}, bf16[8,768,2176]{2,1,0:T(8,128)(2,1)}, bf16[4,3,512,512]{3,2,1,0:T(8,128)(2,1)}, f32[8,256,2048]{2,1,0:T(8,128)}) custom-call(s32[3]{0:T(128)} %pad_add_fusion.refs_0_, bf16[8,768,2176]{2,1,0:T(8,128)(2,1)} %dispatch.7.refs_1_, ...), custom_call_target="tpu_custom_call", output_to_operand_aliasing={{0}: (5, {}), {1}: (6, {}), {3}: (7, {})} | custom-call | flops 7247757312 | bytes 22020096 | tf_op jit(solution)/shard_map/experts/pallas_call | solution.py:209
  696.9 24.4 %experts.11 = (bf16[8,768,2048]{2,1,0:T(8,128)(2,1)}, bf16[8,768,2176]{2,1,0:T(8,128)(2,1)}, bf16[4,3,512,512]{3,2,1,0:T(8,128)(2,1)}, f32[8,256,2048]{2,1,0:T(8,128)}) custom-call(s32[3]{0:T(128)} %pad_add_fusion.refs_0_, bf16[8,768,2176]{2,1,0:T(8,128)(2,1)} %dispatch.7.refs_1_, ...), custom_call_target="tpu_custom_call", output_to_operand_aliasing={{0}: (5, {}), {1}: (6, {}), {2}: (7, {}), {3}: (8, {})} | custom-call | flops 14495514624 | bytes 44040192 | tf_op jit(solution)/shard_map/experts/pallas_call | solution.py:209
  746.7 10.3 combine.4
  782.7 30.4 %collective-permute-done.41 = bf16[512,2176]{1,0:T(8,128)(2,1)S(1)} collective-permute-done((bf16[512,2176]{1,0:T(8,128)(2,1)}, bf16[512,2176]{1,0:T(8,128)(2,1)S(1)}, u32[]{:S(2)}, u32[]{:S(2)}) %collective-permute-start.41) | collective-permute-done | bytes 2228256 | tf_op jit(solution)/shard_map/ppermute | solution.py:511
  813.1 46.8 %collective-permute-done.40 = bf16[512,2176]{1,0:T(8,128)(2,1)S(1)} collective-permute-done((bf16[512,2176]{1,0:T(8,128)(2,1)}, bf16[512,2176]{1,0:T(8,128)(2,1)S(1)}, u32[]{:S(2)}, u32[]{:S(2)}) %collective-permute-start.40) | collective-permute-done | bytes 2228256 | tf_op jit(solution)/shard_map/ppermute | solution.py:511
  862.4 9.9 combine.6
  888.6 15.5 %collective-permute-done.46 = bf16[2,128,2176]{2,1,0:T(8,128)(2,1)S(1)} collective-permute-done((bf16[2,128,2176]{2,1,0:T(8,128)(2,1)S(1)}, bf16[2,128,2176]{2,1,0:T(8,128)(2,1)S(1)}, u32[]{:S(2)}, u32[]{:S(2)}) %collective-permute-start.46) | collective-permute-done | bytes 1114144 | tf_op jit(solution)/shard_map/ppermute | solution.py:511
  916.2 15.4 %all-to-all-start.8 = ((bf16[4,3,512,512]{3,2,1,0:T(8,128)(2,1)}), bf16[4,3,512,512]{3,2,1,0:T(8,128)(2,1)}, u32[]{:S(2)}, u32[]{:S(2)}) async-start(bf16[4,3,512,512]{3,2,1,0:T(8,128)(2,1)} %get-tuple-element.171), calls=%async_computation.8 | async-start | bytes 12582912 | tf_op jit(solution)/shard_map/all_to_all | solution.py:753
  958.6 12.6 %collective-permute-done.52 = bf16[128,2176]{1,0:T(8,128)(2,1)S(1)} collective-permute-done((bf16[128,2176]{1,0:T(8,128)(2,1)S(1)}, bf16[128,2176]{1,0:T(8,128)(2,1)S(1)}, u32[]{:S(2)}, u32[]{:S(2)}) %collective-permute-start.52) | collective-permute-done | bytes 557088 | tf_op jit(solution)/shard_map/ppermute | solution.py:511
  976.3 13.4 %attend_back.1 = (f32[1024,512]{1,0:T(8,128)}, bf16[1024,256]{1,0:T(8,128)(2,1)}, f32[1024,2]{1,0:T(8,128)}, f32[2,256]{1,0:T(2,128)}) custom-call(bf16[1024,768]{1,0:T(8,128)(2,1)} %get-tuple-element.153.turned, bf16[1024,256]{1,0:T(8,128)(2,1)} %fusion.15.grads, f32[1024,768]{1,0:T(8,128)} %copy.270.raw, f32[1024,2]{1,0:T(8,128)} %bitcast.278, ...), custom_call_target="tpu_custom_call" | custom-call | flops 402653184 | bytes 7864320 | tf_op jit(solution)/shard_map/attend_back/pallas_call | solution.py:403
  1023.4 31.2 %collective-permute-done.57 = bf16[2,8,64,512]{3,2,1,0:T(8,128)(2,1)S(1)} collective-permute-done((bf16[2,8,64,512]{3,2,1,0:T(8,128)(2,1)}, bf16[2,8,64,512]{3,2,1,0:T(8,128)(2,1)S(1)}, u32[]{:S(2)}, u32[]{:S(2)}) %collective-permute-start.57) | collective-permute-done | bytes 1048608 | tf_op jit(solution)/shard_map/ppermute | solution.py:511
  1063.2 18.7 %all-to-all-done.8.refs_0_ = bf16[4,3,512,512]{3,2,1,0:T(8,128)(2,1)} async-done(((bf16[4,3,512,512]{3,2,1,0:T(8,128)(2,1)}), bf16[4,3,512,512]{3,2,1,0:T(8,128)(2,1)}, u32[]{:S(2)}, u32[]{:S(2)}) %all-to-all-start.8) | async-done | bytes 6291488 | tf_op jit(solution)/shard_map/all_to_all | solution.py:753
  1107.9 20.1 %collective-permute-done.58 = bf16[2,9,64,512]{3,2,1,0:T(8,128)(2,1)} collective-permute-done((bf16[2,9,64,512]{3,2,1,0:T(8,128)(2,1)}, bf16[2,9,64,512]{3,2,1,0:T(8,128)(2,1)}, u32[]{:S(2)}, u32[]{:S(2)}) %collective-permute-start.58) | collective-permute-done | bytes 1179680 | tf_op jit(solution)/shard_map/ppermute | solution.py:511
  1144.6 22.9 %collective-permute-done.59 = bf16[2,128,2048]{2,1,0:T(8,128)(2,1)S(1)} collective-permute-done((bf16[2,128,2048]{2,1,0:T(8,128)(2,1)S(1)}, bf16[2,128,2048]{2,1,0:T(8,128)(2,1)S(1)}, u32[]{:S(2)}, u32[]{:S(2)}) %collective-permute-start.59) | collective-permute-done | bytes 1048608 | tf_op jit(solution)/shard_map/ppermute | solution.py:511
  (544 shorter events, 478.2 us)
Async XLA Ops:
  0.7 35.7 %collective-permute-start.7 = (bf16[128,2048]{1,0:T(8,128)(2,1)}, bf16[128,2048]{1,0:T(8,128)(2,1)S(1)}, u32[]{:S(2)}, u32[]{:S(2)}) collective-permute-start(bf16[128,2048]{1,0:T(8,128)(2,1)} %param.23), channel_id=1, source_target_pairs={{0,2},{1,3},{2,0},{3,1},{4,6},{5,7},{6,4},{7,5},{8,10},{9,11},{10,... | collective-permute-start | bytes 1572872 | tf_op jit(solution)/shard_map/ppermute | solution.py:511
  65.5 105.2 %all-to-all-start.1 = ((bf16[4,2,512,512]{3,2,1,0:T(8,128)(2,1)}), bf16[4,2,512,512]{3,2,1,0:T(8,128)(2,1)}, u32[]{:S(2)}, u32[]{:S(2)}) async-start(bf16[4,2,512,512]{3,2,1,0:T(8,128)(2,1)} %slice_weights.5), calls=%async_computation.1 | async-start | bytes 8388608 | tf_op jit(solution)/shard_map/all_to_all | solution.py:648
  96.7 96.3 %collective-permute-start.14 = (bf16[1,64,2048]{2,1,0:T(8,128)(2,1)S(1)}, bf16[1,64,2048]{2,1,0:T(8,128)(2,1)S(1)}, u32[]{:S(2)}, u32[]{:S(2)}) collective-permute-start(bf16[1,64,2048]{2,1,0:T(8,128)(2,1)S(1)} %bitcast.309), channel_id=1, source_target_pairs={{0,2},{1,3},{2,0},{3,1},{4,6},{5,7},{6,4},{7,5},{8,10},{9,11},{10,... | collective-permute-start | bytes 786440 | tf_op jit(solution)/shard_map/ppermute | solution.py:511
  100.3 47.7 %collective-permute-start.10 = (bf16[512,2048]{1,0:T(8,128)(2,1)}, bf16[512,2048]{1,0:T(8,128)(2,1)}, u32[]{:S(2)}, u32[]{:S(2)}) collective-permute-start(bf16[512,2048]{1,0:T(8,128)(2,1)} %constant_dynamic-update-slice_fusion.8.refs_1_), channel_id=1, source_target_pairs={{0,16},{4,20},{8,24},{12,28},{16,0},{20,4},{24,8},{28,12},{1,17},{... | collective-permute-start | bytes 6291464 | tf_op jit(solution)/shard_map/ppermute | solution.py:511
  102.0 47.4 %collective-permute-start.9 = (bf16[512,2048]{1,0:T(8,128)(2,1)}, bf16[512,2048]{1,0:T(8,128)(2,1)}, u32[]{:S(2)}, u32[]{:S(2)}) collective-permute-start(bf16[512,2048]{1,0:T(8,128)(2,1)} %constant_dynamic-update-slice_fusion.8.refs_1_), channel_id=1, source_target_pairs={{0,8},{4,12},{8,0},{12,4},{16,24},{20,28},{24,16},{28,20},{1,9},{5... | collective-permute-start | bytes 6291464 | tf_op jit(solution)/shard_map/ppermute | solution.py:511
  170.7 38.8 %collective-permute-start.11 = (bf16[1,8,64,768]{3,2,1,0:T(8,128)(2,1)S(1)}, bf16[1,8,64,768]{3,2,1,0:T(8,128)(2,1)S(1)}, u32[]{:S(2)}, u32[]{:S(2)}) collective-permute-start(bf16[1,8,64,768]{3,2,1,0:T(8,128)(2,1)S(1)} %bitcast.284), channel_id=1, source_target_pairs={{0,2},{1,3},{2,0},{3,1},{4,6},{5,7},{6,4},{7,5},{8,10},{9,11},{10,... | collective-permute-start | bytes 2359304 | tf_op jit(solution)/shard_map/ppermute | solution.py:511
  210.9 43.5 %collective-permute-start.12 = (bf16[2,8,64,768]{3,2,1,0:T(8,128)(2,1)}, bf16[2,8,64,768]{3,2,1,0:T(8,128)(2,1)}, u32[]{:S(2)}, u32[]{:S(2)}) collective-permute-start(bf16[2,8,64,768]{3,2,1,0:T(8,128)(2,1)} %pad_maximum_fusion.1), channel_id=1, source_target_pairs={{0,1},{1,0},{2,3},{3,2},{4,5},{5,4},{6,7},{7,6},{8,9},{9,8},{10,11... | collective-permute-start | bytes 4718600 | tf_op jit(solution)/shard_map/ppermute | solution.py:511
  225.4 49.9 %collective-permute-start.13 = (bf16[512,2048]{1,0:T(8,128)(2,1)}, bf16[512,2048]{1,0:T(8,128)(2,1)}, u32[]{:S(2)}, u32[]{:S(2)}) collective-permute-start(bf16[512,2048]{1,0:T(8,128)(2,1)} %constant_dynamic-update-slice_fusion.8.refs_1_), channel_id=1, source_target_pairs={{0,24},{4,28},{8,16},{12,20},{16,8},{20,12},{24,0},{28,4},{1,25},{... | collective-permute-start | bytes 6291464 | tf_op jit(solution)/shard_map/ppermute | solution.py:511
  256.1 53.5 %all-to-all-start.2 = ((bf16[4,1,512,512]{3,2,1,0:T(8,128)(2,1)}), bf16[4,1,512,512]{3,2,1,0:T(8,128)(2,1)}, u32[]{:S(2)}, u32[]{:S(2)}) async-start(bf16[4,1,512,512]{3,2,1,0:T(8,128)(2,1)} %slice_weights.6), calls=%async_computation.2 | async-start | bytes 4194304 | tf_op jit(solution)/shard_map/all_to_all | solution.py:648
  319.7 54.1 %all-to-all-start.3 = ((bf16[4,1,512,512]{3,2,1,0:T(8,128)(2,1)}), bf16[4,1,512,512]{3,2,1,0:T(8,128)(2,1)}, u32[]{:S(2)}, u32[]{:S(2)}) async-start(bf16[4,1,512,512]{3,2,1,0:T(8,128)(2,1)} %slice_weights.7), calls=%async_computation.3 | async-start | bytes 4194304 | tf_op jit(solution)/shard_map/all_to_all | solution.py:648
  426.5 103.7 %all-to-all-start.4 = ((bf16[4,2,512,512]{3,2,1,0:T(8,128)(2,1)}), bf16[4,2,512,512]{3,2,1,0:T(8,128)(2,1)}, u32[]{:S(2)}, u32[]{:S(2)}) async-start(bf16[4,2,512,512]{3,2,1,0:T(8,128)(2,1)} %slice_weights.8), calls=%async_computation.4 | async-start | bytes 8388608 | tf_op jit(solution)/shard_map/all_to_all | solution.py:648
  431.3 51.4 %collective-permute-start.27 = (bf16[512,2176]{1,0:T(8,128)(2,1)S(1)}, bf16[512,2176]{1,0:T(8,128)(2,1)S(1)}, u32[]{:S(2)}, u32[]{:S(2)}) collective-permute-start(bf16[512,2176]{1,0:T(8,128)(2,1)S(1)} %constant_dynamic-update-slice_fusion.10.refs_1_), channel_id=1, source_target_pairs={{0,8},{4,12},{8,0},{12,4},{16,24},{20,28},{24,16},{28,20},{1,9},{5... | collective-permute-start | bytes 6684680 | tf_op jit(solution)/shard_map/ppermute | solution.py:511
  431.8 97.0 %collective-permute-start.29 = (bf16[512,2176]{1,0:T(8,128)(2,1)S(1)}, bf16[512,2176]{1,0:T(8,128)(2,1)S(1)}, u32[]{:S(2)}, u32[]{:S(2)}) collective-permute-start(bf16[512,2176]{1,0:T(8,128)(2,1)S(1)} %constant_dynamic-update-slice_fusion.10.refs_1_), channel_id=1, source_target_pairs={{0,16},{4,20},{8,24},{12,28},{16,0},{20,4},{24,8},{28,12},{1,17},{... | collective-permute-start | bytes 6684680 | tf_op jit(solution)/shard_map/ppermute | solution.py:511
  433.4 96.7 %collective-permute-start.31 = (bf16[512,2176]{1,0:T(8,128)(2,1)S(1)}, bf16[512,2176]{1,0:T(8,128)(2,1)}, u32[]{:S(2)}, u32[]{:S(2)}) collective-permute-start(bf16[512,2176]{1,0:T(8,128)(2,1)S(1)} %constant_dynamic-update-slice_fusion.10.refs_1_), channel_id=1, source_target_pairs={{0,24},{4,28},{8,16},{12,20},{16,8},{20,12},{24,0},{28,4},{1,25},{... | collective-permute-start | bytes 6684680 | tf_op jit(solution)/shard_map/ppermute | solution.py:511
  530.2 95.4 %all-to-all-start.5 = ((bf16[4,2,512,512]{3,2,1,0:T(8,128)(2,1)}), bf16[4,2,512,512]{3,2,1,0:T(8,128)(2,1)}, u32[]{:S(2)}, u32[]{:S(2)}) async-start(bf16[4,2,512,512]{3,2,1,0:T(8,128)(2,1)} %slice_weights.9), calls=%async_computation.5 | async-start | bytes 8388608 | tf_op jit(solution)/shard_map/all_to_all | solution.py:648
  625.5 97.7 %all-to-all-start.6 = ((bf16[4,2,512,512]{3,2,1,0:T(8,128)(2,1)}), bf16[4,2,512,512]{3,2,1,0:T(8,128)(2,1)}, u32[]{:S(2)}, u32[]{:S(2)}) async-start(bf16[4,2,512,512]{3,2,1,0:T(8,128)(2,1)} %get-tuple-element.154), calls=%async_computation.6 | async-start | bytes 8388608 | tf_op jit(solution)/shard_map/all_to_all | solution.py:753
  723.2 153.4 %all-to-all-start.7 = ((bf16[4,3,512,512]{3,2,1,0:T(8,128)(2,1)}), bf16[4,3,512,512]{3,2,1,0:T(8,128)(2,1)}, u32[]{:S(2)}, u32[]{:S(2)}) async-start(bf16[4,3,512,512]{3,2,1,0:T(8,128)(2,1)} %get-tuple-element.156), calls=%async_computation.7 | async-start | bytes 12582912 | tf_op jit(solution)/shard_map/all_to_all | solution.py:753
  740.6 41.6 %collective-permute-start.38 = (bf16[512,2176]{1,0:T(8,128)(2,1)}, bf16[512,2176]{1,0:T(8,128)(2,1)S(1)}, u32[]{:S(2)}, u32[]{:S(2)}) collective-permute-start(bf16[512,2176]{1,0:T(8,128)(2,1)} %get-tuple-element.146), channel_id=1, source_target_pairs={{0,4},{4,0},{8,12},{12,8},{16,20},{20,16},{24,28},{28,24},{1,5},{5... | collective-permute-start | bytes 6684680 | tf_op jit(solution)/shard_map/ppermute | solution.py:511
  760.7 52.4 %collective-permute-start.41 = (bf16[512,2176]{1,0:T(8,128)(2,1)}, bf16[512,2176]{1,0:T(8,128)(2,1)S(1)}, u32[]{:S(2)}, u32[]{:S(2)}) collective-permute-start(bf16[512,2176]{1,0:T(8,128)(2,1)} %add_convert_fusion.1), channel_id=1, source_target_pairs={{0,24},{4,28},{8,16},{12,20},{16,8},{20,12},{24,0},{28,4},{1,25},{... | collective-permute-start | bytes 6684680 | tf_op jit(solution)/shard_map/ppermute | solution.py:511
  764.1 95.9 %collective-permute-start.40 = (bf16[512,2176]{1,0:T(8,128)(2,1)}, bf16[512,2176]{1,0:T(8,128)(2,1)S(1)}, u32[]{:S(2)}, u32[]{:S(2)}) collective-permute-start(bf16[512,2176]{1,0:T(8,128)(2,1)} %add_convert_fusion.2), channel_id=1, source_target_pairs={{0,16},{4,20},{8,24},{12,28},{16,0},{20,4},{24,8},{28,12},{1,17},{... | collective-permute-start | bytes 6684680 | tf_op jit(solution)/shard_map/ppermute | solution.py:511
  769.2 103.0 %collective-permute-start.39 = (bf16[512,2176]{1,0:T(8,128)(2,1)}, bf16[512,2176]{1,0:T(8,128)(2,1)}, u32[]{:S(2)}, u32[]{:S(2)}) collective-permute-start(bf16[512,2176]{1,0:T(8,128)(2,1)} %add_convert_fusion.3), channel_id=1, source_target_pairs={{0,8},{4,12},{8,0},{12,4},{16,24},{20,28},{24,16},{28,20},{1,9},{5... | collective-permute-start | bytes 6684680 | tf_op jit(solution)/shard_map/ppermute | solution.py:511
  782.2 94.4 %collective-permute-start.36 = (bf16[512,2048]{1,0:T(8,128)(2,1)}, bf16[512,2048]{1,0:T(8,128)(2,1)}, u32[]{:S(2)}, u32[]{:S(2)}) collective-permute-start(bf16[512,2048]{1,0:T(8,128)(2,1)} %get-tuple-element.142), channel_id=1, source_target_pairs={{0,4},{4,0},{8,12},{12,8},{16,20},{20,16},{24,28},{28,24},{1,5},{5... | collective-permute-start | bytes 6291464 | tf_op jit(solution)/shard_map/ppermute | solution.py:511
  782.2 94.4 %collective-permute-start.37 = (bf16[512,2048]{1,0:T(8,128)(2,1)}, bf16[512,2048]{1,0:T(8,128)(2,1)}, u32[]{:S(2)}, u32[]{:S(2)}) collective-permute-start(bf16[512,2048]{1,0:T(8,128)(2,1)} %get-tuple-element.144), channel_id=1, source_target_pairs={{0,4},{4,0},{8,12},{12,8},{16,20},{20,16},{24,28},{28,24},{1,5},{5... | collective-permute-start | bytes 6291464 | tf_op jit(solution)/shard_map/ppermute | solution.py:511
  813.1 63.5 %collective-permute-start.43 = (bf16[512,2048]{1,0:T(8,128)(2,1)}, bf16[512,2048]{1,0:T(8,128)(2,1)}, u32[]{:S(2)}, u32[]{:S(2)}) collective-permute-start(bf16[512,2048]{1,0:T(8,128)(2,1)} %get-tuple-element.149), channel_id=1, source_target_pairs={{0,4},{4,0},{8,12},{12,8},{16,20},{20,16},{24,28},{28,24},{1,5},{5... | collective-permute-start | bytes 6291464 | tf_op jit(solution)/shard_map/ppermute | solution.py:511
  886.5 53.7 %collective-permute-start.44 = (bf16[512,2048]{1,0:T(8,128)(2,1)}, bf16[512,2048]{1,0:T(8,128)(2,1)}, u32[]{:S(2)}, u32[]{:S(2)}) collective-permute-start(bf16[512,2048]{1,0:T(8,128)(2,1)} %add_convert_fusion.6), channel_id=1, source_target_pairs={{0,16},{4,20},{8,24},{12,28},{16,0},{20,4},{24,8},{28,12},{1,17},{... | collective-permute-start | bytes 6291464 | tf_op jit(solution)/shard_map/ppermute | solution.py:511
  888.1 52.2 %collective-permute-start.42 = (bf16[512,2048]{1,0:T(8,128)(2,1)}, bf16[512,2048]{1,0:T(8,128)(2,1)}, u32[]{:S(2)}, u32[]{:S(2)}) collective-permute-start(bf16[512,2048]{1,0:T(8,128)(2,1)} %add_convert_fusion.7), channel_id=1, source_target_pairs={{0,8},{4,12},{8,0},{12,4},{16,24},{20,28},{24,16},{28,20},{1,9},{5... | collective-permute-start | bytes 6291464 | tf_op jit(solution)/shard_map/ppermute | solution.py:511
  916.2 165.7 %all-to-all-start.8 = ((bf16[4,3,512,512]{3,2,1,0:T(8,128)(2,1)}), bf16[4,3,512,512]{3,2,1,0:T(8,128)(2,1)}, u32[]{:S(2)}, u32[]{:S(2)}) async-start(bf16[4,3,512,512]{3,2,1,0:T(8,128)(2,1)} %get-tuple-element.171), calls=%async_computation.8 | async-start | bytes 12582912 | tf_op jit(solution)/shard_map/all_to_all | solution.py:753
  1003.9 50.7 %collective-permute-start.57 = (bf16[2,8,64,512]{3,2,1,0:T(8,128)(2,1)}, bf16[2,8,64,512]{3,2,1,0:T(8,128)(2,1)S(1)}, u32[]{:S(2)}, u32[]{:S(2)}) collective-permute-start(bf16[2,8,64,512]{3,2,1,0:T(8,128)(2,1)} %get-tuple-element.172), channel_id=1, source_target_pairs={{0,1},{1,0},{2,3},{3,2},{4,5},{5,4},{6,7},{7,6},{8,9},{9,8},{10,11... | collective-permute-start | bytes 3145736 | tf_op jit(solution)/shard_map/ppermute | solution.py:511
  1018.2 89.7 %collective-permute-start.56 = (bf16[512,2048]{1,0:T(8,128)(2,1)}, bf16[512,2048]{1,0:T(8,128)(2,1)}, u32[]{:S(2)}, u32[]{:S(2)}) collective-permute-start(bf16[512,2048]{1,0:T(8,128)(2,1)} %add_convert_fusion.5), channel_id=1, source_target_pairs={{0,24},{4,28},{8,16},{12,20},{16,8},{20,12},{24,0},{28,4},{1,25},{... | collective-permute-start | bytes 6291464 | tf_op jit(solution)/shard_map/ppermute | solution.py:511
  1058.0 45.4 %collective-permute-start.66 = (bf16[1,8,64,512]{3,2,1,0:T(8,128)(2,1)}, bf16[1,8,64,512]{3,2,1,0:T(8,128)(2,1)}, u32[]{:S(2)}, u32[]{:S(2)}) collective-permute-start(bf16[1,8,64,512]{3,2,1,0:T(8,128)(2,1)} %slice.631), channel_id=1, source_target_pairs={{0,2},{1,3},{2,0},{3,1},{4,6},{5,7},{6,4},{7,5},{8,10},{9,11},{10,... | collective-permute-start | bytes 1572872 | tf_op jit(solution)/shard_map/ppermute | solution.py:511
  1134.2 33.3 %collective-permute-start.59 = (bf16[2,128,2048]{2,1,0:T(8,128)(2,1)S(1)}, bf16[2,128,2048]{2,1,0:T(8,128)(2,1)S(1)}, u32[]{:S(2)}, u32[]{:S(2)}) collective-permute-start(bf16[2,128,2048]{2,1,0:T(8,128)(2,1)S(1)} %bitcast.308), channel_id=1, source_target_pairs={{0,1},{1,0},{2,3},{3,2},{4,5},{5,4},{6,7},{7,6},{8,9},{9,8},{10,11... | collective-permute-start | bytes 3145736 | tf_op jit(solution)/shard_map/ppermute | solution.py:511
  1137.1 31.7 %collective-permute-start.65 = (bf16[1,9,64,512]{3,2,1,0:T(8,128)(2,1)S(1)}, bf16[1,9,64,512]{3,2,1,0:T(8,128)(2,1)S(1)}, u32[]{:S(2)}, u32[]{:S(2)}) collective-permute-start(bf16[1,9,64,512]{3,2,1,0:T(8,128)(2,1)S(1)} %slice.630), channel_id=1, source_target_pairs={{0,2},{1,3},{2,0},{3,1},{4,6},{5,7},{6,4},{7,5},{8,10},{9,11},{10,... | collective-permute-start | bytes 1769480 | tf_op jit(solution)/shard_map/ppermute | solution.py:511
  (131 other events, 2314.0 us)

commit v7 on v6

--- a/solution.py
+++ b/solution.py
@@ -495,8 +495,8 @@
     heads = H // wide
     features = heads * HD
     if local == 8:
-        sizes, early, groups = [2, 1, 1, 1, 1, 2], 3, [[0], [1, 2, 3], [4, 5]]
-        parts = [[0], [1], [2], [3, 4], [5]]
+        sizes, early, groups = [2, 1, 1, 1, 1, 2], 2, [[0], [1, 2, 3], [4, 5]]
+        parts = [[0], [1, 2], [3, 4], [5]]
     else:
         sizes = [1] * local
         early, groups = min(2, local), [[c] for c in range(local)]

time: 1210 us -> 1200 us (level)
    all_to_all x5 -> x4, waiting for transfers between devices: 74.6 us -> 59.2 us  [send_weights(): expert_weights.append(lax.all_to_all(part, 'narrow', 0, 0, tiled=True))]
    unnamed x199 -> x215, local copies, waits for them, and re-layouts: 41.4 us -> 35.5 us
    all_to_all x5 -> x4, starting transfers between devices: 24.6 us -> 19.8 us  [send_weights(): expert_weights.append(lax.all_to_all(part, 'narrow', 0, 0, tiled=True))]
  transfers between devices with their start and end apart: 77 -> 76, of which waited for: 31 -> 29; matrix products, arithmetic and copies ran while one was open for 16% -> 16% of each run, Pallas kernels for 21% -> 21%
where the time goes in v7:
time: 1200 us; the launch traced here: 1180 us
  waiting for transfers between devices  550 us (46%)
  Pallas kernels  253 us (21%)
  starting transfers between devices  111 us (9%)
  other arithmetic  88.1 us (7%)
  local copies, waits for them, and re-layouts  87.3 us (7%)
  blocking collectives  58.3 us (5%)
  matrix products  33.9 us (3%)
    ppermute x67, waiting for transfers between devices, swap(): return lax.ppermute(x, axis, [(i, i ^ r) for i in range(size)])  470 us
    pallas_call x6, Pallas kernels, expert_chunk(): pl.pallas_call(functools.partial(expert_body, parts, tiles, start, len(al...  111 us
    all_to_all x4, waiting for transfers between devices, send_weights(): expert_weights.append(lax.all_to_all(part, 'narrow', 0, 0, tiled=True))  59.2 us
    ppermute x67, starting transfers between devices, swap(): return lax.ppermute(x, axis, [(i, i ^ r) for i in range(size)])  57.1 us
    pallas_call x4, Pallas kernels, combine(): pl.pallas_call(functools.partial(combine_body, pieces, each), grid=(pairs...  38.3 us
    pallas_call x4, Pallas kernels, dispatch(): pl.pallas_call(functools.partial(dispatch_body, pieces, each), grid=(pair...  36.3 us
    unnamed x215, local copies, waits for them, and re-layouts  35.5 us
    dot_general x11, matrix products, matmul(): return lax.dot_general(a, b, (dims, ((), ())), preferred_element_type=F32)  33.9 us
  transfers between devices with their start and end apart: 76, of which 29 were waited for; matrix products, arithmetic and copies ran while one was open for 16% of the time, Pallas kernels for 21%

profile of v7, /device:TPU:0, one launch (start us, length us, event | category | flops | bytes accessed | tf_op | source)
XLA Modules:
  0.0 1184.6 jit_solution(16447137910663705722)
XLA Ops:
  9.9 26.5 %all-gather = bf16[448,128]{1,0:T(8,128)(2,1)S(1)} all-gather(bf16[112,128]{1,0:T(8,128)(2,1)S(1)} %pad_maximum_fusion.11), channel_id=2, replica_groups=mesh['wide'=8,'narrow'=4] {'narrow'}, dimensions={0}, use_global_device_ids=true | all-gather | bytes 143360 | tf_op jit(solution)/shard_map/all_gather | solution.py:613
  47.1 15.0 %all-gather.1 = bf16[32,112,128]{2,1,0:T(8,128)(2,1)S(1)} all-gather(bf16[4,112,128]{2,1,0:T(8,128)(2,1)S(1)} %bitcast.313), channel_id=3, replica_groups=mesh['wide'=8,'narrow'=4] {'wide'}, dimensions={0}, use_global_device_ids=true | all-gather | bytes 1032192 | tf_op jit(solution)/shard_map/all_gather | solution.py:618
  85.6 10.8 collective-permute-done.3
  107.1 68.7 %collective-permute-done.14 = bf16[1,64,2048]{2,1,0:T(8,128)(2,1)} collective-permute-done((bf16[1,64,2048]{2,1,0:T(8,128)(2,1)}, bf16[1,64,2048]{2,1,0:T(8,128)(2,1)}, u32[]{:S(2)}, u32[]{:S(2)}) %collective-permute-start.14) | collective-permute-done | bytes 262176 | tf_op jit(solution)/shard_map/ppermute | solution.py:511
  197.8 22.7 %collective-permute-done.11 = bf16[1,8,64,768]{3,2,1,0:T(8,128)(2,1)} collective-permute-done((bf16[1,8,64,768]{3,2,1,0:T(8,128)(2,1)S(1)}, bf16[1,8,64,768]{3,2,1,0:T(8,128)(2,1)}, u32[]{:S(2)}, u32[]{:S(2)}) %collective-permute-start.11) | collective-permute-done | bytes 786464 | tf_op jit(solution)/shard_map/ppermute | solution.py:511
  226.6 30.2 %collective-permute-done.12 = bf16[2,8,64,768]{3,2,1,0:T(8,128)(2,1)S(1)} collective-permute-done((bf16[2,8,64,768]{3,2,1,0:T(8,128)(2,1)S(1)}, bf16[2,8,64,768]{3,2,1,0:T(8,128)(2,1)S(1)}, u32[]{:S(2)}, u32[]{:S(2)}) %collective-permute-start.12) | collective-permute-done | bytes 1572896 | tf_op jit(solution)/shard_map/ppermute | solution.py:511
  291.7 9.8 attend.1
  362.6 19.8 %all-to-all-done.2.refs_3_ = bf16[4,2,512,512]{3,2,1,0:T(8,128)(2,1)} async-done(((bf16[4,2,512,512]{3,2,1,0:T(8,128)(2,1)}), bf16[4,2,512,512]{3,2,1,0:T(8,128)(2,1)}, u32[]{:S(2)}, u32[]{:S(2)}) %all-to-all-start.2) | async-done | bytes 4194336 | tf_op jit(solution)/shard_map/all_to_all | solution.py:648
  382.4 11.3 collective-permute-done.24
  399.3 18.1 %collective-permute-done.25 = bf16[256,2176]{1,0:T(8,128)(2,1)S(1)} collective-permute-done((bf16[256,2176]{1,0:T(8,128)(2,1)S(1)}, bf16[256,2176]{1,0:T(8,128)(2,1)S(1)}, u32[]{:S(2)}, u32[]{:S(2)}) %collective-permute-start.25) | collective-permute-done | bytes 1114144 | tf_op jit(solution)/shard_map/ppermute | solution.py:511
  430.7 44.5 %collective-permute-done.27.refs_2_ = bf16[512,2176]{1,0:T(8,128)(2,1)} collective-permute-done((bf16[512,2176]{1,0:T(8,128)(2,1)}, bf16[512,2176]{1,0:T(8,128)(2,1)}, u32[]{:S(2)}, u32[]{:S(2)}) %collective-permute-start.27) | collective-permute-done | bytes 2228256 | tf_op jit(solution)/shard_map/ppermute | solution.py:511
  475.2 43.0 %collective-permute-done.29.refs_3_ = bf16[512,2176]{1,0:T(8,128)(2,1)} collective-permute-done((bf16[512,2176]{1,0:T(8,128)(2,1)}, bf16[512,2176]{1,0:T(8,128)(2,1)}, u32[]{:S(2)}, u32[]{:S(2)}) %collective-permute-start.29) | collective-permute-done | bytes 2228256 | tf_op jit(solution)/shard_map/ppermute | solution.py:511
  548.1 24.4 %experts.6 = (bf16[8,768,2048]{2,1,0:T(8,128)(2,1)}, bf16[8,768,2176]{2,1,0:T(8,128)(2,1)}, bf16[4,2,512,512]{3,2,1,0:T(8,128)(2,1)}, f32[8,256,2048]{2,1,0:T(8,128)}) custom-call(s32[3]{0:T(128)} %pad_add_fusion.refs_0_, bf16[8,768,2176]{2,1,0:T(8,128)(2,1)} %dispatch.7.refs_1_, bf16[8,768,2048]{2,1,0:T(8,128)(2,1)} %dispatch.5.refs_2_, ...), custom_call_target="tpu_custom_call" | custom-call | flops 14495514624 | bytes 44040192 | tf_op jit(solution)/shard_map/experts/pallas_call | solution.py:209
  572.5 39.5 %all-to-all-done.4.refs_3_ = bf16[4,2,512,512]{3,2,1,0:T(8,128)(2,1)} async-done(((bf16[4,2,512,512]{3,2,1,0:T(8,128)(2,1)}), bf16[4,2,512,512]{3,2,1,0:T(8,128)(2,1)}, u32[]{:S(2)}, u32[]{:S(2)}) %all-to-all-start.4) | async-done | bytes 4194336 | tf_op jit(solution)/shard_map/all_to_all | solution.py:648
  621.5 15.3 %experts.7 = (bf16[8,768,2048]{2,1,0:T(8,128)(2,1)}, bf16[8,768,2176]{2,1,0:T(8,128)(2,1)}, bf16[4,3,512,512]{3,2,1,0:T(8,128)(2,1)}, f32[8,256,2048]{2,1,0:T(8,128)}) custom-call(s32[3]{0:T(128)} %pad_add_fusion.refs_0_, bf16[8,768,2176]{2,1,0:T(8,128)(2,1)} %dispatch.7.refs_1_, ...), custom_call_target="tpu_custom_call", output_to_operand_aliasing={{0}: (5, {}), {1}: (6, {}), {3}: (7, {})} | custom-call | flops 7247757312 | bytes 22020096 | tf_op jit(solution)/shard_map/experts/pallas_call | solution.py:209
  636.8 15.5 %experts.8 = (bf16[8,768,2048]{2,1,0:T(8,128)(2,1)}, bf16[8,768,2176]{2,1,0:T(8,128)(2,1)}, bf16[4,3,512,512]{3,2,1,0:T(8,128)(2,1)}, f32[8,256,2048]{2,1,0:T(8,128)}) custom-call(s32[3]{0:T(128)} %pad_add_fusion.refs_0_, bf16[8,768,2176]{2,1,0:T(8,128)(2,1)} %dispatch.7.refs_1_, ...), custom_call_target="tpu_custom_call", output_to_operand_aliasing={{0}: (5, {}), {1}: (6, {}), {2}: (7, {}), {3}: (8, {})} | custom-call | flops 7247757312 | bytes 22020096 | tf_op jit(solution)/shard_map/experts/pallas_call | solution.py:209
  652.4 15.3 %experts.9 = (bf16[8,768,2048]{2,1,0:T(8,128)(2,1)}, bf16[8,768,2176]{2,1,0:T(8,128)(2,1)}, bf16[4,3,512,512]{3,2,1,0:T(8,128)(2,1)}, f32[8,256,2048]{2,1,0:T(8,128)}) custom-call(s32[3]{0:T(128)} %pad_add_fusion.refs_0_, bf16[8,768,2176]{2,1,0:T(8,128)(2,1)} %dispatch.7.refs_1_, ...), custom_call_target="tpu_custom_call", output_to_operand_aliasing={{0}: (5, {}), {1}: (6, {}), {2}: (7, {}), {3}: (8, {})} | custom-call | flops 7247757312 | bytes 22020096 | tf_op jit(solution)/shard_map/experts/pallas_call | solution.py:209
  667.7 15.7 %experts.10 = (bf16[8,768,2048]{2,1,0:T(8,128)(2,1)}, bf16[8,768,2176]{2,1,0:T(8,128)(2,1)}, bf16[4,3,512,512]{3,2,1,0:T(8,128)(2,1)}, f32[8,256,2048]{2,1,0:T(8,128)}) custom-call(s32[3]{0:T(128)} %pad_add_fusion.refs_0_, bf16[8,768,2176]{2,1,0:T(8,128)(2,1)} %dispatch.7.refs_1_, ...), custom_call_target="tpu_custom_call", output_to_operand_aliasing={{0}: (5, {}), {1}: (6, {}), {3}: (7, {})} | custom-call | flops 7247757312 | bytes 22020096 | tf_op jit(solution)/shard_map/experts/pallas_call | solution.py:209
  683.4 24.4 %experts.11 = (bf16[8,768,2048]{2,1,0:T(8,128)(2,1)}, bf16[8,768,2176]{2,1,0:T(8,128)(2,1)}, bf16[4,3,512,512]{3,2,1,0:T(8,128)(2,1)}, f32[8,256,2048]{2,1,0:T(8,128)}) custom-call(s32[3]{0:T(128)} %pad_add_fusion.refs_0_, bf16[8,768,2176]{2,1,0:T(8,128)(2,1)} %dispatch.7.refs_1_, ...), custom_call_target="tpu_custom_call", output_to_operand_aliasing={{0}: (5, {}), {1}: (6, {}), {2}: (7, {}), {3}: (8, {})} | custom-call | flops 14495514624 | bytes 44040192 | tf_op jit(solution)/shard_map/experts/pallas_call | solution.py:209
  717.1 9.4 combine.5
  733.2 10.2 combine.4
  769.2 30.3 %collective-permute-done.41 = bf16[512,2176]{1,0:T(8,128)(2,1)S(1)} collective-permute-done((bf16[512,2176]{1,0:T(8,128)(2,1)}, bf16[512,2176]{1,0:T(8,128)(2,1)S(1)}, u32[]{:S(2)}, u32[]{:S(2)}) %collective-permute-start.41) | collective-permute-done | bytes 2228256 | tf_op jit(solution)/shard_map/ppermute | solution.py:511
  799.5 46.8 %collective-permute-done.40 = bf16[512,2176]{1,0:T(8,128)(2,1)S(1)} collective-permute-done((bf16[512,2176]{1,0:T(8,128)(2,1)}, bf16[512,2176]{1,0:T(8,128)(2,1)S(1)}, u32[]{:S(2)}, u32[]{:S(2)}) %collective-permute-start.40) | collective-permute-done | bytes 2228256 | tf_op jit(solution)/shard_map/ppermute | solution.py:511
  848.7 9.9 combine.6
  874.9 15.5 %collective-permute-done.46 = bf16[2,128,2176]{2,1,0:T(8,128)(2,1)S(1)} collective-permute-done((bf16[2,128,2176]{2,1,0:T(8,128)(2,1)S(1)}, bf16[2,128,2176]{2,1,0:T(8,128)(2,1)S(1)}, u32[]{:S(2)}, u32[]{:S(2)}) %collective-permute-start.46) | collective-permute-done | bytes 1114144 | tf_op jit(solution)/shard_map/ppermute | solution.py:511
  902.6 15.4 %all-to-all-start.7 = ((bf16[4,3,512,512]{3,2,1,0:T(8,128)(2,1)}), bf16[4,3,512,512]{3,2,1,0:T(8,128)(2,1)}, u32[]{:S(2)}, u32[]{:S(2)}) async-start(bf16[4,3,512,512]{3,2,1,0:T(8,128)(2,1)} %get-tuple-element.167), calls=%async_computation.7 | async-start | bytes 12582912 | tf_op jit(solution)/shard_map/all_to_all | solution.py:753
  945.0 12.6 %collective-permute-done.52 = bf16[128,2176]{1,0:T(8,128)(2,1)S(1)} collective-permute-done((bf16[128,2176]{1,0:T(8,128)(2,1)S(1)}, bf16[128,2176]{1,0:T(8,128)(2,1)S(1)}, u32[]{:S(2)}, u32[]{:S(2)}) %collective-permute-start.52) | collective-permute-done | bytes 557088 | tf_op jit(solution)/shard_map/ppermute | solution.py:511
  962.8 13.4 %attend_back.1 = (f32[1024,512]{1,0:T(8,128)}, bf16[1024,256]{1,0:T(8,128)(2,1)}, f32[1024,2]{1,0:T(8,128)}, f32[2,256]{1,0:T(2,128)}) custom-call(bf16[1024,768]{1,0:T(8,128)(2,1)} %get-tuple-element.149.turned, bf16[1024,256]{1,0:T(8,128)(2,1)} %fusion.15.grads, f32[1024,768]{1,0:T(8,128)} %copy.270.raw, f32[1024,2]{1,0:T(8,128)} %bitcast.278, ...), custom_call_target="tpu_custom_call" | custom-call | flops 402653184 | bytes 7864320 | tf_op jit(solution)/shard_map/attend_back/pallas_call | solution.py:403
  1008.0 33.0 %collective-permute-done.57 = bf16[2,8,64,512]{3,2,1,0:T(8,128)(2,1)S(1)} collective-permute-done((bf16[2,8,64,512]{3,2,1,0:T(8,128)(2,1)}, bf16[2,8,64,512]{3,2,1,0:T(8,128)(2,1)S(1)}, u32[]{:S(2)}, u32[]{:S(2)}) %collective-permute-start.57) | collective-permute-done | bytes 1048608 | tf_op jit(solution)/shard_map/ppermute | solution.py:511
  1049.6 18.7 %all-to-all-done.7.refs_0_ = bf16[4,3,512,512]{3,2,1,0:T(8,128)(2,1)} async-done(((bf16[4,3,512,512]{3,2,1,0:T(8,128)(2,1)}), bf16[4,3,512,512]{3,2,1,0:T(8,128)(2,1)}, u32[]{:S(2)}, u32[]{:S(2)}) %all-to-all-start.7) | async-done | bytes 6291488 | tf_op jit(solution)/shard_map/all_to_all | solution.py:753
  1094.4 20.1 %collective-permute-done.58 = bf16[2,9,64,512]{3,2,1,0:T(8,128)(2,1)} collective-permute-done((bf16[2,9,64,512]{3,2,1,0:T(8,128)(2,1)}, bf16[2,9,64,512]{3,2,1,0:T(8,128)(2,1)}, u32[]{:S(2)}, u32[]{:S(2)}) %collective-permute-start.58) | collective-permute-done | bytes 1179680 | tf_op jit(solution)/shard_map/ppermute | solution.py:511
  1131.1 22.8 %collective-permute-done.59 = bf16[2,128,2048]{2,1,0:T(8,128)(2,1)S(1)} collective-permute-done((bf16[2,128,2048]{2,1,0:T(8,128)(2,1)S(1)}, bf16[2,128,2048]{2,1,0:T(8,128)(2,1)S(1)}, u32[]{:S(2)}, u32[]{:S(2)}) %collective-permute-start.59) | collective-permute-done | bytes 1048608 | tf_op jit(solution)/shard_map/ppermute | solution.py:511
  (557 shorter events, 453.2 us)
Async XLA Ops:
  0.7 35.7 %collective-permute-start.7 = (bf16[128,2048]{1,0:T(8,128)(2,1)}, bf16[128,2048]{1,0:T(8,128)(2,1)S(1)}, u32[]{:S(2)}, u32[]{:S(2)}) collective-permute-start(bf16[128,2048]{1,0:T(8,128)(2,1)} %param.23), channel_id=1, source_target_pairs={{0,2},{1,3},{2,0},{3,1},{4,6},{5,7},{6,4},{7,5},{8,10},{9,11},{10,... | collective-permute-start | bytes 1572872 | tf_op jit(solution)/shard_map/ppermute | solution.py:511
  65.6 117.9 %all-to-all-start.1 = ((bf16[4,2,512,512]{3,2,1,0:T(8,128)(2,1)}), bf16[4,2,512,512]{3,2,1,0:T(8,128)(2,1)}, u32[]{:S(2)}, u32[]{:S(2)}) async-start(bf16[4,2,512,512]{3,2,1,0:T(8,128)(2,1)} %slice_weights.4), calls=%async_computation.1 | async-start | bytes 8388608 | tf_op jit(solution)/shard_map/all_to_all | solution.py:648
  74.2 101.7 %collective-permute-start.14 = (bf16[1,64,2048]{2,1,0:T(8,128)(2,1)}, bf16[1,64,2048]{2,1,0:T(8,128)(2,1)}, u32[]{:S(2)}, u32[]{:S(2)}) collective-permute-start(bf16[1,64,2048]{2,1,0:T(8,128)(2,1)} %bitcast.24), channel_id=1, source_target_pairs={{0,2},{1,3},{2,0},{3,1},{4,6},{5,7},{6,4},{7,5},{8,10},{9,11},{10,... | collective-permute-start | bytes 786440 | tf_op jit(solution)/shard_map/ppermute | solution.py:511
  99.2 84.2 %collective-permute-start.10 = (bf16[512,2048]{1,0:T(8,128)(2,1)}, bf16[512,2048]{1,0:T(8,128)(2,1)S(1)}, u32[]{:S(2)}, u32[]{:S(2)}) collective-permute-start(bf16[512,2048]{1,0:T(8,128)(2,1)} %constant_dynamic-update-slice_fusion.8.refs_1_), channel_id=1, source_target_pairs={{0,16},{4,20},{8,24},{12,28},{16,0},{20,4},{24,8},{28,12},{1,17},{... | collective-permute-start | bytes 6291464 | tf_op jit(solution)/shard_map/ppermute | solution.py:511
  100.9 82.6 %collective-permute-start.9 = (bf16[512,2048]{1,0:T(8,128)(2,1)}, bf16[512,2048]{1,0:T(8,128)(2,1)}, u32[]{:S(2)}, u32[]{:S(2)}) collective-permute-start(bf16[512,2048]{1,0:T(8,128)(2,1)} %constant_dynamic-update-slice_fusion.8.refs_1_), channel_id=1, source_target_pairs={{0,8},{4,12},{8,0},{12,4},{16,24},{20,28},{24,16},{28,20},{1,9},{5... | collective-permute-start | bytes 6291464 | tf_op jit(solution)/shard_map/ppermute | solution.py:511
  183.5 37.0 %collective-permute-start.11 = (bf16[1,8,64,768]{3,2,1,0:T(8,128)(2,1)S(1)}, bf16[1,8,64,768]{3,2,1,0:T(8,128)(2,1)}, u32[]{:S(2)}, u32[]{:S(2)}) collective-permute-start(bf16[1,8,64,768]{3,2,1,0:T(8,128)(2,1)S(1)} %bitcast.284), channel_id=1, source_target_pairs={{0,2},{1,3},{2,0},{3,1},{4,6},{5,7},{6,4},{7,5},{8,10},{9,11},{10,... | collective-permute-start | bytes 2359304 | tf_op jit(solution)/shard_map/ppermute | solution.py:511
  221.8 35.1 %collective-permute-start.12 = (bf16[2,8,64,768]{3,2,1,0:T(8,128)(2,1)S(1)}, bf16[2,8,64,768]{3,2,1,0:T(8,128)(2,1)S(1)}, u32[]{:S(2)}, u32[]{:S(2)}) collective-permute-start(bf16[2,8,64,768]{3,2,1,0:T(8,128)(2,1)S(1)} %pad_maximum_fusion.1), channel_id=1, source_target_pairs={{0,1},{1,0},{2,3},{3,2},{4,5},{5,4},{6,7},{7,6},{8,9},{9,8},{10,11... | collective-permute-start | bytes 4718600 | tf_op jit(solution)/shard_map/ppermute | solution.py:511
  221.9 47.5 %collective-permute-start.13 = (bf16[512,2048]{1,0:T(8,128)(2,1)}, bf16[512,2048]{1,0:T(8,128)(2,1)}, u32[]{:S(2)}, u32[]{:S(2)}) collective-permute-start(bf16[512,2048]{1,0:T(8,128)(2,1)} %constant_dynamic-update-slice_fusion.8.refs_1_), channel_id=1, source_target_pairs={{0,24},{4,28},{8,16},{12,20},{16,8},{20,12},{24,0},{28,4},{1,25},{... | collective-permute-start | bytes 6291464 | tf_op jit(solution)/shard_map/ppermute | solution.py:511
  273.5 108.8 %all-to-all-start.2 = ((bf16[4,2,512,512]{3,2,1,0:T(8,128)(2,1)}), bf16[4,2,512,512]{3,2,1,0:T(8,128)(2,1)}, u32[]{:S(2)}, u32[]{:S(2)}) async-start(bf16[4,2,512,512]{3,2,1,0:T(8,128)(2,1)} %slice_weights.5), calls=%async_computation.2 | async-start | bytes 8388608 | tf_op jit(solution)/shard_map/all_to_all | solution.py:648
  418.6 99.7 %all-to-all-start.3 = ((bf16[4,2,512,512]{3,2,1,0:T(8,128)(2,1)}), bf16[4,2,512,512]{3,2,1,0:T(8,128)(2,1)}, u32[]{:S(2)}, u32[]{:S(2)}) async-start(bf16[4,2,512,512]{3,2,1,0:T(8,128)(2,1)} %slice_weights.6), calls=%async_computation.3 | async-start | bytes 8388608 | tf_op jit(solution)/shard_map/all_to_all | solution.py:648
  423.4 51.8 %collective-permute-start.27 = (bf16[512,2176]{1,0:T(8,128)(2,1)}, bf16[512,2176]{1,0:T(8,128)(2,1)}, u32[]{:S(2)}, u32[]{:S(2)}) collective-permute-start(bf16[512,2176]{1,0:T(8,128)(2,1)} %constant_dynamic-update-slice_fusion.10.refs_1_), channel_id=1, source_target_pairs={{0,8},{4,12},{8,0},{12,4},{16,24},{20,28},{24,16},{28,20},{1,9},{5... | collective-permute-start | bytes 6684680 | tf_op jit(solution)/shard_map/ppermute | solution.py:511
  423.9 94.4 %collective-permute-start.29 = (bf16[512,2176]{1,0:T(8,128)(2,1)}, bf16[512,2176]{1,0:T(8,128)(2,1)}, u32[]{:S(2)}, u32[]{:S(2)}) collective-permute-start(bf16[512,2176]{1,0:T(8,128)(2,1)} %constant_dynamic-update-slice_fusion.10.refs_1_), channel_id=1, source_target_pairs={{0,16},{4,20},{8,24},{12,28},{16,0},{20,4},{24,8},{28,12},{1,17},{... | collective-permute-start | bytes 6684680 | tf_op jit(solution)/shard_map/ppermute | solution.py:511
  425.5 92.7 %collective-permute-start.31 = (bf16[512,2176]{1,0:T(8,128)(2,1)}, bf16[512,2176]{1,0:T(8,128)(2,1)}, u32[]{:S(2)}, u32[]{:S(2)}) collective-permute-start(bf16[512,2176]{1,0:T(8,128)(2,1)} %constant_dynamic-update-slice_fusion.10.refs_1_), channel_id=1, source_target_pairs={{0,24},{4,28},{8,16},{12,20},{16,8},{20,12},{24,0},{28,4},{1,25},{... | collective-permute-start | bytes 6684680 | tf_op jit(solution)/shard_map/ppermute | solution.py:511
  518.2 93.8 %all-to-all-start.4 = ((bf16[4,2,512,512]{3,2,1,0:T(8,128)(2,1)}), bf16[4,2,512,512]{3,2,1,0:T(8,128)(2,1)}, u32[]{:S(2)}, u32[]{:S(2)}) async-start(bf16[4,2,512,512]{3,2,1,0:T(8,128)(2,1)} %slice_weights.7), calls=%async_computation.4 | async-start | bytes 8388608 | tf_op jit(solution)/shard_map/all_to_all | solution.py:648
  612.0 97.7 %all-to-all-start.5 = ((bf16[4,2,512,512]{3,2,1,0:T(8,128)(2,1)}), bf16[4,2,512,512]{3,2,1,0:T(8,128)(2,1)}, u32[]{:S(2)}, u32[]{:S(2)}) async-start(bf16[4,2,512,512]{3,2,1,0:T(8,128)(2,1)} %get-tuple-element.150), calls=%async_computation.5 | async-start | bytes 8388608 | tf_op jit(solution)/shard_map/all_to_all | solution.py:753
  709.7 153.4 %all-to-all-start.6 = ((bf16[4,3,512,512]{3,2,1,0:T(8,128)(2,1)}), bf16[4,3,512,512]{3,2,1,0:T(8,128)(2,1)}, u32[]{:S(2)}, u32[]{:S(2)}) async-start(bf16[4,3,512,512]{3,2,1,0:T(8,128)(2,1)} %get-tuple-element.152), calls=%async_computation.6 | async-start | bytes 12582912 | tf_op jit(solution)/shard_map/all_to_all | solution.py:753
  727.0 41.7 %collective-permute-start.38 = (bf16[512,2176]{1,0:T(8,128)(2,1)}, bf16[512,2176]{1,0:T(8,128)(2,1)S(1)}, u32[]{:S(2)}, u32[]{:S(2)}) collective-permute-start(bf16[512,2176]{1,0:T(8,128)(2,1)} %get-tuple-element.142), channel_id=1, source_target_pairs={{0,4},{4,0},{8,12},{12,8},{16,20},{20,16},{24,28},{28,24},{1,5},{5... | collective-permute-start | bytes 6684680 | tf_op jit(solution)/shard_map/ppermute | solution.py:511
  747.0 52.4 %collective-permute-start.41 = (bf16[512,2176]{1,0:T(8,128)(2,1)}, bf16[512,2176]{1,0:T(8,128)(2,1)S(1)}, u32[]{:S(2)}, u32[]{:S(2)}) collective-permute-start(bf16[512,2176]{1,0:T(8,128)(2,1)} %add_convert_fusion.1), channel_id=1, source_target_pairs={{0,24},{4,28},{8,16},{12,20},{16,8},{20,12},{24,0},{28,4},{1,25},{... | collective-permute-start | bytes 6684680 | tf_op jit(solution)/shard_map/ppermute | solution.py:511
  750.4 95.8 %collective-permute-start.40 = (bf16[512,2176]{1,0:T(8,128)(2,1)}, bf16[512,2176]{1,0:T(8,128)(2,1)S(1)}, u32[]{:S(2)}, u32[]{:S(2)}) collective-permute-start(bf16[512,2176]{1,0:T(8,128)(2,1)} %add_convert_fusion.2), channel_id=1, source_target_pairs={{0,16},{4,20},{8,24},{12,28},{16,0},{20,4},{24,8},{28,12},{1,17},{... | collective-permute-start | bytes 6684680 | tf_op jit(solution)/shard_map/ppermute | solution.py:511
  755.7 103.0 %collective-permute-start.39 = (bf16[512,2176]{1,0:T(8,128)(2,1)}, bf16[512,2176]{1,0:T(8,128)(2,1)}, u32[]{:S(2)}, u32[]{:S(2)}) collective-permute-start(bf16[512,2176]{1,0:T(8,128)(2,1)} %add_convert_fusion.3), channel_id=1, source_target_pairs={{0,8},{4,12},{8,0},{12,4},{16,24},{20,28},{24,16},{28,20},{1,9},{5... | collective-permute-start | bytes 6684680 | tf_op jit(solution)/shard_map/ppermute | solution.py:511
  768.7 94.4 %collective-permute-start.36 = (bf16[512,2048]{1,0:T(8,128)(2,1)}, bf16[512,2048]{1,0:T(8,128)(2,1)}, u32[]{:S(2)}, u32[]{:S(2)}) collective-permute-start(bf16[512,2048]{1,0:T(8,128)(2,1)} %get-tuple-element.138), channel_id=1, source_target_pairs={{0,4},{4,0},{8,12},{12,8},{16,20},{20,16},{24,28},{28,24},{1,5},{5... | collective-permute-start | bytes 6291464 | tf_op jit(solution)/shard_map/ppermute | solution.py:511
  768.7 94.4 %collective-permute-start.37 = (bf16[512,2048]{1,0:T(8,128)(2,1)}, bf16[512,2048]{1,0:T(8,128)(2,1)}, u32[]{:S(2)}, u32[]{:S(2)}) collective-permute-start(bf16[512,2048]{1,0:T(8,128)(2,1)} %get-tuple-element.140), channel_id=1, source_target_pairs={{0,4},{4,0},{8,12},{12,8},{16,20},{20,16},{24,28},{28,24},{1,5},{5... | collective-permute-start | bytes 6291464 | tf_op jit(solution)/shard_map/ppermute | solution.py:511
  799.5 63.6 %collective-permute-start.43 = (bf16[512,2048]{1,0:T(8,128)(2,1)}, bf16[512,2048]{1,0:T(8,128)(2,1)}, u32[]{:S(2)}, u32[]{:S(2)}) collective-permute-start(bf16[512,2048]{1,0:T(8,128)(2,1)} %get-tuple-element.145), channel_id=1, source_target_pairs={{0,4},{4,0},{8,12},{12,8},{16,20},{20,16},{24,28},{28,24},{1,5},{5... | collective-permute-start | bytes 6291464 | tf_op jit(solution)/shard_map/ppermute | solution.py:511
  872.9 53.8 %collective-permute-start.44 = (bf16[512,2048]{1,0:T(8,128)(2,1)}, bf16[512,2048]{1,0:T(8,128)(2,1)}, u32[]{:S(2)}, u32[]{:S(2)}) collective-permute-start(bf16[512,2048]{1,0:T(8,128)(2,1)} %add_convert_fusion.6), channel_id=1, source_target_pairs={{0,16},{4,20},{8,24},{12,28},{16,0},{20,4},{24,8},{28,12},{1,17},{... | collective-permute-start | bytes 6291464 | tf_op jit(solution)/shard_map/ppermute | solution.py:511
  874.4 52.3 %collective-permute-start.42 = (bf16[512,2048]{1,0:T(8,128)(2,1)}, bf16[512,2048]{1,0:T(8,128)(2,1)}, u32[]{:S(2)}, u32[]{:S(2)}) collective-permute-start(bf16[512,2048]{1,0:T(8,128)(2,1)} %add_convert_fusion.7), channel_id=1, source_target_pairs={{0,8},{4,12},{8,0},{12,4},{16,24},{20,28},{24,16},{28,20},{1,9},{5... | collective-permute-start | bytes 6291464 | tf_op jit(solution)/shard_map/ppermute | solution.py:511
  894.3 31.2 %collective-permute-start.47 = (bf16[112,2176]{1,0:T(8,128)(2,1)}, bf16[112,2176]{1,0:T(8,128)(2,1)}, u32[]{:S(2)}, u32[]{:S(2)}) collective-permute-start(bf16[112,2176]{1,0:T(8,128)(2,1)} %slice_bitcast_fusion.21), channel_id=1, source_target_pairs={{0,2},{1,3},{2,0},{3,1},{4,6},{5,7},{6,4},{7,5},{8,10},{9,11},{10,... | collective-permute-start | bytes 1462280 | tf_op jit(solution)/shard_map/ppermute | solution.py:511
  902.6 165.8 %all-to-all-start.7 = ((bf16[4,3,512,512]{3,2,1,0:T(8,128)(2,1)}), bf16[4,3,512,512]{3,2,1,0:T(8,128)(2,1)}, u32[]{:S(2)}, u32[]{:S(2)}) async-start(bf16[4,3,512,512]{3,2,1,0:T(8,128)(2,1)} %get-tuple-element.167), calls=%async_computation.7 | async-start | bytes 12582912 | tf_op jit(solution)/shard_map/all_to_all | solution.py:753
  988.4 52.5 %collective-permute-start.57 = (bf16[2,8,64,512]{3,2,1,0:T(8,128)(2,1)}, bf16[2,8,64,512]{3,2,1,0:T(8,128)(2,1)S(1)}, u32[]{:S(2)}, u32[]{:S(2)}) collective-permute-start(bf16[2,8,64,512]{3,2,1,0:T(8,128)(2,1)} %get-tuple-element.168), channel_id=1, source_target_pairs={{0,1},{1,0},{2,3},{3,2},{4,5},{5,4},{6,7},{7,6},{8,9},{9,8},{10,11... | collective-permute-start | bytes 3145736 | tf_op jit(solution)/shard_map/ppermute | solution.py:511
  1002.7 91.7 %collective-permute-start.56 = (bf16[512,2048]{1,0:T(8,128)(2,1)}, bf16[512,2048]{1,0:T(8,128)(2,1)}, u32[]{:S(2)}, u32[]{:S(2)}) collective-permute-start(bf16[512,2048]{1,0:T(8,128)(2,1)} %add_convert_fusion.5), channel_id=1, source_target_pairs={{0,24},{4,28},{8,16},{12,20},{16,8},{20,12},{24,0},{28,4},{1,25},{... | collective-permute-start | bytes 6291464 | tf_op jit(solution)/shard_map/ppermute | solution.py:511
  1044.4 45.6 %collective-permute-start.66 = (bf16[1,8,64,512]{3,2,1,0:T(8,128)(2,1)}, bf16[1,8,64,512]{3,2,1,0:T(8,128)(2,1)}, u32[]{:S(2)}, u32[]{:S(2)}) collective-permute-start(bf16[1,8,64,512]{3,2,1,0:T(8,128)(2,1)} %slice.631), channel_id=1, source_target_pairs={{0,2},{1,3},{2,0},{3,1},{4,6},{5,7},{6,4},{7,5},{8,10},{9,11},{10,... | collective-permute-start | bytes 1572872 | tf_op jit(solution)/shard_map/ppermute | solution.py:511
  1120.6 33.3 %collective-permute-start.59 = (bf16[2,128,2048]{2,1,0:T(8,128)(2,1)S(1)}, bf16[2,128,2048]{2,1,0:T(8,128)(2,1)S(1)}, u32[]{:S(2)}, u32[]{:S(2)}) collective-permute-start(bf16[2,128,2048]{2,1,0:T(8,128)(2,1)S(1)} %bitcast.308), channel_id=1, source_target_pairs={{0,1},{1,0},{2,3},{3,2},{4,5},{5,4},{6,7},{7,6},{8,9},{9,8},{10,11... | collective-permute-start | bytes 3145736 | tf_op jit(solution)/shard_map/ppermute | solution.py:511
  1123.6 31.7 %collective-permute-start.65 = (bf16[1,9,64,512]{3,2,1,0:T(8,128)(2,1)S(1)}, bf16[1,9,64,512]{3,2,1,0:T(8,128)(2,1)S(1)}, u32[]{:S(2)}, u32[]{:S(2)}) collective-permute-start(bf16[1,9,64,512]{3,2,1,0:T(8,128)(2,1)S(1)} %slice.630), channel_id=1, source_target_pairs={{0,2},{1,3},{2,0},{3,1},{4,6},{5,7},{6,4},{7,5},{8,10},{9,11},{10,... | collective-permute-start | bytes 1769480 | tf_op jit(solution)/shard_map/ppermute | solution.py:511
  (138 other events, 2456.9 us)

commit v8 on v7

--- a/solution.py
+++ b/solution.py
@@ -495,8 +495,8 @@
     heads = H // wide
     features = heads * HD
     if local == 8:
-        sizes, early, groups = [2, 1, 1, 1, 1, 2], 2, [[0], [1, 2, 3], [4, 5]]
-        parts = [[0], [1, 2], [3, 4], [5]]
+        sizes, early, groups = [2, 3, 3], 2, [[0], [1], [2]]
+        parts = groups
     else:
         sizes = [1] * local
         early, groups = min(2, local), [[c] for c in range(local)]
@@ -724,7 +724,8 @@
         tokens_own = gather_planes(message)
         while len(expert_weights) < len(parts):
             send_weights(*tokens_own)
-        tokens_own[0] = tie(tokens_own[0], expert_weights[min(early, len(parts) - 1)])
+        if len(parts) > early + 1:
+            tokens_own[0] = tie(tokens_own[0], expert_weights[early])
         tokens_other = cross(tokens_own)
         expert_rows = dispatch(picks_own, tokens_own, 0)
         expert_rows = dispatch(picks_other, tokens_other, 1, expert_rows)

time: 1200 us -> 1190 us (level)
  waiting for transfers between devices: 550 us -> 574 us
  Pallas kernels: 253 us -> 235 us
    all_to_all x3, waiting for transfers between devices: 20.6 us -> 45.3 us  [send_grads(): arrived.append(lax.all_to_all(part, 'narrow', 0, 0, tiled=True))]
    pallas_call x6 -> x3, Pallas kernels: 111 us -> 91.2 us  [expert_chunk(): pl.pallas_call(functools.partial(expert_body, parts, tiles, start, len(al...]
    all_to_all x4 -> x3, waiting for transfers between devices: 59.2 us -> 54.9 us  [send_weights(): expert_weights.append(lax.all_to_all(part, 'narrow', 0, 0, tiled=True))]
    unnamed x215 -> x218, local copies, waits for them, and re-layouts: 35.5 us -> 36 us
  transfers between devices with their start and end apart: 76 -> 75, of which waited for: 29 -> 29; matrix products, arithmetic and copies ran while one was open for 16% -> 16% of each run, Pallas kernels for 21% -> 20%
where the time goes in v8:
time: 1190 us; the launch traced here: 1180 us
  waiting for transfers between devices  574 us (48%)
  Pallas kernels  235 us (20%)
  starting transfers between devices  106 us (9%)
  other arithmetic  88 us (7%)
  local copies, waits for them, and re-layouts  80.9 us (7%)
  blocking collectives  58.4 us (5%)
  matrix products  33.9 us (3%)
    ppermute x67, waiting for transfers between devices, swap(): return lax.ppermute(x, axis, [(i, i ^ r) for i in range(size)])  473 us
    pallas_call x3, Pallas kernels, expert_chunk(): pl.pallas_call(functools.partial(expert_body, parts, tiles, start, len(al...  91.2 us
    ppermute x67, starting transfers between devices, swap(): return lax.ppermute(x, axis, [(i, i ^ r) for i in range(size)])  55.9 us
    all_to_all x3, waiting for transfers between devices, send_weights(): expert_weights.append(lax.all_to_all(part, 'narrow', 0, 0, tiled=True))  54.9 us
    all_to_all x3, waiting for transfers between devices, send_grads(): arrived.append(lax.all_to_all(part, 'narrow', 0, 0, tiled=True))  45.3 us
    pallas_call x4, Pallas kernels, combine(): pl.pallas_call(functools.partial(combine_body, pieces, each), grid=(pairs...  38.3 us
    pallas_call x4, Pallas kernels, dispatch(): pl.pallas_call(functools.partial(dispatch_body, pieces, each), grid=(pair...  36.3 us
    unnamed x218, local copies, waits for them, and re-layouts  36 us
  transfers between devices with their start and end apart: 75, of which 29 were waited for; matrix products, arithmetic and copies ran while one was open for 16% of the time, Pallas kernels for 20%

profile of v8, /device:TPU:0, one launch (start us, length us, event | category | flops | bytes accessed | tf_op | source)
XLA Modules:
  0.0 1179.2 jit_solution(7308867898919092938)
XLA Ops:
  9.9 26.5 %all-gather = bf16[448,128]{1,0:T(8,128)(2,1)S(1)} all-gather(bf16[112,128]{1,0:T(8,128)(2,1)S(1)} %pad_maximum_fusion.11), channel_id=2, replica_groups=mesh['wide'=8,'narrow'=4] {'narrow'}, dimensions={0}, use_global_device_ids=true | all-gather | bytes 143360 | tf_op jit(solution)/shard_map/all_gather | solution.py:613
  47.1 15.0 %all-gather.1 = bf16[32,112,128]{2,1,0:T(8,128)(2,1)S(1)} all-gather(bf16[4,112,128]{2,1,0:T(8,128)(2,1)S(1)} %bitcast.316), channel_id=3, replica_groups=mesh['wide'=8,'narrow'=4] {'wide'}, dimensions={0}, use_global_device_ids=true | all-gather | bytes 1032192 | tf_op jit(solution)/shard_map/all_gather | solution.py:618
  74.1 11.2 collective-permute-done.1
  85.4 10.8 collective-permute-done.3
  110.5 36.3 %collective-permute-done.10.refs_3_ = bf16[512,2048]{1,0:T(8,128)(2,1)} collective-permute-done((bf16[512,2048]{1,0:T(8,128)(2,1)}, bf16[512,2048]{1,0:T(8,128)(2,1)}, u32[]{:S(2)}, u32[]{:S(2)}) %collective-permute-start.10) | collective-permute-done | bytes 2097184 | tf_op jit(solution)/shard_map/ppermute | solution.py:511
  148.2 22.6 %all-to-all-done.1.refs_3_ = bf16[4,2,512,512]{3,2,1,0:T(8,128)(2,1)} async-done(((bf16[4,2,512,512]{3,2,1,0:T(8,128)(2,1)}), bf16[4,2,512,512]{3,2,1,0:T(8,128)(2,1)}, u32[]{:S(2)}, u32[]{:S(2)}) %all-to-all-start.1) | async-done | bytes 4194336 | tf_op jit(solution)/shard_map/all_to_all | solution.py:648
  172.2 37.2 %collective-permute-done.11 = bf16[1,8,64,768]{3,2,1,0:T(8,128)(2,1)S(1)} collective-permute-done((bf16[1,8,64,768]{3,2,1,0:T(8,128)(2,1)S(1)}, bf16[1,8,64,768]{3,2,1,0:T(8,128)(2,1)S(1)}, u32[]{:S(2)}, u32[]{:S(2)}) %collective-permute-start.11) | collective-permute-done | bytes 786464 | tf_op jit(solution)/shard_map/ppermute | solution.py:511
  222.4 35.6 %collective-permute-done.15 = bf16[2,64,2048]{2,1,0:T(8,128)(2,1)S(1)} collective-permute-done((bf16[2,64,2048]{2,1,0:T(8,128)(2,1)S(1)}, bf16[2,64,2048]{2,1,0:T(8,128)(2,1)S(1)}, u32[]{:S(2)}, u32[]{:S(2)}) %collective-permute-start.15) | collective-permute-done | bytes 524320 | tf_op jit(solution)/shard_map/ppermute | solution.py:511
  286.1 22.0 %collective-permute-done.13.refs_4_ = bf16[512,2048]{1,0:T(8,128)(2,1)} collective-permute-done((bf16[512,2048]{1,0:T(8,128)(2,1)}, bf16[512,2048]{1,0:T(8,128)(2,1)}, u32[]{:S(2)}, u32[]{:S(2)}) %collective-permute-start.13) | collective-permute-done | bytes 2097184 | tf_op jit(solution)/shard_map/ppermute | solution.py:511
  326.0 9.8 attend.1
  386.4 32.4 %all-to-all-done.2.refs_3_ = bf16[4,3,512,512]{3,2,1,0:T(8,128)(2,1)} async-done(((bf16[4,3,512,512]{3,2,1,0:T(8,128)(2,1)}), bf16[4,3,512,512]{3,2,1,0:T(8,128)(2,1)}, u32[]{:S(2)}, u32[]{:S(2)}) %all-to-all-start.2) | async-done | bytes 6291488 | tf_op jit(solution)/shard_map/all_to_all | solution.py:648
  418.8 11.9 %collective-permute-done.24 = bf16[128,2176]{1,0:T(8,128)(2,1)S(1)} collective-permute-done((bf16[128,2176]{1,0:T(8,128)(2,1)S(1)}, bf16[128,2176]{1,0:T(8,128)(2,1)S(1)}, u32[]{:S(2)}, u32[]{:S(2)}) %collective-permute-start.24) | collective-permute-done | bytes 557088 | tf_op jit(solution)/shard_map/ppermute | solution.py:511
  439.2 15.3 %collective-permute-done.25 = bf16[256,2176]{1,0:T(8,128)(2,1)S(1)} collective-permute-done((bf16[256,2176]{1,0:T(8,128)(2,1)S(1)}, bf16[256,2176]{1,0:T(8,128)(2,1)S(1)}, u32[]{:S(2)}, u32[]{:S(2)}) %collective-permute-start.25) | collective-permute-done | bytes 1114144 | tf_op jit(solution)/shard_map/ppermute | solution.py:511
  464.6 48.2 %collective-permute-done.27.refs_2_ = bf16[512,2176]{1,0:T(8,128)(2,1)} collective-permute-done((bf16[512,2176]{1,0:T(8,128)(2,1)}, bf16[512,2176]{1,0:T(8,128)(2,1)}, u32[]{:S(2)}, u32[]{:S(2)}) %collective-permute-start.27) | collective-permute-done | bytes 2228256 | tf_op jit(solution)/shard_map/ppermute | solution.py:511
  512.8 44.0 %collective-permute-done.29.refs_3_ = bf16[512,2176]{1,0:T(8,128)(2,1)S(1)} collective-permute-done((bf16[512,2176]{1,0:T(8,128)(2,1)}, bf16[512,2176]{1,0:T(8,128)(2,1)S(1)}, u32[]{:S(2)}, u32[]{:S(2)}) %collective-permute-start.29) | collective-permute-done | bytes 2228256 | tf_op jit(solution)/shard_map/ppermute | solution.py:511
  578.9 24.4 %experts.3 = (bf16[8,768,2048]{2,1,0:T(8,128)(2,1)}, bf16[8,768,2176]{2,1,0:T(8,128)(2,1)}, bf16[4,2,512,512]{3,2,1,0:T(8,128)(2,1)}, f32[8,256,2048]{2,1,0:T(8,128)}) custom-call(s32[3]{0:T(128)} %pad_add_fusion.refs_0_, bf16[8,768,2176]{2,1,0:T(8,128)(2,1)} %dispatch.7.refs_1_, bf16[8,768,2048]{2,1,0:T(8,128)(2,1)} %dispatch.5.refs_2_, ...), custom_call_target="tpu_custom_call" | custom-call | flops 14495514624 | bytes 44040192 | tf_op jit(solution)/shard_map/experts/pallas_call | solution.py:209
  609.3 33.4 %experts.4 = (bf16[8,768,2048]{2,1,0:T(8,128)(2,1)}, bf16[8,768,2176]{2,1,0:T(8,128)(2,1)}, bf16[4,3,512,512]{3,2,1,0:T(8,128)(2,1)}, f32[8,256,2048]{2,1,0:T(8,128)}) custom-call(s32[3]{0:T(128)} %pad_add_fusion.refs_0_, bf16[8,768,2176]{2,1,0:T(8,128)(2,1)} %dispatch.7.refs_1_, ...), custom_call_target="tpu_custom_call", output_to_operand_aliasing={{0}: (5, {}), {1}: (6, {}), {3}: (7, {})} | custom-call | flops 21743271936 | bytes 66060288 | tf_op jit(solution)/shard_map/experts/pallas_call | solution.py:209
  642.7 33.4 %experts.5 = (bf16[8,768,2048]{2,1,0:T(8,128)(2,1)}, bf16[8,768,2176]{2,1,0:T(8,128)(2,1)}, bf16[4,3,512,512]{3,2,1,0:T(8,128)(2,1)}, f32[8,256,2048]{2,1,0:T(8,128)}) custom-call(s32[3]{0:T(128)} %pad_add_fusion.refs_0_, bf16[8,768,2176]{2,1,0:T(8,128)(2,1)} %dispatch.7.refs_1_, ...), custom_call_target="tpu_custom_call", output_to_operand_aliasing={{0}: (5, {}), {1}: (6, {}), {3}: (7, {})} | custom-call | flops 21743271936 | bytes 66060288 | tf_op jit(solution)/shard_map/experts/pallas_call | solution.py:209
  676.1 26.6 %all-to-all-done.4.refs_0_ = bf16[4,2,512,512]{3,2,1,0:T(8,128)(2,1)} async-done(((bf16[4,2,512,512]{3,2,1,0:T(8,128)(2,1)}), bf16[4,2,512,512]{3,2,1,0:T(8,128)(2,1)}, u32[]{:S(2)}, u32[]{:S(2)}) %all-to-all-start.4) | async-done | bytes 4194336 | tf_op jit(solution)/shard_map/all_to_all | solution.py:754
  711.7 9.4 combine.5
  727.8 10.2 combine.4
  763.7 30.4 %collective-permute-done.41 = bf16[512,2176]{1,0:T(8,128)(2,1)S(1)} collective-permute-done((bf16[512,2176]{1,0:T(8,128)(2,1)}, bf16[512,2176]{1,0:T(8,128)(2,1)S(1)}, u32[]{:S(2)}, u32[]{:S(2)}) %collective-permute-start.41) | collective-permute-done | bytes 2228256 | tf_op jit(solution)/shard_map/ppermute | solution.py:511
  794.1 46.8 %collective-permute-done.40 = bf16[512,2176]{1,0:T(8,128)(2,1)S(1)} collective-permute-done((bf16[512,2176]{1,0:T(8,128)(2,1)}, bf16[512,2176]{1,0:T(8,128)(2,1)S(1)}, u32[]{:S(2)}, u32[]{:S(2)}) %collective-permute-start.40) | collective-permute-done | bytes 2228256 | tf_op jit(solution)/shard_map/ppermute | solution.py:511
  843.4 9.9 combine.6
  869.5 15.5 %collective-permute-done.46 = bf16[2,128,2176]{2,1,0:T(8,128)(2,1)S(1)} collective-permute-done((bf16[2,128,2176]{2,1,0:T(8,128)(2,1)S(1)}, bf16[2,128,2176]{2,1,0:T(8,128)(2,1)S(1)}, u32[]{:S(2)}, u32[]{:S(2)}) %collective-permute-start.46) | collective-permute-done | bytes 1114144 | tf_op jit(solution)/shard_map/ppermute | solution.py:511
  897.2 15.4 %all-to-all-start.6 = ((bf16[4,3,512,512]{3,2,1,0:T(8,128)(2,1)}), bf16[4,3,512,512]{3,2,1,0:T(8,128)(2,1)}, u32[]{:S(2)}, u32[]{:S(2)}) async-start(bf16[4,3,512,512]{3,2,1,0:T(8,128)(2,1)} %get-tuple-element.139), calls=%async_computation.6 | async-start | bytes 12582912 | tf_op jit(solution)/shard_map/all_to_all | solution.py:754
  939.7 12.6 %collective-permute-done.52 = bf16[128,2176]{1,0:T(8,128)(2,1)S(1)} collective-permute-done((bf16[128,2176]{1,0:T(8,128)(2,1)S(1)}, bf16[128,2176]{1,0:T(8,128)(2,1)S(1)}, u32[]{:S(2)}, u32[]{:S(2)}) %collective-permute-start.52) | collective-permute-done | bytes 557088 | tf_op jit(solution)/shard_map/ppermute | solution.py:511
  957.4 13.4 %attend_back.1 = (f32[1024,512]{1,0:T(8,128)}, bf16[1024,256]{1,0:T(8,128)(2,1)}, f32[1024,2]{1,0:T(8,128)}, f32[2,256]{1,0:T(2,128)}) custom-call(bf16[1024,768]{1,0:T(8,128)(2,1)} %get-tuple-element.121.turned, bf16[1024,256]{1,0:T(8,128)(2,1)} %fusion.15.grads, f32[1024,768]{1,0:T(8,128)} %copy.258.raw, f32[1024,2]{1,0:T(8,128)} %bitcast.278, ...), custom_call_target="tpu_custom_call" | custom-call | flops 402653184 | bytes 7864320 | tf_op jit(solution)/shard_map/attend_back/pallas_call | solution.py:403
  1002.6 33.0 %collective-permute-done.57 = bf16[2,8,64,512]{3,2,1,0:T(8,128)(2,1)S(1)} collective-permute-done((bf16[2,8,64,512]{3,2,1,0:T(8,128)(2,1)}, bf16[2,8,64,512]{3,2,1,0:T(8,128)(2,1)S(1)}, u32[]{:S(2)}, u32[]{:S(2)}) %collective-permute-start.57) | collective-permute-done | bytes 1048608 | tf_op jit(solution)/shard_map/ppermute | solution.py:511
  1044.3 18.7 %all-to-all-done.6.refs_0_ = bf16[4,3,512,512]{3,2,1,0:T(8,128)(2,1)} async-done(((bf16[4,3,512,512]{3,2,1,0:T(8,128)(2,1)}), bf16[4,3,512,512]{3,2,1,0:T(8,128)(2,1)}, u32[]{:S(2)}, u32[]{:S(2)}) %all-to-all-start.6) | async-done | bytes 6291488 | tf_op jit(solution)/shard_map/all_to_all | solution.py:754
  1089.1 20.1 %collective-permute-done.58 = bf16[2,9,64,512]{3,2,1,0:T(8,128)(2,1)} collective-permute-done((bf16[2,9,64,512]{3,2,1,0:T(8,128)(2,1)}, bf16[2,9,64,512]{3,2,1,0:T(8,128)(2,1)}, u32[]{:S(2)}, u32[]{:S(2)}) %collective-permute-start.58) | collective-permute-done | bytes 1179680 | tf_op jit(solution)/shard_map/ppermute | solution.py:511
  1125.7 22.8 %collective-permute-done.59 = bf16[2,128,2048]{2,1,0:T(8,128)(2,1)S(1)} collective-permute-done((bf16[2,128,2048]{2,1,0:T(8,128)(2,1)S(1)}, bf16[2,128,2048]{2,1,0:T(8,128)(2,1)S(1)}, u32[]{:S(2)}, u32[]{:S(2)}) %collective-permute-start.59) | collective-permute-done | bytes 1048608 | tf_op jit(solution)/shard_map/ppermute | solution.py:511
  (554 shorter events, 421.8 us)
Async XLA Ops:
  0.7 35.7 %collective-permute-start.7 = (bf16[128,2048]{1,0:T(8,128)(2,1)}, bf16[128,2048]{1,0:T(8,128)(2,1)S(1)}, u32[]{:S(2)}, u32[]{:S(2)}) collective-permute-start(bf16[128,2048]{1,0:T(8,128)(2,1)} %param.23), channel_id=1, source_target_pairs={{0,2},{1,3},{2,0},{3,1},{4,6},{5,7},{6,4},{7,5},{8,10},{9,11},{10,... | collective-permute-start | bytes 1572872 | tf_op jit(solution)/shard_map/ppermute | solution.py:511
  65.5 105.2 %all-to-all-start.1 = ((bf16[4,2,512,512]{3,2,1,0:T(8,128)(2,1)}), bf16[4,2,512,512]{3,2,1,0:T(8,128)(2,1)}, u32[]{:S(2)}, u32[]{:S(2)}) async-start(bf16[4,2,512,512]{3,2,1,0:T(8,128)(2,1)} %slice_weights.3), calls=%async_computation.1 | async-start | bytes 8388608 | tf_op jit(solution)/shard_map/all_to_all | solution.py:648
  98.8 48.0 %collective-permute-start.10 = (bf16[512,2048]{1,0:T(8,128)(2,1)}, bf16[512,2048]{1,0:T(8,128)(2,1)}, u32[]{:S(2)}, u32[]{:S(2)}) collective-permute-start(bf16[512,2048]{1,0:T(8,128)(2,1)} %constant_dynamic-update-slice_fusion.8.refs_1_), channel_id=1, source_target_pairs={{0,16},{4,20},{8,24},{12,28},{16,0},{20,4},{24,8},{28,12},{1,17},{... | collective-permute-start | bytes 6291464 | tf_op jit(solution)/shard_map/ppermute | solution.py:511
  100.4 47.7 %collective-permute-start.9 = (bf16[512,2048]{1,0:T(8,128)(2,1)}, bf16[512,2048]{1,0:T(8,128)(2,1)}, u32[]{:S(2)}, u32[]{:S(2)}) collective-permute-start(bf16[512,2048]{1,0:T(8,128)(2,1)} %constant_dynamic-update-slice_fusion.8.refs_1_), channel_id=1, source_target_pairs={{0,8},{4,12},{8,0},{12,4},{16,24},{20,28},{24,16},{28,20},{1,9},{5... | collective-permute-start | bytes 6291464 | tf_op jit(solution)/shard_map/ppermute | solution.py:511
  100.8 110.0 %collective-permute-start.14 = (bf16[1,64,2048]{2,1,0:T(8,128)(2,1)S(1)}, bf16[1,64,2048]{2,1,0:T(8,128)(2,1)S(1)}, u32[]{:S(2)}, u32[]{:S(2)}) collective-permute-start(bf16[1,64,2048]{2,1,0:T(8,128)(2,1)S(1)} %bitcast.309), channel_id=1, source_target_pairs={{0,2},{1,3},{2,0},{3,1},{4,6},{5,7},{6,4},{7,5},{8,10},{9,11},{10,... | collective-permute-start | bytes 786440 | tf_op jit(solution)/shard_map/ppermute | solution.py:511
  170.7 38.7 %collective-permute-start.11 = (bf16[1,8,64,768]{3,2,1,0:T(8,128)(2,1)S(1)}, bf16[1,8,64,768]{3,2,1,0:T(8,128)(2,1)S(1)}, u32[]{:S(2)}, u32[]{:S(2)}) collective-permute-start(bf16[1,8,64,768]{3,2,1,0:T(8,128)(2,1)S(1)} %bitcast.284), channel_id=1, source_target_pairs={{0,2},{1,3},{2,0},{3,1},{4,6},{5,7},{6,4},{7,5},{8,10},{9,11},{10,... | collective-permute-start | bytes 2359304 | tf_op jit(solution)/shard_map/ppermute | solution.py:511
  210.8 51.5 %collective-permute-start.12 = (bf16[2,8,64,768]{3,2,1,0:T(8,128)(2,1)}, bf16[2,8,64,768]{3,2,1,0:T(8,128)(2,1)}, u32[]{:S(2)}, u32[]{:S(2)}) collective-permute-start(bf16[2,8,64,768]{3,2,1,0:T(8,128)(2,1)} %pad_maximum_fusion.1), channel_id=1, source_target_pairs={{0,1},{1,0},{2,3},{3,2},{4,5},{5,4},{6,7},{7,6},{8,9},{9,8},{10,11... | collective-permute-start | bytes 4718600 | tf_op jit(solution)/shard_map/ppermute | solution.py:511
  210.8 47.2 %collective-permute-start.15 = (bf16[2,64,2048]{2,1,0:T(8,128)(2,1)S(1)}, bf16[2,64,2048]{2,1,0:T(8,128)(2,1)S(1)}, u32[]{:S(2)}, u32[]{:S(2)}) collective-permute-start(bf16[2,64,2048]{2,1,0:T(8,128)(2,1)S(1)} %pad_maximum_fusion.8), channel_id=1, source_target_pairs={{0,1},{1,0},{2,3},{3,2},{4,5},{5,4},{6,7},{7,6},{8,9},{9,8},{10,11... | collective-permute-start | bytes 1572872 | tf_op jit(solution)/shard_map/ppermute | solution.py:511
  260.8 47.4 %collective-permute-start.13 = (bf16[512,2048]{1,0:T(8,128)(2,1)}, bf16[512,2048]{1,0:T(8,128)(2,1)}, u32[]{:S(2)}, u32[]{:S(2)}) collective-permute-start(bf16[512,2048]{1,0:T(8,128)(2,1)} %constant_dynamic-update-slice_fusion.8.refs_1_), channel_id=1, source_target_pairs={{0,24},{4,28},{8,16},{12,20},{16,8},{20,12},{24,0},{28,4},{1,25},{... | collective-permute-start | bytes 6291464 | tf_op jit(solution)/shard_map/ppermute | solution.py:511
  264.4 154.4 %all-to-all-start.2 = ((bf16[4,3,512,512]{3,2,1,0:T(8,128)(2,1)}), bf16[4,3,512,512]{3,2,1,0:T(8,128)(2,1)}, u32[]{:S(2)}, u32[]{:S(2)}) async-start(bf16[4,3,512,512]{3,2,1,0:T(8,128)(2,1)} %slice_weights.4), calls=%async_computation.2 | async-start | bytes 12582912 | tf_op jit(solution)/shard_map/all_to_all | solution.py:648
  455.6 147.7 %all-to-all-start.3 = ((bf16[4,3,512,512]{3,2,1,0:T(8,128)(2,1)}), bf16[4,3,512,512]{3,2,1,0:T(8,128)(2,1)}, u32[]{:S(2)}, u32[]{:S(2)}) async-start(bf16[4,3,512,512]{3,2,1,0:T(8,128)(2,1)} %slice_weights.5), calls=%async_computation.3 | async-start | bytes 12582912 | tf_op jit(solution)/shard_map/all_to_all | solution.py:648
  461.0 51.8 %collective-permute-start.27 = (bf16[512,2176]{1,0:T(8,128)(2,1)}, bf16[512,2176]{1,0:T(8,128)(2,1)}, u32[]{:S(2)}, u32[]{:S(2)}) collective-permute-start(bf16[512,2176]{1,0:T(8,128)(2,1)} %constant_dynamic-update-slice_fusion.10.refs_1_), channel_id=1, source_target_pairs={{0,8},{4,12},{8,0},{12,4},{16,24},{20,28},{24,16},{28,20},{1,9},{5... | collective-permute-start | bytes 6684680 | tf_op jit(solution)/shard_map/ppermute | solution.py:511
  461.4 95.3 %collective-permute-start.29 = (bf16[512,2176]{1,0:T(8,128)(2,1)}, bf16[512,2176]{1,0:T(8,128)(2,1)S(1)}, u32[]{:S(2)}, u32[]{:S(2)}) collective-permute-start(bf16[512,2176]{1,0:T(8,128)(2,1)} %constant_dynamic-update-slice_fusion.10.refs_1_), channel_id=1, source_target_pairs={{0,16},{4,20},{8,24},{12,28},{16,0},{20,4},{24,8},{28,12},{1,17},{... | collective-permute-start | bytes 6684680 | tf_op jit(solution)/shard_map/ppermute | solution.py:511
  463.1 93.6 %collective-permute-start.31 = (bf16[512,2176]{1,0:T(8,128)(2,1)}, bf16[512,2176]{1,0:T(8,128)(2,1)S(1)}, u32[]{:S(2)}, u32[]{:S(2)}) collective-permute-start(bf16[512,2176]{1,0:T(8,128)(2,1)} %constant_dynamic-update-slice_fusion.10.refs_1_), channel_id=1, source_target_pairs={{0,24},{4,28},{8,16},{12,20},{16,8},{20,12},{24,0},{28,4},{1,25},{... | collective-permute-start | bytes 6684680 | tf_op jit(solution)/shard_map/ppermute | solution.py:511
  464.6 103.6 %collective-permute-start.26 = (bf16[512,2176]{1,0:T(8,128)(2,1)}, bf16[512,2176]{1,0:T(8,128)(2,1)}, u32[]{:S(2)}, u32[]{:S(2)}) collective-permute-start(bf16[512,2176]{1,0:T(8,128)(2,1)} %constant_dynamic-update-slice_fusion.10.refs_1_), channel_id=1, source_target_pairs={{0,4},{4,0},{8,12},{12,8},{16,20},{20,16},{24,28},{28,24},{1,5},{5... | collective-permute-start | bytes 6684680 | tf_op jit(solution)/shard_map/ppermute | solution.py:511
  512.8 55.4 %collective-permute-start.28 = (bf16[512,2176]{1,0:T(8,128)(2,1)}, bf16[512,2176]{1,0:T(8,128)(2,1)}, u32[]{:S(2)}, u32[]{:S(2)}) collective-permute-start(bf16[512,2176]{1,0:T(8,128)(2,1)} %collective-permute-done.27.refs_2_), channel_id=1, source_target_pairs={{0,4},{4,0},{8,12},{12,8},{16,20},{20,16},{24,28},{28,24},{1,5},{5... | collective-permute-start | bytes 6684680 | tf_op jit(solution)/shard_map/ppermute | solution.py:511
  603.3 99.5 %all-to-all-start.4 = ((bf16[4,2,512,512]{3,2,1,0:T(8,128)(2,1)}), bf16[4,2,512,512]{3,2,1,0:T(8,128)(2,1)}, u32[]{:S(2)}, u32[]{:S(2)}) async-start(bf16[4,2,512,512]{3,2,1,0:T(8,128)(2,1)} %get-tuple-element.122), calls=%async_computation.4 | async-start | bytes 8388608 | tf_op jit(solution)/shard_map/all_to_all | solution.py:754
  702.7 155.0 %all-to-all-start.5 = ((bf16[4,3,512,512]{3,2,1,0:T(8,128)(2,1)}), bf16[4,3,512,512]{3,2,1,0:T(8,128)(2,1)}, u32[]{:S(2)}, u32[]{:S(2)}) async-start(bf16[4,3,512,512]{3,2,1,0:T(8,128)(2,1)} %get-tuple-element.124), calls=%async_computation.5 | async-start | bytes 12582912 | tf_op jit(solution)/shard_map/all_to_all | solution.py:754
  727.3 35.9 %collective-permute-start.38 = (bf16[512,2176]{1,0:T(8,128)(2,1)}, bf16[512,2176]{1,0:T(8,128)(2,1)S(1)}, u32[]{:S(2)}, u32[]{:S(2)}) collective-permute-start(bf16[512,2176]{1,0:T(8,128)(2,1)} %get-tuple-element.114), channel_id=1, source_target_pairs={{0,4},{4,0},{8,12},{12,8},{16,20},{20,16},{24,28},{28,24},{1,5},{5... | collective-permute-start | bytes 6684680 | tf_op jit(solution)/shard_map/ppermute | solution.py:511
  741.7 52.5 %collective-permute-start.41 = (bf16[512,2176]{1,0:T(8,128)(2,1)}, bf16[512,2176]{1,0:T(8,128)(2,1)S(1)}, u32[]{:S(2)}, u32[]{:S(2)}) collective-permute-start(bf16[512,2176]{1,0:T(8,128)(2,1)} %add_convert_fusion.1), channel_id=1, source_target_pairs={{0,24},{4,28},{8,16},{12,20},{16,8},{20,12},{24,0},{28,4},{1,25},{... | collective-permute-start | bytes 6684680 | tf_op jit(solution)/shard_map/ppermute | solution.py:511
  745.1 95.8 %collective-permute-start.40 = (bf16[512,2176]{1,0:T(8,128)(2,1)}, bf16[512,2176]{1,0:T(8,128)(2,1)S(1)}, u32[]{:S(2)}, u32[]{:S(2)}) collective-permute-start(bf16[512,2176]{1,0:T(8,128)(2,1)} %add_convert_fusion.2), channel_id=1, source_target_pairs={{0,16},{4,20},{8,24},{12,28},{16,0},{20,4},{24,8},{28,12},{1,17},{... | collective-permute-start | bytes 6684680 | tf_op jit(solution)/shard_map/ppermute | solution.py:511
  750.3 103.0 %collective-permute-start.39 = (bf16[512,2176]{1,0:T(8,128)(2,1)}, bf16[512,2176]{1,0:T(8,128)(2,1)}, u32[]{:S(2)}, u32[]{:S(2)}) collective-permute-start(bf16[512,2176]{1,0:T(8,128)(2,1)} %add_convert_fusion.3), channel_id=1, source_target_pairs={{0,8},{4,12},{8,0},{12,4},{16,24},{20,28},{24,16},{28,20},{1,9},{5... | collective-permute-start | bytes 6684680 | tf_op jit(solution)/shard_map/ppermute | solution.py:511
  763.2 94.5 %collective-permute-start.36 = (bf16[512,2048]{1,0:T(8,128)(2,1)}, bf16[512,2048]{1,0:T(8,128)(2,1)}, u32[]{:S(2)}, u32[]{:S(2)}) collective-permute-start(bf16[512,2048]{1,0:T(8,128)(2,1)} %get-tuple-element.110), channel_id=1, source_target_pairs={{0,4},{4,0},{8,12},{12,8},{16,20},{20,16},{24,28},{28,24},{1,5},{5... | collective-permute-start | bytes 6291464 | tf_op jit(solution)/shard_map/ppermute | solution.py:511
  763.2 94.5 %collective-permute-start.37 = (bf16[512,2048]{1,0:T(8,128)(2,1)}, bf16[512,2048]{1,0:T(8,128)(2,1)}, u32[]{:S(2)}, u32[]{:S(2)}) collective-permute-start(bf16[512,2048]{1,0:T(8,128)(2,1)} %get-tuple-element.112), channel_id=1, source_target_pairs={{0,4},{4,0},{8,12},{12,8},{16,20},{20,16},{24,28},{28,24},{1,5},{5... | collective-permute-start | bytes 6291464 | tf_op jit(solution)/shard_map/ppermute | solution.py:511
  794.1 63.5 %collective-permute-start.43 = (bf16[512,2048]{1,0:T(8,128)(2,1)}, bf16[512,2048]{1,0:T(8,128)(2,1)}, u32[]{:S(2)}, u32[]{:S(2)}) collective-permute-start(bf16[512,2048]{1,0:T(8,128)(2,1)} %get-tuple-element.117), channel_id=1, source_target_pairs={{0,4},{4,0},{8,12},{12,8},{16,20},{20,16},{24,28},{28,24},{1,5},{5... | collective-permute-start | bytes 6291464 | tf_op jit(solution)/shard_map/ppermute | solution.py:511
  867.5 53.8 %collective-permute-start.44 = (bf16[512,2048]{1,0:T(8,128)(2,1)}, bf16[512,2048]{1,0:T(8,128)(2,1)}, u32[]{:S(2)}, u32[]{:S(2)}) collective-permute-start(bf16[512,2048]{1,0:T(8,128)(2,1)} %add_convert_fusion.6), channel_id=1, source_target_pairs={{0,16},{4,20},{8,24},{12,28},{16,0},{20,4},{24,8},{28,12},{1,17},{... | collective-permute-start | bytes 6291464 | tf_op jit(solution)/shard_map/ppermute | solution.py:511
  869.0 52.3 %collective-permute-start.42 = (bf16[512,2048]{1,0:T(8,128)(2,1)}, bf16[512,2048]{1,0:T(8,128)(2,1)}, u32[]{:S(2)}, u32[]{:S(2)}) collective-permute-start(bf16[512,2048]{1,0:T(8,128)(2,1)} %add_convert_fusion.7), channel_id=1, source_target_pairs={{0,8},{4,12},{8,0},{12,4},{16,24},{20,28},{24,16},{28,20},{1,9},{5... | collective-permute-start | bytes 6291464 | tf_op jit(solution)/shard_map/ppermute | solution.py:511
  897.2 165.8 %all-to-all-start.6 = ((bf16[4,3,512,512]{3,2,1,0:T(8,128)(2,1)}), bf16[4,3,512,512]{3,2,1,0:T(8,128)(2,1)}, u32[]{:S(2)}, u32[]{:S(2)}) async-start(bf16[4,3,512,512]{3,2,1,0:T(8,128)(2,1)} %get-tuple-element.139), calls=%async_computation.6 | async-start | bytes 12582912 | tf_op jit(solution)/shard_map/all_to_all | solution.py:754
  983.1 52.5 %collective-permute-start.57 = (bf16[2,8,64,512]{3,2,1,0:T(8,128)(2,1)}, bf16[2,8,64,512]{3,2,1,0:T(8,128)(2,1)S(1)}, u32[]{:S(2)}, u32[]{:S(2)}) collective-permute-start(bf16[2,8,64,512]{3,2,1,0:T(8,128)(2,1)} %get-tuple-element.140), channel_id=1, source_target_pairs={{0,1},{1,0},{2,3},{3,2},{4,5},{5,4},{6,7},{7,6},{8,9},{9,8},{10,11... | collective-permute-start | bytes 3145736 | tf_op jit(solution)/shard_map/ppermute | solution.py:511
  997.4 91.7 %collective-permute-start.56 = (bf16[512,2048]{1,0:T(8,128)(2,1)}, bf16[512,2048]{1,0:T(8,128)(2,1)}, u32[]{:S(2)}, u32[]{:S(2)}) collective-permute-start(bf16[512,2048]{1,0:T(8,128)(2,1)} %add_convert_fusion.5), channel_id=1, source_target_pairs={{0,24},{4,28},{8,16},{12,20},{16,8},{20,12},{24,0},{28,4},{1,25},{... | collective-permute-start | bytes 6291464 | tf_op jit(solution)/shard_map/ppermute | solution.py:511
  1039.0 45.5 %collective-permute-start.66 = (bf16[1,8,64,512]{3,2,1,0:T(8,128)(2,1)}, bf16[1,8,64,512]{3,2,1,0:T(8,128)(2,1)}, u32[]{:S(2)}, u32[]{:S(2)}) collective-permute-start(bf16[1,8,64,512]{3,2,1,0:T(8,128)(2,1)} %slice.626), channel_id=1, source_target_pairs={{0,2},{1,3},{2,0},{3,1},{4,6},{5,7},{6,4},{7,5},{8,10},{9,11},{10,... | collective-permute-start | bytes 1572872 | tf_op jit(solution)/shard_map/ppermute | solution.py:511
  1115.3 33.3 %collective-permute-start.59 = (bf16[2,128,2048]{2,1,0:T(8,128)(2,1)S(1)}, bf16[2,128,2048]{2,1,0:T(8,128)(2,1)S(1)}, u32[]{:S(2)}, u32[]{:S(2)}) collective-permute-start(bf16[2,128,2048]{2,1,0:T(8,128)(2,1)S(1)} %bitcast.308), channel_id=1, source_target_pairs={{0,1},{1,0},{2,3},{3,2},{4,5},{5,4},{6,7},{7,6},{8,9},{9,8},{10,11... | collective-permute-start | bytes 3145736 | tf_op jit(solution)/shard_map/ppermute | solution.py:511
  (139 other events, 2299.2 us)
